TPU v7x, 32 devices: a whole 2x2x4 slice. The times are simulated.
32 devices in a mesh: dp: 8 (over z, y), vocab: 4 (over x, core).
Axes of the slice: x: 2, y: 2, z: 4, core: 2. Of those that a mesh axis runs over, the one named last changes fastest.
Arguments:
- features: bfloat16 [32, 384, 32], P(('dp', 'vocab')), may hold values from -6 to 6
- scale_ids: int32 [32, 384], P(('dp', 'vocab')), may hold values from 0 to 10, as said below
- class_ids: int32 [32, 8], P(('dp', 'vocab')), may hold values from 0 to 1000
- code_targets: int32 [32, 384], P(('dp', 'vocab')), may hold values from 0 to 4095
- token_weights: float32 [32, 384], P(('dp', 'vocab')), may hold values from 0.5 to 2
- attn_weight: float32 [1024, 4096], P(('dp', 'vocab')), may hold values from -0.1875 to 0.1875
- attn_moment: float32 [1024, 4096], P(('dp', 'vocab')), may hold values from -1.1920929e-07 to 1.1920929e-07
- attn_square: float32 [1024, 4096], P(('dp', 'vocab')), may hold values from 1.9514925e-15 to 7.79113e-15
- mlp_weight: float32 [2, 1024, 4096], P(None, ('dp', 'vocab')), may hold values from -0.125 to 0.125
- mlp_moment: float32 [2, 1024, 4096], P(None, ('dp', 'vocab')), may hold values from -1.1920929e-07 to 1.1920929e-07
- mlp_square: float32 [2, 1024, 4096], P(None, ('dp', 'vocab')), may hold values from 1.9514925e-15 to 7.79113e-15
- ada_weight: float32 [1024, 8192], P(('dp', 'vocab')), may hold values from -0.1875 to 0.1875
- ada_moment: float32 [1024, 8192], P(('dp', 'vocab')), may hold values from -1.3038516e-08 to 1.3038516e-08
- ada_square: float32 [1024, 8192], P(('dp', 'vocab')), may hold values from 2.9680494e-17 to 1.1872198e-16
- embed_weight: float32 [1723, 1024], P(None, ('dp', 'vocab')), may hold values from -0.625 to 0.625
- embed_moment: float32 [1723, 1024], P(None, ('dp', 'vocab')), may hold values from -3.7252903e-08 to 3.7252903e-08
- embed_square: float32 [1723, 1024], P(None, ('dp', 'vocab')), may hold values from 1.7437292e-16 to 7.049118e-16
- gains_weight: float32 [23, 1024], P(None, ('dp', 'vocab')), may hold values from -0.8 to 1.5
- gains_moment: float32 [23, 1024], P(None, ('dp', 'vocab')), may hold values from -1.1920929e-06 to 1.1920929e-06
- gains_square: float32 [23, 1024], P(None, ('dp', 'vocab')), may hold values from 1.9514926e-13 to 7.79113e-13
- head_weight: float32 [1024, 4096], P('dp', 'vocab'), may hold values from -0.1875 to 0.1875
- head_moment: float32 [1024, 4096], P('dp', 'vocab'), may hold values from -1.1920929e-07 to 1.1920929e-07
- head_square: float32 [1024, 4096], P('dp', 'vocab'), may hold values from 1.9514925e-15 to 7.79113e-15
Outputs:
- attn_updated: float32 [1024, 4096], P(('dp', 'vocab'))
- attn_moment_new: float32 [1024, 4096], P(('dp', 'vocab'))
- attn_square_new: float32 [1024, 4096], P(('dp', 'vocab'))
- attn_copy: bfloat16 [1024, 4096], P(('dp', 'vocab'))
- mlp_updated: float32 [2, 1024, 4096], P(None, ('dp', 'vocab'))
- mlp_moment_new: float32 [2, 1024, 4096], P(None, ('dp', 'vocab'))
- mlp_square_new: float32 [2, 1024, 4096], P(None, ('dp', 'vocab'))
- mlp_copy: bfloat16 [2, 1024, 4096], P(None, ('dp', 'vocab'))
- ada_updated: float32 [1024, 8192], P(('dp', 'vocab'))
- ada_moment_new: float32 [1024, 8192], P(('dp', 'vocab'))
- ada_square_new: float32 [1024, 8192], P(('dp', 'vocab'))
- ada_copy: bfloat16 [1024, 8192], P(('dp', 'vocab'))
- embed_updated: float32 [1723, 1024], P(None, ('dp', 'vocab'))
- embed_moment_new: float32 [1723, 1024], P(None, ('dp', 'vocab'))
- embed_square_new: float32 [1723, 1024], P(None, ('dp', 'vocab'))
- embed_copy: bfloat16 [1723, 1024], P(None, ('dp', 'vocab'))
- gains_updated: float32 [23, 1024], P(None, ('dp', 'vocab'))
- gains_moment_new: float32 [23, 1024], P(None, ('dp', 'vocab'))
- gains_square_new: float32 [23, 1024], P(None, ('dp', 'vocab'))
- gains_copy: bfloat16 [23, 1024], P(None, ('dp', 'vocab'))
- head_updated: float32 [1024, 4096], P('dp', 'vocab')
- head_moment_new: float32 [1024, 4096], P('dp', 'vocab')
- head_square_new: float32 [1024, 4096], P('dp', 'vocab')
- head_copy: bfloat16 [1024, 4096], P('dp', 'vocab')
- grad_norm: float32 [], replicated
- loss_sum: float32 [], replicated
- token_count: float32 [], replicated
Inputs may be any that keep to these rules, and one draw needn't show every extreme that they name: `scale_ids`: each row is packed with whole images followed by padding; an image starts with scale 0 and runs through consecutive scales holding 1, 4, 9, 16, 25, 36, 64, 100, 169, 256 tokens, so its ids never fall; 10 marks padding, and every row ends with padding.
All inputs are finite; a program needn't handle non-finite values.
Results may differ from a plain program's by a relative error of at most 0.017.
Values may be sent and summed in bfloat16 or wider, within the bound.
No kernel may reach another device: no remote copies, remote signals or barrier semaphores. Data moves between devices by JAX's collectives and lax.ppermute only.
A program may use at most 320 MiB of HBM per device.

v0:
```python
import jax
import jax.numpy as jnp
from jax import lax
from jax.sharding import PartitionSpec as P

HEADS = 16
HEAD_DIM = 64
FF = 4096
V = 4096
CHANNELS = 32
CLASSES = 1001
POSITIONS = 680
LEVELS = 10
MAXIMG = 8
STEPS = 10


EPS_NORM = 1e-06
BETA_ONE = 0.9
BETA_TWO = 0.95
ADAM_EPS = 1e-08
DECAY = 0.05
CLIP_NORM = 0.001
RATES = (0.03, 0.03, 0.03, 0.15, 0.4, 0.03)
NEG_FILL = -1e30
GROUP_HEADS = 4


def joined(value, axis, join):
    pieces = jax.tree.map(lambda part: lax.all_gather(part, axis), value)
    head = jax.tree.map(lambda part: part[0], pieces)
    tail = jax.tree.map(lambda part: part[1:], pieces)
    so_far, _ = lax.scan(lambda so_far, slab: (join(so_far, slab), None), head, tail)
    return so_far


def matmul(left, right):
    return jnp.dot(left, right, preferred_element_type=jnp.float32)


def matmul_tn(left, right):
    return lax.dot_general(
        left, right, (((0,), (0,)), ((), ())), preferred_element_type=jnp.float32
    )


def matmul_nt(left, right):
    return lax.dot_general(
        left, right, (((1,), (1,)), ((), ())), preferred_element_type=jnp.float32
    )


def precise(left, right):
    return jnp.dot(left, right, precision=lax.Precision.HIGHEST)


def precise_tn(left, right):
    return lax.dot_general(left, right, (((0,), (0,)), ((), ())), precision=lax.Precision.HIGHEST)


def normalize(values):
    center = values - jnp.mean(values, axis=-1, keepdims=True)
    return center * lax.rsqrt(jnp.mean(center * center, axis=-1, keepdims=True) + EPS_NORM)


def modulate(values, shifts, scales):
    return normalize(values) * (1.0 + scales) + shifts


def head_norm(values, gain_vec):
    return (
        values * lax.rsqrt(jnp.mean(values * values, axis=-1, keepdims=True) + EPS_NORM) * gain_vec
    )


def gelu_tanh(values):
    return jax.nn.gelu(values, approximate=True)


def layout(scale_row):
    position = jnp.arange(scale_row.shape[0], dtype=jnp.int32)
    opening = scale_row == 0
    image_id = jnp.cumsum(opening.astype(jnp.int32)) - 1
    starts_at = lax.cummax(jnp.where(opening, position, 0), axis=0)
    return (image_id, position - starts_at, scale_row < LEVELS)


def join_stats(first_part, second_part):
    row_max = jnp.maximum(first_part[0], second_part[0])
    totals = first_part[1] * jnp.exp(first_part[0] - row_max) + second_part[1] * jnp.exp(
        second_part[0] - row_max
    )
    return (row_max, totals, first_part[2] + second_part[2])


def split_groups(values):
    length = values.shape[0]
    return jnp.moveaxis(values.reshape(length, HEADS // GROUP_HEADS, GROUP_HEADS, HEAD_DIM), 1, 0)


def join_groups(values):
    return jnp.moveaxis(values, 0, 1).reshape(values.shape[1], HEADS, HEAD_DIM)


def soft_block(q_group, k_group, allowed):
    scores = jnp.einsum(
        "qhd,khd->hqk", q_group, k_group, preferred_element_type=jnp.float32
    ) * HEAD_DIM ** (-0.5)
    scores = jnp.where(allowed[None], scores, NEG_FILL)
    exp_terms = jnp.exp(scores - jnp.max(scores, axis=-1, keepdims=True))
    return exp_terms / jnp.sum(exp_terms, axis=-1, keepdims=True)


def attention_parts(resid_in, shifts, scales, attn_mats, gain_rows, allowed):
    length, model_width = resid_in.shape
    u_in = modulate(resid_in, shifts, scales).astype(jnp.bfloat16)
    qkv_bias = jnp.concatenate([gain_rows[1], jnp.zeros_like(gain_rows[1]), gain_rows[2]]).astype(
        jnp.float32
    )
    qkv_out = matmul(u_in, attn_mats[:, : 3 * model_width]) + qkv_bias
    queries, keys, values = jnp.split(qkv_out, 3, axis=1)
    split_shape = (length, HEADS, HEAD_DIM)
    queries = queries.reshape(split_shape)
    keys = keys.reshape(split_shape)
    q_gain = gain_rows[5].astype(jnp.float32).reshape(HEADS, HEAD_DIM)
    k_gain = gain_rows[6].astype(jnp.float32).reshape(HEADS, HEAD_DIM)
    q_norm = head_norm(queries, q_gain).astype(jnp.bfloat16)
    k_norm = head_norm(keys, k_gain).astype(jnp.bfloat16)
    v_low = values.reshape(split_shape).astype(jnp.bfloat16)

    def mix_block(item):
        q_group, k_group, v_group = item
        soft_w = soft_block(q_group, k_group, allowed)
        return jnp.einsum(
            "hqk,khd->qhd", soft_w.astype(jnp.bfloat16), v_group, preferred_element_type=jnp.float32
        )

    mixed = lax.map(mix_block, (split_groups(q_norm), split_groups(k_norm), split_groups(v_low)))
    mixture = join_groups(mixed).reshape(length, model_width).astype(jnp.bfloat16)
    attn_out = matmul(mixture, attn_mats[:, 3 * model_width :]) + gain_rows[3].astype(jnp.float32)
    return {
        "u_in": u_in,
        "queries": queries,
        "keys": keys,
        "q_gain": q_gain,
        "k_gain": k_gain,
        "q_norm": q_norm,
        "k_norm": k_norm,
        "v_low": v_low,
        "mixture": mixture,
        "attn_out": attn_out,
    }


def attention_back(resid_in, shifts, scales, attn_mats, gain_rows, allowed, d_out):
    length, model_width = resid_in.shape
    parts = attention_parts(resid_in, shifts, scales, attn_mats, gain_rows, allowed)
    d_low = d_out.astype(jnp.bfloat16)
    d_proj = matmul_tn(parts["mixture"], d_low)
    d_bias_out = jnp.sum(d_low.astype(jnp.float32), axis=0)
    d_mix = (
        matmul_nt(d_low, attn_mats[:, 3 * model_width :])
        .astype(jnp.bfloat16)
        .reshape(length, HEADS, HEAD_DIM)
    )

    def back_block(item):
        q_group, k_group, v_group, dm_group = item
        soft_w = soft_block(q_group, k_group, allowed)
        soft_low = soft_w.astype(jnp.bfloat16)
        d_values = jnp.einsum(
            "hqk,qhd->khd", soft_low, dm_group, preferred_element_type=jnp.float32
        )
        d_soft = jnp.einsum("qhd,khd->hqk", dm_group, v_group, preferred_element_type=jnp.float32)
        d_scores = (soft_w * (d_soft - jnp.sum(d_soft * soft_w, axis=-1, keepdims=True))).astype(
            jnp.bfloat16
        )
        d_qn = jnp.einsum(
            "hqk,khd->qhd", d_scores, k_group, preferred_element_type=jnp.float32
        ) * HEAD_DIM ** (-0.5)
        d_kn = jnp.einsum(
            "hqk,qhd->khd", d_scores, q_group, preferred_element_type=jnp.float32
        ) * HEAD_DIM ** (-0.5)
        return (d_qn, d_kn, d_values)

    d_qn, d_kn, d_values = lax.map(
        back_block,
        (
            split_groups(parts["q_norm"]),
            split_groups(parts["k_norm"]),
            split_groups(parts["v_low"]),
            split_groups(d_mix),
        ),
    )
    d_qn, d_kn, d_values = (join_groups(d_qn), join_groups(d_kn), join_groups(d_values))
    _, q_back = jax.vjp(head_norm, parts["queries"], parts["q_gain"])
    d_queries, d_qgain = q_back(d_qn)
    _, k_back = jax.vjp(head_norm, parts["keys"], parts["k_gain"])
    d_keys, d_kgain = k_back(d_kn)
    d_qkv = jnp.concatenate(
        [
            d_queries.reshape(length, model_width),
            d_keys.reshape(length, model_width),
            d_values.reshape(length, model_width),
        ],
        axis=1,
    ).astype(jnp.bfloat16)
    d_wqkv = matmul_tn(parts["u_in"], d_qkv)
    d_qkv_sum = jnp.sum(d_qkv.astype(jnp.float32), axis=0)
    d_u = matmul_nt(d_qkv, attn_mats[:, : 3 * model_width])
    _, mod_back = jax.vjp(modulate, resid_in, shifts, scales)
    d_resid, d_shifts, d_scales = mod_back(d_u)
    return (
        parts["attn_out"],
        jnp.concatenate([d_wqkv, d_proj], axis=1),
        d_qkv_sum,
        d_bias_out,
        d_qgain.reshape(-1),
        d_kgain.reshape(-1),
        d_resid,
        d_shifts,
        d_scales,
    )


def mlp_parts(resid_mid, shifts, scales, mlp_mats, gain_rows, ff_rows):
    u_in = modulate(resid_mid, shifts, scales).astype(jnp.bfloat16)
    hidden = matmul(u_in, mlp_mats[0]) + gain_rows[7 : 7 + ff_rows].astype(jnp.float32).reshape(-1)
    active = gelu_tanh(hidden).astype(jnp.bfloat16)
    mlp_out = matmul_nt(active, mlp_mats[1]) + gain_rows[4].astype(jnp.float32)
    return (u_in, hidden, active, mlp_out)


def mlp_back(resid_mid, shifts, scales, mlp_mats, gain_rows, ff_rows, d_out):
    u_in, hidden, active, mlp_out = mlp_parts(
        resid_mid, shifts, scales, mlp_mats, gain_rows, ff_rows
    )
    d_low = d_out.astype(jnp.bfloat16)
    d_down = matmul_tn(d_low, active)
    d_bias_down = jnp.sum(d_low.astype(jnp.float32), axis=0)
    d_active = matmul(d_low, mlp_mats[1])
    _, gelu_back = jax.vjp(gelu_tanh, hidden)
    d_hidden = gelu_back(d_active)[0].astype(jnp.bfloat16)
    d_up = matmul_tn(u_in, d_hidden)
    d_bias_up = jnp.sum(d_hidden.astype(jnp.float32), axis=0)
    d_u = matmul_nt(d_hidden, mlp_mats[0])
    _, mod_back = jax.vjp(modulate, resid_mid, shifts, scales)
    d_resid, d_shifts, d_scales = mod_back(d_u)
    return (mlp_out, d_up, d_bias_up, d_down, d_bias_down, d_resid, d_shifts, d_scales)


def adam_step(weight, moment, square, gradient, clip_factor, step_rate):
    gradient = gradient * clip_factor
    moment = BETA_ONE * moment + (1.0 - BETA_ONE) * gradient
    square = BETA_TWO * square + (1.0 - BETA_TWO) * gradient * gradient
    first_hat = moment / (1.0 - BETA_ONE**STEPS)
    second_hat = square / (1.0 - BETA_TWO**STEPS)
    weight = weight - step_rate * (first_hat / (jnp.sqrt(second_hat) + ADAM_EPS) + DECAY * weight)
    return (weight, moment, square, weight.astype(jnp.bfloat16))


def per_device(
    features,
    scale_ids,
    class_ids,
    code_targets,
    token_weights,
    attn_weight,
    attn_moment,
    attn_square,
    mlp_weight,
    mlp_moment,
    mlp_square,
    ada_weight,
    ada_moment,
    ada_square,
    embed_weight,
    embed_moment,
    embed_square,
    gains_weight,
    gains_moment,
    gains_square,
    head_weight,
    head_moment,
    head_square,
):
    attn_mats, mlp_mats, ada_mats, embedding, gain_rows = (
        lax.all_gather(attn_weight.astype(jnp.bfloat16), ("dp", "vocab"), axis=0, tiled=True),
        lax.all_gather(mlp_weight.astype(jnp.bfloat16), ("dp", "vocab"), axis=1, tiled=True),
        lax.all_gather(ada_weight.astype(jnp.bfloat16), ("dp", "vocab"), axis=0, tiled=True),
        lax.all_gather(embed_weight.astype(jnp.bfloat16), ("dp", "vocab"), axis=1, tiled=True),
        lax.all_gather(gains_weight.astype(jnp.bfloat16), ("dp", "vocab"), axis=1, tiled=True),
    )
    head_local = lax.all_gather(head_weight.astype(jnp.bfloat16), "dp", axis=0, tiled=True)
    scale_row = scale_ids[0]
    image_id, inside, counted = layout(scale_row)
    counted = counted.astype(jnp.float32)
    total_count = lax.psum(jnp.sum(counted), ("dp", "vocab"))
    length = scale_row.shape[0]
    model_width = attn_mats.shape[0]
    ff_rows = FF // model_width
    ada_at = 7 + ff_rows
    head_at = ada_at + 8
    off_level = CLASSES + POSITIONS
    off_word = off_level + LEVELS
    feat_row = features[0]
    pos_hot = (inside[:, None] == jnp.arange(POSITIONS, dtype=jnp.int32)[None, :]).astype(
        jnp.bfloat16
    )
    level_hot = (scale_row[:, None] == jnp.arange(LEVELS, dtype=jnp.int32)[None, :]).astype(
        jnp.bfloat16
    )
    resid_in = matmul(feat_row, embedding[off_word : off_word + CHANNELS]) + gain_rows[0].astype(
        jnp.float32
    )
    resid_in = resid_in + matmul(pos_hot, embedding[CLASSES:off_level])
    resid_in = resid_in + matmul(level_hot, embedding[off_level:off_word])
    class_hot = (class_ids[0][:, None] == jnp.arange(CLASSES, dtype=jnp.int32)[None, :]).astype(
        jnp.bfloat16
    )
    class_vec = matmul(class_hot, embedding[:CLASSES])
    class_act = jax.nn.silu(class_vec).astype(jnp.bfloat16)
    modulation = matmul(class_act, ada_mats) + gain_rows[ada_at:head_at].astype(
        jnp.float32
    ).reshape(-1)
    image_hot = (image_id[:, None] == jnp.arange(MAXIMG, dtype=jnp.int32)[None, :]).astype(
        jnp.float32
    )
    pieces = jnp.split(precise(image_hot, modulation), 8, axis=1)
    allowed = (image_id[:, None] == image_id[None, :]) & (scale_row[None, :] <= scale_row[:, None])
    attn_first = attention_parts(resid_in, pieces[0], pieces[1], attn_mats, gain_rows, allowed)
    resid_mid = resid_in + pieces[2] * attn_first["attn_out"]
    mlp_first = mlp_parts(resid_mid, pieces[3], pieces[4], mlp_mats, gain_rows, ff_rows)
    resid_out = resid_mid + pieces[5] * mlp_first[3]
    head_in = modulate(resid_out, pieces[6], pieces[7]).astype(jnp.bfloat16)
    head_bias = gain_rows[head_at:].astype(jnp.float32).reshape(-1)
    weighted = token_weights[0] * counted
    member = lax.axis_index("vocab")
    rows_all = lax.all_gather(head_in, "vocab", axis=0, tiled=True)
    row_info = lax.all_gather(
        jnp.stack([code_targets[0].astype(jnp.float32), weighted]), "vocab", axis=1, tiled=True
    )
    code_span = head_local.shape[1]
    code_start = member * code_span
    logits = matmul(rows_all, head_local) + lax.dynamic_slice_in_dim(
        head_bias, code_start, code_span
    )
    local_max = jnp.max(logits, axis=1)
    exp_sums = jnp.sum(jnp.exp(logits - local_max[:, None]), axis=1)
    is_target = (
        jnp.arange(code_span, dtype=jnp.int32)[None, :] + code_start
        == row_info[0].astype(jnp.int32)[:, None]
    ).astype(jnp.float32)
    picked = jnp.sum(is_target * logits, axis=1)
    row_max, totals, target_logit = joined((local_max, exp_sums, picked), "vocab", join_stats)
    log_total = row_max + jnp.log(totals)
    loss_part = jnp.sum(
        lax.dynamic_slice_in_dim(row_info[1] * (log_total - target_logit), member * length, length)
    )
    row_coef = row_info[1] / total_count
    d_logits = (row_coef[:, None] * (jnp.exp(logits - log_total[:, None]) - is_target)).astype(
        jnp.bfloat16
    )
    d_head_in = lax.psum_scatter(
        matmul_nt(d_logits, head_local), "vocab", scatter_dimension=0, tiled=True
    )
    head_full = matmul_tn(rows_all, d_logits)
    bias_grad = lax.dynamic_update_slice(
        jnp.zeros((V,), jnp.float32), jnp.sum(d_logits.astype(jnp.float32), axis=0), (code_start,)
    )
    head_grad = lax.psum_scatter(
        head_full.astype(jnp.bfloat16), "dp", scatter_dimension=0, tiled=True
    ).astype(jnp.float32)
    _, head_back = jax.vjp(modulate, resid_out, pieces[6], pieces[7])
    d_resid_out, d_shift_head, d_scale_head = head_back(d_head_in)
    mlp_out, d_up, d_bias_up, d_down, d_bias_down, d_mid_branch, d_shift_two, d_scale_two = (
        mlp_back(
            resid_mid, pieces[3], pieces[4], mlp_mats, gain_rows, ff_rows, pieces[5] * d_resid_out
        )
    )
    d_mlp = jnp.stack([d_up, d_down])
    d_gate_two = d_resid_out * mlp_out
    d_resid_mid = d_resid_out + d_mid_branch
    (
        attn_out,
        d_attn,
        d_qkv_sum,
        d_bias_out,
        d_qgain,
        d_kgain,
        d_in_branch,
        d_shift_one,
        d_scale_one,
    ) = attention_back(
        resid_in, pieces[0], pieces[1], attn_mats, gain_rows, allowed, pieces[2] * d_resid_mid
    )
    d_gate_one = d_resid_mid * attn_out
    d_resid_in = d_resid_mid + d_in_branch
    d_token = jnp.concatenate(
        [
            d_shift_one,
            d_scale_one,
            d_gate_one,
            d_shift_two,
            d_scale_two,
            d_gate_two,
            d_shift_head,
            d_scale_head,
        ],
        axis=1,
    )
    d_mod = precise_tn(image_hot, d_token).astype(jnp.bfloat16)
    d_ada = matmul_tn(class_act, d_mod)
    d_ada_bias = jnp.sum(d_mod.astype(jnp.float32), axis=0)
    d_class_act = matmul_nt(d_mod, ada_mats)
    _, silu_back = jax.vjp(jax.nn.silu, class_vec)
    d_class_vec = silu_back(d_class_act)[0]
    d_embed = jnp.concatenate(
        [
            precise_tn(class_hot.astype(jnp.float32), d_class_vec),
            precise_tn(pos_hot.astype(jnp.float32), d_resid_in),
            precise_tn(level_hot.astype(jnp.float32), d_resid_in),
            precise_tn(feat_row.astype(jnp.float32), d_resid_in),
        ],
        axis=0,
    )
    d_gains = jnp.concatenate(
        [
            jnp.sum(d_resid_in, axis=0)[None],
            d_qkv_sum[None, :model_width],
            d_qkv_sum[None, 2 * model_width :],
            d_bias_out[None],
            d_bias_down[None],
            d_qgain[None],
            d_kgain[None],
            d_bias_up.reshape(ff_rows, model_width),
            d_ada_bias.reshape(8, model_width),
            bias_grad.reshape(-1, model_width),
        ],
        axis=0,
    )
    attn_grad, mlp_grad, ada_grad, embed_grad, gains_grad = (
        lax.psum_scatter(d_attn, ("dp", "vocab"), scatter_dimension=0, tiled=True),
        lax.psum_scatter(d_mlp, ("dp", "vocab"), scatter_dimension=1, tiled=True),
        lax.psum_scatter(d_ada, ("dp", "vocab"), scatter_dimension=0, tiled=True),
        lax.psum_scatter(d_embed, ("dp", "vocab"), scatter_dimension=1, tiled=True),
        lax.psum_scatter(d_gains, ("dp", "vocab"), scatter_dimension=1, tiled=True),
    )
    gradients = (attn_grad, mlp_grad, ada_grad, embed_grad, gains_grad, head_grad)
    squares_local = jnp.zeros((), jnp.float32)
    for gradient in gradients:
        squares_local = squares_local + jnp.sum(gradient * gradient)
    total_sq, loss_sum = lax.psum((squares_local, loss_part), ("dp", "vocab"))
    grad_norm = jnp.sqrt(total_sq)
    clip_factor = jnp.minimum(1.0, CLIP_NORM / (grad_norm + 1e-06))
    masters = (attn_weight, mlp_weight, ada_weight, embed_weight, gains_weight, head_weight)
    moments = (attn_moment, mlp_moment, ada_moment, embed_moment, gains_moment, head_moment)
    squares = (attn_square, mlp_square, ada_square, embed_square, gains_square, head_square)
    updates = [
        adam_step(
            masters[number],
            moments[number],
            squares[number],
            gradients[number],
            clip_factor,
            RATES[number],
        )
        for number in range(6)
    ]
    return (
        updates[0][0],
        updates[0][1],
        updates[0][2],
        updates[0][3],
        updates[1][0],
        updates[1][1],
        updates[1][2],
        updates[1][3],
        updates[2][0],
        updates[2][1],
        updates[2][2],
        updates[2][3],
        updates[3][0],
        updates[3][1],
        updates[3][2],
        updates[3][3],
        updates[4][0],
        updates[4][1],
        updates[4][2],
        updates[4][3],
        updates[5][0],
        updates[5][1],
        updates[5][2],
        updates[5][3],
        grad_norm,
        loss_sum,
        total_count,
    )


def solution(mesh):
    placed = (
        P(("dp", "vocab"), None, None),
        P(("dp", "vocab"), None),
        P(("dp", "vocab"), None),
        P(("dp", "vocab"), None),
        P(("dp", "vocab"), None),
        P(("dp", "vocab"), None),
        P(("dp", "vocab"), None),
        P(("dp", "vocab"), None),
        P(None, ("dp", "vocab"), None),
        P(None, ("dp", "vocab"), None),
        P(None, ("dp", "vocab"), None),
        P(("dp", "vocab"), None),
        P(("dp", "vocab"), None),
        P(("dp", "vocab"), None),
        P(None, ("dp", "vocab")),
        P(None, ("dp", "vocab")),
        P(None, ("dp", "vocab")),
        P(None, ("dp", "vocab")),
        P(None, ("dp", "vocab")),
        P(None, ("dp", "vocab")),
        P("dp", "vocab"),
        P("dp", "vocab"),
        P("dp", "vocab"),
    )
    return jax.shard_map(
        per_device,
        mesh=mesh,
        in_specs=placed,
        out_specs=(
            P(("dp", "vocab"), None),
            P(("dp", "vocab"), None),
            P(("dp", "vocab"), None),
            P(("dp", "vocab"), None),
            P(None, ("dp", "vocab"), None),
            P(None, ("dp", "vocab"), None),
            P(None, ("dp", "vocab"), None),
            P(None, ("dp", "vocab"), None),
            P(("dp", "vocab"), None),
            P(("dp", "vocab"), None),
            P(("dp", "vocab"), None),
            P(("dp", "vocab"), None),
            P(None, ("dp", "vocab")),
            P(None, ("dp", "vocab")),
            P(None, ("dp", "vocab")),
            P(None, ("dp", "vocab")),
            P(None, ("dp", "vocab")),
            P(None, ("dp", "vocab")),
            P(None, ("dp", "vocab")),
            P(None, ("dp", "vocab")),
            P("dp", "vocab"),
            P("dp", "vocab"),
            P("dp", "vocab"),
            P("dp", "vocab"),
            P(),
            P(),
            P(),
        ),
        check_vma=False,
    )
```

profile of v0, /device:TPU:0, one launch (start us, length us, event | category | flops | bytes accessed | tf_op | source)
XLA Modules:
  0.0 1966.0 jit_solution(16151335602646498188)
XLA Ops:
  13.8 44.1 %all-gather.3 = bf16[32,32,23]{1,2,0:T(8,128)(2,1)S(1)} all-gather(bf16[1,32,23]{1,2,0:T(8,128)(2,1)S(1)} %convert_bitcast_fusion.3), channel_id=1, replica_groups=mesh['dp'=8,'vocab'=4] {'dp','vocab'}, dimensions={0}, use_global_device_ids=true | all-gather | bytes 48576 | tf_op jit(solution)/shard_map/all_gather | solution.py:292
  60.8 13.9 all-gather.14.cloned.1.call-done
  79.9 112.0 %all-gather.16.cloned.1.call-done = bf16[1024,8192]{1,0:T(8,128)(2,1)} async-done(((bf16[32,8192]{1,0:T(8,128)(2,1)}), bf16[1024,8192]{1,0:T(8,128)(2,1)}) %all-gather.16.cloned.1.call-update) | async-done | bytes 16777232 | tf_op jit(solution)/shard_map/all_gather | solution.py:290
  191.9 8.1 convolution_add_fusion
  199.9 5.1 fusion.176
  205.0 4.5 copy-done.1
  209.9 61.0 %all-gather.18.cloned.1.call-done = bf16[1024,4096]{1,0:T(8,128)(2,1)} async-done(((bf16[32,4096]{1,0:T(8,128)(2,1)}), bf16[1024,4096]{1,0:T(8,128)(2,1)}) %all-gather.18.cloned.1.call-update) | async-done | bytes 8388624 | tf_op jit(solution)/shard_map/all_gather | solution.py:288
  271.0 4.9 fusion.126
  287.5 22.0 %while.48 = (s32[]{:T(128)}, bf16[4,384,4,64]{1,3,2,0:T(8,128)(2,1)}, bf16[4,384,4,64]{1,3,2,0:T(8,128)(2,1)}, bf16[4,384,4,64]{1,3,2,0:T(8,128)(2,1)}, bf16[4,3...) while((s32[]{:T(128)}, bf16[4,384,4,64]{1,3,2,0:T(8,128)(2,1)}, ...), condition=%wide.region_13.14_spmd.clone.clone, body=%wide.region_10.13_spmd.clone.sunk.clone | while | flops 232245504 | bytes 8128645 | solution.py:138
  309.5 4.6 fusion.225
  314.4 2.5 fusion.138
  316.9 70.8 %all-gather.20.cloned.1.call-done = bf16[2,1024,4096]{2,1,0:T(8,128)(2,1)} async-done(((bf16[2,32,4096]{2,1,0:T(8,128)(2,1)}), bf16[2,1024,4096]{2,1,0:T(8,128)(2,1)}) %all-gather.20.cloned.1.call-update) | async-done | bytes 16777232 | tf_op jit(solution)/shard_map/all_gather | solution.py:289
  387.7 6.2 fusion.121
  394.0 11.4 fusion.224
  405.7 3.4 fusion.137
  409.8 39.5 %psum.21 = f32[]{:T(128)} all-reduce(f32[]{:T(128)} %convert_reduce_fusion.6), channel_id=1, replica_groups=mesh['dp'=8,'vocab'=4] {'dp','vocab'}, use_global_device_ids=true, to_apply=%region_9.10 | all-reduce | flops 1 | bytes 8 | tf_op jit(solution)/shard_map/psum | solution.py:298
  449.4 5.5 all_gather.46
  455.7 12.0 all-gather.22.cloned.1.call-done
  467.7 6.0 add_reduce_fusion
  476.3 5.2 all-gather.6
  481.6 5.2 all-gather.5
  486.8 5.2 all-gather.4
  492.7 4.6 convert_reduce_fusion
  499.0 5.4 fusion.240
  505.9 3.1 copy.140
  510.2 3.4 copy.143
  513.8 8.6 convolution_convert_fusion.1
  522.5 40.7 %reduce-scatter.12.cloned.1.call-done = f32[384,1024]{1,0:T(8,128)} async-done(((f32[1536,1024]{1,0:T(8,128)}), f32[384,1024]{1,0:T(8,128)}) %reduce-scatter.12.cloned.1.call-update) | async-done | bytes 1572880 | tf_op jit(solution)/shard_map/reduce_scatter | solution.py:364
  563.1 2.5 multiply_reduce_fusion.3
  570.2 9.2 convert_reduce_fusion.1
  579.4 8.7 multiply_reduce_fusion.2
  588.2 2.6 fusion.222
  590.8 3.0 convert_reduce_fusion.4
  594.7 2.7 fusion.153
  598.6 41.8 %while.49 = (s32[]{:T(128)}, f32[4,384,4,64]{1,3,2,0:T(8,128)}, f32[4,384,4,64]{1,3,2,0:T(8,128)}, bf16[4,384,4,64]{1,3,2,0:T(8,128)(2,1)}, bf16[4,384,4,64]{1,3...) while((s32[]{:T(128)}, f32[4,384,4,64]{1,3,2,0:T(8,128)}, ...), condition=%wide.region_32.33_spmd.clone.clone, body=%wide.region_28.32_spmd.clone.sunk.clone | while | flops 463061760 | bytes 18773092 | solution.py:186
  606.0 2.9 fusion.334
  616.4 2.9 fusion.334
  626.7 2.9 fusion.334
  637.0 2.9 fusion.334
  644.0 3.2 copy.144
  649.2 3.0 copy.141
  654.0 3.1 copy.142
  657.4 6.6 fusion.135
  664.0 6.7 multiply_reduce_fusion.1
  681.1 4.4 convert_reduce_fusion.5
  693.2 10.2 fusion.242
  703.4 3.9 fusion.184
  707.4 4.2 fusion.159
  712.3 21.6 %concatenate.37 = f32[1723,1024]{1,0:T(8,128)} concatenate(f32[1001,1024]{1,0:T(8,128)} %fusion.184, f32[680,1024]{1,0:T(8,128)} %fusion.159, f32[10,1024]{1,0:T(8,128)S(1)} %fusion.177, f32[32,1024]{1,0:T(8,128)S(1)} %convolution_bitcast_fusion.4), dimensions={0} | concatenate | bytes 14114816 | tf_op jit(solution)/shard_map/concatenate | solution.py:418
  733.9 8.1 copy.153
  743.1 2.5 fusion.241
  745.6 3.5 fusion.205
  749.1 6.1 pad_maximum_fusion.1
  756.4 6.5 convolution_bitcast_fusion.3
  762.9 12.1 convolution_bitcast_fusion.2
  775.0 18.7 pad_maximum_fusion
  793.8 13.1 fusion.204
  810.0 35.7 %reduce-scatter.24.cloned.1.call-done = f32[32,23]{1,0:T(8,128)} async-done(((f32[1024,23]{1,0:T(8,128)}), f32[32,23]{1,0:T(8,128)}) %reduce-scatter.24.cloned.1.call-update) | async-done | bytes 2960
  847.1 143.4 %reduce-scatter.22.cloned.1.call-done = f32[32,1723]{1,0:T(8,128)} async-done(((f32[1024,1723]{1,0:T(8,128)}), f32[32,1723]{1,0:T(8,128)}) %reduce-scatter.22.cloned.1.call-update) | async-done | bytes 220560
  992.8 178.9 %reduce-scatter.14.cloned.1.call-done = f32[32,4096]{1,0:T(8,128)} async-done(((f32[1024,4096]{1,0:T(8,128)}), f32[32,4096]{1,0:T(8,128)}) %reduce-scatter.14.cloned.1.call-update) | async-done | bytes 524304 | tf_op jit(solution)/shard_map/reduce_scatter | solution.py:443
  1173.5 356.2 %reduce-scatter.16.cloned.1.call-done = f32[2,32,4096]{2,1,0:T(8,128)} async-done(((f32[2,1024,4096]{2,1,0:T(8,128)}), f32[2,32,4096]{2,1,0:T(8,128)}) %reduce-scatter.16.cloned.1.call-update) | async-done | bytes 1048592 | tf_op jit(solution)/shard_map/reduce_scatter | solution.py:444
  1533.1 360.8 %reduce-scatter.18.cloned.1.call-done = f32[32,8192]{1,0:T(8,128)} async-done(((f32[1024,8192]{1,0:T(8,128)}), f32[32,8192]{1,0:T(8,128)}) %reduce-scatter.18.cloned.1.call-update) | async-done | bytes 1048592 | tf_op jit(solution)/shard_map/reduce_scatter | solution.py:445
  1898.7 47.2 %all-reduce = (f32[]{:T(128)}, f32[]{:T(128)}) all-reduce(f32[]{:T(128)S(6)} %add.448, f32[]{:T(128)} %fusion.197), channel_id=1, replica_groups=mesh['dp'=8,'vocab'=4] {'dp','vocab'}, use_global_device_ids=true, to_apply=%region_58.59 | all-reduce | flops 2 | bytes 16 | tf_op jit(solution)/shard_map/psum | solution.py:453
  1950.5 2.4 fusion.213
  (442 shorter events, 144.5 us)
Async XLA Ops:
  7.2 69.0 %copy-start = (bf16[1,384,32]{1,2,0:T(8,128)(2,1)S(1)}, bf16[1,384,32]{1,2,0:T(8,128)(2,1)}, u32[]{:S(2)}) copy-start(bf16[1,384,32]{1,2,0:T(8,128)(2,1)} %param.29) | copy-start | bytes 73732
  7.2 4.8 copy-start.39
  7.2 67.4 %all-gather.14.cloned.1.call-start = ((), (), s32[]{:S(2)}) async-start(), calls=%async_computation.7 | async-start | bytes 3784704 | tf_op jit(solution)/shard_map/all_gather | solution.py:291
  9.0 182.8 %all-gather.16.cloned.1.call-start = ((), (), s32[]{:S(2)}) async-start(), calls=%async_computation.8 | async-start | bytes 17301504 | tf_op jit(solution)/shard_map/all_gather | solution.py:290
  11.2 259.8 %all-gather.18.cloned.1.call-start = ((), (), s32[]{:S(2)}) async-start(), calls=%async_computation.9 | async-start | bytes 8650752 | tf_op jit(solution)/shard_map/all_gather | solution.py:288
  12.0 46.2 %copy-start.95 = (s32[1,384]{1,0:T(1,128)S(1)}, s32[1,384]{1,0:T(1,128)}, u32[]{:S(2)}) copy-start(s32[1,384]{1,0:T(1,128)} %param.30) | copy-start | bytes 4612
  12.0 375.7 %all-gather.20.cloned.1.call-start = ((), (), s32[]{:S(2)}) async-start(), calls=%async_computation.10 | async-start | bytes 17301504 | tf_op jit(solution)/shard_map/all_gather | solution.py:289
  12.9 442.7 %all-gather.24.cloned.1.call-start = ((), (), s32[]{:S(2)}) async-start(), calls=%async_computation.12 | async-start | bytes 2359296 | tf_op jit(solution)/shard_map/all_gather | solution.py:294
  13.8 453.9 %all-gather.22.cloned.1.call-start = ((), (), s32[]{:S(2)}) async-start(), calls=%async_computation.11 | async-start | bytes 3932160 | tf_op jit(solution)/shard_map/all_gather | solution.py:339
  58.4 19.2 copy-start.26
  59.1 18.6 copy-start.89
  78.9 126.1 %copy-start.6 = (f32[384,1024]{1,0:T(8,128)}, f32[384,1024]{1,0:T(8,128)S(1)}, u32[]{:S(2)}) copy-start(f32[384,1024]{1,0:T(8,128)S(1)} %get-tuple-element.418) | copy-start | bytes 4718596
  78.9 126.1 %copy-start.87 = (f32[384]{0:T(512)}, f32[384]{0:T(512)S(1)}, u32[]{:S(2)}) copy-start(f32[384]{0:T(512)S(1)} %broadcast_multiply_fusion.2) | copy-start | bytes 4612
  79.2 120.7 %copy-start.93 = (f32[384]{0:T(512)}, f32[384]{0:T(512)S(1)}, u32[]{:S(2)}) copy-start(f32[384]{0:T(512)S(1)} %multiply_reduce_fusion.8) | copy-start | bytes 4612
  79.2 125.8 %copy-start.91 = (f32[384]{0:T(512)}, f32[384]{0:T(512)S(1)}, u32[]{:S(2)}) copy-start(f32[384]{0:T(512)S(1)} %fusion.198) | copy-start | bytes 4612
  79.9 120.0 %copy-start.66 = (f32[8,1024]{1,0:T(8,128)}, f32[8,1024]{1,0:T(8,128)S(1)}, u32[]{:S(2)}) copy-start(f32[8,1024]{1,0:T(8,128)S(1)} %fusion.129) | copy-start | bytes 98308
  209.9 61.0 %copy-start.50 = (bf16[384,1024]{1,0:T(8,128)(2,1)}, bf16[384,1024]{1,0:T(8,128)(2,1)S(1)}, u32[]{:S(2)}) copy-start(bf16[384,1024]{1,0:T(8,128)(2,1)S(1)} %fusion.139) | copy-start | bytes 2359300
  279.9 5.9 copy-start.2
  280.2 5.7 copy-start.75
  282.6 4.9 copy-start.4
  287.5 22.0 %copy-start.7 = (f32[384,1024]{1,0:T(8,128)S(1)}, f32[384,1024]{1,0:T(8,128)}, u32[]{:S(2)}) copy-start(f32[384,1024]{1,0:T(8,128)} %copy-done.6) | copy-start | bytes 4718596
  314.0 274.1 %copy-start.9 = (f32[384,1024]{1,0:T(8,128)}, f32[384,1024]{1,0:T(8,128)S(1)}, u32[]{:S(2)}) copy-start(f32[384,1024]{1,0:T(8,128)S(1)} %get-tuple-element.389) | copy-start | bytes 4718596
  316.9 77.1 %copy-start.44 = (bf16[384,1024]{1,0:T(8,128)(2,1)}, bf16[384,1024]{1,0:T(8,128)(2,1)S(1)}, u32[]{:S(2)}) copy-start(bf16[384,1024]{1,0:T(8,128)(2,1)S(1)} %fusion.138) | copy-start | bytes 2359300
  393.9 11.4 copy-start.34
  405.4 160.3 %copy-start.11 = (f32[384,1024]{1,0:T(8,128)}, f32[384,1024]{1,0:T(8,128)S(1)}, u32[]{:S(2)}) copy-start(f32[384,1024]{1,0:T(8,128)S(1)} %get-tuple-element.387) | copy-start | bytes 4718596
  405.7 43.7 %copy-start.100 = (s32[1,384]{1,0:T(1,128)S(1)}, s32[1,384]{1,0:T(1,128)}, u32[]{:S(2)}) copy-start(s32[1,384]{1,0:T(1,128)} %param.32) | copy-start | bytes 4612
  405.7 43.7 %copy-start.101 = (f32[1,384]{1,0:T(1,128)S(1)}, f32[1,384]{1,0:T(1,128)}, u32[]{:S(2)}) copy-start(f32[1,384]{1,0:T(1,128)} %param.33) | copy-start | bytes 4612
  409.1 154.0 %reduce-scatter.12.cloned.1.call-start = ((), (), s32[]{:S(2)}) async-start(), calls=%async_computation.13 | async-start | bytes 7864320 | tf_op jit(solution)/shard_map/reduce_scatter | solution.py:364
  455.0 18.8 copy-start.85
  492.6 4.6 copy-start.72
  492.7 4.6 copy-start.86
  492.7 6.3 copy-start.102
  504.4 304.0 %reduce-scatter.20.cloned.1.call-start = ((), (), s32[]{:S(2)}) async-start(), calls=%async_computation.17 | async-start | bytes 2359296 | tf_op jit(solution)/shard_map/reduce_scatter | solution.py:371
  522.4 323.3 %reduce-scatter.24.cloned.1.call-start = ((), (), s32[]{:S(2)}) async-start(), calls=%async_computation.19 | async-start | bytes 540672
  563.1 7.0 slice-start
  567.8 23.0 %copy-start.14 = (f32[384,1024]{1,0:T(8,128)}, f32[384,1024]{1,0:T(8,128)S(1)}, u32[]{:S(2)}) copy-start(f32[384,1024]{1,0:T(8,128)S(1)} %get-tuple-element.385) | copy-start | bytes 4718596
  570.1 9.2 copy-start.46
  579.4 8.8 copy-start.48
  642.6 4.5 copy-start.5
  657.4 6.6 copy-start.32
  657.4 6.6 copy-start.8
  657.4 6.6 copy-start.88
  664.0 6.8 copy-start.28
  664.0 6.8 copy-start.30
  664.0 6.8 copy-start.94
  664.0 6.8 copy-start.92
  693.2 10.2 copy-start.67
  693.2 10.2 copy-start.99
  711.5 279.0 %reduce-scatter.22.cloned.1.call-start = ((), (), s32[]{:S(2)}) async-start(), calls=%async_computation.18 | async-start | bytes 7569408
  742.0 429.6 %reduce-scatter.14.cloned.1.call-start = ((), (), s32[]{:S(2)}) async-start(), calls=%async_computation.14 | async-start | bytes 17301504 | tf_op jit(solution)/shard_map/reduce_scatter | solution.py:443
  755.2 7.6 copy-start.47
  755.3 774.4 %reduce-scatter.16.cloned.1.call-start = ((), (), s32[]{:S(2)}) async-start(), calls=%async_computation.15 | async-start | bytes 34603008 | tf_op jit(solution)/shard_map/reduce_scatter | solution.py:444
  793.7 1100.2 %reduce-scatter.18.cloned.1.call-start = ((), (), s32[]{:S(2)}) async-start(), calls=%async_computation.16 | async-start | bytes 34603008 | tf_op jit(solution)/shard_map/reduce_scatter | solution.py:445
  990.5 956.1 %copy-start.84 = (f32[23,32]{1,0:T(8,128)S(1)}, f32[23,32]{1,0:T(8,128)}, u32[]{:S(2)}) copy-start(f32[23,32]{1,0:T(8,128)} %param.46) | copy-start | bytes 8836
  990.5 956.1 %copy-start.96 = (f32[23,32]{1,0:T(8,128)S(1)}, f32[23,32]{1,0:T(8,128)}, u32[]{:S(2)}) copy-start(f32[23,32]{1,0:T(8,128)} %param.47) | copy-start | bytes 8836
  990.5 956.2 %copy-start.97 = (f32[23,32]{1,0:T(8,128)S(1)}, f32[23,32]{1,0:T(8,128)}, u32[]{:S(2)}) copy-start(f32[23,32]{1,0:T(8,128)} %param.48) | copy-start | bytes 8836
  990.5 956.8 %copy-start.57 = (f32[128,1024]{1,0:T(8,128)S(1)}, f32[128,1024]{1,0:T(8,128)}, u32[]{:S(2)}) copy-start(f32[128,1024]{1,0:T(8,128)} %param.49) | copy-start | bytes 1572868
  990.5 956.8 %copy-start.63 = (bf16[128,1024]{1,0:T(8,128)(2,1)S(1)}, bf16[128,1024]{1,0:T(8,128)(2,1)}, u32[]{:S(2)}) copy-start(bf16[128,1024]{1,0:T(8,128)(2,1)} %reduce-scatter.20.cloned.1.call-done) | copy-start | bytes 786436
  990.5 956.8 %copy-start.70 = (f32[128,1024]{1,0:T(8,128)S(1)}, f32[128,1024]{1,0:T(8,128)}, u32[]{:S(2)}) copy-start(f32[128,1024]{1,0:T(8,128)} %param.50) | copy-start | bytes 1572868
  990.6 956.8 %copy-start.71 = (f32[128,1024]{1,0:T(8,128)S(1)}, f32[128,1024]{1,0:T(8,128)}, u32[]{:S(2)}) copy-start(f32[128,1024]{1,0:T(8,128)} %param.51) | copy-start | bytes 1572868
  1896.0 52.9 %copy-start.64 = (f32[1723,32]{0,1:T(8,128)S(1)}, f32[1723,32]{0,1:T(8,128)}, u32[]{:S(2)}) copy-start(f32[1723,32]{0,1:T(8,128)} %param.43) | copy-start | bytes 661636
  1896.0 52.9 %copy-start.65 = (f32[32,1723]{1,0:T(8,128)S(1)}, f32[32,1723]{1,0:T(8,128)}, u32[]{:S(2)}) copy-start(f32[32,1723]{1,0:T(8,128)} %reduce-scatter.22.cloned.1.call-done) | copy-start | bytes 661636
  1896.0 52.9 %copy-start.73 = (f32[1723,32]{0,1:T(8,128)S(1)}, f32[1723,32]{0,1:T(8,128)}, u32[]{:S(2)}) copy-start(f32[1723,32]{0,1:T(8,128)} %param.44) | copy-start | bytes 661636
  1896.0 52.9 %copy-start.74 = (f32[1723,32]{0,1:T(8,128)S(1)}, f32[1723,32]{0,1:T(8,128)}, u32[]{:S(2)}) copy-start(f32[1723,32]{0,1:T(8,128)} %param.45) | copy-start | bytes 661636
  (60 other events, 142.5 us)
Sparse Core Ops, SparseCore 0:
  11.5 63.1 all-gather.13
  78.1 113.6 all-gather.15
  195.3 75.6 all-gather.17
  274.3 113.3 all-gather.19
  390.2 47.9 all-gather.23
  440.2 27.4 all-gather.21
  504.5 58.5 reduce-scatter.11
  567.1 68.0 reduce-scatter.19
  711.7 133.9 reduce-scatter.23
  847.9 142.6 reduce-scatter.21
  992.8 178.7 reduce-scatter.13
  1173.8 355.8 reduce-scatter.15
  1532.0 361.8 reduce-scatter.17
where the time goes:
time: 1980 us; the launch traced here: 1970 us
  waiting for transfers between devices  1390 us (70%)
  matrix products  211 us (11%)
  blocking collectives  152 us (8%)
  other arithmetic  104 us (5%)
  local copies, waits for them, and re-layouts  90.7 us (5%)
  between operations  21.7 us (1%)
    reduce_scatter x1, waiting for transfers between devices, per_device(): lax.psum_scatter(d_ada, ('dp', 'vocab'), scatter_dimension=0, tiled=True)  361 us
    reduce_scatter x1, waiting for transfers between devices, per_device(): lax.psum_scatter(d_mlp, ('dp', 'vocab'), scatter_dimension=1, tiled=True)  356 us
    unnamed x15, waiting for transfers between devices  179 us
    reduce_scatter x1, waiting for transfers between devices, per_device(): lax.psum_scatter(d_attn, ('dp', 'vocab'), scatter_dimension=0, tiled=True)  179 us
    all_gather x1, waiting for transfers between devices, per_device(): lax.all_gather(ada_weight.astype(jnp.bfloat16), ('dp', 'vocab'), axis=0,...  112 us
    all_gather x1, waiting for transfers between devices, per_device(): lax.all_gather(mlp_weight.astype(jnp.bfloat16), ('dp', 'vocab'), axis=1,...  70.8 us
    all_gather x1, waiting for transfers between devices, per_device(): lax.all_gather(attn_weight.astype(jnp.bfloat16), ('dp', 'vocab'), axis=0,...  61 us
    psum x1, blocking collectives, per_device(): total_sq, loss_sum = lax.psum((squares_local, loss_part), ('dp', 'vocab'))  47.2 us
  transfers between devices with their start and end apart: 13, of which 11 were waited for; matrix products, arithmetic and copies ran while one was open for 18% of the time, Pallas kernels for 0%

commit v1 on v0

v1 whole, which is shorter than its diff:
```python
import jax
import jax.numpy as jnp
from jax import lax
from jax.sharding import Mesh, PartitionSpec as P

HEADS = 16
HEAD_DIM = 64
FF = 4096
V = 4096
CHANNELS = 32
CLASSES = 1001
POSITIONS = 680
LEVELS = 10
MAXIMG = 8
STEPS = 10


EPS_NORM = 1e-06
BETA_ONE = 0.9
BETA_TWO = 0.95
ADAM_EPS = 1e-08
DECAY = 0.05
CLIP_NORM = 0.001
RATES = (0.03, 0.03, 0.03, 0.15, 0.4, 0.03)
NEG_FILL = -1e30
GROUP_HEADS = 4
BF16 = jnp.bfloat16
F32 = jnp.float32


def matmul(left, right):
    return jnp.dot(left, right, preferred_element_type=F32)


def matmul_tn(left, right):
    return lax.dot_general(left, right, (((0,), (0,)), ((), ())), preferred_element_type=F32)


def matmul_nt(left, right):
    return lax.dot_general(left, right, (((1,), (1,)), ((), ())), preferred_element_type=F32)


def precise(left, right):
    return jnp.dot(left, right, precision=lax.Precision.HIGHEST)


def precise_tn(left, right):
    return lax.dot_general(left, right, (((0,), (0,)), ((), ())), precision=lax.Precision.HIGHEST)


def by_halves(times, values):
    upper = lax.reduce_precision(values, 8, 7)
    return times(upper.astype(BF16)) + times((values - upper).astype(BF16))


def shifted(value, axis, size, shift):
    return lax.ppermute(value, axis, [(i, (i + shift) % size) for i in range(size)])


def gather_axis(value, axis, size):
    return [value] + [shifted(value, axis, size, k) for k in range(1, size)]


def gather(value, order, sizes):
    for axis in order[:-1]:
        value = jnp.concatenate(gather_axis(value, axis, sizes[axis]), axis=0)
    last = order[-1]
    blocks = gather_axis(value, last, sizes[last])
    return blocks + [shifted(block, "c", 2, 1) for block in blocks]


def add_shifts(pieces, axis, size, out):
    total = pieces[0].astype(F32)
    for k in range(1, size):
        total = total + shifted(pieces[k].astype(BF16), axis, size, size - k).astype(F32)
    return total.astype(out)


def scatter(blocks, order, sizes):
    count = len(blocks) // 2
    kept = [
        add_shifts([blocks[k], blocks[count + k]], "c", 2, BF16) for k in reversed(range(count))
    ][::-1]
    axes = list(reversed(order))
    value = add_shifts(kept, axes[0], sizes[axes[0]], BF16)
    for axis in axes[1:]:
        pieces = jnp.split(value, sizes[axis], axis=0)
        value = add_shifts(pieces, axis, sizes[axis], F32 if axis == axes[-1] else BF16)
    return value


def sum_all(value, sizes):
    for axis in ("c", "x", "y", "z"):
        value = sum(gather_axis(value, axis, sizes[axis]))
    return value


def source_rows(order, sizes, rows):
    places = sizes["z"] * sizes["y"] * sizes["x"] * 2 * rows
    place = jnp.arange(places, dtype=jnp.int32)
    row, rest = place % rows, place // rows
    at = {}
    for axis in tuple(order) + ("c",):
        at[axis] = (lax.axis_index(axis) - rest % sizes[axis]) % sizes[axis]
        rest = rest // sizes[axis]
    device = ((at["z"] * sizes["y"] + at["y"]) * sizes["x"] + at["x"]) * 2 + at["c"]
    return device * rows + row


def hot_rows(source):
    width = source.shape[0]
    return (source[:, None] == jnp.arange(width, dtype=jnp.int32)[None, :]).astype(BF16)


def normalize(values):
    center = values - jnp.mean(values, axis=-1, keepdims=True)
    return center * lax.rsqrt(jnp.mean(center * center, axis=-1, keepdims=True) + EPS_NORM)


def modulate(values, shifts, scales):
    return normalize(values) * (1.0 + scales) + shifts


def head_norm(values, gain_vec):
    return (
        values * lax.rsqrt(jnp.mean(values * values, axis=-1, keepdims=True) + EPS_NORM) * gain_vec
    )


def gelu_tanh(values):
    return jax.nn.gelu(values, approximate=True)


def layout(scale_row):
    position = jnp.arange(scale_row.shape[0], dtype=jnp.int32)
    opening = scale_row == 0
    image_id = jnp.cumsum(opening.astype(jnp.int32)) - 1
    starts_at = lax.cummax(jnp.where(opening, position, 0), axis=0)
    return (image_id, position - starts_at, scale_row < LEVELS)


def split_groups(values):
    length = values.shape[0]
    return jnp.moveaxis(values.reshape(length, HEADS // GROUP_HEADS, GROUP_HEADS, HEAD_DIM), 1, 0)


def join_groups(values):
    return jnp.moveaxis(values, 0, 1).reshape(values.shape[1], HEADS, HEAD_DIM)


def soft_block(q_group, k_group, allowed):
    scores = jnp.einsum(
        "qhd,khd->hqk", q_group, k_group, preferred_element_type=F32
    ) * HEAD_DIM ** (-0.5)
    scores = jnp.where(allowed[None], scores, NEG_FILL)
    exp_terms = jnp.exp(scores - jnp.max(scores, axis=-1, keepdims=True))
    return exp_terms / jnp.sum(exp_terms, axis=-1, keepdims=True)


def mix_heads(q_norm, k_norm, v_low, allowed):
    def mix_block(item):
        q_group, k_group, v_group = item
        soft_w = soft_block(q_group, k_group, allowed)
        return jnp.einsum(
            "hqk,khd->qhd", soft_w.astype(BF16), v_group, preferred_element_type=F32
        )

    mixed = lax.map(mix_block, (split_groups(q_norm), split_groups(k_norm), split_groups(v_low)))
    return join_groups(mixed)


def mix_heads_back(q_norm, k_norm, v_low, d_mix, allowed):
    def back_block(item):
        q_group, k_group, v_group, dm_group = item
        soft_w = soft_block(q_group, k_group, allowed)
        soft_low = soft_w.astype(BF16)
        d_values = jnp.einsum("hqk,qhd->khd", soft_low, dm_group, preferred_element_type=F32)
        d_soft = jnp.einsum("qhd,khd->hqk", dm_group, v_group, preferred_element_type=F32)
        d_scores = (soft_w * (d_soft - jnp.sum(d_soft * soft_w, axis=-1, keepdims=True))).astype(
            BF16
        )
        d_qn = jnp.einsum("hqk,khd->qhd", d_scores, k_group, preferred_element_type=F32)
        d_kn = jnp.einsum("hqk,qhd->khd", d_scores, q_group, preferred_element_type=F32)
        return (d_qn * HEAD_DIM ** (-0.5), d_kn * HEAD_DIM ** (-0.5), d_values)

    d_qn, d_kn, d_values = lax.map(
        back_block,
        (split_groups(q_norm), split_groups(k_norm), split_groups(v_low), split_groups(d_mix)),
    )
    return (join_groups(d_qn), join_groups(d_kn), join_groups(d_values))


def adam_step(weight, moment, square, gradient, clip_factor, step_rate):
    gradient = gradient * clip_factor
    moment = BETA_ONE * moment + (1.0 - BETA_ONE) * gradient
    square = BETA_TWO * square + (1.0 - BETA_TWO) * gradient * gradient
    first_hat = moment / (1.0 - BETA_ONE**STEPS)
    second_hat = square / (1.0 - BETA_TWO**STEPS)
    weight = weight - step_rate * (first_hat / (jnp.sqrt(second_hat) + ADAM_EPS) + DECAY * weight)
    return (weight, moment, square, weight.astype(BF16))


def per_device(
    sizes,
    features,
    scale_ids,
    class_ids,
    code_targets,
    token_weights,
    attn_weight,
    attn_moment,
    attn_square,
    mlp_weight,
    mlp_moment,
    mlp_square,
    ada_weight,
    ada_moment,
    ada_square,
    embed_weight,
    embed_moment,
    embed_square,
    gains_weight,
    gains_moment,
    gains_square,
    head_weight,
    head_moment,
    head_square,
):
    path_one, path_two = ("z", "y", "x"), ("z", "x", "y")
    devices = sizes["z"] * sizes["y"] * sizes["x"] * 2
    rows = attn_weight.shape[0]
    width = rows * devices
    ff_rows = FF // width
    ada_at = 7 + ff_rows
    head_at = ada_at + 8
    off_level = CLASSES + POSITIONS
    off_word = off_level + LEVELS
    length = scale_ids.shape[1]
    used = min(POSITIONS, length)
    n_gains = gains_weight.shape[0]

    scale_row = scale_ids[0]
    image_id, inside, counted = layout(scale_row)
    counted = counted.astype(F32)
    facts = jnp.concatenate(
        [class_ids[0], jnp.sum(counted).astype(jnp.int32)[None], jnp.zeros((119,), jnp.int32)]
    )[None]
    facts = jnp.concatenate(gather(facts, path_one, sizes), axis=0)
    total_count = jnp.sum(facts[:, MAXIMG]).astype(F32)
    weighted = token_weights[0] * counted
    row_info = jnp.stack([code_targets[0].astype(F32), weighted])
    row_info = gather_axis(row_info, "x", sizes["x"])
    row_info = row_info + [shifted(part, "c", 2, 1) for part in row_info]
    row_info = jnp.concatenate(row_info, axis=1)

    embed16 = embed_weight.astype(BF16)
    gains16 = gains_weight.astype(BF16)
    slim = jnp.concatenate(
        [
            embed16[CLASSES : CLASSES + used],
            embed16[off_level : off_word + CHANNELS],
            gains16,
        ],
        axis=0,
    )
    n_slim = slim.shape[0]
    fill = -n_slim % 128
    slim = jnp.pad(slim, ((0, fill), (0, 0))).T
    slim_all = jnp.concatenate(gather(slim, path_one, sizes), axis=0)
    perm_one = hot_rows(source_rows(path_one, sizes, rows))
    perm_two = hot_rows(source_rows(path_two, sizes, rows))
    slim_all = matmul_tn(slim_all, perm_one)
    n_embed = used + LEVELS + CHANNELS
    gain_rows = slim_all[n_embed : n_embed + n_gains]

    ids_one = facts[:, :MAXIMG]
    slots = devices * MAXIMG
    class_hot = (
        ids_one.reshape(slots)[:, None] == jnp.arange(CLASSES, dtype=jnp.int32)[None, :]
    ).astype(BF16)
    class_vec = matmul(class_hot, embed16[:CLASSES])
    class_act = jax.nn.silu(class_vec).astype(BF16)

    def to_two(value):
        shaped = value.reshape((2, sizes["x"], sizes["y"], sizes["z"] * MAXIMG) + value.shape[1:])
        return jnp.swapaxes(shaped, 1, 2).reshape(value.shape)

    def to_one(value):
        shaped = value.reshape((2, sizes["y"], sizes["x"], sizes["z"] * MAXIMG) + value.shape[1:])
        return jnp.swapaxes(shaped, 1, 2).reshape(value.shape)

    ada16 = ada_weight.astype(BF16)
    half = ada16.shape[1] // 2
    act_two = to_two(class_act)
    mod_one = matmul(class_act, ada16[:, :half]).astype(BF16)
    mod_two = matmul(act_two, ada16[:, half:]).astype(BF16)
    mod_one = scatter(jnp.split(mod_one, 2 * sizes["x"], axis=0), path_one, sizes)
    mod_two = scatter(jnp.split(mod_two, 2 * sizes["y"], axis=0), path_two, sizes)
    modulation = jnp.concatenate([mod_one, mod_two], axis=1) + gain_rows[ada_at:head_at].reshape(-1)

    attn16 = attn_weight.astype(BF16)
    attn_one = jnp.concatenate(gather(attn16[:, : 2 * width], path_one, sizes), axis=0)
    attn_two = jnp.concatenate(gather(attn16[:, 2 * width :], path_two, sizes), axis=0)
    w_v, w_proj = attn_two[:, :width], attn_two[:, width:]
    mlp16 = mlp_weight.astype(BF16)
    w_up = jnp.concatenate(gather(mlp16[0], path_one, sizes), axis=0)
    w_down = jnp.concatenate(gather(mlp16[1], path_two, sizes), axis=0)
    head16 = head_weight.astype(BF16)
    for axis in ("z", "y"):
        head16 = jnp.concatenate(gather_axis(head16, axis, sizes[axis]), axis=0)
    head_rows = head_weight.shape[0]
    place = jnp.arange(width, dtype=jnp.int32)
    rest = place // head_rows
    z_at = (lax.axis_index("z") - rest % sizes["z"]) % sizes["z"]
    y_at = (lax.axis_index("y") - rest // sizes["z"]) % sizes["y"]
    perm_head = hot_rows((z_at * sizes["y"] + y_at) * head_rows + place % head_rows)

    feat_row = features[0]
    pos_hot = (inside[:, None] == jnp.arange(used, dtype=jnp.int32)[None, :]).astype(BF16)
    level_hot = (scale_row[:, None] == jnp.arange(LEVELS, dtype=jnp.int32)[None, :]).astype(BF16)
    token_hot = jnp.concatenate([pos_hot, level_hot, feat_row], axis=1)
    resid_in = matmul(token_hot, slim_all[:n_embed].astype(BF16)) + gain_rows[0]
    image_hot = (image_id[:, None] == jnp.arange(MAXIMG, dtype=jnp.int32)[None, :]).astype(F32)
    pieces = jnp.split(precise(image_hot, modulation), 8, axis=1)
    allowed = (image_id[:, None] == image_id[None, :]) & (scale_row[None, :] <= scale_row[:, None])
    u_one = modulate(resid_in, pieces[0], pieces[1]).astype(BF16)
    u_rel_one = matmul_nt(u_one, perm_one).astype(BF16)
    u_rel_two = matmul_nt(u_one, perm_two).astype(BF16)
    qk = matmul(u_rel_one, attn_one)
    queries, keys = qk[:, :width] + gain_rows[1], qk[:, width:]
    values = matmul(u_rel_two, w_v) + gain_rows[2]
    split_shape = (length, HEADS, HEAD_DIM)
    queries = queries.reshape(split_shape)
    keys = keys.reshape(split_shape)
    q_gain = gain_rows[5].reshape(HEADS, HEAD_DIM)
    k_gain = gain_rows[6].reshape(HEADS, HEAD_DIM)
    q_norm = head_norm(queries, q_gain).astype(BF16)
    k_norm = head_norm(keys, k_gain).astype(BF16)
    v_low = values.reshape(split_shape).astype(BF16)
    mixture = mix_heads(q_norm, k_norm, v_low, allowed).reshape(length, width).astype(BF16)
    mixture_rel = matmul_nt(mixture, perm_two).astype(BF16)
    attn_out = matmul(mixture_rel, w_proj) + gain_rows[3]
    resid_mid = resid_in + pieces[2] * attn_out
    u_two = modulate(resid_mid, pieces[3], pieces[4]).astype(BF16)
    u_two_rel = matmul_nt(u_two, perm_one).astype(BF16)
    hidden = matmul(u_two_rel, w_up) + gain_rows[7:ada_at].reshape(-1)
    active = gelu_tanh(hidden).astype(BF16)
    mlp_out = by_halves(lambda part: matmul(part, perm_two), matmul_nt(active, w_down)) + gain_rows[4]
    resid_out = resid_mid + pieces[5] * mlp_out
    head_in = modulate(resid_out, pieces[6], pieces[7]).astype(BF16)

    head_rel = matmul_nt(head_in, perm_head).astype(BF16)
    n_x = sizes["x"]
    rows_all = gather_axis(head_rel, "x", n_x)
    rows_all = rows_all + [shifted(part, "c", 2, 1) for part in rows_all]
    rows_all = jnp.concatenate(rows_all, axis=0)
    member = lax.axis_index("x") * 2 + lax.axis_index("c")
    code_span = head_weight.shape[1]
    code_start = member * code_span
    head_bias = gain_rows[head_at:].reshape(-1)
    logits = matmul(rows_all, head16) + lax.dynamic_slice_in_dim(head_bias, code_start, code_span)
    local_max = jnp.max(logits, axis=1)
    exp_sums = jnp.sum(jnp.exp(logits - local_max[:, None]), axis=1)
    is_target = (
        jnp.arange(code_span, dtype=jnp.int32)[None, :] + code_start
        == row_info[0].astype(jnp.int32)[:, None]
    ).astype(F32)
    picked = jnp.sum(is_target * logits, axis=1)
    stats = jnp.stack([local_max, exp_sums, picked]).reshape(3, 2, n_x, length)
    group = [stats]
    for d_c in range(2):
        for d_x in range(n_x):
            if d_c or d_x:
                perm = [
                    (x * 2 + c, ((x + d_x) % n_x) * 2 + (c + d_c) % 2)
                    for x in range(n_x)
                    for c in range(2)
                ]
                group.append(jnp.roll(lax.ppermute(stats, ("x", "c"), perm), (d_c, d_x), (1, 2)))
    row_max = group[0][0]
    for other in group[1:]:
        row_max = jnp.maximum(row_max, other[0])
    totals = sum(other[1] * jnp.exp(other[0] - row_max) for other in group)
    target_logit = sum(other[2] for other in group).reshape(-1)
    log_total = (row_max + jnp.log(totals)).reshape(-1)
    loss_part = jnp.sum((row_info[1] * (log_total - target_logit))[:length])
    row_coef = row_info[1] / total_count
    d_logits = (row_coef[:, None] * (jnp.exp(logits - log_total[:, None]) - is_target)).astype(BF16)
    d_rows = matmul_nt(d_logits, head16).astype(BF16)
    d_rows = jnp.split(d_rows, 2 * n_x, axis=0)
    d_rows = [add_shifts([d_rows[k], d_rows[n_x + k]], "c", 2, BF16) for k in range(n_x)]
    d_head_in = add_shifts(d_rows, "x", n_x, F32)
    d_head_in = by_halves(lambda part: matmul(part, perm_head), d_head_in)
    head_grad = matmul_tn(rows_all, d_logits).astype(BF16)
    head_grad = add_shifts(jnp.split(head_grad, sizes["y"], axis=0), "y", sizes["y"], BF16)
    head_grad = add_shifts(jnp.split(head_grad, sizes["z"], axis=0), "z", sizes["z"], F32)
    bias_grad = lax.dynamic_update_slice(
        jnp.zeros((V,), F32), jnp.sum(d_logits.astype(F32), axis=0), (code_start,)
    )
    _, head_back = jax.vjp(modulate, resid_out, pieces[6], pieces[7])
    d_resid_out, d_shift_head, d_scale_head = head_back(d_head_in)

    d_low = (pieces[5] * d_resid_out).astype(BF16)
    d_low_rel = matmul_nt(d_low, perm_two).astype(BF16)
    d_down = matmul_tn(d_low_rel, active).astype(BF16)
    down_grad = scatter(jnp.split(d_down, 2 * sizes["y"], axis=0), path_two, sizes)
    d_bias_down = jnp.sum(d_low.astype(F32), axis=0)
    d_active = matmul(d_low_rel, w_down)
    _, gelu_back = jax.vjp(gelu_tanh, hidden)
    d_hidden = gelu_back(d_active)[0].astype(BF16)
    d_up = matmul_tn(u_two_rel, d_hidden).astype(BF16)
    up_grad = scatter(jnp.split(d_up, 2 * sizes["x"], axis=0), path_one, sizes)
    d_bias_up = jnp.sum(d_hidden.astype(F32), axis=0)
    d_u = matmul(matmul_nt(d_hidden, w_up).astype(BF16), perm_one)
    _, mod_back = jax.vjp(modulate, resid_mid, pieces[3], pieces[4])
    d_branch, d_shift_two, d_scale_two = mod_back(d_u)
    d_gate_two = d_resid_out * mlp_out
    d_resid_mid = d_resid_out + d_branch

    d_low = (pieces[2] * d_resid_mid).astype(BF16)
    d_proj = matmul_tn(mixture_rel, d_low).astype(BF16)
    proj_grad = scatter(jnp.split(d_proj, 2 * sizes["y"], axis=0), path_two, sizes)
    d_bias_out = jnp.sum(d_low.astype(F32), axis=0)
    d_mix = matmul(matmul_nt(d_low, w_proj).astype(BF16), perm_two).astype(BF16)
    d_qn, d_kn, d_values = mix_heads_back(
        q_norm, k_norm, v_low, d_mix.reshape(split_shape), allowed
    )
    _, q_back = jax.vjp(head_norm, queries, q_gain)
    d_queries, d_qgain = q_back(d_qn)
    _, k_back = jax.vjp(head_norm, keys, k_gain)
    d_keys, d_kgain = k_back(d_kn)
    d_q = d_queries.reshape(length, width).astype(BF16)
    d_k = d_keys.reshape(length, width).astype(BF16)
    d_v = d_values.reshape(length, width).astype(BF16)
    d_qk = jnp.concatenate([d_q, d_k], axis=1)
    d_attn_one = matmul_tn(u_rel_one, d_qk).astype(BF16)
    one_grad = scatter(jnp.split(d_attn_one, 2 * sizes["x"], axis=0), path_one, sizes)
    d_attn_two = matmul_tn(u_rel_two, d_v).astype(BF16)
    v_grad = scatter(jnp.split(d_attn_two, 2 * sizes["y"], axis=0), path_two, sizes)
    d_u = matmul(matmul_nt(d_qk, attn_one).astype(BF16), perm_one)
    d_u = d_u + matmul(matmul_nt(d_v, w_v).astype(BF16), perm_two)
    _, mod_back = jax.vjp(modulate, resid_in, pieces[0], pieces[1])
    d_branch, d_shift_one, d_scale_one = mod_back(d_u)
    d_gate_one = d_resid_mid * attn_out
    d_resid_in = d_resid_mid + d_branch

    d_token = jnp.concatenate(
        [
            d_shift_one,
            d_scale_one,
            d_gate_one,
            d_shift_two,
            d_scale_two,
            d_gate_two,
            d_shift_head,
            d_scale_head,
        ],
        axis=1,
    )
    d_mod = precise_tn(image_hot, d_token).astype(BF16)
    d_ada_bias = jnp.sum(d_mod.astype(F32), axis=0)
    d_mod_one = jnp.concatenate(gather(d_mod[:, :half], path_one, sizes), axis=0)
    d_mod_two = jnp.concatenate(gather(d_mod[:, half:], path_two, sizes), axis=0)
    ada_grad = jnp.concatenate(
        [matmul_tn(class_act, d_mod_one), matmul_tn(act_two, d_mod_two)], axis=1
    )
    d_class_act = matmul_nt(d_mod_one, ada16[:, :half]) + to_one(
        matmul_nt(d_mod_two, ada16[:, half:])
    )
    _, silu_back = jax.vjp(jax.nn.silu, class_vec)
    d_class = precise_tn(class_hot.astype(F32), silu_back(d_class_act)[0])

    d_res16 = d_resid_in.astype(BF16)
    d_gains = jnp.concatenate(
        [
            jnp.sum(d_resid_in, axis=0)[None],
            jnp.sum(d_q.astype(F32), axis=0)[None],
            jnp.sum(d_v.astype(F32), axis=0)[None],
            d_bias_out[None],
            d_bias_down[None],
            d_qgain.reshape(1, width),
            d_kgain.reshape(1, width),
            d_bias_up.reshape(ff_rows, width),
            d_ada_bias.reshape(8, width),
            bias_grad.reshape(-1, width),
        ],
        axis=0,
    ).astype(BF16)
    d_slim = jnp.concatenate(
        [
            matmul_tn(token_hot, d_res16).astype(BF16),
            d_gains,
            jnp.zeros((fill, width), BF16),
        ],
        axis=0,
    )
    d_slim = matmul_nt(perm_one, d_slim).astype(BF16)
    slim_grad = scatter(jnp.split(d_slim, 2 * sizes["x"], axis=0), path_one, sizes).T
    embed_grad = jnp.concatenate(
        [
            d_class,
            slim_grad[:used],
            jnp.zeros((POSITIONS - used, rows), F32),
            slim_grad[used:n_embed],
        ],
        axis=0,
    )
    gains_grad = slim_grad[n_embed : n_embed + n_gains]

    attn_grad = jnp.concatenate([one_grad, v_grad, proj_grad], axis=1)
    mlp_grad = jnp.stack([up_grad, down_grad])
    gradients = (attn_grad, mlp_grad, ada_grad, embed_grad, gains_grad, head_grad)
    squares_local = jnp.zeros((), F32)
    for gradient in gradients:
        squares_local = squares_local + jnp.sum(gradient * gradient)
    sums = sum_all(jnp.stack([squares_local, loss_part])[None], sizes)
    total_sq, loss_sum = sums[0, 0], sums[0, 1]
    grad_norm = jnp.sqrt(total_sq)
    clip_factor = jnp.minimum(1.0, CLIP_NORM / (grad_norm + 1e-06))
    masters = (attn_weight, mlp_weight, ada_weight, embed_weight, gains_weight, head_weight)
    moments = (attn_moment, mlp_moment, ada_moment, embed_moment, gains_moment, head_moment)
    squares = (attn_square, mlp_square, ada_square, embed_square, gains_square, head_square)
    updates = []
    for number in range(6):
        updates.extend(
            adam_step(
                masters[number],
                moments[number],
                squares[number],
                gradients[number],
                clip_factor,
                RATES[number],
            )
        )
    return tuple(updates) + (grad_norm, loss_sum, total_count)


def solution(mesh):
    n_dp, n_vocab = mesh.shape["dp"], mesh.shape["vocab"]
    n_z = 1 << (n_dp.bit_length() // 2)
    sizes = {"z": n_z, "y": n_dp // n_z, "x": n_vocab // 2, "c": 2}
    fine = Mesh(
        mesh.devices.reshape(sizes["z"], sizes["y"], sizes["x"], 2), ("z", "y", "x", "c")
    )
    every, dp, vocab = ("z", "y", "x", "c"), ("z", "y"), ("x", "c")
    by_row = P(every, None)
    by_mid = P(None, every, None)
    by_column = P(None, every)
    head = P(dp, vocab)
    placed = (P(every, None, None), by_row, by_row, by_row, by_row)
    for spec in (by_row, by_mid, by_row, by_column, by_column, head):
        placed = placed + (spec,) * 3
    given = ()
    for spec in (by_row, by_mid, by_row, by_column, by_column, head):
        given = given + (spec,) * 4

    def step(*arrays):
        return per_device(sizes, *arrays)

    return jax.shard_map(
        step, mesh=fine, in_specs=placed, out_specs=given + (P(), P(), P()), check_vma=False
    )
```

time: 1980 us -> 972 us (0.49)
  waiting for transfers between devices: 1390 us -> 338 us
  blocking collectives: 152 us -> 0 us
  starting transfers between devices: 0.54 us -> 138 us
  local copies, waits for them, and re-layouts: 90.7 us -> 128 us
  other arithmetic: 104 us -> 125 us
    reduce_scatter x5 -> x0, waiting for transfers between devices: 937 us -> none  [the longest x1 361 us: per_device(): lax.psum_scatter(d_ada, ('dp', 'vocab'), scatter_dimension=0, tiled=True)]
    ppermute x0 -> x138, waiting for transfers between devices: none -> 338 us  [the longest x135 336 us: shifted(): lax.ppermute(value, axis, [(i, (i + shift) % size) for i in range(size)])]
    all_gather x6 -> x0, waiting for transfers between devices: 270 us -> none  [the longest x1 112 us: per_device(): lax.all_gather(ada_weight.astype(jnp.bfloat16), ('dp', 'vocab'), axis=0,...]
    unnamed x15 -> x0, waiting for transfers between devices: 179 us -> none
    ppermute x0 -> x138, starting transfers between devices: none -> 138 us  [the longest x135 136 us: shifted(): lax.ppermute(value, axis, [(i, (i + shift) % size) for i in range(size)])]
    psum x2 -> x0, blocking collectives: 86.7 us -> none  [the longest x1 47.2 us: per_device(): total_sq, loss_sum = lax.psum((squares_local, loss_part), ('dp', 'vocab'))]
    all_gather x5 -> x0, blocking collectives: 65.2 us -> none  [the longest x1 44.1 us: per_device(): lax.all_gather(gains_weight.astype(jnp.bfloat16), ('dp', 'vocab'), axis=1...]
    dot_general x30 -> x38, matrix products: 84.4 us -> 119 us  [the longest x18 76.9 us: matmul(): return jnp.dot(left, right, preferred_element_type=F32)]
  transfers between devices with their start and end apart: 13 -> 138, of which waited for: 11 -> 55; matrix products, arithmetic and copies ran while one was open for 18% -> 25% of each run, Pallas kernels for 0% -> 0%
where the time goes in v1:
time: 972 us; the launch traced here: 960 us
  waiting for transfers between devices  338 us (35%)
  matrix products  218 us (22%)
  starting transfers between devices  138 us (14%)
  local copies, waits for them, and re-layouts  128 us (13%)
  other arithmetic  125 us (13%)
  between operations  12.2 us (1%)
    ppermute x135, waiting for transfers between devices, shifted(): lax.ppermute(value, axis, [(i, (i + shift) % size) for i in range(size)])  336 us
    ppermute x135, starting transfers between devices, shifted(): lax.ppermute(value, axis, [(i, (i + shift) % size) for i in range(size)])  136 us
    dot_general x18, matrix products, matmul(): return jnp.dot(left, right, preferred_element_type=F32)  76.9 us
    unnamed x362, local copies, waits for them, and re-layouts  58 us
    dot_general x10, matrix products, matmul_tn(): lax.dot_general(left, right, (((0,), (0,)), ((), ())), preferred_element_...  38.3 us
    convert_element_type x26, other arithmetic, add_shifts(): return total.astype(out)  33.1 us
    dot_general x11, matrix products, matmul_nt(): lax.dot_general(left, right, (((1,), (1,)), ((), ())), preferred_element_...  31.3 us
  transfers between devices with their start and end apart: 138, of which 55 were waited for; matrix products, arithmetic and copies ran while one was open for 25% of the time, Pallas kernels for 0%

profile of v1, /device:TPU:0, one launch (start us, length us, event | category | flops | bytes accessed | tf_op | source)
XLA Modules:
  0.0 960.1 jit_solution(14159055062152073194)
XLA Ops:
  54.2 3.6 collective-permute-start.54
  58.5 8.9 collective-permute-done.29
  79.5 7.6 collective-permute-done.53
  87.1 3.8 collective-permute-start.62
  95.9 8.0 collective-permute-done.46
  108.3 3.8 collective-permute-done.4
  117.1 9.6 collective-permute-done.41
  135.5 10.2 %collective-permute-done.23 = bf16[64,4096]{1,0:T(8,128)(2,1)} collective-permute-done((bf16[64,4096]{1,0:T(8,128)(2,1)}, bf16[64,4096]{1,0:T(8,128)(2,1)}, u32[]{:S(2)}, u32[]{:S(2)}) %collective-permute-start.23) | collective-permute-done | bytes 524320 | tf_op jit(solution)/shard_map/ppermute | solution.py:57
  150.3 14.3 %collective-permute-done.16 = bf16[64,4096]{1,0:T(8,128)(2,1)S(1)} collective-permute-done((bf16[64,4096]{1,0:T(8,128)(2,1)S(1)}, bf16[64,4096]{1,0:T(8,128)(2,1)S(1)}, u32[]{:S(2)}, u32[]{:S(2)}) %collective-permute-start.16) | collective-permute-done | bytes 524320 | tf_op jit(solution)/shard_map/ppermute | solution.py:57
  175.0 20.0 %collective-permute-done.17 = bf16[32,4096]{1,0:T(8,128)(2,1)S(1)} collective-permute-done((bf16[32,4096]{1,0:T(8,128)(2,1)S(1)}, bf16[32,4096]{1,0:T(8,128)(2,1)S(1)}, u32[]{:S(2)}, u32[]{:S(2)}) %collective-permute-start.17) | collective-permute-done | bytes 262176 | tf_op jit(solution)/shard_map/ppermute | solution.py:57
  205.7 5.1 fusion.222
  217.8 10.0 %collective-permute-done.32 = bf16[256,2048]{1,0:T(8,128)(2,1)S(1)} collective-permute-done((bf16[256,2048]{1,0:T(8,128)(2,1)S(1)}, bf16[256,2048]{1,0:T(8,128)(2,1)S(1)}, u32[]{:S(2)}, u32[]{:S(2)}) %collective-permute-start.32) | collective-permute-done | bytes 1048608 | tf_op jit(solution)/shard_map/ppermute | solution.py:57
  238.1 4.0 fusion.393
  250.2 21.9 %while.28 = (s32[]{:T(128)}, bf16[4,384,4,64]{1,3,2,0:T(8,128)(2,1)}, bf16[4,384,4,64]{1,3,2,0:T(8,128)(2,1)}, bf16[4,384,4,64]{1,3,2,0:T(8,128)(2,1)}, bf16[4,3...) while((s32[]{:T(128)}, bf16[4,384,4,64]{1,3,2,0:T(8,128)(2,1)}, ...), condition=%wide.region_13.14_spmd.clone.clone, body=%wide.region_10.13_spmd.clone.sunk.clone | while | flops 232245504 | bytes 8128653 | solution.py:168
  274.7 4.7 fusion.355
  303.0 8.5 fusion.331
  312.9 4.6 fusion.354
  317.8 4.4 fusion.184
  327.8 14.3 %collective-permute-done.35 = f32[2,384]{1,0:T(2,128)S(1)} collective-permute-done((f32[2,384]{1,0:T(2,128)S(1)}, f32[2,384]{1,0:T(2,128)S(1)}, u32[]{:S(2)}, u32[]{:S(2)}) %collective-permute-start.35) | collective-permute-done | bytes 3104 | tf_op jit(solution)/shard_map/ppermute | solution.py:57
  354.2 8.9 add_reduce_fusion
  363.1 3.9 fusion.106
  371.5 4.6 convert_reduce_fusion
  376.1 3.8 convolution_convert_fusion.6
  381.1 5.5 convolution_convert_fusion.9
  390.1 22.0 %collective-permute-done.128 = bf16[512,1024]{1,0:T(8,128)(2,1)S(1)} collective-permute-done((bf16[512,1024]{1,0:T(8,128)(2,1)S(1)}, bf16[512,1024]{1,0:T(8,128)(2,1)S(1)}, u32[]{:S(2)}, u32[]{:S(2)}) %collective-permute-start.128) | collective-permute-done | bytes 1048608 | tf_op jit(solution)/shard_map/ppermute | solution.py:57
  428.3 7.3 collective-permute-done.130
  440.8 3.9 multiply_reduce_fusion.3
  451.4 11.2 %fusion.345 = (bf16[4096]{0:T(1024)(128)(2,1)}, bf16[384,4096]{1,0:T(8,128)(2,1)}) fusion(f32[384,4096]{1,0:T(8,128)S(1)} %bitcast.383, bf16[384,1024]{1,0:T(8,128)(2,1)S(1)} %fusion.182, bf16[1024,4096]{1,0:T(8,128)(2,1)} %constant_dynamic-update-slice_fusion.57), kind=kOutput, calls=%fused_computation.687 | convolution fusion | flops 3254251520 | bytes 18620416 | tf_op jit(solution)/shard_map/dot_general | solution.py:32
  462.6 10.4 %multiply_reduce_fusion.2 = (f32[384]{0:T(512)S(1)}, f32[384,1024]{1,0:T(8,128)}) fusion(f32[384,1024]{1,0:T(8,128)S(1)} %get-tuple-element.290, f32[384]{0:T(512)S(1)} %broadcast_multiply_fusion.1, f32[384,8192]{1,0:T(8,128)} %copy-done, s32[1024]{0:T(1024)S(1)} %copy-done.132, bf16[384,4096]{1,0:T(8,128)(2,1)} %get-tuple-element.273, ...), kind=kOutput, calls=%fused_computation.214 | convolution fusion | flops 4029939200 | bytes 16260096 | tf_op jit(solution)/shard_map/dot_general | solution.py:32
  484.7 10.7 %convolution_convert_fusion.1 = bf16[1024,4096]{1,0:T(8,128)(2,1)} fusion(bf16[384,1024]{1,0:T(8,128)(2,1)S(1)} %copy-done.146, f32[384,4096]{1,0:T(8,128)} %copy-done.140), kind=kOutput, calls=%fused_computation.87 | convolution fusion | flops 3239575552 | bytes 15466496 | tf_op jit(solution)/shard_map/dot_general | solution.py:36
  495.4 7.3 convolution_convert_fusion.2
  503.8 43.1 %while.29 = (s32[]{:T(128)}, f32[4,384,4,64]{1,3,2,0:T(8,128)}, f32[4,384,4,64]{1,3,2,0:T(8,128)}, bf16[4,384,4,64]{1,3,2,0:T(8,128)(2,1)S(1)}, bf16[4,384,4,64]...) while((s32[]{:T(128)}, f32[4,384,4,64]{1,3,2,0:T(8,128)}, ...), condition=%wide.region_29.30_spmd.clone.clone, body=%wide.region_25.29_spmd.clone.sunk.clone | while | flops 463061760 | bytes 18773100 | solution.py:186
  547.8 3.8 convolution_convert_fusion.8
  551.6 5.2 fusion.120
  571.5 3.8 fusion.160
  577.9 4.4 convolution_convert_fusion.5
  582.3 8.6 multiply_reduce_fusion.1
  591.1 4.3 fusion.351
  607.0 7.4 fusion.392
  615.2 6.0 collective-permute-start.114
  654.1 5.6 collective-permute-done.117
  661.1 6.1 collective-permute-done.110
  669.4 4.3 collective-permute-done.123
  676.5 7.3 collective-permute-done.124
  691.5 3.6 collective-permute-done.126
  703.7 9.8 %collective-permute-done.111 = bf16[64,4096]{1,0:T(8,128)(2,1)S(1)} collective-permute-done((bf16[64,4096]{1,0:T(8,128)(2,1)}, bf16[64,4096]{1,0:T(8,128)(2,1)S(1)}, u32[]{:S(2)}, u32[]{:S(2)}) %collective-permute-start.111) | collective-permute-done | bytes 524320 | tf_op jit(solution)/shard_map/ppermute | solution.py:57
  718.4 10.0 %collective-permute-done.88 = bf16[256,1024]{1,0:T(8,128)(2,1)S(1)} collective-permute-done((bf16[256,1024]{1,0:T(8,128)(2,1)S(1)}, bf16[256,1024]{1,0:T(8,128)(2,1)S(1)}, u32[]{:S(2)}, u32[]{:S(2)}) %collective-permute-start.88) | collective-permute-done | bytes 524320 | tf_op jit(solution)/shard_map/ppermute | solution.py:57
  730.4 8.8 collective-permute-done.81
  741.1 6.0 collective-permute-done.89
  748.3 5.8 collective-permute-done.82
  770.5 7.0 collective-permute-done.74
  781.6 4.3 add_convert_fusion.1
  789.8 6.1 collective-permute-done.75
  803.3 5.2 collective-permute-done.78
  811.1 6.0 collective-permute-done.77
  825.8 10.9 %collective-permute-done.102 = bf16[256,4096]{1,0:T(8,128)(2,1)} collective-permute-done((bf16[256,4096]{1,0:T(8,128)(2,1)}, bf16[256,4096]{1,0:T(8,128)(2,1)}, u32[]{:S(2)}, u32[]{:S(2)}) %collective-permute-start.102) | collective-permute-done | bytes 2097184 | tf_op jit(solution)/shard_map/ppermute | solution.py:57
  836.7 3.9 add_convert_fusion
  841.2 7.7 collective-permute-done.95
  848.8 3.9 add_convert_fusion.3
  853.4 17.3 %collective-permute-done.103 = bf16[128,4096]{1,0:T(8,128)(2,1)S(1)} collective-permute-done((bf16[128,4096]{1,0:T(8,128)(2,1)S(1)}, bf16[128,4096]{1,0:T(8,128)(2,1)S(1)}, u32[]{:S(2)}, u32[]{:S(2)}) %collective-permute-start.103) | collective-permute-done | bytes 1048608 | tf_op jit(solution)/shard_map/ppermute | solution.py:57
  878.1 4.1 collective-permute-done.106
  882.2 20.0 %collective-permute-done.105 = bf16[32,4096]{1,0:T(8,128)(2,1)S(1)} collective-permute-done((bf16[32,4096]{1,0:T(8,128)(2,1)S(1)}, bf16[32,4096]{1,0:T(8,128)(2,1)S(1)}, u32[]{:S(2)}, u32[]{:S(2)}) %collective-permute-start.105) | collective-permute-done | bytes 262176 | tf_op jit(solution)/shard_map/ppermute | solution.py:57
  902.4 12.3 %collective-permute-done.98 = bf16[32,4096]{1,0:T(8,128)(2,1)S(1)} collective-permute-done((bf16[32,4096]{1,0:T(8,128)(2,1)S(1)}, bf16[32,4096]{1,0:T(8,128)(2,1)S(1)}, u32[]{:S(2)}, u32[]{:S(2)}) %collective-permute-start.98) | collective-permute-done | bytes 262176 | tf_op jit(solution)/shard_map/ppermute | solution.py:57
  930.1 5.0 collective-permute-start.137
  (943 shorter events, 478.4 us)
Async XLA Ops:
  3.4 36.8 %collective-permute-start = (bf16[32,512]{1,0:T(8,128)(2,1)S(1)}, bf16[32,512]{1,0:T(8,128)(2,1)}, u32[]{:S(2)}, u32[]{:S(2)}) collective-permute-start(bf16[32,512]{1,0:T(8,128)(2,1)S(1)} %get-tuple-element.292), channel_id=1, source_target_pairs={{0,8},{8,16},{16,24},{24,0},{1,9},{9,17},{17,25},{25,1},{2,10},{10... | collective-permute-start | bytes 98312 | tf_op jit(solution)/shard_map/ppermute | solution.py:57
  6.4 35.5 %collective-permute-start.1 = (bf16[32,512]{1,0:T(8,128)(2,1)S(1)}, bf16[32,512]{1,0:T(8,128)(2,1)}, u32[]{:S(2)}, u32[]{:S(2)}) collective-permute-start(bf16[32,512]{1,0:T(8,128)(2,1)S(1)} %get-tuple-element.292), channel_id=1, source_target_pairs={{0,16},{8,24},{16,0},{24,8},{1,17},{9,25},{17,1},{25,9},{2,18},{10... | collective-permute-start | bytes 98312 | tf_op jit(solution)/shard_map/ppermute | solution.py:57
  22.3 21.5 %collective-permute-start.2 = (bf16[32,512]{1,0:T(8,128)(2,1)S(1)}, bf16[32,512]{1,0:T(8,128)(2,1)S(1)}, u32[]{:S(2)}, u32[]{:S(2)}) collective-permute-start(bf16[32,512]{1,0:T(8,128)(2,1)S(1)} %get-tuple-element.292), channel_id=1, source_target_pairs={{0,24},{8,0},{16,8},{24,16},{1,25},{9,1},{17,9},{25,17},{2,26},{10... | collective-permute-start | bytes 98312 | tf_op jit(solution)/shard_map/ppermute | solution.py:57
  43.8 23.7 %collective-permute-start.29 = (bf16[32,2048]{1,0:T(8,128)(2,1)S(1)}, bf16[32,2048]{1,0:T(8,128)(2,1)S(1)}, u32[]{:S(2)}, u32[]{:S(2)}) collective-permute-start(bf16[32,2048]{1,0:T(8,128)(2,1)S(1)} %get-tuple-element.388), channel_id=1, source_target_pairs={{0,16},{8,24},{16,0},{24,8},{1,17},{9,25},{17,1},{25,9},{2,18},{10... | collective-permute-start | bytes 393224 | tf_op jit(solution)/shard_map/ppermute | solution.py:57
  45.5 22.0 %collective-permute-start.30 = (bf16[32,2048]{1,0:T(8,128)(2,1)S(1)}, bf16[32,2048]{1,0:T(8,128)(2,1)S(1)}, u32[]{:S(2)}, u32[]{:S(2)}) collective-permute-start(bf16[32,2048]{1,0:T(8,128)(2,1)S(1)} %get-tuple-element.388), channel_id=1, source_target_pairs={{0,24},{8,0},{16,8},{24,16},{1,25},{9,1},{17,9},{25,17},{2,26},{10... | collective-permute-start | bytes 393224 | tf_op jit(solution)/shard_map/ppermute | solution.py:57
  48.6 26.6 %collective-permute-start.52 = (bf16[32,4096]{1,0:T(8,128)(2,1)}, bf16[32,4096]{1,0:T(8,128)(2,1)S(1)}, u32[]{:S(2)}, u32[]{:S(2)}) collective-permute-start(bf16[32,4096]{1,0:T(8,128)(2,1)} %get-tuple-element.356), channel_id=1, source_target_pairs={{0,8},{8,16},{16,24},{24,0},{1,9},{9,17},{17,25},{25,1},{2,10},{10... | collective-permute-start | bytes 786440 | tf_op jit(solution)/shard_map/ppermute | solution.py:57
  50.5 36.6 %collective-permute-start.53 = (bf16[32,4096]{1,0:T(8,128)(2,1)}, bf16[32,4096]{1,0:T(8,128)(2,1)S(1)}, u32[]{:S(2)}, u32[]{:S(2)}) collective-permute-start(bf16[32,4096]{1,0:T(8,128)(2,1)} %get-tuple-element.356), channel_id=1, source_target_pairs={{0,16},{8,24},{16,0},{24,8},{1,17},{9,25},{17,1},{25,9},{2,18},{10... | collective-permute-start | bytes 786440 | tf_op jit(solution)/shard_map/ppermute | solution.py:57
  54.2 36.6 %collective-permute-start.54 = (bf16[32,4096]{1,0:T(8,128)(2,1)}, bf16[32,4096]{1,0:T(8,128)(2,1)S(1)}, u32[]{:S(2)}, u32[]{:S(2)}) collective-permute-start(bf16[32,4096]{1,0:T(8,128)(2,1)} %get-tuple-element.356), channel_id=1, source_target_pairs={{0,24},{8,0},{16,8},{24,16},{1,25},{9,1},{17,9},{25,17},{2,26},{10... | collective-permute-start | bytes 786440 | tf_op jit(solution)/shard_map/ppermute | solution.py:57
  67.4 27.2 %collective-permute-start.45 = (bf16[32,4096]{1,0:T(8,128)(2,1)S(1)}, bf16[32,4096]{1,0:T(8,128)(2,1)S(1)}, u32[]{:S(2)}, u32[]{:S(2)}) collective-permute-start(bf16[32,4096]{1,0:T(8,128)(2,1)S(1)} %copy-done.64), channel_id=1, source_target_pairs={{0,8},{8,16},{16,24},{24,0},{1,9},{9,17},{17,25},{25,1},{2,10},{10... | collective-permute-start | bytes 786440 | tf_op jit(solution)/shard_map/ppermute | solution.py:57
  72.9 31.1 %collective-permute-start.46 = (bf16[32,4096]{1,0:T(8,128)(2,1)S(1)}, bf16[32,4096]{1,0:T(8,128)(2,1)S(1)}, u32[]{:S(2)}, u32[]{:S(2)}) collective-permute-start(bf16[32,4096]{1,0:T(8,128)(2,1)S(1)} %copy-done.64), channel_id=1, source_target_pairs={{0,16},{8,24},{16,0},{24,8},{1,17},{9,25},{17,1},{25,9},{2,18},{10... | collective-permute-start | bytes 786440 | tf_op jit(solution)/shard_map/ppermute | solution.py:57
  75.2 30.4 %collective-permute-start.47 = (bf16[32,4096]{1,0:T(8,128)(2,1)S(1)}, bf16[32,4096]{1,0:T(8,128)(2,1)S(1)}, u32[]{:S(2)}, u32[]{:S(2)}) collective-permute-start(bf16[32,4096]{1,0:T(8,128)(2,1)S(1)} %copy-done.64), channel_id=1, source_target_pairs={{0,24},{8,0},{16,8},{24,16},{1,25},{9,1},{17,9},{25,17},{2,26},{10... | collective-permute-start | bytes 786440 | tf_op jit(solution)/shard_map/ppermute | solution.py:57
  87.1 236.7 %collective-permute-start.62 = (bf16[128,1024]{1,0:T(8,128)(2,1)}, bf16[128,1024]{1,0:T(8,128)(2,1)}, u32[]{:S(2)}, u32[]{:S(2)}) collective-permute-start(bf16[128,1024]{1,0:T(8,128)(2,1)} %get-tuple-element.294), channel_id=1, source_target_pairs={{0,8},{8,16},{16,24},{24,0},{1,9},{9,17},{17,25},{25,1},{2,10},{10... | collective-permute-start | bytes 786440 | tf_op jit(solution)/shard_map/ppermute | solution.py:57
  90.8 21.9 %collective-permute-start.22 = (bf16[64,4096]{1,0:T(8,128)(2,1)S(1)}, bf16[64,4096]{1,0:T(8,128)(2,1)S(1)}, u32[]{:S(2)}, u32[]{:S(2)}) collective-permute-start(bf16[64,4096]{1,0:T(8,128)(2,1)S(1)} %get-tuple-element.326), channel_id=1, source_target_pairs={{0,1},{1,0},{2,3},{3,2},{4,5},{5,4},{6,7},{7,6},{8,9},{9,8},{10,11... | collective-permute-start | bytes 1572872 | tf_op jit(solution)/shard_map/ppermute | solution.py:57
  94.6 40.4 %collective-permute-start.21 = (bf16[64,4096]{1,0:T(8,128)(2,1)}, bf16[64,4096]{1,0:T(8,128)(2,1)}, u32[]{:S(2)}, u32[]{:S(2)}) collective-permute-start(bf16[64,4096]{1,0:T(8,128)(2,1)} %get-tuple-element.325), channel_id=1, source_target_pairs={{0,1},{1,0},{2,3},{3,2},{4,5},{5,4},{6,7},{7,6},{8,9},{9,8},{10,11... | collective-permute-start | bytes 1572872 | tf_op jit(solution)/shard_map/ppermute | solution.py:57
  112.2 36.5 %collective-permute-start.14 = (bf16[64,4096]{1,0:T(8,128)(2,1)}, bf16[64,4096]{1,0:T(8,128)(2,1)}, u32[]{:S(2)}, u32[]{:S(2)}) collective-permute-start(bf16[64,4096]{1,0:T(8,128)(2,1)} %get-tuple-element.323), channel_id=1, source_target_pairs={{0,1},{1,0},{2,3},{3,2},{4,5},{5,4},{6,7},{7,6},{8,9},{9,8},{10,11... | collective-permute-start | bytes 1572872 | tf_op jit(solution)/shard_map/ppermute | solution.py:57
  129.0 38.7 %collective-permute-start.55 = (bf16[128,4096]{1,0:T(8,128)(2,1)}, bf16[128,4096]{1,0:T(8,128)(2,1)}, u32[]{:S(2)}, u32[]{:S(2)}) collective-permute-start(bf16[128,4096]{1,0:T(8,128)(2,1)} %pad_maximum_fusion.3), channel_id=1, source_target_pairs={{0,2},{2,0},{1,3},{3,1},{4,6},{6,4},{5,7},{7,5},{8,10},{10,8},{9,1... | collective-permute-start | bytes 3145736 | tf_op jit(solution)/shard_map/ppermute | solution.py:57
  135.0 37.1 %collective-permute-start.48 = (bf16[128,4096]{1,0:T(8,128)(2,1)}, bf16[128,4096]{1,0:T(8,128)(2,1)S(1)}, u32[]{:S(2)}, u32[]{:S(2)}) collective-permute-start(bf16[128,4096]{1,0:T(8,128)(2,1)} %pad_maximum_fusion.2), channel_id=1, source_target_pairs={{0,4},{4,0},{1,5},{5,1},{2,6},{6,2},{3,7},{7,3},{8,12},{12,8},{9,1... | collective-permute-start | bytes 3145736 | tf_op jit(solution)/shard_map/ppermute | solution.py:57
  148.7 65.3 %collective-permute-start.42 = (bf16[256,2048]{1,0:T(8,128)(2,1)S(1)}, bf16[256,2048]{1,0:T(8,128)(2,1)S(1)}, u32[]{:S(2)}, u32[]{:S(2)}) collective-permute-start(bf16[256,2048]{1,0:T(8,128)(2,1)S(1)} %copy-done.123), channel_id=1, source_target_pairs={{0,4},{4,0},{1,5},{5,1},{2,6},{6,2},{3,7},{7,3},{8,12},{12,8},{9,1... | collective-permute-start | bytes 3145736 | tf_op jit(solution)/shard_map/ppermute | solution.py:57
  167.7 27.3 %collective-permute-start.17 = (bf16[32,4096]{1,0:T(8,128)(2,1)S(1)}, bf16[32,4096]{1,0:T(8,128)(2,1)S(1)}, u32[]{:S(2)}, u32[]{:S(2)}) collective-permute-start(bf16[32,4096]{1,0:T(8,128)(2,1)S(1)} %split.397), channel_id=1, source_target_pairs={{0,4},{4,0},{1,5},{5,1},{2,6},{6,2},{3,7},{7,3},{8,12},{12,8},{9,1... | collective-permute-start | bytes 786440 | tf_op jit(solution)/shard_map/ppermute | solution.py:57
  173.8 21.4 %collective-permute-start.27 = (bf16[8,4096]{1,0:T(8,128)(2,1)S(1)}, bf16[8,4096]{1,0:T(8,128)(2,1)S(1)}, u32[]{:S(2)}, u32[]{:S(2)}) collective-permute-start(bf16[8,4096]{1,0:T(8,128)(2,1)S(1)} %get-tuple-element.393), channel_id=1, source_target_pairs={{0,8},{8,16},{16,24},{24,0},{1,9},{9,17},{17,25},{25,1},{2,10},{10... | collective-permute-start | bytes 196616 | tf_op jit(solution)/shard_map/ppermute | solution.py:57
  175.0 22.2 %collective-permute-start.26 = (bf16[8,4096]{1,0:T(8,128)(2,1)S(1)}, bf16[8,4096]{1,0:T(8,128)(2,1)S(1)}, u32[]{:S(2)}, u32[]{:S(2)}) collective-permute-start(bf16[8,4096]{1,0:T(8,128)(2,1)S(1)} %get-tuple-element.394), channel_id=1, source_target_pairs={{0,16},{8,24},{16,0},{24,8},{1,17},{9,25},{17,1},{25,9},{2,18},{10... | collective-permute-start | bytes 196616 | tf_op jit(solution)/shard_map/ppermute | solution.py:57
  202.2 28.2 %collective-permute-start.43 = (bf16[256,2048]{1,0:T(8,128)(2,1)S(1)}, bf16[256,2048]{1,0:T(8,128)(2,1)S(1)}, u32[]{:S(2)}, u32[]{:S(2)}) collective-permute-start(bf16[256,2048]{1,0:T(8,128)(2,1)S(1)} %copy-done.123), channel_id=1, source_target_pairs={{0,1},{1,0},{2,3},{3,2},{4,5},{5,4},{6,7},{7,6},{8,9},{9,8},{10,11... | collective-permute-start | bytes 3145736 | tf_op jit(solution)/shard_map/ppermute | solution.py:57
  204.3 23.5 %collective-permute-start.32 = (bf16[256,2048]{1,0:T(8,128)(2,1)S(1)}, bf16[256,2048]{1,0:T(8,128)(2,1)S(1)}, u32[]{:S(2)}, u32[]{:S(2)}) collective-permute-start(bf16[256,2048]{1,0:T(8,128)(2,1)S(1)} %copy-done.120), channel_id=1, source_target_pairs={{0,2},{2,0},{1,3},{3,1},{4,6},{6,4},{5,7},{7,5},{8,10},{10,8},{9,1... | collective-permute-start | bytes 3145736 | tf_op jit(solution)/shard_map/ppermute | solution.py:57
  205.6 24.9 %collective-permute-start.33 = (bf16[256,2048]{1,0:T(8,128)(2,1)S(1)}, bf16[256,2048]{1,0:T(8,128)(2,1)S(1)}, u32[]{:S(2)}, u32[]{:S(2)}) collective-permute-start(bf16[256,2048]{1,0:T(8,128)(2,1)S(1)} %copy-done.120), channel_id=1, source_target_pairs={{0,1},{1,0},{2,3},{3,2},{4,5},{5,4},{6,7},{7,6},{8,9},{9,8},{10,11... | collective-permute-start | bytes 3145736 | tf_op jit(solution)/shard_map/ppermute | solution.py:57
  227.8 57.5 %collective-permute-start.56 = (bf16[256,4096]{1,0:T(8,128)(2,1)}, bf16[256,4096]{1,0:T(8,128)(2,1)}, u32[]{:S(2)}, u32[]{:S(2)}) collective-permute-start(bf16[256,4096]{1,0:T(8,128)(2,1)} %get-tuple-element.346), channel_id=1, source_target_pairs={{0,4},{4,0},{1,5},{5,1},{2,6},{6,2},{3,7},{7,3},{8,12},{12,8},{9,1... | collective-permute-start | bytes 6291464 | tf_op jit(solution)/shard_map/ppermute | solution.py:57
  230.5 60.8 %collective-permute-start.57 = (bf16[256,4096]{1,0:T(8,128)(2,1)}, bf16[256,4096]{1,0:T(8,128)(2,1)}, u32[]{:S(2)}, u32[]{:S(2)}) collective-permute-start(bf16[256,4096]{1,0:T(8,128)(2,1)} %get-tuple-element.346), channel_id=1, source_target_pairs={{0,1},{1,0},{2,3},{3,2},{4,5},{5,4},{6,7},{7,6},{8,9},{9,8},{10,11... | collective-permute-start | bytes 6291464 | tf_op jit(solution)/shard_map/ppermute | solution.py:57
  232.1 47.9 %collective-permute-start.49 = (bf16[256,4096]{1,0:T(8,128)(2,1)}, bf16[256,4096]{1,0:T(8,128)(2,1)}, u32[]{:S(2)}, u32[]{:S(2)}) collective-permute-start(bf16[256,4096]{1,0:T(8,128)(2,1)} %get-tuple-element.344), channel_id=1, source_target_pairs={{0,2},{2,0},{1,3},{3,1},{4,6},{6,4},{5,7},{7,5},{8,10},{10,8},{9,1... | collective-permute-start | bytes 6291464 | tf_op jit(solution)/shard_map/ppermute | solution.py:57
  236.6 58.1 %collective-permute-start.50 = (bf16[256,4096]{1,0:T(8,128)(2,1)}, bf16[256,4096]{1,0:T(8,128)(2,1)}, u32[]{:S(2)}, u32[]{:S(2)}) collective-permute-start(bf16[256,4096]{1,0:T(8,128)(2,1)} %get-tuple-element.344), channel_id=1, source_target_pairs={{0,1},{1,0},{2,3},{3,2},{4,5},{5,4},{6,7},{7,6},{8,9},{9,8},{10,11... | collective-permute-start | bytes 6291464 | tf_op jit(solution)/shard_map/ppermute | solution.py:57
  285.4 38.4 %collective-permute-start.63 = (bf16[128,1024]{1,0:T(8,128)(2,1)}, bf16[128,1024]{1,0:T(8,128)(2,1)S(1)}, u32[]{:S(2)}, u32[]{:S(2)}) collective-permute-start(bf16[128,1024]{1,0:T(8,128)(2,1)} %get-tuple-element.294), channel_id=1, source_target_pairs={{0,16},{8,24},{16,0},{24,8},{1,17},{9,25},{17,1},{25,9},{2,18},{10... | collective-permute-start | bytes 786440 | tf_op jit(solution)/shard_map/ppermute | solution.py:57
  294.7 29.1 %collective-permute-start.64 = (bf16[128,1024]{1,0:T(8,128)(2,1)}, bf16[128,1024]{1,0:T(8,128)(2,1)S(1)}, u32[]{:S(2)}, u32[]{:S(2)}) collective-permute-start(bf16[128,1024]{1,0:T(8,128)(2,1)} %get-tuple-element.294), channel_id=1, source_target_pairs={{0,24},{8,0},{16,8},{24,16},{1,25},{9,1},{17,9},{25,17},{2,26},{10... | collective-permute-start | bytes 786440 | tf_op jit(solution)/shard_map/ppermute | solution.py:57
  322.3 21.2 %collective-permute-start.59 = (bf16[384,1024]{1,0:T(8,128)(2,1)}, bf16[384,1024]{1,0:T(8,128)(2,1)}, u32[]{:S(2)}, u32[]{:S(2)}) collective-permute-start(bf16[384,1024]{1,0:T(8,128)(2,1)} %fusion.184), channel_id=1, source_target_pairs={{0,2},{2,0},{1,3},{3,1},{4,6},{6,4},{5,7},{7,5},{8,10},{10,8},{9,1... | collective-permute-start | bytes 2359304 | tf_op jit(solution)/shard_map/ppermute | solution.py:57
  326.7 25.2 %collective-permute-start.65 = (bf16[512,1024]{1,0:T(8,128)(2,1)}, bf16[512,1024]{1,0:T(8,128)(2,1)}, u32[]{:S(2)}, u32[]{:S(2)}) collective-permute-start(bf16[512,1024]{1,0:T(8,128)(2,1)} %pad_maximum_fusion.4), channel_id=1, source_target_pairs={{0,4},{4,0},{1,5},{5,1},{2,6},{6,2},{3,7},{7,3},{8,12},{12,8},{9,1... | collective-permute-start | bytes 3145736 | tf_op jit(solution)/shard_map/ppermute | solution.py:57
  386.7 25.5 %collective-permute-start.128 = (bf16[512,1024]{1,0:T(8,128)(2,1)S(1)}, bf16[512,1024]{1,0:T(8,128)(2,1)S(1)}, u32[]{:S(2)}, u32[]{:S(2)}) collective-permute-start(bf16[512,1024]{1,0:T(8,128)(2,1)S(1)} %split.485), channel_id=1, source_target_pairs={{0,4},{4,0},{1,5},{5,1},{2,6},{6,2},{3,7},{7,3},{8,12},{12,8},{9,1... | collective-permute-start | bytes 3145736 | tf_op jit(solution)/shard_map/ppermute | solution.py:57
  387.2 50.4 %collective-permute-start.69 = (bf16[384,1024]{1,0:T(8,128)(2,1)}, bf16[384,1024]{1,0:T(8,128)(2,1)}, u32[]{:S(2)}, u32[]{:S(2)}) collective-permute-start(bf16[384,1024]{1,0:T(8,128)(2,1)} %get-tuple-element.306), channel_id=1, source_target_pairs={{0,1},{1,0},{2,3},{3,2},{4,5},{5,4},{6,7},{7,6},{8,9},{9,8},{10,11... | collective-permute-start | bytes 2359304 | tf_op jit(solution)/shard_map/ppermute | solution.py:57
  388.5 49.2 %collective-permute-start.71 = (bf16[384,1024]{1,0:T(8,128)(2,1)}, bf16[384,1024]{1,0:T(8,128)(2,1)}, u32[]{:S(2)}, u32[]{:S(2)}) collective-permute-start(bf16[384,1024]{1,0:T(8,128)(2,1)} %add_convert_fusion.12), channel_id=1, source_target_pairs={{0,2},{2,0},{1,3},{3,1},{4,6},{6,4},{5,7},{7,5},{8,10},{10,8},{9,1... | collective-permute-start | bytes 2359304 | tf_op jit(solution)/shard_map/ppermute | solution.py:57
  615.2 30.1 %collective-permute-start.114 = (bf16[8,4096]{1,0:T(8,128)(2,1)}, bf16[8,4096]{1,0:T(8,128)(2,1)}, u32[]{:S(2)}, u32[]{:S(2)}) collective-permute-start(bf16[8,4096]{1,0:T(8,128)(2,1)} %get-tuple-element.402), channel_id=1, source_target_pairs={{0,8},{8,16},{16,24},{24,0},{1,9},{9,17},{17,25},{25,1},{2,10},{10... | collective-permute-start | bytes 196616 | tf_op jit(solution)/shard_map/ppermute | solution.py:57
  621.2 26.9 %collective-permute-start.115 = (bf16[8,4096]{1,0:T(8,128)(2,1)}, bf16[8,4096]{1,0:T(8,128)(2,1)S(1)}, u32[]{:S(2)}, u32[]{:S(2)}) collective-permute-start(bf16[8,4096]{1,0:T(8,128)(2,1)} %get-tuple-element.402), channel_id=1, source_target_pairs={{0,16},{8,24},{16,0},{24,8},{1,17},{9,25},{17,1},{25,9},{2,18},{10... | collective-permute-start | bytes 196616 | tf_op jit(solution)/shard_map/ppermute | solution.py:57
  621.2 26.9 %collective-permute-start.116 = (bf16[8,4096]{1,0:T(8,128)(2,1)}, bf16[8,4096]{1,0:T(8,128)(2,1)S(1)}, u32[]{:S(2)}, u32[]{:S(2)}) collective-permute-start(bf16[8,4096]{1,0:T(8,128)(2,1)} %get-tuple-element.402), channel_id=1, source_target_pairs={{0,24},{8,0},{16,8},{24,16},{1,25},{9,1},{17,9},{25,17},{2,26},{10... | collective-permute-start | bytes 196616 | tf_op jit(solution)/shard_map/ppermute | solution.py:57
  623.6 27.3 %collective-permute-start.107 = (bf16[8,4096]{1,0:T(8,128)(2,1)}, bf16[8,4096]{1,0:T(8,128)(2,1)S(1)}, u32[]{:S(2)}, u32[]{:S(2)}) collective-permute-start(bf16[8,4096]{1,0:T(8,128)(2,1)} %get-tuple-element.403), channel_id=1, source_target_pairs={{0,8},{8,16},{16,24},{24,0},{1,9},{9,17},{17,25},{25,1},{2,10},{10... | collective-permute-start | bytes 196616 | tf_op jit(solution)/shard_map/ppermute | solution.py:57
  623.6 27.4 %collective-permute-start.108 = (bf16[8,4096]{1,0:T(8,128)(2,1)}, bf16[8,4096]{1,0:T(8,128)(2,1)S(1)}, u32[]{:S(2)}, u32[]{:S(2)}) collective-permute-start(bf16[8,4096]{1,0:T(8,128)(2,1)} %get-tuple-element.403), channel_id=1, source_target_pairs={{0,16},{8,24},{16,0},{24,8},{1,17},{9,25},{17,1},{25,9},{2,18},{10... | collective-permute-start | bytes 196616 | tf_op jit(solution)/shard_map/ppermute | solution.py:57
  648.0 26.4 %collective-permute-start.87 = (bf16[256,1024]{1,0:T(8,128)(2,1)S(1)}, bf16[256,1024]{1,0:T(8,128)(2,1)S(1)}, u32[]{:S(2)}, u32[]{:S(2)}) collective-permute-start(bf16[256,1024]{1,0:T(8,128)(2,1)S(1)} %copy-done.82), channel_id=1, source_target_pairs={{0,1},{1,0},{2,3},{3,2},{4,5},{5,4},{6,7},{7,6},{8,9},{9,8},{10,11... | collective-permute-start | bytes 1572872 | tf_op jit(solution)/shard_map/ppermute | solution.py:57
  648.1 70.2 %collective-permute-start.86 = (bf16[256,1024]{1,0:T(8,128)(2,1)}, bf16[256,1024]{1,0:T(8,128)(2,1)}, u32[]{:S(2)}, u32[]{:S(2)}) collective-permute-start(bf16[256,1024]{1,0:T(8,128)(2,1)} %get-tuple-element.314), channel_id=1, source_target_pairs={{0,1},{1,0},{2,3},{3,2},{4,5},{5,4},{6,7},{7,6},{8,9},{9,8},{10,11... | collective-permute-start | bytes 1572872 | tf_op jit(solution)/shard_map/ppermute | solution.py:57
  650.8 35.4 %collective-permute-start.80 = (bf16[256,1024]{1,0:T(8,128)(2,1)S(1)}, bf16[256,1024]{1,0:T(8,128)(2,1)S(1)}, u32[]{:S(2)}, u32[]{:S(2)}) collective-permute-start(bf16[256,1024]{1,0:T(8,128)(2,1)S(1)} %copy-done.81), channel_id=1, source_target_pairs={{0,1},{1,0},{2,3},{3,2},{4,5},{5,4},{6,7},{7,6},{8,9},{9,8},{10,11... | collective-permute-start | bytes 1572872 | tf_op jit(solution)/shard_map/ppermute | solution.py:57
  668.9 30.6 %collective-permute-start.118 = (bf16[64,4096]{1,0:T(8,128)(2,1)}, bf16[64,4096]{1,0:T(8,128)(2,1)}, u32[]{:S(2)}, u32[]{:S(2)}) collective-permute-start(bf16[64,4096]{1,0:T(8,128)(2,1)} %get-tuple-element.363), channel_id=1, source_target_pairs={{0,4},{4,0},{1,5},{5,1},{2,6},{6,2},{3,7},{7,3},{8,12},{12,8},{9,1... | collective-permute-start | bytes 1572872 | tf_op jit(solution)/shard_map/ppermute | solution.py:57
  691.5 38.3 %collective-permute-start.79 = (bf16[256,1024]{1,0:T(8,128)(2,1)}, bf16[256,1024]{1,0:T(8,128)(2,1)}, u32[]{:S(2)}, u32[]{:S(2)}) collective-permute-start(bf16[256,1024]{1,0:T(8,128)(2,1)} %get-tuple-element.312), channel_id=1, source_target_pairs={{0,1},{1,0},{2,3},{3,2},{4,5},{5,4},{6,7},{7,6},{8,9},{9,8},{10,11... | collective-permute-start | bytes 1572872 | tf_op jit(solution)/shard_map/ppermute | solution.py:57
  713.5 56.0 %collective-permute-start.72 = (bf16[256,2048]{1,0:T(8,128)(2,1)}, bf16[256,2048]{1,0:T(8,128)(2,1)}, u32[]{:S(2)}, u32[]{:S(2)}) collective-permute-start(bf16[256,2048]{1,0:T(8,128)(2,1)} %get-tuple-element.303), channel_id=1, source_target_pairs={{0,1},{1,0},{2,3},{3,2},{4,5},{5,4},{6,7},{7,6},{8,9},{9,8},{10,11... | collective-permute-start | bytes 3145736 | tf_op jit(solution)/shard_map/ppermute | solution.py:57
  714.2 25.0 %collective-permute-start.81 = (bf16[256,1024]{1,0:T(8,128)(2,1)S(1)}, bf16[256,1024]{1,0:T(8,128)(2,1)S(1)}, u32[]{:S(2)}, u32[]{:S(2)}) collective-permute-start(bf16[256,1024]{1,0:T(8,128)(2,1)S(1)} %copy-done.80), channel_id=1, source_target_pairs={{0,4},{4,0},{1,5},{5,1},{2,6},{6,2},{3,7},{7,3},{8,12},{12,8},{9,1... | collective-permute-start | bytes 1572872 | tf_op jit(solution)/shard_map/ppermute | solution.py:57
  718.4 62.7 %collective-permute-start.101 = (bf16[256,4096]{1,0:T(8,128)(2,1)}, bf16[256,4096]{1,0:T(8,128)(2,1)}, u32[]{:S(2)}, u32[]{:S(2)}) collective-permute-start(bf16[256,4096]{1,0:T(8,128)(2,1)} %get-tuple-element.302), channel_id=1, source_target_pairs={{0,1},{1,0},{2,3},{3,2},{4,5},{5,4},{6,7},{7,6},{8,9},{9,8},{10,11... | collective-permute-start | bytes 6291464 | tf_op jit(solution)/shard_map/ppermute | solution.py:57
  728.3 27.0 %collective-permute-start.120 = (bf16[64,4096]{1,0:T(8,128)(2,1)}, bf16[64,4096]{1,0:T(8,128)(2,1)S(1)}, u32[]{:S(2)}, u32[]{:S(2)}) collective-permute-start(bf16[64,4096]{1,0:T(8,128)(2,1)} %collective-permute-done.118), channel_id=1, source_target_pairs={{0,1},{1,0},{2,3},{3,2},{4,5},{5,4},{6,7},{7,6},{8,9},{9,8},{10,11... | collective-permute-start | bytes 1572872 | tf_op jit(solution)/shard_map/ppermute | solution.py:57
  729.9 28.1 %collective-permute-start.113 = (bf16[64,4096]{1,0:T(8,128)(2,1)S(1)}, bf16[64,4096]{1,0:T(8,128)(2,1)S(1)}, u32[]{:S(2)}, u32[]{:S(2)}) collective-permute-start(bf16[64,4096]{1,0:T(8,128)(2,1)S(1)} %collective-permute-done.111), channel_id=1, source_target_pairs={{0,1},{1,0},{2,3},{3,2},{4,5},{5,4},{6,7},{7,6},{8,9},{9,8},{10,11... | collective-permute-start | bytes 1572872 | tf_op jit(solution)/shard_map/ppermute | solution.py:57
  754.2 23.3 %collective-permute-start.74 = (bf16[256,2048]{1,0:T(8,128)(2,1)}, bf16[256,2048]{1,0:T(8,128)(2,1)}, u32[]{:S(2)}, u32[]{:S(2)}) collective-permute-start(bf16[256,2048]{1,0:T(8,128)(2,1)} %add_convert_fusion.10), channel_id=1, source_target_pairs={{0,2},{2,0},{1,3},{3,1},{4,6},{6,4},{5,7},{7,5},{8,10},{10,8},{9,1... | collective-permute-start | bytes 3145736 | tf_op jit(solution)/shard_map/ppermute | solution.py:57
  765.4 60.4 %collective-permute-start.100 = (bf16[256,4096]{1,0:T(8,128)(2,1)}, bf16[256,4096]{1,0:T(8,128)(2,1)}, u32[]{:S(2)}, u32[]{:S(2)}) collective-permute-start(bf16[256,4096]{1,0:T(8,128)(2,1)} %get-tuple-element.301), channel_id=1, source_target_pairs={{0,1},{1,0},{2,3},{3,2},{4,5},{5,4},{6,7},{7,6},{8,9},{9,8},{10,11... | collective-permute-start | bytes 6291464 | tf_op jit(solution)/shard_map/ppermute | solution.py:57
  769.5 30.7 %collective-permute-start.85 = (bf16[32,1024]{1,0:T(8,128)(2,1)S(1)}, bf16[32,1024]{1,0:T(8,128)(2,1)S(1)}, u32[]{:S(2)}, u32[]{:S(2)}) collective-permute-start(bf16[32,1024]{1,0:T(8,128)(2,1)S(1)} %copy-done.105), channel_id=1, source_target_pairs={{0,8},{8,16},{16,24},{24,0},{1,9},{9,17},{17,25},{25,1},{2,10},{10... | collective-permute-start | bytes 196616 | tf_op jit(solution)/shard_map/ppermute | solution.py:57
  777.5 22.8 %collective-permute-start.84 = (bf16[32,1024]{1,0:T(8,128)(2,1)S(1)}, bf16[32,1024]{1,0:T(8,128)(2,1)S(1)}, u32[]{:S(2)}, u32[]{:S(2)}) collective-permute-start(bf16[32,1024]{1,0:T(8,128)(2,1)S(1)} %copy-done.104), channel_id=1, source_target_pairs={{0,16},{8,24},{16,0},{24,8},{1,17},{9,25},{17,1},{25,9},{2,18},{10... | collective-permute-start | bytes 196616 | tf_op jit(solution)/shard_map/ppermute | solution.py:57
  785.9 50.8 %collective-permute-start.102 = (bf16[256,4096]{1,0:T(8,128)(2,1)}, bf16[256,4096]{1,0:T(8,128)(2,1)}, u32[]{:S(2)}, u32[]{:S(2)}) collective-permute-start(bf16[256,4096]{1,0:T(8,128)(2,1)} %add_convert_fusion.1), channel_id=1, source_target_pairs={{0,4},{4,0},{1,5},{5,1},{2,6},{6,2},{3,7},{7,3},{8,12},{12,8},{9,1... | collective-permute-start | bytes 6291464 | tf_op jit(solution)/shard_map/ppermute | solution.py:57
  800.2 41.0 %collective-permute-start.93 = (bf16[256,4096]{1,0:T(8,128)(2,1)}, bf16[256,4096]{1,0:T(8,128)(2,1)}, u32[]{:S(2)}, u32[]{:S(2)}) collective-permute-start(bf16[256,4096]{1,0:T(8,128)(2,1)} %get-tuple-element.299), channel_id=1, source_target_pairs={{0,1},{1,0},{2,3},{3,2},{4,5},{5,4},{6,7},{7,6},{8,9},{9,8},{10,11... | collective-permute-start | bytes 6291464 | tf_op jit(solution)/shard_map/ppermute | solution.py:57
  800.2 48.6 %collective-permute-start.95 = (bf16[256,4096]{1,0:T(8,128)(2,1)S(1)}, bf16[256,4096]{1,0:T(8,128)(2,1)}, u32[]{:S(2)}, u32[]{:S(2)}) collective-permute-start(bf16[256,4096]{1,0:T(8,128)(2,1)S(1)} %add_convert_fusion.4), channel_id=1, source_target_pairs={{0,2},{2,0},{1,3},{3,1},{4,6},{6,4},{5,7},{7,5},{8,10},{10,8},{9,1... | collective-permute-start | bytes 6291464 | tf_op jit(solution)/shard_map/ppermute | solution.py:57
  840.7 30.0 %collective-permute-start.103 = (bf16[128,4096]{1,0:T(8,128)(2,1)S(1)}, bf16[128,4096]{1,0:T(8,128)(2,1)S(1)}, u32[]{:S(2)}, u32[]{:S(2)}) collective-permute-start(bf16[128,4096]{1,0:T(8,128)(2,1)S(1)} %split.469), channel_id=1, source_target_pairs={{0,2},{2,0},{1,3},{3,1},{4,6},{6,4},{5,7},{7,5},{8,10},{10,8},{9,1... | collective-permute-start | bytes 3145736 | tf_op jit(solution)/shard_map/ppermute | solution.py:57
  852.8 24.3 %collective-permute-start.96 = (bf16[128,4096]{1,0:T(8,128)(2,1)S(1)}, bf16[128,4096]{1,0:T(8,128)(2,1)S(1)}, u32[]{:S(2)}, u32[]{:S(2)}) collective-permute-start(bf16[128,4096]{1,0:T(8,128)(2,1)S(1)} %split.459), channel_id=1, source_target_pairs={{0,4},{4,0},{1,5},{5,1},{2,6},{6,2},{3,7},{7,3},{8,12},{12,8},{9,1... | collective-permute-start | bytes 3145736 | tf_op jit(solution)/shard_map/ppermute | solution.py:57
  871.1 31.1 %collective-permute-start.105 = (bf16[32,4096]{1,0:T(8,128)(2,1)S(1)}, bf16[32,4096]{1,0:T(8,128)(2,1)S(1)}, u32[]{:S(2)}, u32[]{:S(2)}) collective-permute-start(bf16[32,4096]{1,0:T(8,128)(2,1)S(1)} %get-tuple-element.343), channel_id=1, source_target_pairs={{0,16},{8,24},{16,0},{24,8},{1,17},{9,25},{17,1},{25,9},{2,18},{10... | collective-permute-start | bytes 786440 | tf_op jit(solution)/shard_map/ppermute | solution.py:57
  871.7 30.6 %collective-permute-start.104 = (bf16[32,4096]{1,0:T(8,128)(2,1)S(1)}, bf16[32,4096]{1,0:T(8,128)(2,1)S(1)}, u32[]{:S(2)}, u32[]{:S(2)}) collective-permute-start(bf16[32,4096]{1,0:T(8,128)(2,1)S(1)} %get-tuple-element.341), channel_id=1, source_target_pairs={{0,24},{8,0},{16,8},{24,16},{1,25},{9,1},{17,9},{25,17},{2,26},{10... | collective-permute-start | bytes 786440 | tf_op jit(solution)/shard_map/ppermute | solution.py:57
  877.5 24.9 %collective-permute-start.99 = (bf16[32,4096]{1,0:T(8,128)(2,1)S(1)}, bf16[32,4096]{1,0:T(8,128)(2,1)S(1)}, u32[]{:S(2)}, u32[]{:S(2)}) collective-permute-start(bf16[32,4096]{1,0:T(8,128)(2,1)S(1)} %get-tuple-element.339), channel_id=1, source_target_pairs={{0,8},{8,16},{16,24},{24,0},{1,9},{9,17},{17,25},{25,1},{2,10},{10... | collective-permute-start | bytes 786440 | tf_op jit(solution)/shard_map/ppermute | solution.py:57
  877.5 37.2 %collective-permute-start.98 = (bf16[32,4096]{1,0:T(8,128)(2,1)S(1)}, bf16[32,4096]{1,0:T(8,128)(2,1)S(1)}, u32[]{:S(2)}, u32[]{:S(2)}) collective-permute-start(bf16[32,4096]{1,0:T(8,128)(2,1)S(1)} %get-tuple-element.340), channel_id=1, source_target_pairs={{0,16},{8,24},{16,0},{24,8},{1,17},{9,25},{17,1},{25,9},{2,18},{10... | collective-permute-start | bytes 786440 | tf_op jit(solution)/shard_map/ppermute | solution.py:57
  882.2 32.5 %collective-permute-start.97 = (bf16[32,4096]{1,0:T(8,128)(2,1)S(1)}, bf16[32,4096]{1,0:T(8,128)(2,1)S(1)}, u32[]{:S(2)}, u32[]{:S(2)}) collective-permute-start(bf16[32,4096]{1,0:T(8,128)(2,1)S(1)} %get-tuple-element.338), channel_id=1, source_target_pairs={{0,24},{8,0},{16,8},{24,16},{1,25},{9,1},{17,9},{25,17},{2,26},{10... | collective-permute-start | bytes 786440 | tf_op jit(solution)/shard_map/ppermute | solution.py:57
  (237 other events, 3135.5 us)

commit v2 on v1

v2 whole, which is shorter than its diff:
```python
import jax
import jax.numpy as jnp
from jax import lax
from jax.experimental import pallas as pl
from jax.experimental.pallas import tpu as pltpu
from jax.sharding import PartitionSpec as P

HEADS = 16
HEAD_DIM = 64
FF = 4096
V = 4096
CHANNELS = 32
CLASSES = 1001
POSITIONS = 680
LEVELS = 10
MAXIMG = 8
STEPS = 10


EPS_NORM = 1e-06
BETA_ONE = 0.9
BETA_TWO = 0.95
ADAM_EPS = 1e-08
DECAY = 0.05
CLIP_NORM = 0.001
RATES = (0.03, 0.03, 0.03, 0.15, 0.4, 0.03)
NEG_FILL = -1e30
BF16 = jnp.bfloat16
F32 = jnp.float32
SPAN = 512
TOKENS = 128
PAIR = 2 * HEAD_DIM


def matmul(left, right):
    return jnp.dot(left, right, preferred_element_type=F32)


def matmul_tn(left, right):
    return lax.dot_general(left, right, (((0,), (0,)), ((), ())), preferred_element_type=F32)


def matmul_nt(left, right):
    return lax.dot_general(left, right, (((1,), (1,)), ((), ())), preferred_element_type=F32)


def precise(left, right):
    return jnp.dot(left, right, precision=lax.Precision.HIGHEST, preferred_element_type=F32)


def precise_tn(left, right):
    return lax.dot_general(left, right, (((0,), (0,)), ((), ())), precision=lax.Precision.HIGHEST)


def in_halves(times, values):
    upper = values.astype(BF16)
    return times(upper) + times((values - upper.astype(F32)).astype(BF16))


def in_halves_outside(times, values):
    upper = lax.reduce_precision(values, 8, 7)
    return times(upper.astype(BF16)) + times((values - upper).astype(BF16))


def swapped(value, mask, devices):
    return lax.ppermute(value, ("dp", "vocab"), [(i, i ^ mask) for i in range(devices)])


def tie(*values):
    return lax.optimization_barrier(values)


def grow(value, mask, devices):
    return jnp.concatenate([value, swapped(value, mask, devices)], axis=0)


def added(mine, theirs, out=BF16):
    return (mine.astype(F32) + theirs.astype(F32)).astype(out)


def keep_half(value, mask, devices, out=BF16):
    half = value.shape[0] // 2
    return added(value[:half], swapped(value[half:].astype(BF16), mask, devices), out)


def keep_all(value, masks, devices):
    for mask in reversed(masks):
        value = keep_half(value, mask, devices, F32 if mask == masks[0] else BF16)
    return value


def halves_of(mine, back, out=BF16):
    half = mine.shape[0] // 2
    return (added(mine[:half], back[:half], out), added(mine[half:], back[half:], out))


def sum_all(value, bits, devices):
    for at in range(0, len(bits), 2):
        masks = bits[at : at + 2]
        if len(masks) == 2:
            masks = masks + [masks[0] ^ masks[1]]
        value = value + sum(swapped(value, mask, devices) for mask in masks)
    return value


def place_masks(masks):
    places = [0]
    for mask in masks:
        places = places + [place ^ mask for place in places]
    return places


def source_rows(masks, me, rows):
    differ = jnp.repeat(jnp.array(place_masks(masks), jnp.int32), rows)
    row = jnp.tile(jnp.arange(rows, dtype=jnp.int32), 1 << len(masks))
    return (differ ^ me) * rows + row


def hot_rows(source):
    place = jnp.arange(source.shape[0], dtype=jnp.int32)
    return (
        (source[:, None] == place[None, :]).astype(BF16),
        (place[:, None] == source[None, :]).astype(BF16),
    )


def run(body, grid, given, specs, outs, out_specs, scratch=(), work=0):
    moved = sum(value.size * value.dtype.itemsize for value in given)
    return pl.pallas_call(
        body,
        grid=grid,
        in_specs=specs,
        out_shape=outs,
        out_specs=out_specs,
        scratch_shapes=scratch,
        compiler_params=pltpu.CompilerParams(vmem_limit_bytes=48 << 20),
        cost_estimate=pl.CostEstimate(flops=work, bytes_accessed=moved, transcendentals=0),
    )(*given)


def whole(value):
    return pl.BlockSpec(value.shape, lambda j: (0,) * value.ndim)


def two_sets(sets):
    first = sets[0][0].shape[1] // SPAN
    specs = [
        pl.BlockSpec((block.shape[0], SPAN), lambda j: (0, jnp.minimum(j, first - 1)))
        for block in sets[0]
    ]
    specs += [
        pl.BlockSpec((block.shape[0], SPAN), lambda j: (0, jnp.maximum(j - first, 0)))
        for block in sets[1]
    ]
    return first, specs


def gelu_parts(value):
    inner = 0.7978845608028654 * (value + 0.044715 * (value * value * value))
    bend = jnp.tanh(inner)
    return bend


def gelu(value):
    return 0.5 * value * (1.0 + gelu_parts(value))


def gelu_slope(value):
    bend = gelu_parts(value)
    rise = 0.7978845608028654 * (1.0 + 3.0 * 0.044715 * value * value)
    return 0.5 * (1.0 + bend) + 0.5 * value * (1.0 - bend * bend) * rise


def times_sets(left, sets, bias=None, hidden=None, bend=False):
    tokens = left[0].shape[0]
    first, specs = two_sets(sets)
    steps = first + sets[1][0].shape[1] // SPAN
    count = len(sets[0])
    extra = [value for value in (bias, hidden) if value is not None]
    column = lambda j: (0, j)
    extra_specs = [pl.BlockSpec((value.shape[0], SPAN), column) for value in extra]

    def body(one_ref, two_ref, *refs):
        extras, blocks = refs[: len(extra)], refs[len(extra) : len(extra) + 2 * count]
        outs = refs[len(extra) + 2 * count :]

        def part(u_ref, blocks):
            total, at = None, 0
            for block in blocks:
                rows = block.shape[0]
                term = matmul(u_ref[:, at : at + rows], block[...])
                total = term if total is None else total + term
                at += rows
            if bias is not None:
                total = total + extras[0][...]
            if hidden is not None:
                slope = gelu_slope(extras[-1][...])
                low = (total * slope).astype(BF16)
                outs[0][...] = low
                outs[1][...] = jnp.sum(low.astype(F32), axis=0, keepdims=True)
            else:
                outs[0][...] = total
                if bend:
                    outs[1][...] = gelu(total).astype(BF16)

        pl.when(pl.program_id(0) < first)(lambda: part(one_ref, blocks[:count]))
        pl.when(pl.program_id(0) >= first)(lambda: part(two_ref, blocks[count:]))

    wide = steps * SPAN
    shape = jax.ShapeDtypeStruct
    outs, out_specs = [shape((tokens, wide), F32)], [pl.BlockSpec((tokens, SPAN), column)]
    if hidden is not None:
        outs = [shape((tokens, wide), BF16), shape((1, wide), F32)]
        out_specs.append(pl.BlockSpec((1, SPAN), column))
    elif bend:
        outs.append(shape((tokens, wide), BF16))
        out_specs.append(pl.BlockSpec((tokens, SPAN), column))
    given = list(left) + extra + list(sets[0]) + list(sets[1])
    specs = [whole(value) for value in left] + extra_specs + specs
    work = 2 * tokens * left[0].shape[1] * wide
    found = run(body, (steps,), given, specs, outs, out_specs, work=work)
    return found if len(outs) > 1 else found[0]


def span_spec(value):
    each = value.shape[2] // SPAN
    return pl.BlockSpec((1, value.shape[1], SPAN), lambda j: (j // each, 0, j % each))


def back_sets(right, sets, perms, bias=None, exact=False, out=F32):
    tokens = right.shape[1]
    first, specs = two_sets(sets)
    steps = first + sets[1][0].shape[1] // SPAN
    count = len(sets[0])
    width = perms[0].shape[0]
    extra = [] if bias is None else [bias]

    def body(right_ref, one_ref, two_ref, *refs):
        extras, blocks = refs[: len(extra)], refs[len(extra) : len(extra) + 2 * count]
        out_ref, one_sum, two_sum = refs[len(extra) + 2 * count :]
        step = pl.program_id(0)

        def part(sums, blocks, start):
            terms = [matmul_nt(right_ref[0], block[...]) for block in blocks]
            term = jnp.concatenate(terms, axis=1)

            @pl.when(step == start)
            def _():
                sums[...] = term

            @pl.when(step > start)
            def _():
                sums[...] += term

        pl.when(step < first)(lambda: part(one_sum, blocks[:count], 0))
        pl.when(step >= first)(lambda: part(two_sum, blocks[count:], first))

        @pl.when(step == steps - 1)
        def _():
            total = None
            for sums, perm in ((one_sum, one_ref), (two_sum, two_ref)):
                if exact:
                    term = in_halves(lambda part: matmul(part, perm[...]), sums[...])
                else:
                    term = matmul(sums[...].astype(BF16), perm[...])
                total = term if total is None else total + term
            if bias is not None:
                total = total + extras[0][...]
            out_ref[...] = total.astype(out)

    given = [right] + list(perms) + extra + list(sets[0]) + list(sets[1])
    specs = [span_spec(right)] + [whole(value) for value in list(perms) + extra] + specs
    outs = jax.ShapeDtypeStruct((tokens, width), out)
    scratch = [pltpu.VMEM((tokens, width), F32)] * 2
    work = 2 * tokens * width * steps * SPAN
    return run(body, (steps,), given, specs, outs, whole(outs), scratch, work)


def grad_rows(left, right, rows, columns, back=None):
    tokens = left.shape[0]
    count = rows[1] - rows[0]
    each = right.shape[2] // SPAN
    start, steps = columns[0] // SPAN, (columns[1] - columns[0]) // SPAN

    def body(left_ref, right_ref, *refs):
        total = matmul_tn(left_ref[...], right_ref[0])
        if back is not None:
            total = total + refs[0][...].astype(F32)
        refs[-1][...] = total.astype(BF16)

    given = [left, right]
    at = rows[0] // count
    specs = [
        pl.BlockSpec((tokens, count), lambda j: (0, at)),
        pl.BlockSpec(
            (1, tokens, SPAN), lambda j: ((j + start) // each, 0, (j + start) % each)
        ),
    ]
    if back is not None:
        given.append(back)
        specs.append(pl.BlockSpec((count, SPAN), lambda j: (at, j)))
    outs = jax.ShapeDtypeStruct((count, steps * SPAN), BF16)
    spec = pl.BlockSpec((count, SPAN), lambda j: (0, j))
    work = 2 * tokens * count * steps * SPAN
    return run(body, (steps,), given, specs, outs, spec, work=work)


def head_scale(value, left_half):
    square = value * value
    one = jnp.sum(jnp.where(left_half, square, 0.0), axis=1, keepdims=True)
    two = jnp.sum(jnp.where(left_half, 0.0, square), axis=1, keepdims=True)
    return jnp.where(
        left_half,
        lax.rsqrt(one * (1.0 / HEAD_DIM) + EPS_NORM),
        lax.rsqrt(two * (1.0 / HEAD_DIM) + EPS_NORM),
    )


def soft_rows(q_norm, k_norm, mask):
    scores = matmul_nt(q_norm, k_norm) * HEAD_DIM ** (-0.5) + mask
    terms = jnp.exp(scores - jnp.max(scores, axis=1, keepdims=True))
    return terms * (1.0 / jnp.sum(terms, axis=1, keepdims=True))


def pair_specs(tokens):
    pairs = HEADS // 2
    return [
        pl.BlockSpec((tokens, PAIR), lambda j: (0, j)),
        pl.BlockSpec((tokens, PAIR), lambda j: (0, pairs + j)),
        pl.BlockSpec((tokens, PAIR), lambda j: (0, 2 * pairs + j)),
        pl.BlockSpec((1, PAIR), lambda j: (0, j)),
        pl.BlockSpec((1, PAIR), lambda j: (0, j)),
        pl.BlockSpec((tokens, tokens), lambda j: (0, 0)),
    ]


def attend(qkv, q_gain, k_gain, mask):
    tokens, width = qkv.shape[0], qkv.shape[1] // 3

    def body(q_ref, k_ref, v_ref, qg_ref, kg_ref, mask_ref, out_ref):
        left_half = lax.broadcasted_iota(jnp.int32, (1, PAIR), 1) < HEAD_DIM
        query, key = q_ref[...], k_ref[...]
        q_norm = (query * head_scale(query, left_half) * qg_ref[...]).astype(BF16)
        k_norm = (key * head_scale(key, left_half) * kg_ref[...]).astype(BF16)
        v_low = v_ref[...].astype(BF16)
        zero = jnp.zeros_like(q_norm)
        mixed = []
        for one in (jnp.where(left_half, q_norm, zero), jnp.where(left_half, zero, q_norm)):
            probs = soft_rows(one, k_norm, mask_ref[...])
            mixed.append(matmul(probs.astype(BF16), v_low))
        out_ref[...] = jnp.where(left_half, mixed[0], mixed[1]).astype(BF16)

    outs = jax.ShapeDtypeStruct((tokens, width), BF16)
    spec = pl.BlockSpec((tokens, PAIR), lambda j: (0, j))
    given = [qkv, qkv, qkv, q_gain, k_gain, mask]
    return run(body, (HEADS // 2,), given, pair_specs(tokens), outs, spec, work=10**10)


def attend_back(qkv, q_gain, k_gain, mask, d_mix):
    tokens, width = qkv.shape[0], qkv.shape[1] // 3

    def body(q_ref, k_ref, v_ref, qg_ref, kg_ref, mask_ref, dm_ref, out_ref, sums_ref):
        left_half = lax.broadcasted_iota(jnp.int32, (1, PAIR), 1) < HEAD_DIM
        query, key = q_ref[...], k_ref[...]
        q_scale, k_scale = head_scale(query, left_half), head_scale(key, left_half)
        q_norm = (query * q_scale * qg_ref[...]).astype(BF16)
        k_norm = (key * k_scale * kg_ref[...]).astype(BF16)
        v_low, d_mix = v_ref[...].astype(BF16), dm_ref[...]
        zero = jnp.zeros_like(q_norm)
        found = []
        for side in range(2):
            own = (lambda v: jnp.where(left_half, v, zero)) if side == 0 else (
                lambda v: jnp.where(left_half, zero, v)
            )
            probs = soft_rows(own(q_norm), k_norm, mask_ref[...])
            d_values = matmul_tn(probs.astype(BF16), d_mix)
            d_probs = matmul_nt(own(d_mix), v_low)
            inner = jnp.sum(d_probs * probs, axis=1, keepdims=True)
            d_scores = (probs * (d_probs - inner)).astype(BF16)
            found.append((matmul(d_scores, k_norm), matmul_tn(d_scores, q_norm), d_values))
        d_qn, d_kn, d_values = (jnp.where(left_half, one, two) for one, two in zip(*found))
        sums = []
        for at, value, scale, gain, d_norm in (
            (0, query, q_scale, qg_ref[...], d_qn * HEAD_DIM ** (-0.5)),
            (1, key, k_scale, kg_ref[...], d_kn * HEAD_DIM ** (-0.5)),
        ):
            product = d_norm * value
            sums.append(jnp.sum(product * scale, axis=0, keepdims=True))
            product = product * gain
            one = jnp.sum(jnp.where(left_half, product, 0.0), axis=1, keepdims=True)
            two = jnp.sum(jnp.where(left_half, 0.0, product), axis=1, keepdims=True)
            mean = jnp.where(left_half, one, two) * (1.0 / HEAD_DIM)
            d_value = scale * (gain * d_norm - value * (scale * scale) * mean)
            out_ref[at] = d_value.astype(BF16)
        out_ref[2] = d_values.astype(BF16)
        sums.append(jnp.sum(out_ref[0].astype(F32), axis=0, keepdims=True))
        sums.append(jnp.sum(out_ref[2].astype(F32), axis=0, keepdims=True))
        sums_ref[...] = jnp.concatenate(sums + [jnp.zeros((4, PAIR), F32)], axis=0)

    outs = [
        jax.ShapeDtypeStruct((3, tokens, width), BF16),
        jax.ShapeDtypeStruct((8, width), F32),
    ]
    out_specs = [
        pl.BlockSpec((3, tokens, PAIR), lambda j: (0, 0, j)),
        pl.BlockSpec((8, PAIR), lambda j: (0, j)),
    ]
    given = [qkv, qkv, qkv, q_gain, k_gain, mask, d_mix]
    specs = pair_specs(tokens) + [pl.BlockSpec((tokens, PAIR), lambda j: (0, j))]
    return run(body, (HEADS // 2,), given, specs, outs, out_specs, work=3 * 10**10)


def row_stats(value):
    center = value - jnp.mean(value, axis=1, keepdims=True)
    return center, lax.rsqrt(jnp.mean(center * center, axis=1, keepdims=True) + EPS_NORM)


def by_tokens(value):
    return pl.BlockSpec((TOKENS, value.shape[1]), lambda j: (j, 0))


def norm_ahead(value, hot, shift, scale, perms, gate=None, branch=None):
    tokens, width = value.shape
    extra = [] if gate is None else [gate, branch]

    def body(value_ref, hot_ref, shift_ref, scale_ref, *refs):
        total = value_ref[...]
        outs = refs[len(extra) + len(perms) :]
        if gate is not None:
            total = total + precise(hot_ref[...], refs[0][...]) * refs[1][...]
            outs[-1][...] = total
        center, inverse = row_stats(total)
        scales = 1.0 + precise(hot_ref[...], scale_ref[...])
        normed = center * inverse * scales + precise(hot_ref[...], shift_ref[...])
        normed = normed.astype(BF16)
        for perm_ref, out_ref in zip(refs[len(extra) : len(extra) + len(perms)], outs):
            out_ref[...] = matmul(normed, perm_ref[...]).astype(BF16)

    given = [value, hot, shift, scale] + extra + list(perms)
    specs = [by_tokens(value), by_tokens(hot), whole(shift), whole(scale)]
    specs += [whole(gate), by_tokens(branch)] if extra else []
    specs += [whole(perm) for perm in perms]
    outs = [jax.ShapeDtypeStruct((tokens, width), BF16) for _ in perms]
    outs += [jax.ShapeDtypeStruct((tokens, width), F32)] if extra else []
    out_specs = [by_tokens(value) for _ in outs]
    return run(body, (tokens // TOKENS,), given, specs, outs, out_specs, work=10**9)


def norm_back(value, d_out, hot, hot_t, scale, beyond=None, gate=None, branch=None, perms=()):
    tokens, width = value.shape
    gated = gate is not None
    tall = [value, d_out] + ([] if beyond is None else [beyond]) + ([branch] if gated else [])
    flat = [scale] + ([gate] if gated else []) + list(perms)

    def body(hot_ref, hot_t_ref, *refs):
        talls, flats = refs[: len(tall)], refs[len(tall) : len(tall) + len(flat)]
        outs = refs[len(tall) + len(flat) :]
        total_ref, shift_ref, scale_ref, column_ref = outs[:4]
        d_out = talls[1][...]
        center, inverse = row_stats(talls[0][...])
        normed = center * inverse
        d_norm = d_out * (1.0 + precise(hot_ref[...], flats[0][...]))
        mean = jnp.mean(d_norm, axis=1, keepdims=True)
        along = jnp.mean(d_norm * normed, axis=1, keepdims=True)
        total = (d_norm - mean - normed * along) * inverse
        if beyond is not None:
            total = total + talls[2][...]
        total_ref[...] = total
        sums = [
            (shift_ref, precise(hot_t_ref[...], d_out)),
            (scale_ref, precise(hot_t_ref[...], d_out * normed)),
        ]
        if gated:
            sums.append((outs[4], precise(hot_t_ref[...], total * talls[-1][...])))
            low = (precise(hot_ref[...], flats[1][...]) * total).astype(BF16)
            column = jnp.sum(low.astype(F32), axis=0, keepdims=True)
        else:
            low = total.astype(BF16)
            column = jnp.sum(total, axis=0, keepdims=True)
        sums.append((column_ref, column))
        lows = outs[5:] if gated else outs[4:]
        if perms:
            for perm_ref, low_ref in zip(flats[2:], lows):
                low_ref[...] = matmul(low, perm_ref[...]).astype(BF16)
        else:
            lows[0][...] = low

        @pl.when(pl.program_id(0) == 0)
        def _():
            for ref, term in sums:
                ref[...] = term

        @pl.when(pl.program_id(0) > 0)
        def _():
            for ref, term in sums:
                ref[...] += term

    given = [hot, hot_t] + tall + flat
    specs = [by_tokens(hot), pl.BlockSpec((hot_t.shape[0], TOKENS), lambda j: (0, j))]
    specs += [by_tokens(part) for part in tall] + [whole(part) for part in flat]
    shape = jax.ShapeDtypeStruct
    image = shape(scale.shape, F32)
    outs = [shape((tokens, width), F32), image, image, shape((1, width), F32)]
    outs += [image] if gated else []
    outs += [shape((tokens, width), BF16) for _ in range(max(len(perms), 1))]
    out_specs = [by_tokens(part) if part.shape[0] == tokens else whole(part) for part in outs]
    return run(body, (tokens // TOKENS,), given, specs, outs, out_specs, work=10**9)


def slim_back(d_resid, token_hot, arrays, plan, perm, n_embed):
    width, wide = perm.shape[0], token_hot.shape[1]
    rows = sum(arrays[which].shape[1] // width for which, _ in plan)
    room = rows + (-rows % 16)

    def body(d_ref, hot_ref, perm_ref, *refs):
        out_ref, gains = refs[-2], refs[-1]
        gains[...] = jnp.zeros_like(gains)
        at = 0
        for which, row in plan:
            for column in range(0, arrays[which].shape[1], width):
                gains[at : at + 1, :] = refs[which][row : row + 1, column : column + width]
                at += 1
        place = lax.broadcasted_iota(jnp.int32, (room, wide), 1)
        own = lax.broadcasted_iota(jnp.int32, (room, wide), 0) + n_embed
        own = jnp.where(own < n_embed + rows, own, -1)
        total = matmul_tn(d_ref[...], hot_ref[...])
        chosen = jnp.where(place == own, 1.0, 0.0).astype(BF16)
        total = total + matmul_tn(gains[...].astype(BF16), chosen)
        out_ref[...] = matmul(perm_ref[...], total.astype(BF16)).astype(BF16)

    given = [d_resid, token_hot, perm] + list(arrays)
    outs = jax.ShapeDtypeStruct((width, wide), BF16)
    specs = [whole(value) for value in given]
    scratch = [pltpu.VMEM((room, width), F32)]
    return run(body, (1,), given, specs, outs, whole(outs), scratch, 3 * 10**9)


def layout(scale_row):
    position = jnp.arange(scale_row.shape[0], dtype=jnp.int32)
    opening = scale_row == 0
    image_id = jnp.cumsum(opening.astype(jnp.int32)) - 1
    starts_at = lax.cummax(jnp.where(opening, position, 0), axis=0)
    return (image_id, position - starts_at, scale_row < LEVELS)


def adam_step(weight, moment, square, gradient, clip_factor, step_rate):
    gradient = gradient * clip_factor
    moment = BETA_ONE * moment + (1.0 - BETA_ONE) * gradient
    square = BETA_TWO * square + (1.0 - BETA_TWO) * gradient * gradient
    first_hat = moment / (1.0 - BETA_ONE**STEPS)
    second_hat = square / (1.0 - BETA_TWO**STEPS)
    weight = weight - step_rate * (first_hat / (jnp.sqrt(second_hat) + ADAM_EPS) + DECAY * weight)
    return (weight, moment, square, weight.astype(BF16))


def per_device(
    ways,
    features,
    scale_ids,
    class_ids,
    code_targets,
    token_weights,
    attn_weight,
    attn_moment,
    attn_square,
    mlp_weight,
    mlp_moment,
    mlp_square,
    ada_weight,
    ada_moment,
    ada_square,
    embed_weight,
    embed_moment,
    embed_square,
    gains_weight,
    gains_moment,
    gains_square,
    head_weight,
    head_moment,
    head_square,
):
    devices, n_vocab = ways["devices"], ways["n_vocab"]
    bits_y, bits_x, bits_z = ways["y"], ways["x"], ways["z"]
    path_one = bits_z + bits_y + bits_x
    path_two = bits_z + bits_x + bits_y
    me = lax.axis_index("dp") * n_vocab + lax.axis_index("vocab")
    rows = attn_weight.shape[0]
    width = rows * devices
    top, quarter = width // 2, width // 4
    ff_rows = FF // width
    ada_at = 7 + ff_rows
    head_at = ada_at + 8
    off_level = CLASSES + POSITIONS
    off_word = off_level + LEVELS
    length = scale_ids.shape[1]
    used = min(POSITIONS, length)
    n_gains = gains_weight.shape[0]
    n_embed = used + LEVELS + CHANNELS
    half_ff, half_qkv = FF // 2, 3 * width // 2

    def swap(value, mask):
        return swapped(value, mask, devices)

    def grown(masks, *values):
        for mask in masks:
            values = [grow(value, mask, devices) for value in values]
        return values if len(values) > 1 else values[0]

    scale_row = scale_ids[0]
    image_id, inside, counted = layout(scale_row)
    counted = counted.astype(F32)
    facts = jnp.concatenate(
        [class_ids[0], jnp.sum(counted).astype(jnp.int32)[None], jnp.zeros((119,), jnp.int32)]
    )[None]
    weighted = token_weights[0] * counted
    row_info = jnp.stack([code_targets[0].astype(F32), weighted])[None]

    embed16 = embed_weight.astype(BF16)
    slim = jnp.concatenate(
        [
            embed16[CLASSES : CLASSES + used],
            embed16[off_level : off_word + CHANNELS],
            gains_weight.astype(BF16),
        ],
        axis=0,
    )
    fill = -slim.shape[0] % 128
    slim = jnp.pad(slim, ((0, fill), (0, 0))).T
    wide = slim.shape[1]
    qkv_one = attn_weight[:, :half_qkv].astype(BF16)
    qkv_two = attn_weight[:, half_qkv : 3 * width].astype(BF16)
    up = jnp.concatenate(
        [
            mlp_weight[0, :, :half_ff],
            attn_weight[:, 3 * width : 3 * width + top],
            mlp_weight[0, :, half_ff:],
            attn_weight[:, 3 * width + top :],
        ],
        axis=1,
    ).astype(BF16)
    down = mlp_weight[1].astype(BF16)
    head16 = head_weight.astype(BF16)
    ada16 = ada_weight.astype(BF16)

    one_y, one_x, two_x, two_y = bits_y, bits_x, bits_x, bits_y
    slots = devices * MAXIMG
    n_x, n_y, n_z = 1 << len(bits_x), 1 << len(bits_y), 1 << len(bits_z)

    def to_two(value):
        shaped = value.reshape((2, n_x, n_y, n_z * MAXIMG) + value.shape[1:])
        return jnp.swapaxes(shaped, 1, 2).reshape(value.shape)

    def to_one(value):
        shaped = value.reshape((2, n_y, n_x, n_z * MAXIMG) + value.shape[1:])
        return jnp.swapaxes(shaped, 1, 2).reshape(value.shape)

    facts = grown(bits_z[:1], facts)
    slim, qkv_one, qkv_two = grown(bits_z[:1], slim, qkv_one, qkv_two)
    facts, slim, qkv_one, qkv_two, up = tie(facts, slim, qkv_one, qkv_two, up)
    facts = grown(bits_z[1:] + bits_y + bits_x + [1], facts)
    slim, qkv_one, qkv_two = grown(bits_z[1:], slim, qkv_one, qkv_two)
    perm_one, perm_one_t = hot_rows(source_rows(path_one + [1], me, rows))
    perm_two, perm_two_t = hot_rows(source_rows(path_two + [1], me, rows))
    facts, slim, qkv_one, qkv_two, up, perm_one, perm_two = tie(
        facts, slim, qkv_one, qkv_two, up, perm_one, perm_two
    )

    total_count = jnp.sum(facts[:, MAXIMG]).astype(F32)
    class_hot = (
        facts[:, :MAXIMG].reshape(slots)[:, None] == jnp.arange(CLASSES, dtype=jnp.int32)[None, :]
    ).astype(BF16)
    class_vec = matmul(class_hot, embed16[:CLASSES])
    class_act = jax.nn.silu(class_vec).astype(BF16)
    cuts = (2 * width, 5 * width)
    act_two = to_two(class_act)
    first = matmul(class_act, ada16[:, : cuts[0]]).astype(BF16)
    up = grown(bits_z[:1], up)
    qkv_one, qkv_two = grown(one_y, qkv_one), grown(two_x, qkv_two)
    slim = grown(bits_y, slim)
    first = keep_half(first, 1, devices)
    for mask in reversed(bits_x):
        first = keep_half(first, mask, devices)
    slim = grown(bits_x, slim)
    first, slim, qkv_one, qkv_two, up, down, head16 = tie(
        first, slim, qkv_one, qkv_two, up, down, head16
    )

    for mask in bits_x[:-1]:
        qkv_one = grown([mask], qkv_one)
    for mask in bits_y[:-1]:
        qkv_two = grown([mask], qkv_two)
    one_far, two_far = swap(qkv_one, bits_x[-1]), swap(qkv_two, bits_y[-1])
    up = grown(bits_z[1:], up)
    slim = grown([1], slim)
    first = keep_all(first, bits_z + bits_y, devices)
    pos_hot = (inside[:, None] == jnp.arange(used, dtype=jnp.int32)[None, :]).astype(BF16)
    level_hot = (scale_row[:, None] == jnp.arange(LEVELS, dtype=jnp.int32)[None, :]).astype(BF16)
    token_hot = jnp.concatenate(
        [pos_hot, level_hot, features[0], jnp.zeros((length, wide - n_embed), BF16)], axis=1
    )
    image = jnp.arange(MAXIMG, dtype=jnp.int32)
    hot = (image_id[:, None] == image[None, :]).astype(F32)
    hot_t = (image[:, None] == image_id[None, :]).astype(F32)
    allowed = (image_id[:, None] == image_id[None, :]) & (scale_row[None, :] <= scale_row[:, None])
    mask_rows = jnp.where(allowed, 0.0, NEG_FILL).astype(F32)
    mod_one = matmul(class_act, ada16[:, cuts[0] : cuts[1]]).astype(BF16)
    mod_two = matmul(act_two, ada16[:, cuts[1] :]).astype(BF16)
    first, slim, token_hot, mask_rows, mod_one, mod_two = tie(
        first, slim, token_hot, mask_rows, mod_one, mod_two
    )

    one_near_c, two_near_c = swap(qkv_one, 1), swap(qkv_two, 1)
    slim = matmul_tn(slim, perm_one)
    gain_rows = slim[n_embed : n_embed + n_gains]
    ada_bias = gain_rows[ada_at:head_at].reshape(1, -1)
    resid_in = matmul(token_hot, slim.astype(BF16)) + gain_rows[0]
    first = first + ada_bias[:, : cuts[0]]
    mods = [first[:, :width], first[:, width:]]
    u_one, u_two = norm_ahead(resid_in, hot, mods[0], mods[1], [perm_one_t, perm_two_t])
    u_one, u_two, one_far, two_far, one_near_c, two_near_c, mod_one, mod_two, up = tie(
        u_one, u_two, one_far, two_far, one_near_c, two_near_c, mod_one, mod_two, up
    )

    one_far_c, two_far_c = swap(one_far, 1), swap(two_far, 1)
    half_up = half_ff + top
    up_one, up_two = grown(one_y, up[:, :half_up]), grown(two_x, up[:, half_up:])
    mod_one, mod_two = keep_half(mod_one, 1, devices), keep_half(mod_two, 1, devices)
    one_far_c, two_far_c, u_one, u_two, mod_one, mod_two, down = tie(
        one_far_c, two_far_c, u_one, u_two, mod_one, mod_two, down
    )

    for mask in reversed(bits_x):
        mod_one = keep_half(mod_one, mask, devices)
    for mask in reversed(bits_y):
        mod_two = keep_half(mod_two, mask, devices)
    down = grown(bits_z[:1], down)
    w_qkv = (
        [qkv_one, one_far, one_near_c, one_far_c],
        [qkv_two, two_far, two_near_c, two_far_c],
    )
    qkv_bias = jnp.concatenate(
        [gain_rows[1:2], jnp.zeros((1, width), F32), gain_rows[2:3]], axis=1
    )
    q_gain, k_gain = gain_rows[5:6], gain_rows[6:7]
    qkv = times_sets([u_one, u_two], w_qkv, qkv_bias)
    mixture = attend(qkv, q_gain, k_gain, mask_rows)
    mixture, up_one, up_two, mod_one, mod_two, down, head16 = tie(
        mixture, up_one, up_two, mod_one, mod_two, down, head16
    )

    for mask in bits_x[:-1]:
        up_one = grown([mask], up_one)
    for mask in bits_y[:-1]:
        up_two = grown([mask], up_two)
    proj_one, proj_two = up_one[:, half_ff:], up_two[:, half_ff:]
    up_one, up_two = up_one[:, :half_ff], up_two[:, :half_ff]
    proj_one_far, proj_two_far = swap(proj_one, bits_x[-1]), swap(proj_two, bits_y[-1])
    for mask in reversed(bits_y):
        mod_one = keep_half(mod_one, mask, devices)
    for mask in reversed(bits_x):
        mod_two = keep_half(mod_two, mask, devices)
    proj_one_c, proj_two_c = swap(proj_one, 1), swap(proj_two, 1)
    mix_one = matmul(mixture, perm_one_t).astype(BF16)
    mix_two = matmul(mixture, perm_two_t).astype(BF16)
    mods_rest = jnp.concatenate([mod_one, mod_two], axis=1)
    (
        mix_one,
        mix_two,
        proj_one_far,
        proj_two_far,
        proj_one_c,
        proj_two_c,
        up_one,
        up_two,
        mods_rest,
        down,
    ) = tie(
        mix_one,
        mix_two,
        proj_one_far,
        proj_two_far,
        proj_one_c,
        proj_two_c,
        up_one,
        up_two,
        mods_rest,
        down,
    )

    up_one_far, up_two_far = swap(up_one, bits_x[-1]), swap(up_two, bits_y[-1])
    w_proj = (
        [proj_one, proj_one_far, proj_one_c, swap(proj_one_far, 1)],
        [proj_two, proj_two_far, proj_two_c, swap(proj_two_far, 1)],
    )
    down = grown(bits_z[1:], down)
    mods_rest = keep_all(mods_rest, bits_z, devices)
    attn_out = times_sets([mix_one, mix_two], w_proj, gain_rows[3:4])
    attn_out, mods_rest, head16 = tie(attn_out, mods_rest, head16)
    mods_rest = mods_rest + ada_bias[:, cuts[0] :]
    mods += [mods_rest[:, at : at + width] for at in range(0, 6 * width, width)]
    u_mid_one, u_mid_two, resid_mid = norm_ahead(
        resid_in, hot, mods[3], mods[4], [perm_one_t, perm_two_t], mods[2], attn_out
    )
    up_one_c, up_two_c = swap(up_one, 1), swap(up_two, 1)
    head16 = grown(bits_y, head16)
    u_mid_one, u_mid_two, up_one_far, up_two_far, up_one_c, up_two_c, down, head16 = tie(
        u_mid_one, u_mid_two, up_one_far, up_two_far, up_one_c, up_two_c, down, head16
    )

    up_one_fc, up_two_fc = swap(up_one_far, 1), swap(up_two_far, 1)
    down_one, down_two = grown(one_y, down[:, :half_ff]), grown(two_x, down[:, half_ff:])
    head16 = grown(bits_z[:1], head16)
    w_up = (
        [up_one, up_one_far, up_one_c, up_one_fc],
        [up_two, up_two_far, up_two_c, up_two_fc],
    )
    up_bias = gain_rows[7:ada_at].reshape(1, -1)
    hidden, active = times_sets([u_mid_one, u_mid_two], w_up, up_bias, bend=True)
    for mask in bits_x[:-1]:
        down_one = grown([mask], down_one)
    for mask in bits_y[:-1]:
        down_two = grown([mask], down_two)
    active, down_one, down_two, row_info = tie(active, down_one, down_two, row_info)

    down_one_far, down_two_far = swap(down_one, bits_x[-1]), swap(down_two, bits_y[-1])
    down_one_c, down_two_c = swap(down_one, 1), swap(down_two, 1)
    for mask in bits_x + [1]:
        row_info = grown([mask], row_info)
    row_info = jnp.swapaxes(row_info, 0, 1).reshape(2, -1)
    active, down_one_far, down_two_far, down_one_c, down_two_c, head16, row_info = tie(
        active, down_one_far, down_two_far, down_one_c, down_two_c, head16, row_info
    )

    head16 = grown(bits_z[1:], head16)
    w_down = (
        [down_one, down_one_far, down_one_c, swap(down_one_far, 1)],
        [down_two, down_two_far, down_two_c, swap(down_two_far, 1)],
    )
    perms = [perm_one, perm_two]
    mlp_out = back_sets(active[None], w_down, perms, gain_rows[4:5], exact=True)
    head_masks = bits_y + bits_z
    perm_head, perm_head_t = hot_rows(
        source_rows(
            [mask // n_vocab for mask in head_masks], lax.axis_index("dp"), head_weight.shape[0]
        )
    )
    head_rel, resid_out = norm_ahead(
        resid_mid, hot, mods[6], mods[7], [perm_head_t], mods[5], mlp_out
    )
    head_rel, head16 = tie(head_rel, head16)

    vocab_masks = bits_x + [1]
    rows_all = grown(bits_x[:-1], head_rel)
    far = swap(rows_all, bits_x[-1])
    near_c = swap(rows_all, 1)
    code_span = head_weight.shape[1]
    code_start = lax.axis_index("vocab") * code_span
    head_bias = lax.dynamic_slice_in_dim(gain_rows[head_at:].reshape(-1), code_start, code_span)
    code = jnp.arange(code_span, dtype=jnp.int32)[None, :] + code_start

    def part_stats(part, info):
        logits = matmul(part, head16) + head_bias
        local_max = jnp.max(logits, axis=1)
        exp_sums = jnp.sum(jnp.exp(logits - local_max[:, None]), axis=1)
        is_target = (code == info[0].astype(jnp.int32)[:, None]).astype(F32)
        picked = jnp.sum(is_target * logits, axis=1)
        return logits, is_target, jnp.stack([local_max, exp_sums, picked])

    each = rows_all.shape[0]
    info_of = [row_info[:, at * each : (at + 1) * each] for at in range(4)]
    near_rows = jnp.concatenate([rows_all, near_c], axis=0)
    near_info = jnp.concatenate([info_of[0], info_of[2]], axis=1)
    far_info = jnp.concatenate([info_of[1], info_of[3]], axis=1)
    near_logits, near_target, near_stats = part_stats(near_rows, near_info)
    near_stats, far = tie(near_stats, far)
    far_rows = jnp.concatenate([far, swap(far, 1)], axis=0)
    far_logits, far_target, far_stats = part_stats(far_rows, far_info)
    places = [x ^ c for x in (0, bits_x[-1]) for c in (0, 1)]
    places = [place ^ other for place in places for other in place_masks(bits_x[:-1])]
    stats = jnp.concatenate([near_stats, far_stats], axis=1)
    group = [stats]
    for other in place_masks(vocab_masks)[1:]:
        their = jnp.split(swap(stats, other), n_vocab, axis=1)
        group.append(
            jnp.concatenate([their[places.index(place ^ other)] for place in places], axis=1)
        )
    row_max = group[0][0]
    for other in group[1:]:
        row_max = jnp.maximum(row_max, other[0])
    totals = sum(other[1] * jnp.exp(other[0] - row_max) for other in group)
    target_logit = sum(other[2] for other in group)
    log_total = row_max + jnp.log(totals)
    loss_part = jnp.sum((near_info[1] * (log_total - target_logit)[: 2 * each])[:length])
    mid = 2 * each

    def part_back(logits, is_target, info, log_total):
        coef = info[1] / total_count
        grad = coef[:, None] * (jnp.exp(logits - log_total[:, None]) - is_target)
        return grad.astype(BF16)

    d_far_logits = part_back(far_logits, far_target, far_info, log_total[mid:])
    d_near_logits = part_back(near_logits, near_target, near_info, log_total[:mid])
    d_far = matmul_nt(d_far_logits, head16).astype(BF16)
    d_near = matmul_nt(d_near_logits, head16).astype(BF16)
    to_core = jnp.concatenate([d_near[each:], d_far[each:]], axis=0)
    back = swap(to_core, 1)
    d_far, d_near = added(d_far[:each], back[each:]), added(d_near[:each], back[:each])
    rows_all = jnp.concatenate([near_rows, far_rows], axis=0)
    d_logits = jnp.concatenate([d_near_logits, d_far_logits], axis=0)
    d_far, head16 = tie(d_far, head16)
    d_head_in = added(d_near, swap(d_far, bits_x[-1]), F32)
    for mask in reversed(bits_x[:-1]):
        d_head_in = keep_half(d_head_in.astype(BF16), mask, devices, F32)
    head_far = matmul_tn(rows_all[:, top:], d_logits).astype(BF16)
    head_near = matmul_tn(rows_all[:, :top], d_logits).astype(BF16)
    bias_grad = lax.dynamic_update_slice(
        jnp.zeros((V,), F32), jnp.sum(d_logits.astype(F32), axis=0), (code_start,)
    )
    d_head_in, head_far, head_near = tie(d_head_in, head_far, head_near)

    def far_rows_of(left, right, columns):
        return grad_rows(left, right, (top, width), columns)

    def meet_far(left, right, columns, back):
        return grad_rows(left, right, (quarter, top), columns, back)

    def meet_near(left, right, columns, back):
        return grad_rows(left, right, (0, quarter), columns, back)

    def cross(one, two):
        return swap(one, bits_x[-1]), swap(two, bits_y[-1])

    def join(one, two, one_back, two_back):
        one, two = added(one, one_back), added(two, two_back)
        for mask in reversed(bits_y[:-1]):
            two = keep_half(two, mask, devices)
        for mask in reversed(bits_x[:-1]):
            one = keep_half(one, mask, devices)
        half = one.shape[0] // 2
        return tuple(
            jnp.concatenate([one[at : at + half], two[at : at + half]], axis=1) for at in (0, half)
        )

    def turn(one, two, one_back, two_back):
        one, one_far = halves_of(one, one_back)
        two, two_far = halves_of(two, two_back)
        for mask in reversed(bits_x[:-1]):
            whole_one = jnp.concatenate([one, one_far], axis=0)
            one, one_far = halves_of(
                whole_one[: whole_one.shape[0] // 2],
                swap(whole_one[whole_one.shape[0] // 2 :], mask),
            )
        for mask in reversed(bits_y[:-1]):
            whole_two = jnp.concatenate([two, two_far], axis=0)
            two, two_far = halves_of(
                whole_two[: whole_two.shape[0] // 2],
                swap(whole_two[whole_two.shape[0] // 2 :], mask),
            )
        return one, one_far, two, two_far

    def cross_back(one_far, two_far):
        return swap(one_far, bits_y[-1]), swap(two_far, bits_x[-1])

    ones, twos = (0, half_ff), (half_ff, FF)
    q_ones, q_twos = (0, half_qkv), (half_qkv, 3 * width)
    active = active[None]
    head_back = swap(head_far, head_masks[-1])
    d_head_in = in_halves_outside(lambda part: matmul(part, perm_head), d_head_in)
    d_resid_out, d_shift_head, d_scale_head, down_bias, d_gate_two, d_low_one, d_low_two = (
        norm_back(
            resid_out,
            d_head_in,
            hot,
            hot_t,
            mods[7],
            gate=mods[5],
            branch=mlp_out,
            perms=[perm_one_t, perm_two_t],
        )
    )
    down_f1, down_f2 = far_rows_of(d_low_one, active, ones), far_rows_of(d_low_two, active, twos)
    d_low_one, d_low_two, down_f1, down_f2 = tie(d_low_one, d_low_two, down_f1, down_f2)
    down_b1, down_b2 = swap(down_f1, 1), swap(down_f2, 1)
    d_hid, up_bias_sum = times_sets([d_low_one, d_low_two], w_down, hidden=hidden)
    d_hid = d_hid[None]
    d_hid, down_b1, down_b2, head_back, head_near = tie(
        d_hid, down_b1, down_b2, head_back, head_near
    )
    head_near, head_far = halves_of(head_near, head_back)
    down_f1 = meet_far(d_low_one, active, ones, down_b1)
    down_f2 = meet_far(d_low_two, active, twos, down_b2)
    d_hid, down_f1, down_f2, head_far = tie(d_hid, down_f1, down_f2, head_far)
    down_x1, down_x2 = cross(down_f1, down_f2)
    head_back = swap(head_far, head_masks[-2])
    up_f1, up_f2 = far_rows_of(u_mid_one, d_hid, ones), far_rows_of(u_mid_two, d_hid, twos)
    up_b1, up_b2 = swap(up_f1, 1), swap(up_f2, 1)
    down_n1 = meet_near(d_low_one, active, ones, down_b1)
    down_n2 = meet_near(d_low_two, active, twos, down_b2)
    d_u = back_sets(d_hid, w_up, perms)
    d_u, down_x1, down_x2, down_n1, down_n2, up_b1, up_b2, head_back, head_near = tie(
        d_u, down_x1, down_x2, down_n1, down_n2, up_b1, up_b2, head_back, head_near
    )
    down_n1, down_f1, down_n2, down_f2 = turn(down_n1, down_n2, down_x1, down_x2)
    head_near = added(head_near, head_back)
    down_x1, down_x2 = cross_back(down_f1, down_f2)
    head_grad = keep_all(head_near, head_masks[:-2], devices)
    up_f1 = meet_far(u_mid_one, d_hid, ones, up_b1)
    up_f2 = meet_far(u_mid_two, d_hid, twos, up_b2)
    d_resid_mid, d_shift_two, d_scale_two, proj_bias, d_gate_one, d_low = norm_back(
        resid_mid, d_u, hot, hot_t, mods[4], beyond=d_resid_out, gate=mods[2], branch=attn_out
    )
    d_mod = jnp.concatenate(
        [d_gate_one, d_shift_two, d_scale_two, d_gate_two, d_shift_head, d_scale_head], axis=1
    ).astype(BF16)
    d_low, d_mod, down_x1, down_x2, down_n1, down_n2, up_f1, up_f2, head_grad = tie(
        d_low, d_mod, down_x1, down_x2, down_n1, down_n2, up_f1, up_f2, head_grad
    )
    up_x1, up_x2 = cross(up_f1, up_f2)
    down_near, down_far = join(down_n1, down_n2, down_x1, down_x2)
    down_back = swap(down_far, bits_z[-1])
    all_mod = grown(bits_z[:1], d_mod)
    d_low3 = d_low[None]
    p_ones, p_twos = (0, top), (top, width)
    proj_f1 = far_rows_of(mix_one, d_low3, p_ones)
    proj_f2 = far_rows_of(mix_two, d_low3, p_twos)
    proj_b1, proj_b2 = swap(proj_f1, 1), swap(proj_f2, 1)
    up_n1 = meet_near(u_mid_one, d_hid, ones, up_b1)
    up_n2 = meet_near(u_mid_two, d_hid, twos, up_b2)
    d_mix = back_sets(d_low3, w_proj, perms, out=BF16)
    d_mix, proj_b1, proj_b2 = tie(d_mix, proj_b1, proj_b2)
    proj_f1 = meet_far(mix_one, d_low3, p_ones, proj_b1)
    proj_f2 = meet_far(mix_two, d_low3, p_twos, proj_b2)
    proj_n1 = meet_near(mix_one, d_low3, p_ones, proj_b1)
    proj_n2 = meet_near(mix_two, d_low3, p_twos, proj_b2)
    d_qkv, attn_sums = attend_back(qkv, q_gain, k_gain, mask_rows, d_mix)
    d_qkv, up_x1, up_x2, up_n1, up_n2, down_back, down_near, all_mod, proj_f1, proj_f2 = tie(
        d_qkv, up_x1, up_x2, up_n1, up_n2, down_back, down_near, all_mod, proj_f1, proj_f2
    )
    up_n1, up_f1, up_n2, up_f2 = turn(up_n1, up_n2, up_x1, up_x2)
    up_x1, up_x2 = cross_back(up_f1, up_f2)
    down_near, down_far = halves_of(down_near, down_back)
    down_back = swap(down_far, bits_z[-2])
    proj_x1, proj_x2 = cross(proj_f1, proj_f2)
    qkv_f1, qkv_f2 = far_rows_of(u_one, d_qkv, q_ones), far_rows_of(u_two, d_qkv, q_twos)
    d_u = back_sets(d_qkv, w_qkv, perms)
    d_u, up_x1, up_x2, up_n1, up_n2, down_back, proj_x1, proj_x2, qkv_f1, qkv_f2, all_mod = tie(
        d_u, up_x1, up_x2, up_n1, up_n2, down_back, proj_x1, proj_x2, qkv_f1, qkv_f2, all_mod
    )
    qkv_b1, qkv_b2 = swap(qkv_f1, 1), swap(qkv_f2, 1)
    up_near, up_far = join(up_n1, up_n2, up_x1, up_x2)
    up_back = swap(up_far, bits_z[-1])
    all_mod = grown(bits_z[1:], all_mod)
    d_resid_in, d_shift_one, d_scale_one, word_bias, d_res16 = norm_back(
        resid_in, d_u, hot, hot_t, mods[1], beyond=d_resid_mid
    )
    d_first = jnp.concatenate([d_shift_one, d_scale_one], axis=1).astype(BF16)
    d_res16, d_first, qkv_b1, qkv_b2 = tie(d_res16, d_first, qkv_b1, qkv_b2)
    qkv_f1 = meet_far(u_one, d_qkv, q_ones, qkv_b1)
    qkv_f2 = meet_far(u_two, d_qkv, q_twos, qkv_b2)
    d_res16, qkv_f1, qkv_f2, d_first = tie(d_res16, qkv_f1, qkv_f2, d_first)
    qkv_x1, qkv_x2 = cross(qkv_f1, qkv_f2)
    all_first = grown(bits_z, d_first)
    ada_sums = jnp.sum(
        jnp.concatenate([d_first, d_mod], axis=1).astype(F32), axis=0, keepdims=True
    )
    arrays = [word_bias, attn_sums, proj_bias, down_bias, up_bias_sum, ada_sums, bias_grad[None]]
    plan = [(0, 0), (1, 2), (1, 3), (2, 0), (3, 0), (1, 0), (1, 1), (4, 0), (5, 0), (6, 0)]
    d_slim = slim_back(d_res16, token_hot, arrays, plan, perm_one, n_embed)
    d_slim = keep_half(d_slim, 1, devices)
    proj_n1, proj_f1, proj_n2, proj_f2 = turn(proj_n1, proj_n2, proj_x1, proj_x2)
    proj_x1, proj_x2 = cross_back(proj_f1, proj_f2)
    qkv_n1 = meet_near(u_one, d_qkv, q_ones, qkv_b1)
    qkv_n2 = meet_near(u_two, d_qkv, q_twos, qkv_b2)
    (
        qkv_x1,
        qkv_x2,
        qkv_n1,
        qkv_n2,
        all_first,
        d_slim,
        proj_x1,
        proj_x2,
        proj_n1,
        proj_n2,
        up_back,
        up_near,
        all_mod,
    ) = tie(
        qkv_x1,
        qkv_x2,
        qkv_n1,
        qkv_n2,
        all_first,
        d_slim,
        proj_x1,
        proj_x2,
        proj_n1,
        proj_n2,
        up_back,
        up_near,
        all_mod,
    )
    qkv_n1, qkv_f1, qkv_n2, qkv_f2 = turn(qkv_n1, qkv_n2, qkv_x1, qkv_x2)
    qkv_x1, qkv_x2 = cross_back(qkv_f1, qkv_f2)
    up_near, up_far = halves_of(up_near, up_back)
    up_back = swap(up_far, bits_z[-2])
    cut = cuts[1] - cuts[0]
    all_first = jnp.concatenate([all_first, all_mod[:, :cut]], axis=1)
    all_first = grown(bits_y, all_first)
    for mask in reversed(bits_x):
        d_slim = keep_half(d_slim, mask, devices)
    qkv_x1, qkv_x2, qkv_n1, qkv_n2, up_back, up_near, all_first, all_mod, d_slim = tie(
        qkv_x1, qkv_x2, qkv_n1, qkv_n2, up_back, up_near, all_first, all_mod, d_slim
    )
    near, far = join(
        jnp.concatenate([qkv_n1, proj_n1], axis=1),
        jnp.concatenate([qkv_n2, proj_n2], axis=1),
        jnp.concatenate([qkv_x1, proj_x1], axis=1),
        jnp.concatenate([qkv_x2, proj_x2], axis=1),
    )
    attn_back = swap(far, bits_z[-1])
    all_two = grown(bits_x, all_mod[:, cut:])
    all_first = grown(bits_x, all_first)
    d_slim = keep_all(d_slim, bits_z + bits_y, devices)
    attn_back, near, all_two, all_first, d_slim = tie(attn_back, near, all_two, all_first, d_slim)
    near, far = halves_of(near, attn_back)
    attn_back = swap(far, bits_z[-2])
    all_two = grown(bits_y + [1], all_two)
    all_first = grown([1], all_first)

    def close(near, back):
        masks = bits_z[:-2]
        near = added(near, back, BF16 if masks else F32)
        return keep_all(near, masks, devices)

    attn_rows, up_rows, down_rows = (
        close(near, attn_back),
        close(up_near, up_back),
        close(down_near, down_back),
    )
    slim_grad = d_slim.T
    half_attn = half_qkv + top
    attn_grad = jnp.concatenate(
        [
            attn_rows[:, :half_qkv],
            attn_rows[:, half_attn : half_attn + half_qkv],
            attn_rows[:, half_qkv:half_attn],
            attn_rows[:, half_attn + half_qkv :],
        ],
        axis=1,
    )
    mlp_grad = jnp.stack([up_rows, down_rows])
    ada_grad = jnp.concatenate([matmul_tn(class_act, all_first), matmul_tn(act_two, all_two)], axis=1)
    d_class_act = matmul_nt(all_first, ada16[:, : cuts[1]]) + to_one(
        matmul_nt(all_two, ada16[:, cuts[1] :])
    )
    _, silu_back = jax.vjp(jax.nn.silu, class_vec)
    d_class = precise_tn(class_hot.astype(F32), silu_back(d_class_act)[0])
    embed_grad = jnp.concatenate(
        [
            d_class,
            slim_grad[:used],
            jnp.zeros((POSITIONS - used, rows), F32),
            slim_grad[used:n_embed],
        ],
        axis=0,
    )
    gains_grad = slim_grad[n_embed : n_embed + n_gains]

    gradients = (attn_grad, mlp_grad, ada_grad, embed_grad, gains_grad, head_grad)
    squares_local = jnp.zeros((), F32)
    for gradient in gradients:
        squares_local = squares_local + jnp.sum(gradient * gradient)
    sums = sum_all(
        jnp.stack([squares_local, loss_part])[None], [1] + bits_x + bits_y + bits_z, devices
    )
    total_sq, loss_sum = sums[0, 0], sums[0, 1]
    grad_norm = jnp.sqrt(total_sq)
    clip_factor = jnp.minimum(1.0, CLIP_NORM / (grad_norm + 1e-06))
    masters = (attn_weight, mlp_weight, ada_weight, embed_weight, gains_weight, head_weight)
    moments = (attn_moment, mlp_moment, ada_moment, embed_moment, gains_moment, head_moment)
    squares = (attn_square, mlp_square, ada_square, embed_square, gains_square, head_square)
    updates = []
    for number in range(6):
        updates.extend(
            adam_step(
                masters[number],
                moments[number],
                squares[number],
                gradients[number],
                clip_factor,
                RATES[number],
            )
        )
    return tuple(updates) + (grad_norm, loss_sum, total_count)


def solution(mesh):
    n_dp, n_vocab = mesh.shape["dp"], mesh.shape["vocab"]
    n_z = 1 << (n_dp.bit_length() // 2)
    devices = n_dp * n_vocab

    def bits(least, top):
        found = []
        while least < top:
            found, least = [least] + found, least * 2
        return found

    ways = {"devices": devices, "n_vocab": n_vocab}
    ways["x"] = bits(2, n_vocab)
    ways["y"] = bits(n_vocab, devices // n_z)
    ways["z"] = bits(devices // n_z, devices)
    every = ("dp", "vocab")
    by_row = P(every, None)
    by_mid = P(None, every, None)
    by_column = P(None, every)
    head = P("dp", "vocab")
    placed = (P(every, None, None), by_row, by_row, by_row, by_row)
    for spec in (by_row, by_mid, by_row, by_column, by_column, head):
        placed = placed + (spec,) * 3
    given = ()
    for spec in (by_row, by_mid, by_row, by_column, by_column, head):
        given = given + (spec,) * 4

    def step(*arrays):
        return per_device(ways, *arrays)

    return jax.shard_map(
        step, mesh=mesh, in_specs=placed, out_specs=given + (P(), P(), P()), check_vma=False
    )
```

time: 972 us -> 767 us (0.79)
  Pallas kernels: 0 us -> 206 us
  matrix products: 218 us -> 37.4 us
  waiting for transfers between devices: 338 us -> 243 us
  local copies, waits for them, and re-layouts: 128 us -> 44.3 us
  other arithmetic: 125 us -> 98.3 us
  starting transfers between devices: 138 us -> 114 us
    pallas_call x0 -> x41, Pallas kernels: none -> 206 us  [run(): pl.pallas_call(body, grid=grid, in_specs=specs, out_shape=outs, out_specs...]
    ppermute x138 -> x129, waiting for transfers between devices: 338 us -> 243 us  [swapped(): lax.ppermute(value, ('dp', 'vocab'), [(i, i ^ mask) for i in range(device...]
    dot_general x18 -> x11, matrix products: 76.9 us -> 20.3 us  [matmul(): return jnp.dot(left, right, preferred_element_type=F32)]
    dot_general x21 -> x0, matrix products: 47.1 us -> none  [the longest x4 9.45 us: back_block(): jnp.einsum('hqk,qhd->khd', soft_low, dm_group, preferred_element_type=F32)]
    unnamed x362 -> x417, local copies, waits for them, and re-layouts: 58 us -> 28.7 us
    dot_general x10 -> x5, matrix products: 38.3 us -> 10.1 us  [matmul_tn(): lax.dot_general(left, right, (((0,), (0,)), ((), ())), preferred_element_...]
    reduce_sum x19 -> x4, other arithmetic: 29.9 us -> 4.59 us  [the longest x2 3.91 us: part_stats(): exp_sums = jnp.sum(jnp.exp(logits - local_max[:, None]), axis=1)]
    dot_general x11 -> x4, matrix products: 31.3 us -> 6.5 us  [matmul_nt(): lax.dot_general(left, right, (((1,), (1,)), ((), ())), preferred_element_...]
  transfers between devices with their start and end apart: 138 -> 129, of which waited for: 55 -> 48; matrix products, arithmetic and copies ran while one was open for 25% -> 14% of each run, Pallas kernels for 0% -> 21%
where the time goes in v2:
time: 767 us; the launch traced here: 756 us
  waiting for transfers between devices  243 us (32%)
  Pallas kernels  206 us (27%)
  starting transfers between devices  114 us (15%)
  other arithmetic  98.3 us (13%)
  local copies, waits for them, and re-layouts  44.3 us (6%)
  matrix products  37.4 us (5%)
  between operations  13 us (2%)
    ppermute x129, waiting for transfers between devices, swapped(): lax.ppermute(value, ('dp', 'vocab'), [(i, i ^ mask) for i in range(device...  243 us
    pallas_call x41, Pallas kernels, run(): pl.pallas_call(body, grid=grid, in_specs=specs, out_shape=outs, out_specs...  206 us
    ppermute x129, starting transfers between devices, swapped(): lax.ppermute(value, ('dp', 'vocab'), [(i, i ^ mask) for i in range(device...  114 us
    unnamed x417, local copies, waits for them, and re-layouts  28.7 us
    convert_element_type x35, other arithmetic, added(): return (mine.astype(F32) + theirs.astype(F32)).astype(out)  21.8 us
    concatenate x36, other arithmetic, grow(): return jnp.concatenate([value, swapped(value, mask, devices)], axis=0)  20.7 us
    dot_general x11, matrix products, matmul(): return jnp.dot(left, right, preferred_element_type=F32)  20.3 us
  transfers between devices with their start and end apart: 129, of which 48 were waited for; matrix products, arithmetic and copies ran while one was open for 14% of the time, Pallas kernels for 21%

profile of v2, /device:TPU:0, one launch (start us, length us, event | category | flops | bytes accessed | tf_op | source)
XLA Modules:
  0.0 756.3 jit_solution(2184640990617689852)
XLA Ops:
  2.8 4.0 collective-permute-start.1
  8.0 2.9 collective-permute-start.2
  14.8 2.6 fusion.3
  17.5 2.7 fusion.5
  44.2 3.1 collective-permute-done.9
  57.4 8.1 %collective-permute-done.13 = bf16[128,512]{1,0:T(8,128)(2,1)S(1)} collective-permute-done((bf16[128,512]{1,0:T(8,128)(2,1)S(1)}, bf16[128,512]{1,0:T(8,128)(2,1)S(1)}, u32[]{:S(2)}, u32[]{:S(2)}) %collective-permute-start.13) | collective-permute-done | bytes 131104 | tf_op jit(solution)/shard_map/ppermute | solution.py:66
  79.4 3.3 collective-permute-done.18
  85.6 2.7 convolution_convert_fusion.1
  91.1 2.7 collective-permute-start.20
  101.7 6.8 shard_map.457
  108.4 7.0 collective-permute-done.26
  120.8 13.5 %collective-permute-done.32 = bf16[128,2560]{1,0:T(8,128)(2,1)S(1)} collective-permute-done((bf16[128,2560]{1,0:T(8,128)(2,1)S(1)}, bf16[128,2560]{1,0:T(8,128)(2,1)S(1)}, u32[]{:S(2)}, u32[]{:S(2)}) %collective-permute-start.32) | collective-permute-done | bytes 655392 | tf_op jit(solution)/shard_map/ppermute | solution.py:66
  141.8 7.1 shard_map.458.q_ref.k_ref.v_ref
  151.2 10.7 %shard_map.459 = bf16[384,1024]{1,0:T(8,128)(2,1)S(1)} custom-call(f32[384,3072]{1,0:T(8,128)S(1)} %copy-done.43, f32[384,3072]{1,0:T(8,128)S(1)} %copy-done.43, f32[384,3072]{1,0:T(8,128)S(1)} %copy-done.43, f32[1,1024]{1,0:T(1,128)S(1)} %get-tuple-element.576.qg_ref, f32[1,1024]{1,0:T(1,128)S(1)} %get-tuple-element.575.kg_ref, f32[384,384]{1,0:T(8,128)S(1)} %copy-done.88), custom_call_target="tpu_custom_call" | custom-call | flops 10000000000 | bytes 14753792 | tf_op jit(solution)/shard_map/pallas_call | solution.py:129
  171.2 8.4 %collective-permute-done.40 = bf16[32,3072]{1,0:T(8,128)(2,1)S(1)} collective-permute-done((bf16[32,3072]{1,0:T(8,128)(2,1)S(1)}, bf16[32,3072]{1,0:T(8,128)(2,1)S(1)}, u32[]{:S(2)}, u32[]{:S(2)}) %collective-permute-start.40) | collective-permute-done | bytes 196640 | tf_op jit(solution)/shard_map/ppermute | solution.py:66
  180.4 5.7 collective-permute-done.41
  187.4 4.7 collective-permute-done.44
  199.5 8.6 %shard_map.461 = (bf16[384,1024]{1,0:T(8,128)(2,1)S(1)}, bf16[384,1024]{1,0:T(8,128)(2,1)S(1)}, f32[384,1024]{1,0:T(8,128)S(1)}) custom-call(f32[384,1024]{1,0:T(8,128)S(1)} %convolution_add_fusion.value_ref.refs_0_, f32[384,8]{1,0:T(8,128)S(1)} %fusion.57.hot_ref, f32[8,1024]{1,0:T(8,128)S(1)} %get-tuple-element.621.shift_ref, ...), custom_call_target="tpu_custom_call" | custom-call | flops 1000000000 | bytes 7450624 | tf_op jit(solution)/shard_map/pallas_call | solution.py:129
  208.1 5.6 collective-permute-done.50
  216.2 10.8 %collective-permute-done.51 = bf16[128,1024]{1,0:T(8,128)(2,1)S(1)} collective-permute-done((bf16[128,1024]{1,0:T(8,128)(2,1)S(1)}, bf16[128,1024]{1,0:T(8,128)(2,1)S(1)}, u32[]{:S(2)}, u32[]{:S(2)}) %collective-permute-start.51) | collective-permute-done | bytes 262176 | tf_op jit(solution)/shard_map/ppermute | solution.py:66
  229.0 11.7 %collective-permute-done.55 = bf16[128,2048]{1,0:T(8,128)(2,1)S(1)} collective-permute-done((bf16[128,2048]{1,0:T(8,128)(2,1)S(1)}, bf16[128,2048]{1,0:T(8,128)(2,1)S(1)}, u32[]{:S(2)}, u32[]{:S(2)}) %collective-permute-start.55) | collective-permute-done | bytes 524320 | tf_op jit(solution)/shard_map/ppermute | solution.py:66
  243.5 10.7 %shard_map.462 = (f32[384,4096]{1,0:T(8,128)}, bf16[384,4096]{1,0:T(8,128)(2,1)}) custom-call(bf16[384,1024]{1,0:T(8,128)(2,1)S(1)} %get-tuple-element.300.one_ref.left_ref, bf16[384,1024]{1,0:T(8,128)(2,1)S(1)} %get-tuple-element.301.two_ref.left_ref, f32[1,4096]{1,0:T(1,128)S(1)} %bitcast.119, bf16[256,2048]{1,0:T(8,128)(2,1)S(1)} %slice.644.refs_1_.refs_0_, ...), custom_call_target="tpu_custom_call" | custom-call | flops 3221225472 | bytes 9977856 | tf_op jit(solution)/shard_map/pallas_call | solution.py:129
  257.5 21.0 %collective-permute-done.61 = f32[1,2,384]{2,1,0:T(2,128)S(1)} collective-permute-done((f32[1,2,384]{2,1,0:T(2,128)S(1)}, f32[1,2,384]{2,1,0:T(2,128)S(1)}, u32[]{:S(2)}, u32[]{:S(2)}) %collective-permute-start.61) | collective-permute-done | bytes 3104 | tf_op jit(solution)/shard_map/ppermute | solution.py:66
  279.6 22.8 %collective-permute-done.60 = bf16[256,1024]{1,0:T(8,128)(2,1)S(1)} collective-permute-done((bf16[256,1024]{1,0:T(8,128)(2,1)S(1)}, bf16[256,1024]{1,0:T(8,128)(2,1)S(1)}, u32[]{:S(2)}, u32[]{:S(2)}) %collective-permute-start.60) | collective-permute-done | bytes 524320 | tf_op jit(solution)/shard_map/ppermute | solution.py:66
  308.9 14.7 %shard_map.463.refs_1_.refs_2_ = f32[384,1024]{1,0:T(8,128)} custom-call(bf16[1,384,4096]{2,1,0:T(8,128)(2,1)} %bitcast.97, bf16[1024,1024]{1,0:T(8,128)(2,1)} %copy-done.4, bf16[1024,1024]{1,0:T(8,128)(2,1)} %get-tuple-element.314.two_ref, f32[1,1024]{1,0:T(1,128)S(1)} %get-tuple-element.573.refs_0_, bf16[256,2048]{1,0:T(8,128)(2,1)S(1)} %pad_maximum_fusion.9.refs_1_, ...), custom_call_target="tpu_custom_call" | custom-call | flops 3221225472 | bytes 15732736 | tf_op jit(solution)/shard_map/pallas_call | solution.py:129
  325.0 7.4 shard_map.464
  337.0 4.0 add_reduce_fusion.1
  342.0 12.6 %collective-permute-done.67 = bf16[384,1024]{1,0:T(8,128)(2,1)S(1)} collective-permute-done((bf16[384,1024]{1,0:T(8,128)(2,1)}, bf16[384,1024]{1,0:T(8,128)(2,1)S(1)}, u32[]{:S(2)}, u32[]{:S(2)}) %collective-permute-start.67) | collective-permute-done | bytes 786464 | tf_op jit(solution)/shard_map/ppermute | solution.py:66
  356.9 3.4 add_reduce_fusion
  360.4 2.9 exponential_reduce_fusion
  366.8 2.8 collective-permute-done.71
  369.8 4.6 fusion.12
  383.1 2.8 fusion.37
  386.0 2.8 fusion.34
  388.8 13.0 %collective-permute-done.73 = bf16[384,1024]{1,0:T(8,128)(2,1)S(1)} collective-permute-done((bf16[384,1024]{1,0:T(8,128)(2,1)S(1)}, bf16[384,1024]{1,0:T(8,128)(2,1)S(1)}, u32[]{:S(2)}, u32[]{:S(2)}) %collective-permute-start.73) | collective-permute-done | bytes 786464 | tf_op jit(solution)/shard_map/ppermute | solution.py:66
  406.0 10.0 %shard_map.465 = (f32[384,1024]{1,0:T(8,128)S(1)}, f32[8,1024]{1,0:T(8,128)S(1)}, f32[8,1024]{1,0:T(8,128)S(1)}, f32[1,1024]{1,0:T(1,128)S(1)}, f32[8,1024]{1,0:...) custom-call(f32[384,8]{1,0:T(8,128)S(1)} %fusion.57.hot_ref, f32[8,384]{1,0:T(8,128)S(1)} %fusion.77.hot_t_ref, ...), custom_call_target="tpu_custom_call" | custom-call | flops 1000000000 | bytes 9003008 | tf_op jit(solution)/shard_map/pallas_call | solution.py:129
  422.1 11.9 %shard_map.468 = (bf16[384,4096]{1,0:T(8,128)(2,1)}, f32[1,4096]{1,0:T(1,128)S(1)}) custom-call(bf16[384,1024]{1,0:T(8,128)(2,1)S(1)} %get-tuple-element.331.left_ref.one_ref, bf16[384,1024]{1,0:T(8,128)(2,1)S(1)} %get-tuple-element.332.left_ref.two_ref, f32[384,4096]{1,0:T(8,128)} %get-tuple-element.333.refs_0_, bf16[256,2048]{1,0:T(8,128)(2,1)S(1)} %copy-done.26, ...), custom_call_target="tpu_custom_call" | custom-call | flops 3221225472 | bytes 16252928 | tf_op jit(solution)/shard_map/pallas_call | solution.py:129
  433.9 12.9 %collective-permute-done.76 = bf16[512,1024]{1,0:T(8,128)(2,1)} collective-permute-done((bf16[512,1024]{1,0:T(8,128)(2,1)}, bf16[512,1024]{1,0:T(8,128)(2,1)}, u32[]{:S(2)}, u32[]{:S(2)}) %collective-permute-start.76) | collective-permute-done | bytes 1048608 | tf_op jit(solution)/shard_map/ppermute | solution.py:66
  446.9 4.4 shard_map.470
  451.3 4.2 shard_map.469
  455.5 2.7 add_convert_fusion.20
  458.2 3.3 shard_map.475
  461.5 3.2 shard_map.474
  473.7 3.3 shard_map.473
  477.1 3.5 shard_map.472
  480.7 13.2 %shard_map.471.refs_1_ = f32[384,1024]{1,0:T(8,128)} custom-call(bf16[1,384,4096]{2,1,0:T(8,128)(2,1)} %bitcast.104, bf16[1024,1024]{1,0:T(8,128)(2,1)} %copy-done.4, bf16[1024,1024]{1,0:T(8,128)(2,1)} %get-tuple-element.314.two_ref, bf16[256,2048]{1,0:T(8,128)(2,1)S(1)} %copy-done.49, bf16[256,2048]{1,0:T(8,128)(2,1)S(1)} %copy-done.71, ...), custom_call_target="tpu_custom_call" | custom-call | flops 3221225472 | bytes 15728640 | tf_op jit(solution)/shard_map/pallas_call | solution.py:129
  493.9 4.7 collective-permute-done.81
  498.6 3.3 shard_map.478
  501.9 3.4 shard_map.484
  513.8 6.9 shard_map.476
  520.8 3.5 shard_map.477
  524.3 3.2 shard_map.483
  534.8 4.9 shard_map.479.dm_ref
  542.1 21.5 %shard_map.482 = (bf16[3,384,1024]{2,1,0:T(8,128)(2,1)S(1)}, f32[8,1024]{1,0:T(8,128)S(1)}) custom-call(f32[384,3072]{1,0:T(8,128)} %shard_map.458.q_ref.k_ref.v_ref, f32[384,3072]{1,0:T(8,128)} %shard_map.458.q_ref.k_ref.v_ref, f32[384,3072]{1,0:T(8,128)} %shard_map.458.q_ref.k_ref.v_ref, f32[1,1024]{1,0:T(1,128)S(1)} %get-tuple-element.576.qg_ref, ...), custom_call_target="tpu_custom_call" | custom-call | flops 30000001024 | bytes 15540224 | tf_op jit(solution)/shard_map/pallas_call | solution.py:129
  578.9 11.1 %shard_map.487.refs_1_ = f32[384,1024]{1,0:T(8,128)} custom-call(bf16[3,384,1024]{2,1,0:T(8,128)(2,1)} %copy-done.2, bf16[1024,1024]{1,0:T(8,128)(2,1)} %copy-done.4, bf16[1024,1024]{1,0:T(8,128)(2,1)} %get-tuple-element.314.two_ref, bf16[256,1536]{1,0:T(8,128)(2,1)S(1)} %copy-done.34, bf16[256,1536]{1,0:T(8,128)(2,1)S(1)} %copy-done.53, ...), custom_call_target="tpu_custom_call" | custom-call | flops 2415919104 | bytes 12845056 | tf_op jit(solution)/shard_map/pallas_call | solution.py:129
  596.2 5.6 shard_map.490
  623.6 12.5 %collective-permute-done.104 = bf16[128,512]{1,0:T(8,128)(2,1)S(1)} collective-permute-done((bf16[128,512]{1,0:T(8,128)(2,1)S(1)}, bf16[128,512]{1,0:T(8,128)(2,1)S(1)}, u32[]{:S(2)}, u32[]{:S(2)}) %collective-permute-start.104) | collective-permute-done | bytes 131104 | tf_op jit(solution)/shard_map/ppermute | solution.py:66
  647.8 5.7 collective-permute-done.109
  661.8 9.8 %collective-permute-done.116 = bf16[64,512]{1,0:T(8,128)(2,1)S(1)} collective-permute-done((bf16[64,512]{1,0:T(8,128)(2,1)S(1)}, bf16[64,512]{1,0:T(8,128)(2,1)S(1)}, u32[]{:S(2)}, u32[]{:S(2)}) %collective-permute-start.116) | collective-permute-done | bytes 65568 | tf_op jit(solution)/shard_map/ppermute | solution.py:66
  682.0 2.6 collective-permute-start.118
  685.4 11.6 %collective-permute-done.118 = bf16[32,4096]{1,0:T(8,128)(2,1)S(1)} collective-permute-done((bf16[32,4096]{1,0:T(8,128)(2,1)S(1)}, bf16[32,4096]{1,0:T(8,128)(2,1)S(1)}, u32[]{:S(2)}, u32[]{:S(2)}) %collective-permute-start.118) | collective-permute-done | bytes 262176 | tf_op jit(solution)/shard_map/ppermute | solution.py:66
  726.6 3.2 collective-permute-start.127
  731.9 3.1 collective-permute-start.128
  741.5 2.9 fusion.93
  (934 shorter events, 292.9 us)
Async XLA Ops:
  2.8 20.4 %collective-permute-start.1 = (bf16[32,512]{1,0:T(8,128)(2,1)S(1)}, bf16[32,512]{1,0:T(8,128)(2,1)S(1)}, u32[]{:S(2)}, u32[]{:S(2)}) collective-permute-start(bf16[32,512]{1,0:T(8,128)(2,1)S(1)} %fusion.72), channel_id=1, source_target_pairs={{0,16},{1,17},{2,18},{3,19},{4,20},{5,21},{6,22},{7,23},{8,24},{9,... | collective-permute-start | bytes 98312 | tf_op jit(solution)/shard_map/ppermute | solution.py:66
  8.0 15.3 %collective-permute-start.3 = (bf16[32,1536]{1,0:T(8,128)(2,1)S(1)}, bf16[32,1536]{1,0:T(8,128)(2,1)S(1)}, u32[]{:S(2)}, u32[]{:S(2)}) collective-permute-start(bf16[32,1536]{1,0:T(8,128)(2,1)S(1)} %get-tuple-element.614), channel_id=1, source_target_pairs={{0,16},{1,17},{2,18},{3,19},{4,20},{5,21},{6,22},{7,23},{8,24},{9,... | collective-permute-start | bytes 294920 | tf_op jit(solution)/shard_map/ppermute | solution.py:66
  8.0 15.3 %collective-permute-start.2 = (bf16[32,1536]{1,0:T(8,128)(2,1)S(1)}, bf16[32,1536]{1,0:T(8,128)(2,1)S(1)}, u32[]{:S(2)}, u32[]{:S(2)}) collective-permute-start(bf16[32,1536]{1,0:T(8,128)(2,1)S(1)} %get-tuple-element.615), channel_id=1, source_target_pairs={{0,16},{1,17},{2,18},{3,19},{4,20},{5,21},{6,22},{7,23},{8,24},{9,... | collective-permute-start | bytes 294920 | tf_op jit(solution)/shard_map/ppermute | solution.py:66
  49.0 17.3 %collective-permute-start.17 = (bf16[32,5120]{1,0:T(8,128)(2,1)}, bf16[32,5120]{1,0:T(8,128)(2,1)}, u32[]{:S(2)}, u32[]{:S(2)}) collective-permute-start(bf16[32,5120]{1,0:T(8,128)(2,1)} %pad_maximum_fusion.36), channel_id=1, source_target_pairs={{0,16},{1,17},{2,18},{3,19},{4,20},{5,21},{6,22},{7,23},{8,24},{9,... | collective-permute-start | bytes 983048 | tf_op jit(solution)/shard_map/ppermute | solution.py:66
  51.6 16.7 %collective-permute-start.16 = (bf16[128,1536]{1,0:T(8,128)(2,1)}, bf16[128,1536]{1,0:T(8,128)(2,1)}, u32[]{:S(2)}, u32[]{:S(2)}) collective-permute-start(bf16[128,1536]{1,0:T(8,128)(2,1)} %pad_maximum_fusion.32), channel_id=1, source_target_pairs={{0,2},{1,3},{2,0},{3,1},{4,6},{5,7},{6,4},{7,5},{8,10},{9,11},{10,... | collective-permute-start | bytes 1179656 | tf_op jit(solution)/shard_map/ppermute | solution.py:66
  52.9 20.8 %collective-permute-start.15 = (bf16[128,1536]{1,0:T(8,128)(2,1)}, bf16[128,1536]{1,0:T(8,128)(2,1)}, u32[]{:S(2)}, u32[]{:S(2)}) collective-permute-start(bf16[128,1536]{1,0:T(8,128)(2,1)} %pad_maximum_fusion.31), channel_id=1, source_target_pairs={{0,4},{1,5},{2,6},{3,7},{4,0},{5,1},{6,2},{7,3},{8,12},{9,13},{10,... | collective-permute-start | bytes 1179656 | tf_op jit(solution)/shard_map/ppermute | solution.py:66
  95.3 21.4 %collective-permute-start.22 = (bf16[256,1536]{1,0:T(8,128)(2,1)}, bf16[256,1536]{1,0:T(8,128)(2,1)S(1)}, u32[]{:S(2)}, u32[]{:S(2)}) collective-permute-start(bf16[256,1536]{1,0:T(8,128)(2,1)} %pad_maximum_fusion.16.refs_1_.refs_0_), channel_id=1, source_target_pairs={{0,2},{1,3},{2,0},{3,1},{4,6},{5,7},{6,4},{7,5},{8,10},{9,11},{10,... | collective-permute-start | bytes 2359304 | tf_op jit(solution)/shard_map/ppermute | solution.py:66
  96.6 20.1 %collective-permute-start.24 = (bf16[256,1536]{1,0:T(8,128)(2,1)}, bf16[256,1536]{1,0:T(8,128)(2,1)S(1)}, u32[]{:S(2)}, u32[]{:S(2)}) collective-permute-start(bf16[256,1536]{1,0:T(8,128)(2,1)} %pad_maximum_fusion.16.refs_1_.refs_0_), channel_id=1, source_target_pairs={{0,1},{1,0},{2,3},{3,2},{4,5},{5,4},{6,7},{7,6},{8,9},{9,8},{10,11... | collective-permute-start | bytes 2359304 | tf_op jit(solution)/shard_map/ppermute | solution.py:66
  96.6 20.1 %collective-permute-start.23 = (bf16[256,1536]{1,0:T(8,128)(2,1)S(1)}, bf16[256,1536]{1,0:T(8,128)(2,1)S(1)}, u32[]{:S(2)}, u32[]{:S(2)}) collective-permute-start(bf16[256,1536]{1,0:T(8,128)(2,1)S(1)} %pad_maximum_fusion.17.refs_5_.refs_4_), channel_id=1, source_target_pairs={{0,4},{1,5},{2,6},{3,7},{4,0},{5,1},{6,2},{7,3},{8,12},{9,13},{10,... | collective-permute-start | bytes 2359304 | tf_op jit(solution)/shard_map/ppermute | solution.py:66
  98.1 18.6 %collective-permute-start.25 = (bf16[256,1536]{1,0:T(8,128)(2,1)S(1)}, bf16[256,1536]{1,0:T(8,128)(2,1)S(1)}, u32[]{:S(2)}, u32[]{:S(2)}) collective-permute-start(bf16[256,1536]{1,0:T(8,128)(2,1)S(1)} %pad_maximum_fusion.17.refs_5_.refs_4_), channel_id=1, source_target_pairs={{0,1},{1,0},{2,3},{3,2},{4,5},{5,4},{6,7},{7,6},{8,9},{9,8},{10,11... | collective-permute-start | bytes 2359304 | tf_op jit(solution)/shard_map/ppermute | solution.py:66
  98.4 17.1 %collective-permute-start.26 = (bf16[64,5120]{1,0:T(8,128)(2,1)S(1)}, bf16[64,5120]{1,0:T(8,128)(2,1)}, u32[]{:S(2)}, u32[]{:S(2)}) collective-permute-start(bf16[64,5120]{1,0:T(8,128)(2,1)S(1)} %copy-done.119), channel_id=1, source_target_pairs={{0,8},{1,9},{2,10},{3,11},{4,12},{5,13},{6,14},{7,15},{8,0},{9,1},... | collective-permute-start | bytes 1966088 | tf_op jit(solution)/shard_map/ppermute | solution.py:66
  116.8 19.1 %collective-permute-start.30 = (bf16[128,3072]{1,0:T(8,128)(2,1)S(1)}, bf16[128,3072]{1,0:T(8,128)(2,1)S(1)}, u32[]{:S(2)}, u32[]{:S(2)}) collective-permute-start(bf16[128,3072]{1,0:T(8,128)(2,1)S(1)} %slice.631), channel_id=1, source_target_pairs={{0,1},{1,0},{2,3},{3,2},{4,5},{5,4},{6,7},{7,6},{8,9},{9,8},{10,11... | collective-permute-start | bytes 2359304 | tf_op jit(solution)/shard_map/ppermute | solution.py:66
  118.0 16.3 %collective-permute-start.32 = (bf16[128,2560]{1,0:T(8,128)(2,1)S(1)}, bf16[128,2560]{1,0:T(8,128)(2,1)S(1)}, u32[]{:S(2)}, u32[]{:S(2)}) collective-permute-start(bf16[128,2560]{1,0:T(8,128)(2,1)S(1)} %get-tuple-element.584), channel_id=1, source_target_pairs={{0,2},{1,3},{2,0},{3,1},{4,6},{5,7},{6,4},{7,5},{8,10},{9,11},{10,... | collective-permute-start | bytes 1966088 | tf_op jit(solution)/shard_map/ppermute | solution.py:66
  118.8 16.0 %collective-permute-start.31 = (bf16[128,2560]{1,0:T(8,128)(2,1)S(1)}, bf16[128,2560]{1,0:T(8,128)(2,1)S(1)}, u32[]{:S(2)}, u32[]{:S(2)}) collective-permute-start(bf16[128,2560]{1,0:T(8,128)(2,1)S(1)} %get-tuple-element.585), channel_id=1, source_target_pairs={{0,4},{1,5},{2,6},{3,7},{4,0},{5,1},{6,2},{7,3},{8,12},{9,13},{10,... | collective-permute-start | bytes 1966088 | tf_op jit(solution)/shard_map/ppermute | solution.py:66
  120.2 15.9 %collective-permute-start.29 = (bf16[128,3072]{1,0:T(8,128)(2,1)S(1)}, bf16[128,3072]{1,0:T(8,128)(2,1)S(1)}, u32[]{:S(2)}, u32[]{:S(2)}) collective-permute-start(bf16[128,3072]{1,0:T(8,128)(2,1)S(1)} %slice.629), channel_id=1, source_target_pairs={{0,1},{1,0},{2,3},{3,2},{4,5},{5,4},{6,7},{7,6},{8,9},{9,8},{10,11... | collective-permute-start | bytes 2359304 | tf_op jit(solution)/shard_map/ppermute | solution.py:66
  120.3 16.1 %collective-permute-start.27 = (bf16[256,1536]{1,0:T(8,128)(2,1)S(1)}, bf16[256,1536]{1,0:T(8,128)(2,1)S(1)}, u32[]{:S(2)}, u32[]{:S(2)}) collective-permute-start(bf16[256,1536]{1,0:T(8,128)(2,1)S(1)} %collective-permute-done.22.refs_2_.refs_1_), channel_id=1, source_target_pairs={{0,1},{1,0},{2,3},{3,2},{4,5},{5,4},{6,7},{7,6},{8,9},{9,8},{10,11... | collective-permute-start | bytes 2359304 | tf_op jit(solution)/shard_map/ppermute | solution.py:66
  136.9 25.0 %collective-permute-start.35 = (bf16[32,4096]{1,0:T(8,128)(2,1)S(1)}, bf16[32,4096]{1,0:T(8,128)(2,1)S(1)}, u32[]{:S(2)}, u32[]{:S(2)}) collective-permute-start(bf16[32,4096]{1,0:T(8,128)(2,1)S(1)} %copy-done.139), channel_id=1, source_target_pairs={{0,16},{1,17},{2,18},{3,19},{4,20},{5,21},{6,22},{7,23},{8,24},{9,... | collective-permute-start | bytes 786440 | tf_op jit(solution)/shard_map/ppermute | solution.py:66
  138.6 24.1 %collective-permute-start.34 = (bf16[64,3072]{1,0:T(8,128)(2,1)}, bf16[64,3072]{1,0:T(8,128)(2,1)}, u32[]{:S(2)}, u32[]{:S(2)}) collective-permute-start(bf16[64,3072]{1,0:T(8,128)(2,1)} %slice.641), channel_id=1, source_target_pairs={{0,4},{1,5},{2,6},{3,7},{4,0},{5,1},{6,2},{7,3},{8,12},{9,13},{10,... | collective-permute-start | bytes 1179656 | tf_op jit(solution)/shard_map/ppermute | solution.py:66
  140.9 22.9 %collective-permute-start.33 = (bf16[64,3072]{1,0:T(8,128)(2,1)}, bf16[64,3072]{1,0:T(8,128)(2,1)}, u32[]{:S(2)}, u32[]{:S(2)}) collective-permute-start(bf16[64,3072]{1,0:T(8,128)(2,1)} %slice.639), channel_id=1, source_target_pairs={{0,2},{1,3},{2,0},{3,1},{4,6},{5,7},{6,4},{7,5},{8,10},{9,11},{10,... | collective-permute-start | bytes 1179656 | tf_op jit(solution)/shard_map/ppermute | solution.py:66
  165.4 20.9 %collective-permute-start.36 = (bf16[256,512]{1,0:T(8,128)(2,1)S(1)}, bf16[256,512]{1,0:T(8,128)(2,1)S(1)}, u32[]{:S(2)}, u32[]{:S(2)}) collective-permute-start(bf16[256,512]{1,0:T(8,128)(2,1)S(1)} %slice.642.refs_1_.refs_0_), channel_id=1, source_target_pairs={{0,2},{1,3},{2,0},{3,1},{4,6},{5,7},{6,4},{7,5},{8,10},{9,11},{10,... | collective-permute-start | bytes 786440 | tf_op jit(solution)/shard_map/ppermute | solution.py:66
  166.6 19.6 %collective-permute-start.38 = (bf16[256,512]{1,0:T(8,128)(2,1)S(1)}, bf16[256,512]{1,0:T(8,128)(2,1)S(1)}, u32[]{:S(2)}, u32[]{:S(2)}) collective-permute-start(bf16[256,512]{1,0:T(8,128)(2,1)S(1)} %slice.642.refs_1_.refs_0_), channel_id=1, source_target_pairs={{0,1},{1,0},{2,3},{3,2},{4,5},{5,4},{6,7},{7,6},{8,9},{9,8},{10,11... | collective-permute-start | bytes 786440 | tf_op jit(solution)/shard_map/ppermute | solution.py:66
  166.6 19.6 %collective-permute-start.37 = (bf16[256,512]{1,0:T(8,128)(2,1)S(1)}, bf16[256,512]{1,0:T(8,128)(2,1)S(1)}, u32[]{:S(2)}, u32[]{:S(2)}) collective-permute-start(bf16[256,512]{1,0:T(8,128)(2,1)S(1)} %slice.643.refs_5_.refs_4_), channel_id=1, source_target_pairs={{0,4},{1,5},{2,6},{3,7},{4,0},{5,1},{6,2},{7,3},{8,12},{9,13},{10,... | collective-permute-start | bytes 786440 | tf_op jit(solution)/shard_map/ppermute | solution.py:66
  167.2 19.1 %collective-permute-start.39 = (bf16[256,512]{1,0:T(8,128)(2,1)S(1)}, bf16[256,512]{1,0:T(8,128)(2,1)S(1)}, u32[]{:S(2)}, u32[]{:S(2)}) collective-permute-start(bf16[256,512]{1,0:T(8,128)(2,1)S(1)} %slice.643.refs_5_.refs_4_), channel_id=1, source_target_pairs={{0,1},{1,0},{2,3},{3,2},{4,5},{5,4},{6,7},{7,6},{8,9},{9,8},{10,11... | collective-permute-start | bytes 786440 | tf_op jit(solution)/shard_map/ppermute | solution.py:66
  194.0 32.9 %collective-permute-start.46 = (bf16[256,2048]{1,0:T(8,128)(2,1)S(1)}, bf16[256,2048]{1,0:T(8,128)(2,1)S(1)}, u32[]{:S(2)}, u32[]{:S(2)}) collective-permute-start(bf16[256,2048]{1,0:T(8,128)(2,1)S(1)} %slice.644.refs_1_.refs_0_), channel_id=1, source_target_pairs={{0,2},{1,3},{2,0},{3,1},{4,6},{5,7},{6,4},{7,5},{8,10},{9,11},{10,... | collective-permute-start | bytes 3145736 | tf_op jit(solution)/shard_map/ppermute | solution.py:66
  195.7 31.3 %collective-permute-start.48 = (bf16[256,2048]{1,0:T(8,128)(2,1)S(1)}, bf16[256,2048]{1,0:T(8,128)(2,1)S(1)}, u32[]{:S(2)}, u32[]{:S(2)}) collective-permute-start(bf16[256,2048]{1,0:T(8,128)(2,1)S(1)} %slice.644.refs_1_.refs_0_), channel_id=1, source_target_pairs={{0,1},{1,0},{2,3},{3,2},{4,5},{5,4},{6,7},{7,6},{8,9},{9,8},{10,11... | collective-permute-start | bytes 3145736 | tf_op jit(solution)/shard_map/ppermute | solution.py:66
  195.8 31.2 %collective-permute-start.47 = (bf16[256,2048]{1,0:T(8,128)(2,1)S(1)}, bf16[256,2048]{1,0:T(8,128)(2,1)}, u32[]{:S(2)}, u32[]{:S(2)}) collective-permute-start(bf16[256,2048]{1,0:T(8,128)(2,1)S(1)} %slice.645.refs_5_.refs_4_), channel_id=1, source_target_pairs={{0,4},{1,5},{2,6},{3,7},{4,0},{5,1},{6,2},{7,3},{8,12},{9,13},{10,... | collective-permute-start | bytes 3145736 | tf_op jit(solution)/shard_map/ppermute | solution.py:66
  196.6 30.4 %collective-permute-start.49 = (bf16[256,2048]{1,0:T(8,128)(2,1)S(1)}, bf16[256,2048]{1,0:T(8,128)(2,1)}, u32[]{:S(2)}, u32[]{:S(2)}) collective-permute-start(bf16[256,2048]{1,0:T(8,128)(2,1)S(1)} %slice.645.refs_5_.refs_4_), channel_id=1, source_target_pairs={{0,1},{1,0},{2,3},{3,2},{4,5},{5,4},{6,7},{7,6},{8,9},{9,8},{10,11... | collective-permute-start | bytes 3145736 | tf_op jit(solution)/shard_map/ppermute | solution.py:66
  254.2 49.4 %collective-permute-start.56 = (bf16[256,2048]{1,0:T(8,128)(2,1)S(1)}, bf16[256,2048]{1,0:T(8,128)(2,1)S(1)}, u32[]{:S(2)}, u32[]{:S(2)}) collective-permute-start(bf16[256,2048]{1,0:T(8,128)(2,1)S(1)} %pad_maximum_fusion.9.refs_1_), channel_id=1, source_target_pairs={{0,2},{1,3},{2,0},{3,1},{4,6},{5,7},{6,4},{7,5},{8,10},{9,11},{10,... | collective-permute-start | bytes 3145736 | tf_op jit(solution)/shard_map/ppermute | solution.py:66
  255.9 47.7 %collective-permute-start.57 = (bf16[256,2048]{1,0:T(8,128)(2,1)S(1)}, bf16[256,2048]{1,0:T(8,128)(2,1)S(1)}, u32[]{:S(2)}, u32[]{:S(2)}) collective-permute-start(bf16[256,2048]{1,0:T(8,128)(2,1)S(1)} %pad_maximum_fusion.10.refs_5_), channel_id=1, source_target_pairs={{0,4},{1,5},{2,6},{3,7},{4,0},{5,1},{6,2},{7,3},{8,12},{9,13},{10,... | collective-permute-start | bytes 3145736 | tf_op jit(solution)/shard_map/ppermute | solution.py:66
  256.7 47.0 %collective-permute-start.58 = (bf16[256,2048]{1,0:T(8,128)(2,1)S(1)}, bf16[256,2048]{1,0:T(8,128)(2,1)S(1)}, u32[]{:S(2)}, u32[]{:S(2)}) collective-permute-start(bf16[256,2048]{1,0:T(8,128)(2,1)S(1)} %pad_maximum_fusion.9.refs_1_), channel_id=1, source_target_pairs={{0,1},{1,0},{2,3},{3,2},{4,5},{5,4},{6,7},{7,6},{8,9},{9,8},{10,11... | collective-permute-start | bytes 3145736 | tf_op jit(solution)/shard_map/ppermute | solution.py:66
  256.7 47.0 %collective-permute-start.59 = (bf16[256,2048]{1,0:T(8,128)(2,1)S(1)}, bf16[256,2048]{1,0:T(8,128)(2,1)S(1)}, u32[]{:S(2)}, u32[]{:S(2)}) collective-permute-start(bf16[256,2048]{1,0:T(8,128)(2,1)S(1)} %pad_maximum_fusion.10.refs_5_), channel_id=1, source_target_pairs={{0,1},{1,0},{2,3},{3,2},{4,5},{5,4},{6,7},{7,6},{8,9},{9,8},{10,11... | collective-permute-start | bytes 3145736 | tf_op jit(solution)/shard_map/ppermute | solution.py:66
  257.2 21.4 %collective-permute-start.61 = (f32[1,2,384]{2,1,0:T(2,128)S(1)}, f32[1,2,384]{2,1,0:T(2,128)S(1)}, u32[]{:S(2)}, u32[]{:S(2)}) collective-permute-start(f32[1,2,384]{2,1,0:T(2,128)S(1)} %maximum_bitcast_fusion), channel_id=1, source_target_pairs={{0,2},{1,3},{2,0},{3,1},{4,6},{5,7},{6,4},{7,5},{8,10},{9,11},{10,... | collective-permute-start | bytes 9224 | tf_op jit(solution)/shard_map/ppermute | solution.py:66
  278.5 23.9 %collective-permute-start.60 = (bf16[256,1024]{1,0:T(8,128)(2,1)S(1)}, bf16[256,1024]{1,0:T(8,128)(2,1)S(1)}, u32[]{:S(2)}, u32[]{:S(2)}) collective-permute-start(bf16[256,1024]{1,0:T(8,128)(2,1)S(1)} %pad_maximum_fusion.23), channel_id=1, source_target_pairs={{0,16},{1,17},{2,18},{3,19},{4,20},{5,21},{6,22},{7,23},{8,24},{9,... | collective-permute-start | bytes 1572872 | tf_op jit(solution)/shard_map/ppermute | solution.py:66
  304.3 28.2 %collective-permute-start.65 = (bf16[512,1024]{1,0:T(8,128)(2,1)S(1)}, bf16[512,1024]{1,0:T(8,128)(2,1)S(1)}, u32[]{:S(2)}, u32[]{:S(2)}) collective-permute-start(bf16[512,1024]{1,0:T(8,128)(2,1)S(1)} %pad_maximum_fusion.11), channel_id=1, source_target_pairs={{0,8},{1,9},{2,10},{3,11},{4,12},{5,13},{6,14},{7,15},{8,0},{9,1},... | collective-permute-start | bytes 3145736 | tf_op jit(solution)/shard_map/ppermute | solution.py:66
  334.6 20.1 %collective-permute-start.67 = (bf16[384,1024]{1,0:T(8,128)(2,1)}, bf16[384,1024]{1,0:T(8,128)(2,1)S(1)}, u32[]{:S(2)}, u32[]{:S(2)}) collective-permute-start(bf16[384,1024]{1,0:T(8,128)(2,1)} %get-tuple-element.323), channel_id=1, source_target_pairs={{0,2},{1,3},{2,0},{3,1},{4,6},{5,7},{6,4},{7,5},{8,10},{9,11},{10,... | collective-permute-start | bytes 2359304 | tf_op jit(solution)/shard_map/ppermute | solution.py:66
  382.2 19.6 %collective-permute-start.73 = (bf16[384,1024]{1,0:T(8,128)(2,1)S(1)}, bf16[384,1024]{1,0:T(8,128)(2,1)S(1)}, u32[]{:S(2)}, u32[]{:S(2)}) collective-permute-start(bf16[384,1024]{1,0:T(8,128)(2,1)S(1)} %add_convert_fusion), channel_id=1, source_target_pairs={{0,2},{1,3},{2,0},{3,1},{4,6},{5,7},{6,4},{7,5},{8,10},{9,11},{10,... | collective-permute-start | bytes 2359304 | tf_op jit(solution)/shard_map/ppermute | solution.py:66
  420.8 26.0 %collective-permute-start.74 = (bf16[512,2048]{1,0:T(8,128)(2,1)S(1)}, bf16[512,2048]{1,0:T(8,128)(2,1)S(1)}, u32[]{:S(2)}, u32[]{:S(2)}) collective-permute-start(bf16[512,2048]{1,0:T(8,128)(2,1)S(1)} %shard_map.466), channel_id=1, source_target_pairs={{0,1},{1,0},{2,3},{3,2},{4,5},{5,4},{6,7},{7,6},{8,9},{9,8},{10,11... | collective-permute-start | bytes 6291464 | tf_op jit(solution)/shard_map/ppermute | solution.py:66
  420.9 26.0 %collective-permute-start.75 = (bf16[512,2048]{1,0:T(8,128)(2,1)S(1)}, bf16[512,2048]{1,0:T(8,128)(2,1)S(1)}, u32[]{:S(2)}, u32[]{:S(2)}) collective-permute-start(bf16[512,2048]{1,0:T(8,128)(2,1)S(1)} %shard_map.467), channel_id=1, source_target_pairs={{0,1},{1,0},{2,3},{3,2},{4,5},{5,4},{6,7},{7,6},{8,9},{9,8},{10,11... | collective-permute-start | bytes 6291464 | tf_op jit(solution)/shard_map/ppermute | solution.py:66
  421.4 25.5 %collective-permute-start.76 = (bf16[512,1024]{1,0:T(8,128)(2,1)}, bf16[512,1024]{1,0:T(8,128)(2,1)}, u32[]{:S(2)}, u32[]{:S(2)}) collective-permute-start(bf16[512,1024]{1,0:T(8,128)(2,1)} %fusion.34), channel_id=1, source_target_pairs={{0,8},{1,9},{2,10},{3,11},{4,12},{5,13},{6,14},{7,15},{8,0},{9,1},... | collective-permute-start | bytes 3145736 | tf_op jit(solution)/shard_map/ppermute | solution.py:66
  464.7 33.9 %collective-permute-start.80 = (bf16[512,2048]{1,0:T(8,128)(2,1)}, bf16[512,2048]{1,0:T(8,128)(2,1)}, u32[]{:S(2)}, u32[]{:S(2)}) collective-permute-start(bf16[512,2048]{1,0:T(8,128)(2,1)} %shard_map.475), channel_id=1, source_target_pairs={{0,1},{1,0},{2,3},{3,2},{4,5},{5,4},{6,7},{7,6},{8,9},{9,8},{10,11... | collective-permute-start | bytes 6291464 | tf_op jit(solution)/shard_map/ppermute | solution.py:66
  464.7 33.9 %collective-permute-start.79 = (bf16[512,2048]{1,0:T(8,128)(2,1)}, bf16[512,2048]{1,0:T(8,128)(2,1)S(1)}, u32[]{:S(2)}, u32[]{:S(2)}) collective-permute-start(bf16[512,2048]{1,0:T(8,128)(2,1)} %shard_map.474), channel_id=1, source_target_pairs={{0,1},{1,0},{2,3},{3,2},{4,5},{5,4},{6,7},{7,6},{8,9},{9,8},{10,11... | collective-permute-start | bytes 6291464 | tf_op jit(solution)/shard_map/ppermute | solution.py:66
  465.2 33.3 %collective-permute-start.77 = (bf16[256,2048]{1,0:T(8,128)(2,1)}, bf16[256,2048]{1,0:T(8,128)(2,1)}, u32[]{:S(2)}, u32[]{:S(2)}) collective-permute-start(bf16[256,2048]{1,0:T(8,128)(2,1)} %shard_map.469), channel_id=1, source_target_pairs={{0,2},{1,3},{2,0},{3,1},{4,6},{5,7},{6,4},{7,5},{8,10},{9,11},{10,... | collective-permute-start | bytes 3145736 | tf_op jit(solution)/shard_map/ppermute | solution.py:66
  466.1 32.5 %collective-permute-start.78 = (bf16[256,2048]{1,0:T(8,128)(2,1)}, bf16[256,2048]{1,0:T(8,128)(2,1)}, u32[]{:S(2)}, u32[]{:S(2)}) collective-permute-start(bf16[256,2048]{1,0:T(8,128)(2,1)} %shard_map.470), channel_id=1, source_target_pairs={{0,4},{1,5},{2,6},{3,7},{4,0},{5,1},{6,2},{7,3},{8,12},{9,13},{10,... | collective-permute-start | bytes 3145736 | tf_op jit(solution)/shard_map/ppermute | solution.py:66
  472.9 25.7 %collective-permute-start.81 = (bf16[256,1024]{1,0:T(8,128)(2,1)}, bf16[256,1024]{1,0:T(8,128)(2,1)S(1)}, u32[]{:S(2)}, u32[]{:S(2)}) collective-permute-start(bf16[256,1024]{1,0:T(8,128)(2,1)} %get-tuple-element.347), channel_id=1, source_target_pairs={{0,16},{1,17},{2,18},{3,19},{4,20},{5,21},{6,22},{7,23},{8,24},{9,... | collective-permute-start | bytes 1572872 | tf_op jit(solution)/shard_map/ppermute | solution.py:66
  505.6 22.0 %collective-permute-start.84 = (bf16[128,1024]{1,0:T(8,128)(2,1)S(1)}, bf16[128,1024]{1,0:T(8,128)(2,1)}, u32[]{:S(2)}, u32[]{:S(2)}) collective-permute-start(bf16[128,1024]{1,0:T(8,128)(2,1)S(1)} %slice.844), channel_id=1, source_target_pairs={{0,4},{1,5},{2,6},{3,7},{4,0},{5,1},{6,2},{7,3},{8,12},{9,13},{10,... | collective-permute-start | bytes 786440 | tf_op jit(solution)/shard_map/ppermute | solution.py:66
  509.3 19.4 %collective-permute-start.83 = (bf16[128,2048]{1,0:T(8,128)(2,1)S(1)}, bf16[128,2048]{1,0:T(8,128)(2,1)S(1)}, u32[]{:S(2)}, u32[]{:S(2)}) collective-permute-start(bf16[128,2048]{1,0:T(8,128)(2,1)S(1)} %get-tuple-element.566), channel_id=1, source_target_pairs={{0,2},{1,3},{2,0},{3,1},{4,6},{5,7},{6,4},{7,5},{8,10},{9,11},{10,... | collective-permute-start | bytes 1572872 | tf_op jit(solution)/shard_map/ppermute | solution.py:66
  513.0 15.7 %collective-permute-start.82 = (bf16[128,2048]{1,0:T(8,128)(2,1)}, bf16[128,2048]{1,0:T(8,128)(2,1)S(1)}, u32[]{:S(2)}, u32[]{:S(2)}) collective-permute-start(bf16[128,2048]{1,0:T(8,128)(2,1)} %get-tuple-element.568), channel_id=1, source_target_pairs={{0,4},{1,5},{2,6},{3,7},{4,0},{5,1},{6,2},{7,3},{8,12},{9,13},{10,... | collective-permute-start | bytes 1572872 | tf_op jit(solution)/shard_map/ppermute | solution.py:66
  532.0 32.9 %collective-permute-start.89 = (bf16[64,4096]{1,0:T(8,128)(2,1)}, bf16[64,4096]{1,0:T(8,128)(2,1)}, u32[]{:S(2)}, u32[]{:S(2)}) collective-permute-start(bf16[64,4096]{1,0:T(8,128)(2,1)} %pad_maximum_fusion.24), channel_id=1, source_target_pairs={{0,8},{1,9},{2,10},{3,11},{4,12},{5,13},{6,14},{7,15},{8,0},{9,1},... | collective-permute-start | bytes 1572872 | tf_op jit(solution)/shard_map/ppermute | solution.py:66
  532.9 32.1 %collective-permute-start.87 = (bf16[256,2048]{1,0:T(8,128)(2,1)S(1)}, bf16[256,2048]{1,0:T(8,128)(2,1)}, u32[]{:S(2)}, u32[]{:S(2)}) collective-permute-start(bf16[256,2048]{1,0:T(8,128)(2,1)S(1)} %shard_map.477), channel_id=1, source_target_pairs={{0,2},{1,3},{2,0},{3,1},{4,6},{5,7},{6,4},{7,5},{8,10},{9,11},{10,... | collective-permute-start | bytes 3145736 | tf_op jit(solution)/shard_map/ppermute | solution.py:66
  539.7 25.2 %collective-permute-start.88 = (bf16[256,2048]{1,0:T(8,128)(2,1)S(1)}, bf16[256,2048]{1,0:T(8,128)(2,1)S(1)}, u32[]{:S(2)}, u32[]{:S(2)}) collective-permute-start(bf16[256,2048]{1,0:T(8,128)(2,1)S(1)} %shard_map.478), channel_id=1, source_target_pairs={{0,4},{1,5},{2,6},{3,7},{4,0},{5,1},{6,2},{7,3},{8,12},{9,13},{10,... | collective-permute-start | bytes 3145736 | tf_op jit(solution)/shard_map/ppermute | solution.py:66
  566.2 23.9 %collective-permute-start.92 = (bf16[128,2048]{1,0:T(8,128)(2,1)}, bf16[128,2048]{1,0:T(8,128)(2,1)S(1)}, u32[]{:S(2)}, u32[]{:S(2)}) collective-permute-start(bf16[128,2048]{1,0:T(8,128)(2,1)} %get-tuple-element.562), channel_id=1, source_target_pairs={{0,2},{1,3},{2,0},{3,1},{4,6},{5,7},{6,4},{7,5},{8,10},{9,11},{10,... | collective-permute-start | bytes 1572872 | tf_op jit(solution)/shard_map/ppermute | solution.py:66
  569.5 20.6 %collective-permute-start.91 = (bf16[128,2048]{1,0:T(8,128)(2,1)}, bf16[128,2048]{1,0:T(8,128)(2,1)}, u32[]{:S(2)}, u32[]{:S(2)}) collective-permute-start(bf16[128,2048]{1,0:T(8,128)(2,1)} %get-tuple-element.564), channel_id=1, source_target_pairs={{0,4},{1,5},{2,6},{3,7},{4,0},{5,1},{6,2},{7,3},{8,12},{9,13},{10,... | collective-permute-start | bytes 1572872 | tf_op jit(solution)/shard_map/ppermute | solution.py:66
  571.2 18.8 %collective-permute-start.93 = (bf16[32,4096]{1,0:T(8,128)(2,1)S(1)}, bf16[32,4096]{1,0:T(8,128)(2,1)S(1)}, u32[]{:S(2)}, u32[]{:S(2)}) collective-permute-start(bf16[32,4096]{1,0:T(8,128)(2,1)S(1)} %add_convert_fusion.35), channel_id=1, source_target_pairs={{0,16},{1,17},{2,18},{3,19},{4,20},{5,21},{6,22},{7,23},{8,24},{9,... | collective-permute-start | bytes 786440 | tf_op jit(solution)/shard_map/ppermute | solution.py:66
  572.9 17.1 %collective-permute-start.94 = (bf16[256,512]{1,0:T(8,128)(2,1)S(1)}, bf16[256,512]{1,0:T(8,128)(2,1)S(1)}, u32[]{:S(2)}, u32[]{:S(2)}) collective-permute-start(bf16[256,512]{1,0:T(8,128)(2,1)S(1)} %shard_map.485), channel_id=1, source_target_pairs={{0,2},{1,3},{2,0},{3,1},{4,6},{5,7},{6,4},{7,5},{8,10},{9,11},{10,... | collective-permute-start | bytes 786440 | tf_op jit(solution)/shard_map/ppermute | solution.py:66
  573.9 16.2 %collective-permute-start.95 = (bf16[256,512]{1,0:T(8,128)(2,1)S(1)}, bf16[256,512]{1,0:T(8,128)(2,1)S(1)}, u32[]{:S(2)}, u32[]{:S(2)}) collective-permute-start(bf16[256,512]{1,0:T(8,128)(2,1)S(1)} %shard_map.486), channel_id=1, source_target_pairs={{0,4},{1,5},{2,6},{3,7},{4,0},{5,1},{6,2},{7,3},{8,12},{9,13},{10,... | collective-permute-start | bytes 786440 | tf_op jit(solution)/shard_map/ppermute | solution.py:66
  590.9 25.1 %collective-permute-start.106 = (bf16[16,6144]{1,0:T(8,128)(2,1)}, bf16[16,6144]{1,0:T(8,128)(2,1)}, u32[]{:S(2)}, u32[]{:S(2)}) collective-permute-start(bf16[16,6144]{1,0:T(8,128)(2,1)} %pad_maximum_fusion.41), channel_id=1, source_target_pairs={{0,8},{1,9},{2,10},{3,11},{4,12},{5,13},{6,14},{7,15},{8,0},{9,1},... | collective-permute-start | bytes 589832 | tf_op jit(solution)/shard_map/ppermute | solution.py:66
  595.2 41.6 %collective-permute-start.105 = (bf16[64,4096]{1,0:T(8,128)(2,1)}, bf16[64,4096]{1,0:T(8,128)(2,1)}, u32[]{:S(2)}, u32[]{:S(2)}) collective-permute-start(bf16[64,4096]{1,0:T(8,128)(2,1)} %pad_maximum_fusion.26), channel_id=1, source_target_pairs={{0,8},{1,9},{2,10},{3,11},{4,12},{5,13},{6,14},{7,15},{8,0},{9,1},... | collective-permute-start | bytes 1572872 | tf_op jit(solution)/shard_map/ppermute | solution.py:66
  613.3 23.4 %collective-permute-start.98 = (bf16[256,1536]{1,0:T(8,128)(2,1)S(1)}, bf16[256,1536]{1,0:T(8,128)(2,1)S(1)}, u32[]{:S(2)}, u32[]{:S(2)}) collective-permute-start(bf16[256,1536]{1,0:T(8,128)(2,1)S(1)} %shard_map.491), channel_id=1, source_target_pairs={{0,2},{1,3},{2,0},{3,1},{4,6},{5,7},{6,4},{7,5},{8,10},{9,11},{10,... | collective-permute-start | bytes 2359304 | tf_op jit(solution)/shard_map/ppermute | solution.py:66
  615.2 21.6 %collective-permute-start.99 = (bf16[256,1536]{1,0:T(8,128)(2,1)S(1)}, bf16[256,1536]{1,0:T(8,128)(2,1)S(1)}, u32[]{:S(2)}, u32[]{:S(2)}) collective-permute-start(bf16[256,1536]{1,0:T(8,128)(2,1)S(1)} %shard_map.492), channel_id=1, source_target_pairs={{0,4},{1,5},{2,6},{3,7},{4,0},{5,1},{6,2},{7,3},{8,12},{9,13},{10,... | collective-permute-start | bytes 2359304 | tf_op jit(solution)/shard_map/ppermute | solution.py:66
  656.0 20.6 %collective-permute-start.114 = (bf16[64,5120]{1,0:T(8,128)(2,1)S(1)}, bf16[64,5120]{1,0:T(8,128)(2,1)S(1)}, u32[]{:S(2)}, u32[]{:S(2)}) collective-permute-start(bf16[64,5120]{1,0:T(8,128)(2,1)S(1)} %pad_maximum_fusion.20), channel_id=1, source_target_pairs={{0,2},{1,3},{2,0},{3,1},{4,6},{5,7},{6,4},{7,5},{8,10},{9,11},{10,... | collective-permute-start | bytes 1966088 | tf_op jit(solution)/shard_map/ppermute | solution.py:66
  656.9 18.3 %collective-permute-start.113 = (bf16[32,3072]{1,0:T(8,128)(2,1)S(1)}, bf16[32,3072]{1,0:T(8,128)(2,1)S(1)}, u32[]{:S(2)}, u32[]{:S(2)}) collective-permute-start(bf16[32,3072]{1,0:T(8,128)(2,1)S(1)} %slice.755), channel_id=1, source_target_pairs={{0,2},{1,3},{2,0},{3,1},{4,6},{5,7},{6,4},{7,5},{8,10},{9,11},{10,... | collective-permute-start | bytes 589832 | tf_op jit(solution)/shard_map/ppermute | solution.py:66
  658.5 19.3 %collective-permute-start.112 = (bf16[64,4096]{1,0:T(8,128)(2,1)S(1)}, bf16[64,4096]{1,0:T(8,128)(2,1)S(1)}, u32[]{:S(2)}, u32[]{:S(2)}) collective-permute-start(bf16[64,4096]{1,0:T(8,128)(2,1)S(1)} %pad_maximum_fusion.28), channel_id=1, source_target_pairs={{0,8},{1,9},{2,10},{3,11},{4,12},{5,13},{6,14},{7,15},{8,0},{9,1},... | collective-permute-start | bytes 1572872 | tf_op jit(solution)/shard_map/ppermute | solution.py:66
  679.2 30.2 %collective-permute-start.119 = (bf16[128,5120]{1,0:T(8,128)(2,1)}, bf16[128,5120]{1,0:T(8,128)(2,1)}, u32[]{:S(2)}, u32[]{:S(2)}) collective-permute-start(bf16[128,5120]{1,0:T(8,128)(2,1)} %pad_maximum_fusion.6), channel_id=1, source_target_pairs={{0,1},{1,0},{2,3},{3,2},{4,5},{5,4},{6,7},{7,6},{8,9},{9,8},{10,11... | collective-permute-start | bytes 3932168 | tf_op jit(solution)/shard_map/ppermute | solution.py:66
  681.2 16.0 %collective-permute-start.120 = (bf16[64,3072]{1,0:T(8,128)(2,1)S(1)}, bf16[64,3072]{1,0:T(8,128)(2,1)S(1)}, u32[]{:S(2)}, u32[]{:S(2)}) collective-permute-start(bf16[64,3072]{1,0:T(8,128)(2,1)S(1)} %pad_maximum_fusion.35), channel_id=1, source_target_pairs={{0,4},{1,5},{2,6},{3,7},{4,0},{5,1},{6,2},{7,3},{8,12},{9,13},{10,... | collective-permute-start | bytes 1179656 | tf_op jit(solution)/shard_map/ppermute | solution.py:66
  (264 other events, 3306.1 us)

commit v3 on v2

--- a/solution.py
+++ b/solution.py
@@ -27,7 +27,7 @@
 NEG_FILL = -1e30
 BF16 = jnp.bfloat16
 F32 = jnp.float32
-SPAN = 512
+SPANS = (1024, 512)
 TOKENS = 128
 PAIR = 2 * HEAD_DIM
 
@@ -44,12 +44,12 @@
     return lax.dot_general(left, right, (((1,), (1,)), ((), ())), preferred_element_type=F32)
 
 
-def precise(left, right):
-    return jnp.dot(left, right, precision=lax.Precision.HIGHEST, preferred_element_type=F32)
-
-
 def precise_tn(left, right):
     return lax.dot_general(left, right, (((0,), (0,)), ((), ())), precision=lax.Precision.HIGHEST)
+
+
+def pick(hot, values):
+    return in_halves(lambda part: matmul(hot, part), values)
 
 
 def in_halves(times, values):
@@ -74,6 +74,22 @@
     return jnp.concatenate([value, swapped(value, mask, devices)], axis=0)
 
 
+def spread(value, masks, devices):
+    if len(masks) == 2:
+        masks = masks + [masks[0] ^ masks[1]]
+    return [value] + [swapped(value, mask, devices) for mask in masks]
+
+
+def stack(parts):
+    return jnp.concatenate(parts, axis=0)
+
+
+def widen(value, masks, devices):
+    for mask in masks[:-1]:
+        value = grow(value, mask, devices)
+    return [value, swapped(value, masks[-1], devices)]
+
+
 def added(mine, theirs, out=BF16):
     return (mine.astype(F32) + theirs.astype(F32)).astype(out)
 
@@ -81,6 +97,13 @@
 def keep_half(value, mask, devices, out=BF16):
     half = value.shape[0] // 2
     return added(value[:half], swapped(value[half:].astype(BF16), mask, devices), out)
+
+
+def lend(value, masks, devices):
+    for mask in reversed(masks[1:]):
+        value = keep_half(value, mask, devices)
+    half = value.shape[0] // 2
+    return [value[:half], swapped(value[half:].astype(BF16), masks[0], devices)]
 
 
 def keep_all(value, masks, devices):
@@ -124,8 +147,7 @@
     )
 
 
-def run(body, grid, given, specs, outs, out_specs, scratch=(), work=0):
-    moved = sum(value.size * value.dtype.itemsize for value in given)
+def run(body, grid, given, specs, outs, out_specs, scratch=()):
     return pl.pallas_call(
         body,
         grid=grid,
@@ -134,7 +156,7 @@
         out_specs=out_specs,
         scratch_shapes=scratch,
         compiler_params=pltpu.CompilerParams(vmem_limit_bytes=48 << 20),
-        cost_estimate=pl.CostEstimate(flops=work, bytes_accessed=moved, transcendentals=0),
+        cost_estimate=pl.CostEstimate(flops=1000, bytes_accessed=1000, transcendentals=0),
     )(*given)
 
 
@@ -142,17 +164,24 @@
     return pl.BlockSpec(value.shape, lambda j: (0,) * value.ndim)
 
 
-def two_sets(sets):
-    first = sets[0][0].shape[1] // SPAN
+def span_of(*sizes):
+    return [span for span in SPANS if all(size % span == 0 for size in sizes)][0]
+
+
+def columns_of(sets):
+    return [blocks[0].shape[1] if used is None else used for blocks, used in sets]
+
+
+def two_sets(sets, first, span):
     specs = [
-        pl.BlockSpec((block.shape[0], SPAN), lambda j: (0, jnp.minimum(j, first - 1)))
-        for block in sets[0]
+        pl.BlockSpec((block.shape[0], span), lambda j: (0, jnp.minimum(j, first - 1)))
+        for block in sets[0][0]
     ]
     specs += [
-        pl.BlockSpec((block.shape[0], SPAN), lambda j: (0, jnp.maximum(j - first, 0)))
-        for block in sets[1]
+        pl.BlockSpec((block.shape[0], span), lambda j: (0, jnp.maximum(j - first, 0)))
+        for block in sets[1][0]
     ]
-    return first, specs
+    return specs
 
 
 def gelu_parts(value):
@@ -173,12 +202,14 @@
 
 def times_sets(left, sets, bias=None, hidden=None, bend=False):
     tokens = left[0].shape[0]
-    first, specs = two_sets(sets)
-    steps = first + sets[1][0].shape[1] // SPAN
-    count = len(sets[0])
+    columns = columns_of(sets)
+    span = span_of(*columns)
+    first, steps = columns[0] // span, sum(columns) // span
+    specs = two_sets(sets, first, span)
+    count = len(sets[0][0])
     extra = [value for value in (bias, hidden) if value is not None]
     column = lambda j: (0, j)
-    extra_specs = [pl.BlockSpec((value.shape[0], SPAN), column) for value in extra]
+    extra_specs = [pl.BlockSpec((value.shape[0], span), column) for value in extra]
 
     def body(one_ref, two_ref, *refs):
         extras, blocks = refs[: len(extra)], refs[len(extra) : len(extra) + 2 * count]
@@ -206,32 +237,33 @@
         pl.when(pl.program_id(0) < first)(lambda: part(one_ref, blocks[:count]))
         pl.when(pl.program_id(0) >= first)(lambda: part(two_ref, blocks[count:]))
 
-    wide = steps * SPAN
+    wide = steps * span
     shape = jax.ShapeDtypeStruct
-    outs, out_specs = [shape((tokens, wide), F32)], [pl.BlockSpec((tokens, SPAN), column)]
+    outs, out_specs = [shape((tokens, wide), F32)], [pl.BlockSpec((tokens, span), column)]
     if hidden is not None:
         outs = [shape((tokens, wide), BF16), shape((1, wide), F32)]
-        out_specs.append(pl.BlockSpec((1, SPAN), column))
+        out_specs.append(pl.BlockSpec((1, span), column))
     elif bend:
         outs.append(shape((tokens, wide), BF16))
-        out_specs.append(pl.BlockSpec((tokens, SPAN), column))
-    given = list(left) + extra + list(sets[0]) + list(sets[1])
+        out_specs.append(pl.BlockSpec((tokens, span), column))
+    given = list(left) + extra + list(sets[0][0]) + list(sets[1][0])
     specs = [whole(value) for value in left] + extra_specs + specs
-    work = 2 * tokens * left[0].shape[1] * wide
-    found = run(body, (steps,), given, specs, outs, out_specs, work=work)
+    found = run(body, (steps,), given, specs, outs, out_specs)
     return found if len(outs) > 1 else found[0]
 
 
-def span_spec(value):
-    each = value.shape[2] // SPAN
-    return pl.BlockSpec((1, value.shape[1], SPAN), lambda j: (j // each, 0, j % each))
+def span_spec(value, span):
+    each = value.shape[2] // span
+    return pl.BlockSpec((1, value.shape[1], span), lambda j: (j // each, 0, j % each))
 
 
 def back_sets(right, sets, perms, bias=None, exact=False, out=F32):
     tokens = right.shape[1]
-    first, specs = two_sets(sets)
-    steps = first + sets[1][0].shape[1] // SPAN
-    count = len(sets[0])
+    columns = columns_of(sets)
+    span = span_of(right.shape[2], *columns)
+    first, steps = columns[0] // span, sum(columns) // span
+    specs = two_sets(sets, first, span)
+    count = len(sets[0][0])
     width = perms[0].shape[0]
     extra = [] if bias is None else [bias]
 
@@ -268,41 +300,58 @@
                 total = total + extras[0][...]
             out_ref[...] = total.astype(out)
 
-    given = [right] + list(perms) + extra + list(sets[0]) + list(sets[1])
-    specs = [span_spec(right)] + [whole(value) for value in list(perms) + extra] + specs
+    given = [right] + list(perms) + extra + list(sets[0][0]) + list(sets[1][0])
+    specs = [span_spec(right, span)] + [whole(value) for value in list(perms) + extra] + specs
     outs = jax.ShapeDtypeStruct((tokens, width), out)
     scratch = [pltpu.VMEM((tokens, width), F32)] * 2
-    work = 2 * tokens * width * steps * SPAN
-    return run(body, (steps,), given, specs, outs, whole(outs), scratch, work)
-
-
-def grad_rows(left, right, rows, columns, back=None):
-    tokens = left.shape[0]
-    count = rows[1] - rows[0]
-    each = right.shape[2] // SPAN
-    start, steps = columns[0] // SPAN, (columns[1] - columns[0]) // SPAN
-
-    def body(left_ref, right_ref, *refs):
-        total = matmul_tn(left_ref[...], right_ref[0])
-        if back is not None:
-            total = total + refs[0][...].astype(F32)
-        refs[-1][...] = total.astype(BF16)
-
-    given = [left, right]
-    at = rows[0] // count
-    specs = [
-        pl.BlockSpec((tokens, count), lambda j: (0, at)),
-        pl.BlockSpec(
-            (1, tokens, SPAN), lambda j: ((j + start) // each, 0, (j + start) % each)
-        ),
-    ]
-    if back is not None:
-        given.append(back)
-        specs.append(pl.BlockSpec((count, SPAN), lambda j: (at, j)))
-    outs = jax.ShapeDtypeStruct((count, steps * SPAN), BF16)
-    spec = pl.BlockSpec((count, SPAN), lambda j: (0, j))
-    work = 2 * tokens * count * steps * SPAN
-    return run(body, (steps,), given, specs, outs, spec, work=work)
+    return run(body, (steps,), given, specs, outs, whole(outs), scratch)
+
+
+def grad_sets(left, right, columns, back=None):
+    tokens, width = left[0].shape
+    parts = 2 if back is not None else 1
+    half = width // 2
+    count = half // parts
+    wide = [stop - start for start, stop in columns]
+    span = span_of(right.shape[2], *wide, *[start for start, _ in columns])
+    each = right.shape[2] // span
+    first, steps = wide[0] // span, sum(wide) // span
+    at = [start // span for start, _ in columns]
+
+    def place(j):
+        block = jnp.where(j < first, j + at[0], j - first + at[1])
+        return (block // each, 0, block % each)
+
+    def body(one_ref, two_ref, right_ref, *refs):
+        def part(left_ref, outs):
+            total = matmul_tn(left_ref[...], right_ref[0])
+            if back is not None:
+                total = total + refs[0][...].astype(F32)
+            for which, out in enumerate(outs):
+                out[...] = total[which * count : (which + 1) * count].astype(BF16)
+
+        step = pl.program_id(0)
+        if back is None:
+            pl.when(step < first)(lambda: part(one_ref, refs))
+            pl.when(step >= first)(lambda: part(two_ref, refs))
+        else:
+            pl.when(step < first)(lambda: part(one_ref, refs[1:3]))
+            pl.when(step >= first)(lambda: part(two_ref, refs[3:]))
+
+    side = 0 if back is not None else 1
+    given = list(left) + [right]
+    specs = [pl.BlockSpec((tokens, half), lambda j: (0, side)) for _ in left]
+    specs.append(pl.BlockSpec((1, tokens, span), place))
+    own = pl.BlockSpec((half, span), lambda j: (0, j))
+    if back is None:
+        outs = jax.ShapeDtypeStruct((half, sum(wide)), BF16)
+        return run(body, (steps,), given, specs, outs, own)
+    outs, out_specs = [], []
+    indices = (lambda j: (0, jnp.minimum(j, first - 1)), lambda j: (0, jnp.maximum(j - first, 0)))
+    for size, index in zip(wide, indices):
+        outs += [jax.ShapeDtypeStruct((count, size), BF16)] * 2
+        out_specs += [pl.BlockSpec((count, span), index)] * 2
+    return run(body, (steps,), given + [back], specs + [own], outs, out_specs)
 
 
 def head_scale(value, left_half):
@@ -353,7 +402,7 @@
     outs = jax.ShapeDtypeStruct((tokens, width), BF16)
     spec = pl.BlockSpec((tokens, PAIR), lambda j: (0, j))
     given = [qkv, qkv, qkv, q_gain, k_gain, mask]
-    return run(body, (HEADS // 2,), given, pair_specs(tokens), outs, spec, work=10**10)
+    return run(body, (HEADS // 2,), given, pair_specs(tokens), outs, spec)
 
 
 def attend_back(qkv, q_gain, k_gain, mask, d_mix):
@@ -407,7 +456,7 @@
     ]
     given = [qkv, qkv, qkv, q_gain, k_gain, mask, d_mix]
     specs = pair_specs(tokens) + [pl.BlockSpec((tokens, PAIR), lambda j: (0, j))]
-    return run(body, (HEADS // 2,), given, specs, outs, out_specs, work=3 * 10**10)
+    return run(body, (HEADS // 2,), given, specs, outs, out_specs)
 
 
 def row_stats(value):
@@ -427,11 +476,11 @@
         total = value_ref[...]
         outs = refs[len(extra) + len(perms) :]
         if gate is not None:
-            total = total + precise(hot_ref[...], refs[0][...]) * refs[1][...]
+            total = total + pick(hot_ref[...], refs[0][...]) * refs[1][...]
             outs[-1][...] = total
         center, inverse = row_stats(total)
-        scales = 1.0 + precise(hot_ref[...], scale_ref[...])
-        normed = center * inverse * scales + precise(hot_ref[...], shift_ref[...])
+        scales = 1.0 + pick(hot_ref[...], scale_ref[...])
+        normed = center * inverse * scales + pick(hot_ref[...], shift_ref[...])
         normed = normed.astype(BF16)
         for perm_ref, out_ref in zip(refs[len(extra) : len(extra) + len(perms)], outs):
             out_ref[...] = matmul(normed, perm_ref[...]).astype(BF16)
@@ -443,7 +492,7 @@
     outs = [jax.ShapeDtypeStruct((tokens, width), BF16) for _ in perms]
     outs += [jax.ShapeDtypeStruct((tokens, width), F32)] if extra else []
     out_specs = [by_tokens(value) for _ in outs]
-    return run(body, (tokens // TOKENS,), given, specs, outs, out_specs, work=10**9)
+    return run(body, (tokens // TOKENS,), given, specs, outs, out_specs)
 
 
 def norm_back(value, d_out, hot, hot_t, scale, beyond=None, gate=None, branch=None, perms=()):
@@ -459,7 +508,7 @@
         d_out = talls[1][...]
         center, inverse = row_stats(talls[0][...])
         normed = center * inverse
-        d_norm = d_out * (1.0 + precise(hot_ref[...], flats[0][...]))
+        d_norm = d_out * (1.0 + pick(hot_ref[...], flats[0][...]))
         mean = jnp.mean(d_norm, axis=1, keepdims=True)
         along = jnp.mean(d_norm * normed, axis=1, keepdims=True)
         total = (d_norm - mean - normed * along) * inverse
@@ -467,12 +516,12 @@
             total = total + talls[2][...]
         total_ref[...] = total
         sums = [
-            (shift_ref, precise(hot_t_ref[...], d_out)),
-            (scale_ref, precise(hot_t_ref[...], d_out * normed)),
+            (shift_ref, pick(hot_t_ref[...], d_out)),
+            (scale_ref, pick(hot_t_ref[...], d_out * normed)),
         ]
         if gated:
-            sums.append((outs[4], precise(hot_t_ref[...], total * talls[-1][...])))
-            low = (precise(hot_ref[...], flats[1][...]) * total).astype(BF16)
+            sums.append((outs[4], pick(hot_t_ref[...], total * talls[-1][...])))
+            low = (pick(hot_ref[...], flats[1][...]) * total).astype(BF16)
             column = jnp.sum(low.astype(F32), axis=0, keepdims=True)
         else:
             low = total.astype(BF16)
@@ -504,7 +553,7 @@
     outs += [image] if gated else []
     outs += [shape((tokens, width), BF16) for _ in range(max(len(perms), 1))]
     out_specs = [by_tokens(part) if part.shape[0] == tokens else whole(part) for part in outs]
-    return run(body, (tokens // TOKENS,), given, specs, outs, out_specs, work=10**9)
+    return run(body, (tokens // TOKENS,), given, specs, outs, out_specs)
 
 
 def slim_back(d_resid, token_hot, arrays, plan, perm, n_embed):
@@ -532,7 +581,7 @@
     outs = jax.ShapeDtypeStruct((width, wide), BF16)
     specs = [whole(value) for value in given]
     scratch = [pltpu.VMEM((room, width), F32)]
-    return run(body, (1,), given, specs, outs, whole(outs), scratch, 3 * 10**9)
+    return run(body, (1,), given, specs, outs, whole(outs), scratch)
 
 
 def layout(scale_row):
@@ -627,8 +676,13 @@
     fill = -slim.shape[0] % 128
     slim = jnp.pad(slim, ((0, fill), (0, 0))).T
     wide = slim.shape[1]
-    qkv_one = attn_weight[:, :half_qkv].astype(BF16)
-    qkv_two = attn_weight[:, half_qkv : 3 * width].astype(BF16)
+    half_slim = wide // 2
+    qkv_one = jnp.concatenate(
+        [attn_weight[:, :half_qkv].astype(BF16), slim[:, :half_slim]], axis=1
+    )
+    qkv_two = jnp.concatenate(
+        [attn_weight[:, half_qkv : 3 * width].astype(BF16), slim[:, half_slim:]], axis=1
+    )
     up = jnp.concatenate(
         [
             mlp_weight[0, :, :half_ff],
@@ -654,17 +708,23 @@
         shaped = value.reshape((2, n_y, n_x, n_z * MAXIMG) + value.shape[1:])
         return jnp.swapaxes(shaped, 1, 2).reshape(value.shape)
 
-    facts = grown(bits_z[:1], facts)
-    slim, qkv_one, qkv_two = grown(bits_z[:1], slim, qkv_one, qkv_two)
-    facts, slim, qkv_one, qkv_two, up = tie(facts, slim, qkv_one, qkv_two, up)
-    facts = grown(bits_z[1:] + bits_y + bits_x + [1], facts)
-    slim, qkv_one, qkv_two = grown(bits_z[1:], slim, qkv_one, qkv_two)
+    order = path_one + [1]
+    groups = [order[at : at + 2] for at in range(0, len(order), 2)]
+    parts = spread(facts, groups[0], devices)
+    qkv_one, qkv_two = widen(qkv_one, bits_z[:1], devices), widen(qkv_two, bits_z[:1], devices)
+    parts, qkv_one, qkv_two = tie(parts, qkv_one, qkv_two)
+    parts = spread(stack(parts), groups[1], devices)
+    qkv_one = widen(stack(qkv_one), bits_z[1:], devices)
+    qkv_two = widen(stack(qkv_two), bits_z[1:], devices)
     perm_one, perm_one_t = hot_rows(source_rows(path_one + [1], me, rows))
     perm_two, perm_two_t = hot_rows(source_rows(path_two + [1], me, rows))
-    facts, slim, qkv_one, qkv_two, up, perm_one, perm_two = tie(
-        facts, slim, qkv_one, qkv_two, up, perm_one, perm_two
-    )
-
+    parts, qkv_one, qkv_two, up = tie(parts, qkv_one, qkv_two, up)
+    for group in groups[2:]:
+        parts = spread(stack(parts), group, devices)
+    qkv_one, qkv_two = widen(stack(qkv_one), one_y, devices), widen(stack(qkv_two), two_x, devices)
+    parts, perm_one, perm_two, up = tie(parts, perm_one, perm_two, up)
+
+    facts = stack(parts)
     total_count = jnp.sum(facts[:, MAXIMG]).astype(F32)
     class_hot = (
         facts[:, :MAXIMG].reshape(slots)[:, None] == jnp.arange(CLASSES, dtype=jnp.int32)[None, :]
@@ -673,168 +733,171 @@
     class_act = jax.nn.silu(class_vec).astype(BF16)
     cuts = (2 * width, 5 * width)
     act_two = to_two(class_act)
-    first = matmul(class_act, ada16[:, : cuts[0]]).astype(BF16)
-    up = grown(bits_z[:1], up)
-    qkv_one, qkv_two = grown(one_y, qkv_one), grown(two_x, qkv_two)
-    slim = grown(bits_y, slim)
-    first = keep_half(first, 1, devices)
-    for mask in reversed(bits_x):
-        first = keep_half(first, mask, devices)
-    slim = grown(bits_x, slim)
-    first, slim, qkv_one, qkv_two, up, down, head16 = tie(
-        first, slim, qkv_one, qkv_two, up, down, head16
-    )
-
+    act_first = class_act.reshape(2, n_x, n_y, n_z, MAXIMG, rows)
+    act_first = jnp.transpose(act_first, (0, 3, 1, 2, 4, 5)).reshape(slots, rows)
+    path_first = bits_y + bits_x + bits_z
+    first = matmul(act_first, ada16[:, : cuts[0]]).astype(BF16)
+    first = lend(first, [1], devices)
+    row_info = widen(row_info, bits_x, devices)
+    first, row_info = tie(first, row_info)
+    for mask in reversed(bits_z):
+        first = lend(added(*first), [mask], devices)
+        (first,) = tie(first)
+    first, qkv_one, qkv_two, up, row_info = tie(first, qkv_one, qkv_two, up, row_info)
+
+    first = lend(added(*first), bits_x, devices)
+    up = widen(up, bits_z[:1], devices)
+    qkv_one, qkv_two = stack(qkv_one), stack(qkv_two)
     for mask in bits_x[:-1]:
-        qkv_one = grown([mask], qkv_one)
+        qkv_one = grow(qkv_one, mask, devices)
     for mask in bits_y[:-1]:
-        qkv_two = grown([mask], qkv_two)
+        qkv_two = grow(qkv_two, mask, devices)
     one_far, two_far = swap(qkv_one, bits_x[-1]), swap(qkv_two, bits_y[-1])
-    up = grown(bits_z[1:], up)
-    slim = grown([1], slim)
-    first = keep_all(first, bits_z + bits_y, devices)
+    row_info = widen(stack(row_info), [1], devices)
+    first, row_info, qkv_one, qkv_two = tie(first, row_info, qkv_one, qkv_two)
+    first = lend(added(*first), bits_y, devices)
+    first, qkv_one, qkv_two, up = tie(first, qkv_one, qkv_two, up)
+    first = added(*first, F32)
+    up = widen(stack(up), bits_z[1:], devices)
+    one_near_c, two_near_c = swap(qkv_one, 1), swap(qkv_two, 1)
     pos_hot = (inside[:, None] == jnp.arange(used, dtype=jnp.int32)[None, :]).astype(BF16)
     level_hot = (scale_row[:, None] == jnp.arange(LEVELS, dtype=jnp.int32)[None, :]).astype(BF16)
     token_hot = jnp.concatenate(
         [pos_hot, level_hot, features[0], jnp.zeros((length, wide - n_embed), BF16)], axis=1
     )
     image = jnp.arange(MAXIMG, dtype=jnp.int32)
-    hot = (image_id[:, None] == image[None, :]).astype(F32)
-    hot_t = (image[:, None] == image_id[None, :]).astype(F32)
+    hot = (image_id[:, None] == image[None, :]).astype(BF16)
+    hot_t = (image[:, None] == image_id[None, :]).astype(BF16)
     allowed = (image_id[:, None] == image_id[None, :]) & (scale_row[None, :] <= scale_row[:, None])
     mask_rows = jnp.where(allowed, 0.0, NEG_FILL).astype(F32)
-    mod_one = matmul(class_act, ada16[:, cuts[0] : cuts[1]]).astype(BF16)
-    mod_two = matmul(act_two, ada16[:, cuts[1] :]).astype(BF16)
-    first, slim, token_hot, mask_rows, mod_one, mod_two = tie(
-        first, slim, token_hot, mask_rows, mod_one, mod_two
-    )
-
-    one_near_c, two_near_c = swap(qkv_one, 1), swap(qkv_two, 1)
-    slim = matmul_tn(slim, perm_one)
+    mods_rest = jnp.concatenate(
+        [
+            matmul(class_act, ada16[:, cuts[0] : cuts[1]]).astype(BF16),
+            matmul(act_two, ada16[:, cuts[1] :]).astype(BF16),
+        ],
+        axis=1,
+    )
+    first, one_far, two_far, one_near_c, two_near_c, mods_rest, token_hot, mask_rows = tie(
+        first, one_far, two_far, one_near_c, two_near_c, mods_rest, token_hot, mask_rows
+    )
+    row_info = jnp.swapaxes(stack(row_info), 0, 1).reshape(2, -1)
+
+    one_far_c, two_far_c = swap(one_far, 1), swap(two_far, 1)
+    mods_rest = lend(mods_rest, [1], devices)
+    one_far_c, two_far_c, mods_rest, first, down, up = tie(
+        one_far_c, two_far_c, mods_rest, first, down, up
+    )
+
+    half_up = half_ff + top
+    up = stack(up)
+    up_one, up_two = widen(up[:, :half_up], one_y, devices), widen(up[:, half_up:], two_x, devices)
+    mods_rest = added(*mods_rest)
+    cut = cuts[1] - cuts[0]
+    mod_one = lend(mods_rest[:, :cut], bits_x, devices)
+    mod_two = lend(mods_rest[:, cut:], bits_y, devices)
+    down = widen(down, bits_z[:1], devices)
+    blocks_one = [qkv_one, one_far, one_near_c, one_far_c]
+    blocks_two = [qkv_two, two_far, two_near_c, two_far_c]
+    slim = jnp.concatenate(
+        [
+            matmul_tn(stack([block[:, half_qkv:] for block in blocks_one]), perm_one),
+            matmul_tn(stack([block[:, half_qkv:] for block in blocks_two]), perm_two),
+        ],
+        axis=0,
+    )
     gain_rows = slim[n_embed : n_embed + n_gains]
     ada_bias = gain_rows[ada_at:head_at].reshape(1, -1)
     resid_in = matmul(token_hot, slim.astype(BF16)) + gain_rows[0]
     first = first + ada_bias[:, : cuts[0]]
     mods = [first[:, :width], first[:, width:]]
     u_one, u_two = norm_ahead(resid_in, hot, mods[0], mods[1], [perm_one_t, perm_two_t])
-    u_one, u_two, one_far, two_far, one_near_c, two_near_c, mod_one, mod_two, up = tie(
-        u_one, u_two, one_far, two_far, one_near_c, two_near_c, mod_one, mod_two, up
-    )
-
-    one_far_c, two_far_c = swap(one_far, 1), swap(two_far, 1)
-    half_up = half_ff + top
-    up_one, up_two = grown(one_y, up[:, :half_up]), grown(two_x, up[:, half_up:])
-    mod_one, mod_two = keep_half(mod_one, 1, devices), keep_half(mod_two, 1, devices)
-    one_far_c, two_far_c, u_one, u_two, mod_one, mod_two, down = tie(
-        one_far_c, two_far_c, u_one, u_two, mod_one, mod_two, down
-    )
-
-    for mask in reversed(bits_x):
-        mod_one = keep_half(mod_one, mask, devices)
-    for mask in reversed(bits_y):
-        mod_two = keep_half(mod_two, mask, devices)
-    down = grown(bits_z[:1], down)
-    w_qkv = (
-        [qkv_one, one_far, one_near_c, one_far_c],
-        [qkv_two, two_far, two_near_c, two_far_c],
-    )
+    w_qkv = ((blocks_one, half_qkv), (blocks_two, half_qkv))
     qkv_bias = jnp.concatenate(
         [gain_rows[1:2], jnp.zeros((1, width), F32), gain_rows[2:3]], axis=1
     )
     q_gain, k_gain = gain_rows[5:6], gain_rows[6:7]
     qkv = times_sets([u_one, u_two], w_qkv, qkv_bias)
-    mixture = attend(qkv, q_gain, k_gain, mask_rows)
-    mixture, up_one, up_two, mod_one, mod_two, down, head16 = tie(
-        mixture, up_one, up_two, mod_one, mod_two, down, head16
-    )
-
+    qkv, up_one, up_two, mod_one, mod_two, down, head16 = tie(
+        qkv, up_one, up_two, mod_one, mod_two, down, head16
+    )
+
+    up_one, up_two = stack(up_one), stack(up_two)
     for mask in bits_x[:-1]:
-        up_one = grown([mask], up_one)
+        up_one = grow(up_one, mask, devices)
     for mask in bits_y[:-1]:
-        up_two = grown([mask], up_two)
+        up_two = grow(up_two, mask, devices)
     proj_one, proj_two = up_one[:, half_ff:], up_two[:, half_ff:]
     up_one, up_two = up_one[:, :half_ff], up_two[:, :half_ff]
     proj_one_far, proj_two_far = swap(proj_one, bits_x[-1]), swap(proj_two, bits_y[-1])
-    for mask in reversed(bits_y):
-        mod_one = keep_half(mod_one, mask, devices)
-    for mask in reversed(bits_x):
-        mod_two = keep_half(mod_two, mask, devices)
+    mod_one = lend(added(*mod_one), bits_y, devices)
+    mod_two = lend(added(*mod_two), bits_x, devices)
+    head16 = widen(head16, bits_y, devices)
+    mixture = attend(qkv, q_gain, k_gain, mask_rows)
+    mixture, proj_one_far, proj_two_far, up_one, up_two, mod_one, mod_two, head16, down = tie(
+        mixture, proj_one_far, proj_two_far, up_one, up_two, mod_one, mod_two, head16, down
+    )
+
+    up_one_far, up_two_far = swap(up_one, bits_x[-1]), swap(up_two, bits_y[-1])
+    mods_rest = jnp.concatenate([added(*mod_one), added(*mod_two)], axis=1)
+    mods_rest = lend(mods_rest, bits_z[-1:], devices)
     proj_one_c, proj_two_c = swap(proj_one, 1), swap(proj_two, 1)
+    proj_one_fc, proj_two_fc = swap(proj_one_far, 1), swap(proj_two_far, 1)
     mix_one = matmul(mixture, perm_one_t).astype(BF16)
     mix_two = matmul(mixture, perm_two_t).astype(BF16)
-    mods_rest = jnp.concatenate([mod_one, mod_two], axis=1)
-    (
-        mix_one,
-        mix_two,
-        proj_one_far,
-        proj_two_far,
-        proj_one_c,
-        proj_two_c,
-        up_one,
-        up_two,
-        mods_rest,
-        down,
-    ) = tie(
-        mix_one,
-        mix_two,
-        proj_one_far,
-        proj_two_far,
-        proj_one_c,
-        proj_two_c,
-        up_one,
-        up_two,
-        mods_rest,
-        down,
-    )
-
-    up_one_far, up_two_far = swap(up_one, bits_x[-1]), swap(up_two, bits_y[-1])
+    mix_one, mix_two, proj_one_c, proj_two_c, proj_one_fc, proj_two_fc, mods_rest = tie(
+        mix_one, mix_two, proj_one_c, proj_two_c, proj_one_fc, proj_two_fc, mods_rest
+    )
     w_proj = (
-        [proj_one, proj_one_far, proj_one_c, swap(proj_one_far, 1)],
-        [proj_two, proj_two_far, proj_two_c, swap(proj_two_far, 1)],
-    )
-    down = grown(bits_z[1:], down)
-    mods_rest = keep_all(mods_rest, bits_z, devices)
+        ([proj_one, proj_one_far, proj_one_c, proj_one_fc], None),
+        ([proj_two, proj_two_far, proj_two_c, proj_two_fc], None),
+    )
+    mods_rest = lend(added(*mods_rest), bits_z[:-1], devices)
     attn_out = times_sets([mix_one, mix_two], w_proj, gain_rows[3:4])
-    attn_out, mods_rest, head16 = tie(attn_out, mods_rest, head16)
-    mods_rest = mods_rest + ada_bias[:, cuts[0] :]
+    attn_out, mods_rest, down = tie(attn_out, mods_rest, down)
+    mods_rest = added(*mods_rest, F32) + ada_bias[:, cuts[0] :]
     mods += [mods_rest[:, at : at + width] for at in range(0, 6 * width, width)]
+    up_one_c, up_two_c = swap(up_one, 1), swap(up_two, 1)
+    down = widen(stack(down), bits_z[1:], devices)
     u_mid_one, u_mid_two, resid_mid = norm_ahead(
         resid_in, hot, mods[3], mods[4], [perm_one_t, perm_two_t], mods[2], attn_out
     )
-    up_one_c, up_two_c = swap(up_one, 1), swap(up_two, 1)
-    head16 = grown(bits_y, head16)
-    u_mid_one, u_mid_two, up_one_far, up_two_far, up_one_c, up_two_c, down, head16 = tie(
-        u_mid_one, u_mid_two, up_one_far, up_two_far, up_one_c, up_two_c, down, head16
+    u_mid_one, u_mid_two, up_one_far, up_two_far, up_one_c, up_two_c, down = tie(
+        u_mid_one, u_mid_two, up_one_far, up_two_far, up_one_c, up_two_c, down
     )
 
     up_one_fc, up_two_fc = swap(up_one_far, 1), swap(up_two_far, 1)
-    down_one, down_two = grown(one_y, down[:, :half_ff]), grown(two_x, down[:, half_ff:])
-    head16 = grown(bits_z[:1], head16)
+    u_mid_one, u_mid_two, up_one_fc, up_two_fc, down = tie(
+        u_mid_one, u_mid_two, up_one_fc, up_two_fc, down
+    )
+    down = stack(down)
+    down_one = widen(down[:, :half_ff], one_y, devices)
+    down_two = widen(down[:, half_ff:], two_x, devices)
+    head16 = widen(stack(head16), bits_z[:1], devices)
     w_up = (
-        [up_one, up_one_far, up_one_c, up_one_fc],
-        [up_two, up_two_far, up_two_c, up_two_fc],
+        ([up_one, up_one_far, up_one_c, up_one_fc], None),
+        ([up_two, up_two_far, up_two_c, up_two_fc], None),
     )
     up_bias = gain_rows[7:ada_at].reshape(1, -1)
     hidden, active = times_sets([u_mid_one, u_mid_two], w_up, up_bias, bend=True)
+    active, down_one, down_two = tie(active, down_one, down_two)
+
+    down_one, down_two = stack(down_one), stack(down_two)
     for mask in bits_x[:-1]:
-        down_one = grown([mask], down_one)
+        down_one = grow(down_one, mask, devices)
     for mask in bits_y[:-1]:
-        down_two = grown([mask], down_two)
-    active, down_one, down_two, row_info = tie(active, down_one, down_two, row_info)
-
+        down_two = grow(down_two, mask, devices)
     down_one_far, down_two_far = swap(down_one, bits_x[-1]), swap(down_two, bits_y[-1])
     down_one_c, down_two_c = swap(down_one, 1), swap(down_two, 1)
-    for mask in bits_x + [1]:
-        row_info = grown([mask], row_info)
-    row_info = jnp.swapaxes(row_info, 0, 1).reshape(2, -1)
-    active, down_one_far, down_two_far, down_one_c, down_two_c, head16, row_info = tie(
-        active, down_one_far, down_two_far, down_one_c, down_two_c, head16, row_info
-    )
-
-    head16 = grown(bits_z[1:], head16)
+    active, down_one_far, down_two_far, down_one_c, down_two_c, head16 = tie(
+        active, down_one_far, down_two_far, down_one_c, down_two_c, head16
+    )
+
+    down_one_fc, down_two_fc = swap(down_one_far, 1), swap(down_two_far, 1)
+    head16 = widen(stack(head16), bits_z[1:], devices)
+    active, down_one_fc, down_two_fc = tie(active, down_one_fc, down_two_fc)
     w_down = (
-        [down_one, down_one_far, down_one_c, swap(down_one_far, 1)],
-        [down_two, down_two_far, down_two_c, swap(down_two_far, 1)],
+        ([down_one, down_one_far, down_one_c, down_one_fc], None),
+        ([down_two, down_two_far, down_two_c, down_two_fc], None),
     )
     perms = [perm_one, perm_two]
     mlp_out = back_sets(active[None], w_down, perms, gain_rows[4:5], exact=True)
@@ -848,6 +911,7 @@
         resid_mid, hot, mods[6], mods[7], [perm_head_t], mods[5], mlp_out
     )
     head_rel, head16 = tie(head_rel, head16)
+    head16 = stack(head16)
 
     vocab_masks = bits_x + [1]
     rows_all = grown(bits_x[:-1], head_rel)
@@ -918,15 +982,6 @@
     )
     d_head_in, head_far, head_near = tie(d_head_in, head_far, head_near)
 
-    def far_rows_of(left, right, columns):
-        return grad_rows(left, right, (top, width), columns)
-
-    def meet_far(left, right, columns, back):
-        return grad_rows(left, right, (quarter, top), columns, back)
-
-    def meet_near(left, right, columns, back):
-        return grad_rows(left, right, (0, quarter), columns, back)
-
     def cross(one, two):
         return swap(one, bits_x[-1]), swap(two, bits_y[-1])
 
@@ -961,172 +1016,141 @@
     def cross_back(one_far, two_far):
         return swap(one_far, bits_y[-1]), swap(two_far, bits_x[-1])
 
+    perms = [perm_one, perm_two]
     ones, twos = (0, half_ff), (half_ff, FF)
     q_ones, q_twos = (0, half_qkv), (half_qkv, 3 * width)
+    downs, ups = [None, None], [u_mid_one, u_mid_two]
+    mixes, ins = [mix_one, mix_two], [u_one, u_two]
+    ffs, projs, qkvs = [ones, twos], [(0, top), (top, width)], [q_ones, q_twos]
+
     active = active[None]
     head_back = swap(head_far, head_masks[-1])
     d_head_in = in_halves_outside(lambda part: matmul(part, perm_head), d_head_in)
-    d_resid_out, d_shift_head, d_scale_head, down_bias, d_gate_two, d_low_one, d_low_two = (
-        norm_back(
-            resid_out,
-            d_head_in,
-            hot,
-            hot_t,
-            mods[7],
-            gate=mods[5],
-            branch=mlp_out,
-            perms=[perm_one_t, perm_two_t],
-        )
-    )
-    down_f1, down_f2 = far_rows_of(d_low_one, active, ones), far_rows_of(d_low_two, active, twos)
-    d_low_one, d_low_two, down_f1, down_f2 = tie(d_low_one, d_low_two, down_f1, down_f2)
-    down_b1, down_b2 = swap(down_f1, 1), swap(down_f2, 1)
-    d_hid, up_bias_sum = times_sets([d_low_one, d_low_two], w_down, hidden=hidden)
+    d_resid_out, d_shift_head, d_scale_head, down_bias, d_gate_two, *downs = norm_back(
+        resid_out,
+        d_head_in,
+        hot,
+        hot_t,
+        mods[7],
+        gate=mods[5],
+        branch=mlp_out,
+        perms=[perm_one_t, perm_two_t],
+    )
+    down_f = grad_sets(downs, active, ffs)
+    downs, down_f = tie(downs, down_f)
+    down_b = swap(down_f, 1)
+    d_hid, up_bias_sum = times_sets(downs, w_down, hidden=hidden)
+    d_hid, down_b = tie(d_hid, down_b)
     d_hid = d_hid[None]
-    d_hid, down_b1, down_b2, head_back, head_near = tie(
-        d_hid, down_b1, down_b2, head_back, head_near
-    )
-    head_near, head_far = halves_of(head_near, head_back)
-    down_f1 = meet_far(d_low_one, active, ones, down_b1)
-    down_f2 = meet_far(d_low_two, active, twos, down_b2)
-    d_hid, down_f1, down_f2, head_far = tie(d_hid, down_f1, down_f2, head_far)
+    down_n1, down_f1, down_n2, down_f2 = grad_sets(downs, active, ffs, down_b)
+    up_f = grad_sets(ups, d_hid, ffs)
+    d_hid, down_f1, down_f2, down_n1, down_n2, up_f = tie(
+        d_hid, down_f1, down_f2, down_n1, down_n2, up_f
+    )
     down_x1, down_x2 = cross(down_f1, down_f2)
-    head_back = swap(head_far, head_masks[-2])
-    up_f1, up_f2 = far_rows_of(u_mid_one, d_hid, ones), far_rows_of(u_mid_two, d_hid, twos)
-    up_b1, up_b2 = swap(up_f1, 1), swap(up_f2, 1)
-    down_n1 = meet_near(d_low_one, active, ones, down_b1)
-    down_n2 = meet_near(d_low_two, active, twos, down_b2)
+    up_b = swap(up_f, 1)
     d_u = back_sets(d_hid, w_up, perms)
-    d_u, down_x1, down_x2, down_n1, down_n2, up_b1, up_b2, head_back, head_near = tie(
-        d_u, down_x1, down_x2, down_n1, down_n2, up_b1, up_b2, head_back, head_near
-    )
-    down_n1, down_f1, down_n2, down_f2 = turn(down_n1, down_n2, down_x1, down_x2)
-    head_near = added(head_near, head_back)
-    down_x1, down_x2 = cross_back(down_f1, down_f2)
-    head_grad = keep_all(head_near, head_masks[:-2], devices)
-    up_f1 = meet_far(u_mid_one, d_hid, ones, up_b1)
-    up_f2 = meet_far(u_mid_two, d_hid, twos, up_b2)
+    d_u, up_b = tie(d_u, up_b)
+    up_n1, up_f1, up_n2, up_f2 = grad_sets(ups, d_hid, ffs, up_b)
     d_resid_mid, d_shift_two, d_scale_two, proj_bias, d_gate_one, d_low = norm_back(
         resid_mid, d_u, hot, hot_t, mods[4], beyond=d_resid_out, gate=mods[2], branch=attn_out
     )
-    d_mod = jnp.concatenate(
-        [d_gate_one, d_shift_two, d_scale_two, d_gate_two, d_shift_head, d_scale_head], axis=1
-    ).astype(BF16)
-    d_low, d_mod, down_x1, down_x2, down_n1, down_n2, up_f1, up_f2, head_grad = tie(
-        d_low, d_mod, down_x1, down_x2, down_n1, down_n2, up_f1, up_f2, head_grad
-    )
+    d_low, down_x1, down_x2, up_f1, up_f2, up_n1, up_n2, head_back, head_near = tie(
+        d_low, down_x1, down_x2, up_f1, up_f2, up_n1, up_n2, head_back, head_near
+    )
+    down_n1, down_f1, down_n2, down_f2 = turn(down_n1, down_n2, down_x1, down_x2)
+    head_near, head_far = halves_of(head_near, head_back)
+    d_low, down_f1, down_f2, up_f1, up_f2, head_far = tie(
+        d_low, down_f1, down_f2, up_f1, up_f2, head_far
+    )
+    down_x1, down_x2 = cross_back(down_f1, down_f2)
     up_x1, up_x2 = cross(up_f1, up_f2)
+    head_back = swap(head_far, head_masks[-2])
+    d_low = d_low[None]
+    proj_f = grad_sets(mixes, d_low, projs)
+    d_mix = back_sets(d_low, w_proj, perms, out=BF16)
+    d_qkv, attn_sums = attend_back(qkv, q_gain, k_gain, mask_rows, d_mix)
+    d_qkv, proj_f, down_x1, down_x2, down_n1, down_n2, up_x1, up_x2, head_back, head_near = tie(
+        d_qkv, proj_f, down_x1, down_x2, down_n1, down_n2, up_x1, up_x2, head_back, head_near
+    )
+    up_n1, up_f1, up_n2, up_f2 = turn(up_n1, up_n2, up_x1, up_x2)
     down_near, down_far = join(down_n1, down_n2, down_x1, down_x2)
+    d_qkv, up_f1, up_f2, down_far, proj_f = tie(d_qkv, up_f1, up_f2, down_far, proj_f)
+    up_x1, up_x2 = cross_back(up_f1, up_f2)
     down_back = swap(down_far, bits_z[-1])
-    all_mod = grown(bits_z[:1], d_mod)
-    d_low3 = d_low[None]
-    p_ones, p_twos = (0, top), (top, width)
-    proj_f1 = far_rows_of(mix_one, d_low3, p_ones)
-    proj_f2 = far_rows_of(mix_two, d_low3, p_twos)
-    proj_b1, proj_b2 = swap(proj_f1, 1), swap(proj_f2, 1)
-    up_n1 = meet_near(u_mid_one, d_hid, ones, up_b1)
-    up_n2 = meet_near(u_mid_two, d_hid, twos, up_b2)
-    d_mix = back_sets(d_low3, w_proj, perms, out=BF16)
-    d_mix, proj_b1, proj_b2 = tie(d_mix, proj_b1, proj_b2)
-    proj_f1 = meet_far(mix_one, d_low3, p_ones, proj_b1)
-    proj_f2 = meet_far(mix_two, d_low3, p_twos, proj_b2)
-    proj_n1 = meet_near(mix_one, d_low3, p_ones, proj_b1)
-    proj_n2 = meet_near(mix_two, d_low3, p_twos, proj_b2)
-    d_qkv, attn_sums = attend_back(qkv, q_gain, k_gain, mask_rows, d_mix)
-    d_qkv, up_x1, up_x2, up_n1, up_n2, down_back, down_near, all_mod, proj_f1, proj_f2 = tie(
-        d_qkv, up_x1, up_x2, up_n1, up_n2, down_back, down_near, all_mod, proj_f1, proj_f2
-    )
-    up_n1, up_f1, up_n2, up_f2 = turn(up_n1, up_n2, up_x1, up_x2)
-    up_x1, up_x2 = cross_back(up_f1, up_f2)
+    proj_b = swap(proj_f, 1)
+    qkv_f = grad_sets(ins, d_qkv, qkvs)
+    d_qkv, qkv_f, proj_b = tie(d_qkv, qkv_f, proj_b)
+    qkv_b = swap(qkv_f, 1)
+    head_near = added(head_near, head_back)
+    head_grad = lend(head_near, head_masks[:-2], devices)
+    d_u = back_sets(d_qkv, w_qkv, perms)
+    d_u, qkv_b, up_x1, up_x2, down_back, down_near, head_grad = tie(
+        d_u, qkv_b, up_x1, up_x2, down_back, down_near, head_grad
+    )
+    head_grad = added(*head_grad, F32)
     down_near, down_far = halves_of(down_near, down_back)
+    d_u, down_far, qkv_b, up_x1, up_x2 = tie(d_u, down_far, qkv_b, up_x1, up_x2)
     down_back = swap(down_far, bits_z[-2])
-    proj_x1, proj_x2 = cross(proj_f1, proj_f2)
-    qkv_f1, qkv_f2 = far_rows_of(u_one, d_qkv, q_ones), far_rows_of(u_two, d_qkv, q_twos)
-    d_u = back_sets(d_qkv, w_qkv, perms)
-    d_u, up_x1, up_x2, up_n1, up_n2, down_back, proj_x1, proj_x2, qkv_f1, qkv_f2, all_mod = tie(
-        d_u, up_x1, up_x2, up_n1, up_n2, down_back, proj_x1, proj_x2, qkv_f1, qkv_f2, all_mod
-    )
-    qkv_b1, qkv_b2 = swap(qkv_f1, 1), swap(qkv_f2, 1)
+
+    def beside(one, two):
+        return jnp.concatenate([one, two], axis=1)
+
+    qkv_n1, qkv_f1, qkv_n2, qkv_f2 = grad_sets(ins, d_qkv, qkvs, qkv_b)
+    proj_n1, proj_f1, proj_n2, proj_f2 = grad_sets(mixes, d_low, projs, proj_b)
     up_near, up_far = join(up_n1, up_n2, up_x1, up_x2)
-    up_back = swap(up_far, bits_z[-1])
-    all_mod = grown(bits_z[1:], all_mod)
     d_resid_in, d_shift_one, d_scale_one, word_bias, d_res16 = norm_back(
         resid_in, d_u, hot, hot_t, mods[1], beyond=d_resid_mid
     )
-    d_first = jnp.concatenate([d_shift_one, d_scale_one], axis=1).astype(BF16)
-    d_res16, d_first, qkv_b1, qkv_b2 = tie(d_res16, d_first, qkv_b1, qkv_b2)
-    qkv_f1 = meet_far(u_one, d_qkv, q_ones, qkv_b1)
-    qkv_f2 = meet_far(u_two, d_qkv, q_twos, qkv_b2)
-    d_res16, qkv_f1, qkv_f2, d_first = tie(d_res16, qkv_f1, qkv_f2, d_first)
+    d_mod = jnp.concatenate(
+        [
+            d_shift_one,
+            d_scale_one,
+            d_gate_one,
+            d_shift_two,
+            d_scale_two,
+            d_gate_two,
+            d_shift_head,
+            d_scale_head,
+        ],
+        axis=1,
+    ).astype(BF16)
+    qkv_f1, qkv_f2 = beside(qkv_f1, proj_f1), beside(qkv_f2, proj_f2)
+    d_mod, d_res16, up_far, qkv_f1, qkv_f2, qkv_n1, qkv_n2, proj_n1, proj_n2 = tie(
+        d_mod, d_res16, up_far, qkv_f1, qkv_f2, qkv_n1, qkv_n2, proj_n1, proj_n2
+    )
     qkv_x1, qkv_x2 = cross(qkv_f1, qkv_f2)
-    all_first = grown(bits_z, d_first)
-    ada_sums = jnp.sum(
-        jnp.concatenate([d_first, d_mod], axis=1).astype(F32), axis=0, keepdims=True
-    )
+    up_back = swap(up_far, bits_z[-1])
+    all_mod = widen(d_mod, bits_z, devices)
+    ada_sums = jnp.sum(d_mod.astype(F32), axis=0, keepdims=True)
     arrays = [word_bias, attn_sums, proj_bias, down_bias, up_bias_sum, ada_sums, bias_grad[None]]
     plan = [(0, 0), (1, 2), (1, 3), (2, 0), (3, 0), (1, 0), (1, 1), (4, 0), (5, 0), (6, 0)]
     d_slim = slim_back(d_res16, token_hot, arrays, plan, perm_one, n_embed)
-    d_slim = keep_half(d_slim, 1, devices)
-    proj_n1, proj_f1, proj_n2, proj_f2 = turn(proj_n1, proj_n2, proj_x1, proj_x2)
-    proj_x1, proj_x2 = cross_back(proj_f1, proj_f2)
-    qkv_n1 = meet_near(u_one, d_qkv, q_ones, qkv_b1)
-    qkv_n2 = meet_near(u_two, d_qkv, q_twos, qkv_b2)
-    (
-        qkv_x1,
-        qkv_x2,
-        qkv_n1,
-        qkv_n2,
-        all_first,
-        d_slim,
-        proj_x1,
-        proj_x2,
-        proj_n1,
-        proj_n2,
-        up_back,
-        up_near,
-        all_mod,
-    ) = tie(
-        qkv_x1,
-        qkv_x2,
-        qkv_n1,
-        qkv_n2,
-        all_first,
-        d_slim,
-        proj_x1,
-        proj_x2,
-        proj_n1,
-        proj_n2,
-        up_back,
-        up_near,
-        all_mod,
+    d_slim = lend(d_slim, bits_x + [1], devices)
+    qkv_n1, qkv_n2 = beside(qkv_n1, proj_n1), beside(qkv_n2, proj_n2)
+    qkv_x1, qkv_x2, qkv_n1, qkv_n2, all_mod, d_slim, up_back, up_near, down_back = tie(
+        qkv_x1, qkv_x2, qkv_n1, qkv_n2, all_mod, d_slim, up_back, up_near, down_back
     )
     qkv_n1, qkv_f1, qkv_n2, qkv_f2 = turn(qkv_n1, qkv_n2, qkv_x1, qkv_x2)
+    up_near, up_far = halves_of(up_near, up_back)
     qkv_x1, qkv_x2 = cross_back(qkv_f1, qkv_f2)
-    up_near, up_far = halves_of(up_near, up_back)
     up_back = swap(up_far, bits_z[-2])
-    cut = cuts[1] - cuts[0]
-    all_first = jnp.concatenate([all_first, all_mod[:, :cut]], axis=1)
-    all_first = grown(bits_y, all_first)
-    for mask in reversed(bits_x):
-        d_slim = keep_half(d_slim, mask, devices)
-    qkv_x1, qkv_x2, qkv_n1, qkv_n2, up_back, up_near, all_first, all_mod, d_slim = tie(
-        qkv_x1, qkv_x2, qkv_n1, qkv_n2, up_back, up_near, all_first, all_mod, d_slim
-    )
-    near, far = join(
-        jnp.concatenate([qkv_n1, proj_n1], axis=1),
-        jnp.concatenate([qkv_n2, proj_n2], axis=1),
-        jnp.concatenate([qkv_x1, proj_x1], axis=1),
-        jnp.concatenate([qkv_x2, proj_x2], axis=1),
-    )
+    all_mod = stack(all_mod)
+    all_first = widen(all_mod[:, : cuts[1]], bits_y, devices)
+    all_two = widen(all_mod[:, cuts[1] :], bits_x, devices)
+    qkv_x1, qkv_x2, qkv_n1, qkv_n2, up_back, all_first, all_two, d_slim = tie(
+        qkv_x1, qkv_x2, qkv_n1, qkv_n2, up_back, all_first, all_two, d_slim
+    )
+    near, far = join(qkv_n1, qkv_n2, qkv_x1, qkv_x2)
     attn_back = swap(far, bits_z[-1])
-    all_two = grown(bits_x, all_mod[:, cut:])
-    all_first = grown(bits_x, all_first)
-    d_slim = keep_all(d_slim, bits_z + bits_y, devices)
+    all_two = widen(stack(all_two), bits_y, devices)
+    all_first = widen(stack(all_first), bits_x, devices)
+    d_slim = lend(added(*d_slim), bits_z + bits_y, devices)
     attn_back, near, all_two, all_first, d_slim = tie(attn_back, near, all_two, all_first, d_slim)
     near, far = halves_of(near, attn_back)
     attn_back = swap(far, bits_z[-2])
-    all_two = grown(bits_y + [1], all_two)
-    all_first = grown([1], all_first)
+    all_two = grown([1], stack(all_two))
+    all_first = grown([1], stack(all_first))
 
     def close(near, back):
         masks = bits_z[:-2]
@@ -1138,7 +1162,7 @@
         close(up_near, up_back),
         close(down_near, down_back),
     )
-    slim_grad = d_slim.T
+    slim_grad = added(*d_slim, F32).T
     half_attn = half_qkv + top
     attn_grad = jnp.concatenate(
         [

time: 767 us -> 678 us (0.88)
  waiting for transfers between devices: 243 us -> 205 us
  Pallas kernels: 206 us -> 174 us
  other arithmetic: 98.3 us -> 71.8 us
  local copies, waits for them, and re-layouts: 44.3 us -> 62.8 us
  starting transfers between devices: 114 us -> 103 us
    ppermute x129 -> x115, waiting for transfers between devices: 243 us -> 205 us  [swapped(): lax.ppermute(value, ('dp', 'vocab'), [(i, i ^ mask) for i in range(device...]
    pallas_call x41 -> x25, Pallas kernels: 206 us -> 174 us  [run(): pl.pallas_call(body, grid=grid, in_specs=specs, out_shape=outs, out_specs...]
    concatenate x40 -> x14, other arithmetic: 20.8 us -> 2.05 us  [the longest x5 1.24 us: stack(): return jnp.concatenate(parts, axis=0)]
    unnamed x417 -> x529, local copies, waits for them, and re-layouts: 28.7 us -> 42.1 us
    ppermute x129 -> x115, starting transfers between devices: 114 us -> 103 us  [swapped(): lax.ppermute(value, ('dp', 'vocab'), [(i, i ^ mask) for i in range(device...]
    concatenate x0 -> x22, local copies, waits for them, and re-layouts: none -> 8.01 us  [stack(): return jnp.concatenate(parts, axis=0)]
    convert_element_type x35 -> x32, other arithmetic: 21.8 us -> 18.8 us  [added(): return (mine.astype(F32) + theirs.astype(F32)).astype(out)]
  transfers between devices with their start and end apart: 129 -> 115, of which waited for: 48 -> 44; matrix products, arithmetic and copies ran while one was open for 14% -> 12% of each run, Pallas kernels for 21% -> 21%
where the time goes in v3:
time: 678 us; the launch traced here: 667 us
  waiting for transfers between devices  205 us (30%)
  Pallas kernels  174 us (26%)
  starting transfers between devices  103 us (15%)
  other arithmetic  71.8 us (11%)
  local copies, waits for them, and re-layouts  62.8 us (9%)
  matrix products  36.7 us (5%)
  between operations  13.7 us (2%)
    ppermute x115, waiting for transfers between devices, swapped(): lax.ppermute(value, ('dp', 'vocab'), [(i, i ^ mask) for i in range(device...  205 us
    pallas_call x25, Pallas kernels, run(): pl.pallas_call(body, grid=grid, in_specs=specs, out_shape=outs, out_specs...  174 us
    ppermute x115, starting transfers between devices, swapped(): lax.ppermute(value, ('dp', 'vocab'), [(i, i ^ mask) for i in range(device...  103 us
    unnamed x529, local copies, waits for them, and re-layouts  42.1 us
    dot_general x11, matrix products, matmul(): return jnp.dot(left, right, preferred_element_type=F32)  19.5 us
    convert_element_type x32, other arithmetic, added(): return (mine.astype(F32) + theirs.astype(F32)).astype(out)  18.8 us
  transfers between devices with their start and end apart: 115, of which 44 were waited for; matrix products, arithmetic and copies ran while one was open for 12% of the time, Pallas kernels for 21%

profile of v3, /device:TPU:0, one launch (start us, length us, event | category | flops | bytes accessed | tf_op | source)
XLA Modules:
  0.0 666.8 jit_solution(11928228965589496049)
XLA Ops:
  3.5 4.0 collective-permute-start
  17.0 2.6 fusion.3
  19.8 2.7 fusion.5
  55.8 2.9 collective-permute-done.13
  61.8 2.7 convolution_convert_fusion.1
  64.8 3.0 collective-permute-done.14
  80.9 9.7 %collective-permute-done.20 = bf16[32,5120]{1,0:T(8,128)(2,1)S(1)} collective-permute-done((bf16[32,5120]{1,0:T(8,128)(2,1)}, bf16[32,5120]{1,0:T(8,128)(2,1)S(1)}, u32[]{:S(2)}, u32[]{:S(2)}) %collective-permute-start.20) | collective-permute-done | bytes 327712 | tf_op jit(solution)/shard_map/ppermute | solution.py:66
  91.4 9.4 %collective-permute-done.22.refs_6_.refs_5_ = bf16[256,1792]{1,0:T(8,128)(2,1)S(1)} collective-permute-done((bf16[256,1792]{1,0:T(8,128)(2,1)S(1)}, bf16[256,1792]{1,0:T(8,128)(2,1)S(1)}, u32[]{:S(2)}, u32[]{:S(2)}) %collective-permute-start.22) | collective-permute-done | bytes 917536 | tf_op jit(solution)/shard_map/ppermute | solution.py:66
  106.2 14.5 %collective-permute-done.28 = bf16[64,5120]{1,0:T(8,128)(2,1)S(1)} collective-permute-done((bf16[64,5120]{1,0:T(8,128)(2,1)S(1)}, bf16[64,5120]{1,0:T(8,128)(2,1)S(1)}, u32[]{:S(2)}, u32[]{:S(2)}) %collective-permute-start.28) | collective-permute-done | bytes 655392 | tf_op jit(solution)/shard_map/ppermute | solution.py:66
  132.4 4.9 shard_map.457
  137.4 7.5 %shard_map.458.q_ref.k_ref.v_ref = f32[384,3072]{1,0:T(8,128)} custom-call(bf16[384,1024]{1,0:T(8,128)(2,1)S(1)} %get-tuple-element.373.one_ref, bf16[384,1024]{1,0:T(8,128)(2,1)S(1)} %get-tuple-element.374.two_ref, f32[1,3072]{1,0:T(1,128)S(1)} %pad_maximum_fusion.24.refs_0_, bf16[256,1792]{1,0:T(8,128)(2,1)S(1)} %constant_dynamic-update-slice_fusion.12.refs_1_.refs_0_, ...), custom_call_target="tpu_custom_call" | custom-call | flops 1000 | bytes 1000 | tf_op jit(solution)/shard_map/pallas_call | solution.py:151
  144.9 4.9 collective-permute-done.29
  157.5 10.7 %shard_map.459 = bf16[384,1024]{1,0:T(8,128)(2,1)S(1)} custom-call(f32[384,3072]{1,0:T(8,128)S(1)} %copy-done, f32[384,3072]{1,0:T(8,128)S(1)} %copy-done, f32[384,3072]{1,0:T(8,128)S(1)} %copy-done, f32[1,1024]{1,0:T(1,128)S(1)} %get-tuple-element.742.qg_ref, f32[1,1024]{1,0:T(1,128)S(1)} %get-tuple-element.741.kg_ref, f32[384,384]{1,0:T(8,128)S(1)} %and_select_fusion.mask_ref), custom_call_target="tpu_custom_call" | custom-call | flops 1000 | bytes 1000 | tf_op jit(solution)/shard_map/pallas_call | solution.py:151
  173.7 3.1 collective-permute-done.43
  185.6 6.1 shard_map.461
  191.7 6.8 %collective-permute-done.49 = bf16[64,4096]{1,0:T(8,128)(2,1)S(1)} collective-permute-done((bf16[64,4096]{1,0:T(8,128)(2,1)S(1)}, bf16[64,4096]{1,0:T(8,128)(2,1)S(1)}, u32[]{:S(2)}, u32[]{:S(2)}) %collective-permute-start.49) | collective-permute-done | bytes 524320 | tf_op jit(solution)/shard_map/ppermute | solution.py:66
  198.5 3.3 collective-permute-done.45.refs_2_.refs_1_
  201.8 2.5 collective-permute-done.46.refs_6_.refs_5_
  212.5 10.2 %shard_map.462 = (f32[384,4096]{1,0:T(8,128)}, bf16[384,4096]{1,0:T(8,128)(2,1)}) custom-call(bf16[384,1024]{1,0:T(8,128)(2,1)S(1)} %get-tuple-element.426.one_ref, bf16[384,1024]{1,0:T(8,128)(2,1)S(1)} %get-tuple-element.427.two_ref, f32[1,4096]{1,0:T(1,128)S(1)} %bitcast.112, bf16[256,2048]{1,0:T(8,128)(2,1)S(1)} %slice.833.refs_1_.refs_0_, ...), custom_call_target="tpu_custom_call" | custom-call | flops 1000 | bytes 1000 | tf_op jit(solution)/shard_map/pallas_call | solution.py:151
  230.1 24.3 %collective-permute-done.58 = bf16[256,1024]{1,0:T(8,128)(2,1)S(1)} collective-permute-done((bf16[256,1024]{1,0:T(8,128)(2,1)S(1)}, bf16[256,1024]{1,0:T(8,128)(2,1)S(1)}, u32[]{:S(2)}, u32[]{:S(2)}) %collective-permute-start.58) | collective-permute-done | bytes 524320 | tf_op jit(solution)/shard_map/ppermute | solution.py:66
  259.7 12.7 %shard_map.463.refs_1_.refs_2_ = f32[384,1024]{1,0:T(8,128)} custom-call(bf16[1,384,4096]{2,1,0:T(8,128)(2,1)} %bitcast.102, bf16[1024,1024]{1,0:T(8,128)(2,1)} %copy-done.1, bf16[1024,1024]{1,0:T(8,128)(2,1)} %get-tuple-element.371.two_ref, f32[1,1024]{1,0:T(1,128)S(1)} %get-tuple-element.739.refs_0_, ...), custom_call_target="tpu_custom_call" | custom-call | flops 1000 | bytes 1000 | tf_op jit(solution)/shard_map/pallas_call | solution.py:151
  273.8 4.6 shard_map.464
  283.9 3.6 add_reduce_fusion.1
  288.6 12.8 %collective-permute-done.63 = bf16[384,1024]{1,0:T(8,128)(2,1)S(1)} collective-permute-done((bf16[384,1024]{1,0:T(8,128)(2,1)S(1)}, bf16[384,1024]{1,0:T(8,128)(2,1)S(1)}, u32[]{:S(2)}, u32[]{:S(2)}) %collective-permute-start.63) | collective-permute-done | bytes 786464 | tf_op jit(solution)/shard_map/ppermute | solution.py:66
  311.8 2.6 collective-permute-done.67
  315.2 4.4 fusion.12
  328.4 2.8 fusion.37
  331.3 2.8 fusion.34
  334.1 13.0 %collective-permute-done.69 = bf16[384,1024]{1,0:T(8,128)(2,1)S(1)} collective-permute-done((bf16[384,1024]{1,0:T(8,128)(2,1)S(1)}, bf16[384,1024]{1,0:T(8,128)(2,1)S(1)}, u32[]{:S(2)}, u32[]{:S(2)}) %collective-permute-start.69) | collective-permute-done | bytes 786464 | tf_op jit(solution)/shard_map/ppermute | solution.py:66
  351.1 7.5 %shard_map.465 = (f32[384,1024]{1,0:T(8,128)S(1)}, f32[8,1024]{1,0:T(8,128)S(1)}, f32[8,1024]{1,0:T(8,128)S(1)}, f32[1,1024]{1,0:T(1,128)S(1)}, f32[8,1024]{1,0:...) custom-call(bf16[384,8]{1,0:T(8,128)(2,1)S(1)} %copy-done.42, ...), custom_call_target="tpu_custom_call" | custom-call | flops 1000 | bytes 1000 | tf_op jit(solution)/shard_map/pallas_call | solution.py:151
  362.2 5.0 shard_map.466
  367.4 10.9 %shard_map.467 = (bf16[384,4096]{1,0:T(8,128)(2,1)}, f32[1,4096]{1,0:T(1,128)S(1)}) custom-call(bf16[384,1024]{1,0:T(8,128)(2,1)S(1)} %get-tuple-element.465.one_ref, bf16[384,1024]{1,0:T(8,128)(2,1)S(1)} %get-tuple-element.466.two_ref, f32[384,4096]{1,0:T(8,128)} %get-tuple-element.467.refs_0_, bf16[256,2048]{1,0:T(8,128)(2,1)S(1)} %copy-done.31, ...), custom_call_target="tpu_custom_call" | custom-call | flops 1000 | bytes 1000 | tf_op jit(solution)/shard_map/pallas_call | solution.py:151
  380.2 4.7 shard_map.469
  384.9 6.6 shard_map.468
  394.4 11.2 %shard_map.470.refs_1_ = f32[384,1024]{1,0:T(8,128)} custom-call(bf16[1,384,4096]{2,1,0:T(8,128)(2,1)} %bitcast.105, bf16[1024,1024]{1,0:T(8,128)(2,1)} %copy-done.1, bf16[1024,1024]{1,0:T(8,128)(2,1)} %get-tuple-element.371.two_ref, bf16[256,2048]{1,0:T(8,128)(2,1)S(1)} %slice.833.refs_1_.refs_0_, bf16[256,2048]{1,0:T(8,128)(2,1)S(1)} %copy-done.54, ...), custom_call_target="tpu_custom_call" | custom-call | flops 1000 | bytes 1000 | tf_op jit(solution)/shard_map/pallas_call | solution.py:151
  405.7 6.6 shard_map.472
  412.3 5.5 shard_map.471
  418.0 3.4 add_convert_fusion.19
  421.4 2.5 add_convert_fusion.20
  424.0 2.5 add_convert_fusion.21
  430.6 3.4 collective-permute-start.79
  434.0 5.0 shard_map.473.dm_ref
  440.3 21.5 %shard_map.474 = (bf16[3,384,1024]{2,1,0:T(8,128)(2,1)S(1)}, f32[8,1024]{1,0:T(8,128)S(1)}) custom-call(f32[384,3072]{1,0:T(8,128)} %shard_map.458.q_ref.k_ref.v_ref, f32[384,3072]{1,0:T(8,128)} %shard_map.458.q_ref.k_ref.v_ref, f32[384,3072]{1,0:T(8,128)} %shard_map.458.q_ref.k_ref.v_ref, f32[1,1024]{1,0:T(1,128)S(1)} %get-tuple-element.742.qg_ref, ...), custom_call_target="tpu_custom_call" | custom-call | flops 1000 | bytes 1000 | tf_op jit(solution)/shard_map/pallas_call | solution.py:151
  467.7 4.6 shard_map.476
  475.9 2.5 convert_reduce_fusion
  484.3 11.3 %shard_map.477.refs_1_ = f32[384,1024]{1,0:T(8,128)} custom-call(bf16[3,384,1024]{2,1,0:T(8,128)(2,1)} %copy-done.7, bf16[1024,1024]{1,0:T(8,128)(2,1)} %copy-done.1, bf16[1024,1024]{1,0:T(8,128)(2,1)} %get-tuple-element.371.two_ref, bf16[256,1792]{1,0:T(8,128)(2,1)S(1)} %copy-done.33, bf16[256,1792]{1,0:T(8,128)(2,1)S(1)} %copy-done.47, ...), custom_call_target="tpu_custom_call" | custom-call | flops 1000 | bytes 1000 | tf_op jit(solution)/shard_map/pallas_call | solution.py:151
  501.5 6.1 shard_map.479
  507.7 4.5 shard_map.478
  513.3 3.3 collective-permute-start.88
  522.5 2.9 collective-permute-start.89
  525.5 13.6 %collective-permute-done.93 = bf16[32,4096]{1,0:T(8,128)(2,1)S(1)} collective-permute-done((bf16[32,4096]{1,0:T(8,128)(2,1)S(1)}, bf16[32,4096]{1,0:T(8,128)(2,1)S(1)}, u32[]{:S(2)}, u32[]{:S(2)}) %collective-permute-start.93) | collective-permute-done | bytes 262176 | tf_op jit(solution)/shard_map/ppermute | solution.py:66
  540.9 4.9 collective-permute-done.89
  545.8 4.2 collective-permute-done.91
  556.1 2.8 collective-permute-done.98
  558.9 6.5 collective-permute-done.96
  565.4 3.1 collective-permute-done.95
  577.4 10.5 %collective-permute-done.103 = bf16[64,512]{1,0:T(8,128)(2,1)S(1)} collective-permute-done((bf16[64,512]{1,0:T(8,128)(2,1)S(1)}, bf16[64,512]{1,0:T(8,128)(2,1)S(1)}, u32[]{:S(2)}, u32[]{:S(2)}) %collective-permute-start.103) | collective-permute-done | bytes 65568 | tf_op jit(solution)/shard_map/ppermute | solution.py:66
  589.0 4.1 collective-permute-done.104
  598.1 13.6 %collective-permute-done.105 = bf16[32,4096]{1,0:T(8,128)(2,1)S(1)} collective-permute-done((bf16[32,4096]{1,0:T(8,128)(2,1)S(1)}, bf16[32,4096]{1,0:T(8,128)(2,1)S(1)}, u32[]{:S(2)}, u32[]{:S(2)}) %collective-permute-start.105) | collective-permute-done | bytes 262176 | tf_op jit(solution)/shard_map/ppermute | solution.py:66
  619.8 2.5 fusion.164
  638.7 3.5 collective-permute-start.113
  651.9 2.9 fusion.115
  656.8 2.4 fusion.121
  660.3 2.4 fusion.123
  (1004 shorter events, 249.7 us)
Async XLA Ops:
  3.5 22.1 %collective-permute-start = (s32[1,128]{1,0:T(1,128)S(1)}, s32[1,128]{1,0:T(1,128)S(1)}, u32[]{:S(2)}, u32[]{:S(2)}) collective-permute-start(s32[1,128]{1,0:T(1,128)S(1)} %add_bitcast_fusion.5), channel_id=1, source_target_pairs={{0,16},{1,17},{2,18},{3,19},{4,20},{5,21},{6,22},{7,23},{8,24},{9,... | collective-permute-start | bytes 1544 | tf_op jit(solution)/shard_map/ppermute | solution.py:66
  7.5 18.1 %collective-permute-start.1 = (s32[1,128]{1,0:T(1,128)S(1)}, s32[1,128]{1,0:T(1,128)S(1)}, u32[]{:S(2)}, u32[]{:S(2)}) collective-permute-start(s32[1,128]{1,0:T(1,128)S(1)} %add_bitcast_fusion.5), channel_id=1, source_target_pairs={{0,8},{1,9},{2,10},{3,11},{4,12},{5,13},{6,14},{7,15},{8,0},{9,1},... | collective-permute-start | bytes 1544 | tf_op jit(solution)/shard_map/ppermute | solution.py:66
  9.1 16.5 %collective-permute-start.2 = (s32[1,128]{1,0:T(1,128)S(1)}, s32[1,128]{1,0:T(1,128)S(1)}, u32[]{:S(2)}, u32[]{:S(2)}) collective-permute-start(s32[1,128]{1,0:T(1,128)S(1)} %add_bitcast_fusion.5), channel_id=1, source_target_pairs={{0,24},{1,25},{2,26},{3,27},{4,28},{5,29},{6,30},{7,31},{8,16},{9,... | collective-permute-start | bytes 1544 | tf_op jit(solution)/shard_map/ppermute | solution.py:66
  34.1 16.4 %collective-permute-start.12 = (f32[1,2,384]{2,1,0:T(2,128)S(1)}, f32[1,2,384]{2,1,0:T(2,128)S(1)}, u32[]{:S(2)}, u32[]{:S(2)}) collective-permute-start(f32[1,2,384]{2,1,0:T(2,128)S(1)} %maximum_bitcast_fusion), channel_id=1, source_target_pairs={{0,2},{1,3},{2,0},{3,1},{4,6},{5,7},{6,4},{7,5},{8,10},{9,11},{10,... | collective-permute-start | bytes 9224 | tf_op jit(solution)/shard_map/ppermute | solution.py:66
  49.0 18.9 %collective-permute-start.15 = (bf16[128,1792]{1,0:T(8,128)(2,1)}, bf16[128,1792]{1,0:T(8,128)(2,1)}, u32[]{:S(2)}, u32[]{:S(2)}) collective-permute-start(bf16[128,1792]{1,0:T(8,128)(2,1)} %constant_dynamic-update-slice_fusion.6), channel_id=1, source_target_pairs={{0,4},{1,5},{2,6},{3,7},{4,0},{5,1},{6,2},{7,3},{8,12},{9,13},{10,... | collective-permute-start | bytes 1376264 | tf_op jit(solution)/shard_map/ppermute | solution.py:66
  54.3 13.5 %collective-permute-start.16 = (bf16[128,1792]{1,0:T(8,128)(2,1)}, bf16[128,1792]{1,0:T(8,128)(2,1)}, u32[]{:S(2)}, u32[]{:S(2)}) collective-permute-start(bf16[128,1792]{1,0:T(8,128)(2,1)} %constant_dynamic-update-slice_fusion.8), channel_id=1, source_target_pairs={{0,2},{1,3},{2,0},{3,1},{4,6},{5,7},{6,4},{7,5},{8,10},{9,11},{10,... | collective-permute-start | bytes 1376264 | tf_op jit(solution)/shard_map/ppermute | solution.py:66
  72.6 18.0 %collective-permute-start.20 = (bf16[32,5120]{1,0:T(8,128)(2,1)}, bf16[32,5120]{1,0:T(8,128)(2,1)S(1)}, u32[]{:S(2)}, u32[]{:S(2)}) collective-permute-start(bf16[32,5120]{1,0:T(8,128)(2,1)} %pad_maximum_fusion.20), channel_id=1, source_target_pairs={{0,16},{1,17},{2,18},{3,19},{4,20},{5,21},{6,22},{7,23},{8,24},{9,... | collective-permute-start | bytes 983048 | tf_op jit(solution)/shard_map/ppermute | solution.py:66
  78.8 22.0 %collective-permute-start.22 = (bf16[256,1792]{1,0:T(8,128)(2,1)S(1)}, bf16[256,1792]{1,0:T(8,128)(2,1)S(1)}, u32[]{:S(2)}, u32[]{:S(2)}) collective-permute-start(bf16[256,1792]{1,0:T(8,128)(2,1)S(1)} %constant_dynamic-update-slice_fusion.14.refs_5_.refs_4_), channel_id=1, source_target_pairs={{0,4},{1,5},{2,6},{3,7},{4,0},{5,1},{6,2},{7,3},{8,12},{9,13},{10,... | collective-permute-start | bytes 2752520 | tf_op jit(solution)/shard_map/ppermute | solution.py:66
  80.4 21.6 %collective-permute-start.21 = (bf16[256,1792]{1,0:T(8,128)(2,1)S(1)}, bf16[256,1792]{1,0:T(8,128)(2,1)S(1)}, u32[]{:S(2)}, u32[]{:S(2)}) collective-permute-start(bf16[256,1792]{1,0:T(8,128)(2,1)S(1)} %constant_dynamic-update-slice_fusion.12.refs_1_.refs_0_), channel_id=1, source_target_pairs={{0,2},{1,3},{2,0},{3,1},{4,6},{5,7},{6,4},{7,5},{8,10},{9,11},{10,... | collective-permute-start | bytes 2752520 | tf_op jit(solution)/shard_map/ppermute | solution.py:66
  102.2 18.5 %collective-permute-start.27 = (bf16[128,6144]{1,0:T(8,128)(2,1)S(1)}, bf16[128,6144]{1,0:T(8,128)(2,1)S(1)}, u32[]{:S(2)}, u32[]{:S(2)}) collective-permute-start(bf16[128,6144]{1,0:T(8,128)(2,1)S(1)} %get-tuple-element.719), channel_id=1, source_target_pairs={{0,1},{1,0},{2,3},{3,2},{4,5},{5,4},{6,7},{7,6},{8,9},{9,8},{10,11... | collective-permute-start | bytes 4718600 | tf_op jit(solution)/shard_map/ppermute | solution.py:66
  102.4 18.3 %collective-permute-start.25 = (bf16[256,1792]{1,0:T(8,128)(2,1)S(1)}, bf16[256,1792]{1,0:T(8,128)(2,1)S(1)}, u32[]{:S(2)}, u32[]{:S(2)}) collective-permute-start(bf16[256,1792]{1,0:T(8,128)(2,1)S(1)} %collective-permute-done.21.refs_2_.refs_1_), channel_id=1, source_target_pairs={{0,1},{1,0},{2,3},{3,2},{4,5},{5,4},{6,7},{7,6},{8,9},{9,8},{10,11... | collective-permute-start | bytes 2752520 | tf_op jit(solution)/shard_map/ppermute | solution.py:66
  102.9 17.8 %collective-permute-start.26 = (bf16[256,1792]{1,0:T(8,128)(2,1)S(1)}, bf16[256,1792]{1,0:T(8,128)(2,1)S(1)}, u32[]{:S(2)}, u32[]{:S(2)}) collective-permute-start(bf16[256,1792]{1,0:T(8,128)(2,1)S(1)} %collective-permute-done.22.refs_6_.refs_5_), channel_id=1, source_target_pairs={{0,1},{1,0},{2,3},{3,2},{4,5},{5,4},{6,7},{7,6},{8,9},{9,8},{10,11... | collective-permute-start | bytes 2752520 | tf_op jit(solution)/shard_map/ppermute | solution.py:66
  103.0 17.7 %collective-permute-start.28 = (bf16[64,5120]{1,0:T(8,128)(2,1)S(1)}, bf16[64,5120]{1,0:T(8,128)(2,1)S(1)}, u32[]{:S(2)}, u32[]{:S(2)}) collective-permute-start(bf16[64,5120]{1,0:T(8,128)(2,1)S(1)} %constant_dynamic-update-slice_fusion.16), channel_id=1, source_target_pairs={{0,8},{1,9},{2,10},{3,11},{4,12},{5,13},{6,14},{7,15},{8,0},{9,1},... | collective-permute-start | bytes 1966088 | tf_op jit(solution)/shard_map/ppermute | solution.py:66
  124.7 20.2 %collective-permute-start.31 = (bf16[64,3072]{1,0:T(8,128)(2,1)S(1)}, bf16[64,3072]{1,0:T(8,128)(2,1)}, u32[]{:S(2)}, u32[]{:S(2)}) collective-permute-start(bf16[64,3072]{1,0:T(8,128)(2,1)S(1)} %get-tuple-element.733), channel_id=1, source_target_pairs={{0,2},{1,3},{2,0},{3,1},{4,6},{5,7},{6,4},{7,5},{8,10},{9,11},{10,... | collective-permute-start | bytes 1179656 | tf_op jit(solution)/shard_map/ppermute | solution.py:66
  125.2 19.7 %collective-permute-start.32 = (bf16[64,3072]{1,0:T(8,128)(2,1)S(1)}, bf16[64,3072]{1,0:T(8,128)(2,1)}, u32[]{:S(2)}, u32[]{:S(2)}) collective-permute-start(bf16[64,3072]{1,0:T(8,128)(2,1)S(1)} %get-tuple-element.731), channel_id=1, source_target_pairs={{0,4},{1,5},{2,6},{3,7},{4,0},{5,1},{6,2},{7,3},{8,12},{9,13},{10,... | collective-permute-start | bytes 1179656 | tf_op jit(solution)/shard_map/ppermute | solution.py:66
  125.9 23.9 %collective-permute-start.29 = (bf16[128,2560]{1,0:T(8,128)(2,1)S(1)}, bf16[128,2560]{1,0:T(8,128)(2,1)S(1)}, u32[]{:S(2)}, u32[]{:S(2)}) collective-permute-start(bf16[128,2560]{1,0:T(8,128)(2,1)S(1)} %get-tuple-element.382), channel_id=1, source_target_pairs={{0,4},{1,5},{2,6},{3,7},{4,0},{5,1},{6,2},{7,3},{8,12},{9,13},{10,... | collective-permute-start | bytes 1966088 | tf_op jit(solution)/shard_map/ppermute | solution.py:66
  127.5 22.3 %collective-permute-start.30 = (bf16[128,2560]{1,0:T(8,128)(2,1)S(1)}, bf16[128,2560]{1,0:T(8,128)(2,1)S(1)}, u32[]{:S(2)}, u32[]{:S(2)}) collective-permute-start(bf16[128,2560]{1,0:T(8,128)(2,1)S(1)} %get-tuple-element.384), channel_id=1, source_target_pairs={{0,2},{1,3},{2,0},{3,1},{4,6},{5,7},{6,4},{7,5},{8,10},{9,11},{10,... | collective-permute-start | bytes 1966088 | tf_op jit(solution)/shard_map/ppermute | solution.py:66
  129.1 15.8 %collective-permute-start.33 = (bf16[32,4096]{1,0:T(8,128)(2,1)}, bf16[32,4096]{1,0:T(8,128)(2,1)S(1)}, u32[]{:S(2)}, u32[]{:S(2)}) collective-permute-start(bf16[32,4096]{1,0:T(8,128)(2,1)} %slice_bitcast_fusion), channel_id=1, source_target_pairs={{0,16},{1,17},{2,18},{3,19},{4,20},{5,21},{6,22},{7,23},{8,24},{9,... | collective-permute-start | bytes 786440 | tf_op jit(solution)/shard_map/ppermute | solution.py:66
  151.0 17.5 %collective-permute-start.37 = (bf16[32,3072]{1,0:T(8,128)(2,1)S(1)}, bf16[32,3072]{1,0:T(8,128)(2,1)S(1)}, u32[]{:S(2)}, u32[]{:S(2)}) collective-permute-start(bf16[32,3072]{1,0:T(8,128)(2,1)S(1)} %get-tuple-element.776), channel_id=1, source_target_pairs={{0,2},{1,3},{2,0},{3,1},{4,6},{5,7},{6,4},{7,5},{8,10},{9,11},{10,... | collective-permute-start | bytes 589832 | tf_op jit(solution)/shard_map/ppermute | solution.py:66
  152.7 16.5 %collective-permute-start.35 = (bf16[256,512]{1,0:T(8,128)(2,1)S(1)}, bf16[256,512]{1,0:T(8,128)(2,1)S(1)}, u32[]{:S(2)}, u32[]{:S(2)}) collective-permute-start(bf16[256,512]{1,0:T(8,128)(2,1)S(1)} %slice.832.refs_5_.refs_4_), channel_id=1, source_target_pairs={{0,4},{1,5},{2,6},{3,7},{4,0},{5,1},{6,2},{7,3},{8,12},{9,13},{10,... | collective-permute-start | bytes 786440 | tf_op jit(solution)/shard_map/ppermute | solution.py:66
  153.4 15.8 %collective-permute-start.34 = (bf16[256,512]{1,0:T(8,128)(2,1)S(1)}, bf16[256,512]{1,0:T(8,128)(2,1)S(1)}, u32[]{:S(2)}, u32[]{:S(2)}) collective-permute-start(bf16[256,512]{1,0:T(8,128)(2,1)S(1)} %slice.831.refs_1_.refs_0_), channel_id=1, source_target_pairs={{0,2},{1,3},{2,0},{3,1},{4,6},{5,7},{6,4},{7,5},{8,10},{9,11},{10,... | collective-permute-start | bytes 786440 | tf_op jit(solution)/shard_map/ppermute | solution.py:66
  154.0 15.2 %collective-permute-start.38 = (bf16[128,1024]{1,0:T(8,128)(2,1)S(1)}, bf16[128,1024]{1,0:T(8,128)(2,1)S(1)}, u32[]{:S(2)}, u32[]{:S(2)}) collective-permute-start(bf16[128,1024]{1,0:T(8,128)(2,1)S(1)} %copy-done.163), channel_id=1, source_target_pairs={{0,4},{1,5},{2,6},{3,7},{4,0},{5,1},{6,2},{7,3},{8,12},{9,13},{10,... | collective-permute-start | bytes 786440 | tf_op jit(solution)/shard_map/ppermute | solution.py:66
  177.5 24.4 %collective-permute-start.45 = (bf16[256,2048]{1,0:T(8,128)(2,1)S(1)}, bf16[256,2048]{1,0:T(8,128)(2,1)S(1)}, u32[]{:S(2)}, u32[]{:S(2)}) collective-permute-start(bf16[256,2048]{1,0:T(8,128)(2,1)S(1)} %slice.833.refs_1_.refs_0_), channel_id=1, source_target_pairs={{0,2},{1,3},{2,0},{3,1},{4,6},{5,7},{6,4},{7,5},{8,10},{9,11},{10,... | collective-permute-start | bytes 3145736 | tf_op jit(solution)/shard_map/ppermute | solution.py:66
  178.7 25.6 %collective-permute-start.47 = (bf16[256,2048]{1,0:T(8,128)(2,1)S(1)}, bf16[256,2048]{1,0:T(8,128)(2,1)S(1)}, u32[]{:S(2)}, u32[]{:S(2)}) collective-permute-start(bf16[256,2048]{1,0:T(8,128)(2,1)S(1)} %slice.833.refs_1_.refs_0_), channel_id=1, source_target_pairs={{0,1},{1,0},{2,3},{3,2},{4,5},{5,4},{6,7},{7,6},{8,9},{9,8},{10,11... | collective-permute-start | bytes 3145736 | tf_op jit(solution)/shard_map/ppermute | solution.py:66
  178.7 25.6 %collective-permute-start.46 = (bf16[256,2048]{1,0:T(8,128)(2,1)S(1)}, bf16[256,2048]{1,0:T(8,128)(2,1)S(1)}, u32[]{:S(2)}, u32[]{:S(2)}) collective-permute-start(bf16[256,2048]{1,0:T(8,128)(2,1)S(1)} %slice.834.refs_5_.refs_4_), channel_id=1, source_target_pairs={{0,4},{1,5},{2,6},{3,7},{4,0},{5,1},{6,2},{7,3},{8,12},{9,13},{10,... | collective-permute-start | bytes 3145736 | tf_op jit(solution)/shard_map/ppermute | solution.py:66
  179.9 24.4 %collective-permute-start.48 = (bf16[256,2048]{1,0:T(8,128)(2,1)S(1)}, bf16[256,2048]{1,0:T(8,128)(2,1)S(1)}, u32[]{:S(2)}, u32[]{:S(2)}) collective-permute-start(bf16[256,2048]{1,0:T(8,128)(2,1)S(1)} %slice.834.refs_5_.refs_4_), channel_id=1, source_target_pairs={{0,1},{1,0},{2,3},{3,2},{4,5},{5,4},{6,7},{7,6},{8,9},{9,8},{10,11... | collective-permute-start | bytes 3145736 | tf_op jit(solution)/shard_map/ppermute | solution.py:66
  208.7 16.0 %collective-permute-start.52 = (bf16[128,2048]{1,0:T(8,128)(2,1)S(1)}, bf16[128,2048]{1,0:T(8,128)(2,1)S(1)}, u32[]{:S(2)}, u32[]{:S(2)}) collective-permute-start(bf16[128,2048]{1,0:T(8,128)(2,1)S(1)} %get-tuple-element.436), channel_id=1, source_target_pairs={{0,4},{1,5},{2,6},{3,7},{4,0},{5,1},{6,2},{7,3},{8,12},{9,13},{10,... | collective-permute-start | bytes 1572872 | tf_op jit(solution)/shard_map/ppermute | solution.py:66
  209.9 14.8 %collective-permute-start.53 = (bf16[128,2048]{1,0:T(8,128)(2,1)S(1)}, bf16[128,2048]{1,0:T(8,128)(2,1)S(1)}, u32[]{:S(2)}, u32[]{:S(2)}) collective-permute-start(bf16[128,2048]{1,0:T(8,128)(2,1)S(1)} %get-tuple-element.438), channel_id=1, source_target_pairs={{0,2},{1,3},{2,0},{3,1},{4,6},{5,7},{6,4},{7,5},{8,10},{9,11},{10,... | collective-permute-start | bytes 1572872 | tf_op jit(solution)/shard_map/ppermute | solution.py:66
  225.6 28.7 %collective-permute-start.55 = (bf16[256,2048]{1,0:T(8,128)(2,1)S(1)}, bf16[256,2048]{1,0:T(8,128)(2,1)S(1)}, u32[]{:S(2)}, u32[]{:S(2)}) collective-permute-start(bf16[256,2048]{1,0:T(8,128)(2,1)S(1)} %constant_dynamic-update-slice_fusion.30.refs_5_), channel_id=1, source_target_pairs={{0,4},{1,5},{2,6},{3,7},{4,0},{5,1},{6,2},{7,3},{8,12},{9,13},{10,... | collective-permute-start | bytes 3145736 | tf_op jit(solution)/shard_map/ppermute | solution.py:66
  226.3 28.1 %collective-permute-start.57 = (bf16[256,2048]{1,0:T(8,128)(2,1)S(1)}, bf16[256,2048]{1,0:T(8,128)(2,1)S(1)}, u32[]{:S(2)}, u32[]{:S(2)}) collective-permute-start(bf16[256,2048]{1,0:T(8,128)(2,1)S(1)} %constant_dynamic-update-slice_fusion.30.refs_5_), channel_id=1, source_target_pairs={{0,1},{1,0},{2,3},{3,2},{4,5},{5,4},{6,7},{7,6},{8,9},{9,8},{10,11... | collective-permute-start | bytes 3145736 | tf_op jit(solution)/shard_map/ppermute | solution.py:66
  226.7 27.7 %collective-permute-start.54 = (bf16[256,2048]{1,0:T(8,128)(2,1)S(1)}, bf16[256,2048]{1,0:T(8,128)(2,1)S(1)}, u32[]{:S(2)}, u32[]{:S(2)}) collective-permute-start(bf16[256,2048]{1,0:T(8,128)(2,1)S(1)} %constant_dynamic-update-slice_fusion.28.refs_1_), channel_id=1, source_target_pairs={{0,2},{1,3},{2,0},{3,1},{4,6},{5,7},{6,4},{7,5},{8,10},{9,11},{10,... | collective-permute-start | bytes 3145736 | tf_op jit(solution)/shard_map/ppermute | solution.py:66
  227.7 26.6 %collective-permute-start.56 = (bf16[256,2048]{1,0:T(8,128)(2,1)S(1)}, bf16[256,2048]{1,0:T(8,128)(2,1)S(1)}, u32[]{:S(2)}, u32[]{:S(2)}) collective-permute-start(bf16[256,2048]{1,0:T(8,128)(2,1)S(1)} %constant_dynamic-update-slice_fusion.28.refs_1_), channel_id=1, source_target_pairs={{0,1},{1,0},{2,3},{3,2},{4,5},{5,4},{6,7},{7,6},{8,9},{9,8},{10,11... | collective-permute-start | bytes 3145736 | tf_op jit(solution)/shard_map/ppermute | solution.py:66
  228.0 26.3 %collective-permute-start.58 = (bf16[256,1024]{1,0:T(8,128)(2,1)S(1)}, bf16[256,1024]{1,0:T(8,128)(2,1)S(1)}, u32[]{:S(2)}, u32[]{:S(2)}) collective-permute-start(bf16[256,1024]{1,0:T(8,128)(2,1)S(1)} %constant_dynamic-update-slice_fusion.32), channel_id=1, source_target_pairs={{0,16},{1,17},{2,18},{3,19},{4,20},{5,21},{6,22},{7,23},{8,24},{9,... | collective-permute-start | bytes 1572872 | tf_op jit(solution)/shard_map/ppermute | solution.py:66
  255.1 25.2 %collective-permute-start.61 = (bf16[512,1024]{1,0:T(8,128)(2,1)S(1)}, bf16[512,1024]{1,0:T(8,128)(2,1)S(1)}, u32[]{:S(2)}, u32[]{:S(2)}) collective-permute-start(bf16[512,1024]{1,0:T(8,128)(2,1)S(1)} %constant_dynamic-update-slice_fusion.34), channel_id=1, source_target_pairs={{0,8},{1,9},{2,10},{3,11},{4,12},{5,13},{6,14},{7,15},{8,0},{9,1},... | collective-permute-start | bytes 3145736 | tf_op jit(solution)/shard_map/ppermute | solution.py:66
  281.4 20.0 %collective-permute-start.63 = (bf16[384,1024]{1,0:T(8,128)(2,1)S(1)}, bf16[384,1024]{1,0:T(8,128)(2,1)S(1)}, u32[]{:S(2)}, u32[]{:S(2)}) collective-permute-start(bf16[384,1024]{1,0:T(8,128)(2,1)S(1)} %get-tuple-element.456), channel_id=1, source_target_pairs={{0,2},{1,3},{2,0},{3,1},{4,6},{5,7},{6,4},{7,5},{8,10},{9,11},{10,... | collective-permute-start | bytes 2359304 | tf_op jit(solution)/shard_map/ppermute | solution.py:66
  327.4 19.6 %collective-permute-start.69 = (bf16[384,1024]{1,0:T(8,128)(2,1)S(1)}, bf16[384,1024]{1,0:T(8,128)(2,1)S(1)}, u32[]{:S(2)}, u32[]{:S(2)}) collective-permute-start(bf16[384,1024]{1,0:T(8,128)(2,1)S(1)} %add_convert_fusion.1), channel_id=1, source_target_pairs={{0,2},{1,3},{2,0},{3,1},{4,6},{5,7},{6,4},{7,5},{8,10},{9,11},{10,... | collective-permute-start | bytes 2359304 | tf_op jit(solution)/shard_map/ppermute | solution.py:66
  391.5 14.1 %collective-permute-start.71 = (bf16[512,4096]{1,0:T(8,128)(2,1)}, bf16[512,4096]{1,0:T(8,128)(2,1)}, u32[]{:S(2)}, u32[]{:S(2)}) collective-permute-start(bf16[512,4096]{1,0:T(8,128)(2,1)} %shard_map.469), channel_id=1, source_target_pairs={{0,1},{1,0},{2,3},{3,2},{4,5},{5,4},{6,7},{7,6},{8,9},{9,8},{10,11... | collective-permute-start | bytes 12582920 | tf_op jit(solution)/shard_map/ppermute | solution.py:66
  392.0 25.9 %collective-permute-start.74 = (bf16[512,1024]{1,0:T(8,128)(2,1)}, bf16[512,1024]{1,0:T(8,128)(2,1)}, u32[]{:S(2)}, u32[]{:S(2)}) collective-permute-start(bf16[512,1024]{1,0:T(8,128)(2,1)} %fusion.34), channel_id=1, source_target_pairs={{0,8},{1,9},{2,10},{3,11},{4,12},{5,13},{6,14},{7,15},{8,0},{9,1},... | collective-permute-start | bytes 3145736 | tf_op jit(solution)/shard_map/ppermute | solution.py:66
  392.3 25.7 %collective-permute-start.72 = (bf16[256,2048]{1,0:T(8,128)(2,1)}, bf16[256,2048]{1,0:T(8,128)(2,1)}, u32[]{:S(2)}, u32[]{:S(2)}) collective-permute-start(bf16[256,2048]{1,0:T(8,128)(2,1)} %get-tuple-element.481), channel_id=1, source_target_pairs={{0,2},{1,3},{2,0},{3,1},{4,6},{5,7},{6,4},{7,5},{8,10},{9,11},{10,... | collective-permute-start | bytes 3145736 | tf_op jit(solution)/shard_map/ppermute | solution.py:66
  393.3 24.7 %collective-permute-start.73 = (bf16[256,2048]{1,0:T(8,128)(2,1)S(1)}, bf16[256,2048]{1,0:T(8,128)(2,1)}, u32[]{:S(2)}, u32[]{:S(2)}) collective-permute-start(bf16[256,2048]{1,0:T(8,128)(2,1)S(1)} %get-tuple-element.482), channel_id=1, source_target_pairs={{0,4},{1,5},{2,6},{3,7},{4,0},{5,1},{6,2},{7,3},{8,12},{9,13},{10,... | collective-permute-start | bytes 3145736 | tf_op jit(solution)/shard_map/ppermute | solution.py:66
  426.5 36.3 %collective-permute-start.77 = (bf16[256,2048]{1,0:T(8,128)(2,1)}, bf16[256,2048]{1,0:T(8,128)(2,1)S(1)}, u32[]{:S(2)}, u32[]{:S(2)}) collective-permute-start(bf16[256,2048]{1,0:T(8,128)(2,1)} %get-tuple-element.503), channel_id=1, source_target_pairs={{0,2},{1,3},{2,0},{3,1},{4,6},{5,7},{6,4},{7,5},{8,10},{9,11},{10,... | collective-permute-start | bytes 3145736 | tf_op jit(solution)/shard_map/ppermute | solution.py:66
  427.5 35.3 %collective-permute-start.78 = (bf16[256,2048]{1,0:T(8,128)(2,1)S(1)}, bf16[256,2048]{1,0:T(8,128)(2,1)S(1)}, u32[]{:S(2)}, u32[]{:S(2)}) collective-permute-start(bf16[256,2048]{1,0:T(8,128)(2,1)S(1)} %copy-done.117), channel_id=1, source_target_pairs={{0,4},{1,5},{2,6},{3,7},{4,0},{5,1},{6,2},{7,3},{8,12},{9,13},{10,... | collective-permute-start | bytes 3145736 | tf_op jit(solution)/shard_map/ppermute | solution.py:66
  428.4 34.4 %collective-permute-start.75 = (bf16[128,2048]{1,0:T(8,128)(2,1)}, bf16[128,2048]{1,0:T(8,128)(2,1)S(1)}, u32[]{:S(2)}, u32[]{:S(2)}) collective-permute-start(bf16[128,2048]{1,0:T(8,128)(2,1)} %get-tuple-element.501), channel_id=1, source_target_pairs={{0,4},{1,5},{2,6},{3,7},{4,0},{5,1},{6,2},{7,3},{8,12},{9,13},{10,... | collective-permute-start | bytes 1572872 | tf_op jit(solution)/shard_map/ppermute | solution.py:66
  429.6 33.2 %collective-permute-start.76 = (bf16[128,2048]{1,0:T(8,128)(2,1)}, bf16[128,2048]{1,0:T(8,128)(2,1)S(1)}, u32[]{:S(2)}, u32[]{:S(2)}) collective-permute-start(bf16[128,2048]{1,0:T(8,128)(2,1)} %get-tuple-element.502), channel_id=1, source_target_pairs={{0,2},{1,3},{2,0},{3,1},{4,6},{5,7},{6,4},{7,5},{8,10},{9,11},{10,... | collective-permute-start | bytes 1572872 | tf_op jit(solution)/shard_map/ppermute | solution.py:66
  430.6 32.3 %collective-permute-start.79 = (bf16[256,1024]{1,0:T(8,128)(2,1)}, bf16[256,1024]{1,0:T(8,128)(2,1)S(1)}, u32[]{:S(2)}, u32[]{:S(2)}) collective-permute-start(bf16[256,1024]{1,0:T(8,128)(2,1)} %get-tuple-element.505), channel_id=1, source_target_pairs={{0,16},{1,17},{2,18},{3,19},{4,20},{5,21},{6,22},{7,23},{8,24},{9,... | collective-permute-start | bytes 1572872 | tf_op jit(solution)/shard_map/ppermute | solution.py:66
  473.4 25.5 %collective-permute-start.81 = (bf16[512,3072]{1,0:T(8,128)(2,1)}, bf16[512,3072]{1,0:T(8,128)(2,1)}, u32[]{:S(2)}, u32[]{:S(2)}) collective-permute-start(bf16[512,3072]{1,0:T(8,128)(2,1)} %shard_map.476), channel_id=1, source_target_pairs={{0,1},{1,0},{2,3},{3,2},{4,5},{5,4},{6,7},{7,6},{8,9},{9,8},{10,11... | collective-permute-start | bytes 9437192 | tf_op jit(solution)/shard_map/ppermute | solution.py:66
  479.1 19.7 %collective-permute-start.82 = (bf16[128,2048]{1,0:T(8,128)(2,1)}, bf16[128,2048]{1,0:T(8,128)(2,1)S(1)}, u32[]{:S(2)}, u32[]{:S(2)}) collective-permute-start(bf16[128,2048]{1,0:T(8,128)(2,1)} %add_convert_fusion.18), channel_id=1, source_target_pairs={{0,4},{1,5},{2,6},{3,7},{4,0},{5,1},{6,2},{7,3},{8,12},{9,13},{10,... | collective-permute-start | bytes 1572872 | tf_op jit(solution)/shard_map/ppermute | solution.py:66
  480.0 18.9 %collective-permute-start.83 = (bf16[128,2048]{1,0:T(8,128)(2,1)}, bf16[128,2048]{1,0:T(8,128)(2,1)S(1)}, u32[]{:S(2)}, u32[]{:S(2)}) collective-permute-start(bf16[128,2048]{1,0:T(8,128)(2,1)} %add_convert_fusion.17), channel_id=1, source_target_pairs={{0,2},{1,3},{2,0},{3,1},{4,6},{5,7},{6,4},{7,5},{8,10},{9,11},{10,... | collective-permute-start | bytes 1572872 | tf_op jit(solution)/shard_map/ppermute | solution.py:66
  480.9 17.9 %collective-permute-start.84 = (bf16[64,4096]{1,0:T(8,128)(2,1)}, bf16[64,4096]{1,0:T(8,128)(2,1)S(1)}, u32[]{:S(2)}, u32[]{:S(2)}) collective-permute-start(bf16[64,4096]{1,0:T(8,128)(2,1)} %pad_maximum_fusion.13), channel_id=1, source_target_pairs={{0,8},{1,9},{2,10},{3,11},{4,12},{5,13},{6,14},{7,15},{8,0},{9,1},... | collective-permute-start | bytes 1572872 | tf_op jit(solution)/shard_map/ppermute | solution.py:66
  482.9 15.9 %collective-permute-start.85 = (bf16[128,1024]{1,0:T(8,128)(2,1)S(1)}, bf16[128,1024]{1,0:T(8,128)(2,1)S(1)}, u32[]{:S(2)}, u32[]{:S(2)}) collective-permute-start(bf16[128,1024]{1,0:T(8,128)(2,1)S(1)} %get-tuple-element.764), channel_id=1, source_target_pairs={{0,4},{1,5},{2,6},{3,7},{4,0},{5,1},{6,2},{7,3},{8,12},{9,13},{10,... | collective-permute-start | bytes 786440 | tf_op jit(solution)/shard_map/ppermute | solution.py:66
  518.8 31.2 %collective-permute-start.86 = (bf16[256,2048]{1,0:T(8,128)(2,1)S(1)}, bf16[256,2048]{1,0:T(8,128)(2,1)S(1)}, u32[]{:S(2)}, u32[]{:S(2)}) collective-permute-start(bf16[256,2048]{1,0:T(8,128)(2,1)S(1)} %pad_maximum_fusion.4), channel_id=1, source_target_pairs={{0,2},{1,3},{2,0},{3,1},{4,6},{5,7},{6,4},{7,5},{8,10},{9,11},{10,... | collective-permute-start | bytes 3145736 | tf_op jit(solution)/shard_map/ppermute | solution.py:66
  520.0 30.0 %collective-permute-start.87 = (bf16[256,2048]{1,0:T(8,128)(2,1)S(1)}, bf16[256,2048]{1,0:T(8,128)(2,1)S(1)}, u32[]{:S(2)}, u32[]{:S(2)}) collective-permute-start(bf16[256,2048]{1,0:T(8,128)(2,1)S(1)} %pad_maximum_fusion.5), channel_id=1, source_target_pairs={{0,4},{1,5},{2,6},{3,7},{4,0},{5,1},{6,2},{7,3},{8,12},{9,13},{10,... | collective-permute-start | bytes 3145736 | tf_op jit(solution)/shard_map/ppermute | solution.py:66
  520.9 25.0 %collective-permute-start.92 = (bf16[64,4096]{1,0:T(8,128)(2,1)S(1)}, bf16[64,4096]{1,0:T(8,128)(2,1)S(1)}, u32[]{:S(2)}, u32[]{:S(2)}) collective-permute-start(bf16[64,4096]{1,0:T(8,128)(2,1)S(1)} %pad_maximum_fusion.15), channel_id=1, source_target_pairs={{0,8},{1,9},{2,10},{3,11},{4,12},{5,13},{6,14},{7,15},{8,0},{9,1},... | collective-permute-start | bytes 1572872 | tf_op jit(solution)/shard_map/ppermute | solution.py:66
  522.2 16.9 %collective-permute-start.93 = (bf16[32,4096]{1,0:T(8,128)(2,1)S(1)}, bf16[32,4096]{1,0:T(8,128)(2,1)S(1)}, u32[]{:S(2)}, u32[]{:S(2)}) collective-permute-start(bf16[32,4096]{1,0:T(8,128)(2,1)S(1)} %copy-done.200), channel_id=1, source_target_pairs={{0,16},{1,17},{2,18},{3,19},{4,20},{5,21},{6,22},{7,23},{8,24},{9,... | collective-permute-start | bytes 786440 | tf_op jit(solution)/shard_map/ppermute | solution.py:66
  522.5 23.4 %collective-permute-start.89 = (bf16[16,8192]{1,0:T(8,128)(2,1)S(1)}, bf16[16,8192]{1,0:T(8,128)(2,1)S(1)}, u32[]{:S(2)}, u32[]{:S(2)}) collective-permute-start(bf16[16,8192]{1,0:T(8,128)(2,1)S(1)} %constant_dynamic-update-slice_fusion.50), channel_id=1, source_target_pairs={{0,8},{1,9},{2,10},{3,11},{4,12},{5,13},{6,14},{7,15},{8,0},{9,1},... | collective-permute-start | bytes 786440 | tf_op jit(solution)/shard_map/ppermute | solution.py:66
  550.1 15.2 %collective-permute-start.97 = (bf16[32,5120]{1,0:T(8,128)(2,1)S(1)}, bf16[32,5120]{1,0:T(8,128)(2,1)S(1)}, u32[]{:S(2)}, u32[]{:S(2)}) collective-permute-start(bf16[32,5120]{1,0:T(8,128)(2,1)S(1)} %slice.891), channel_id=1, source_target_pairs={{0,4},{1,5},{2,6},{3,7},{4,0},{5,1},{6,2},{7,3},{8,12},{9,13},{10,... | collective-permute-start | bytes 983048 | tf_op jit(solution)/shard_map/ppermute | solution.py:66
  553.4 15.1 %collective-permute-start.95 = (bf16[128,2048]{1,0:T(8,128)(2,1)S(1)}, bf16[128,2048]{1,0:T(8,128)(2,1)S(1)}, u32[]{:S(2)}, u32[]{:S(2)}) collective-permute-start(bf16[128,2048]{1,0:T(8,128)(2,1)S(1)} %get-tuple-element.722), channel_id=1, source_target_pairs={{0,2},{1,3},{2,0},{3,1},{4,6},{5,7},{6,4},{7,5},{8,10},{9,11},{10,... | collective-permute-start | bytes 1572872 | tf_op jit(solution)/shard_map/ppermute | solution.py:66
  554.8 15.9 %collective-permute-start.94 = (bf16[128,2048]{1,0:T(8,128)(2,1)S(1)}, bf16[128,2048]{1,0:T(8,128)(2,1)S(1)}, u32[]{:S(2)}, u32[]{:S(2)}) collective-permute-start(bf16[128,2048]{1,0:T(8,128)(2,1)S(1)} %get-tuple-element.724), channel_id=1, source_target_pairs={{0,4},{1,5},{2,6},{3,7},{4,0},{5,1},{6,2},{7,3},{8,12},{9,13},{10,... | collective-permute-start | bytes 1572872 | tf_op jit(solution)/shard_map/ppermute | solution.py:66
  571.8 21.3 %collective-permute-start.101 = (bf16[64,5120]{1,0:T(8,128)(2,1)S(1)}, bf16[64,5120]{1,0:T(8,128)(2,1)S(1)}, u32[]{:S(2)}, u32[]{:S(2)}) collective-permute-start(bf16[64,5120]{1,0:T(8,128)(2,1)S(1)} %constant_dynamic-update-slice_fusion.56), channel_id=1, source_target_pairs={{0,2},{1,3},{2,0},{3,1},{4,6},{5,7},{6,4},{7,5},{8,10},{9,11},{10,... | collective-permute-start | bytes 1966088 | tf_op jit(solution)/shard_map/ppermute | solution.py:66
  573.0 20.1 %collective-permute-start.100 = (bf16[64,3072]{1,0:T(8,128)(2,1)S(1)}, bf16[64,3072]{1,0:T(8,128)(2,1)S(1)}, u32[]{:S(2)}, u32[]{:S(2)}) collective-permute-start(bf16[64,3072]{1,0:T(8,128)(2,1)S(1)} %constant_dynamic-update-slice_fusion.54), channel_id=1, source_target_pairs={{0,4},{1,5},{2,6},{3,7},{4,0},{5,1},{6,2},{7,3},{8,12},{9,13},{10,... | collective-permute-start | bytes 1179656 | tf_op jit(solution)/shard_map/ppermute | solution.py:66
  574.7 18.4 %collective-permute-start.99 = (bf16[64,4096]{1,0:T(8,128)(2,1)S(1)}, bf16[64,4096]{1,0:T(8,128)(2,1)S(1)}, u32[]{:S(2)}, u32[]{:S(2)}) collective-permute-start(bf16[64,4096]{1,0:T(8,128)(2,1)S(1)} %pad_maximum_fusion.17), channel_id=1, source_target_pairs={{0,8},{1,9},{2,10},{3,11},{4,12},{5,13},{6,14},{7,15},{8,0},{9,1},... | collective-permute-start | bytes 1572872 | tf_op jit(solution)/shard_map/ppermute | solution.py:66
  595.7 26.6 %collective-permute-start.106 = (bf16[128,5120]{1,0:T(8,128)(2,1)}, bf16[128,5120]{1,0:T(8,128)(2,1)}, u32[]{:S(2)}, u32[]{:S(2)}) collective-permute-start(bf16[128,5120]{1,0:T(8,128)(2,1)} %pad_maximum_fusion.3), channel_id=1, source_target_pairs={{0,1},{1,0},{2,3},{3,2},{4,5},{5,4},{6,7},{7,6},{8,9},{9,8},{10,11... | collective-permute-start | bytes 3932168 | tf_op jit(solution)/shard_map/ppermute | solution.py:66
  596.6 18.1 %collective-permute-start.107 = (bf16[128,3072]{1,0:T(8,128)(2,1)S(1)}, bf16[128,3072]{1,0:T(8,128)(2,1)}, u32[]{:S(2)}, u32[]{:S(2)}) collective-permute-start(bf16[128,3072]{1,0:T(8,128)(2,1)S(1)} %pad_maximum_fusion.12), channel_id=1, source_target_pairs={{0,1},{1,0},{2,3},{3,2},{4,5},{5,4},{6,7},{7,6},{8,9},{9,8},{10,11... | collective-permute-start | bytes 2359304 | tf_op jit(solution)/shard_map/ppermute | solution.py:66
  597.2 14.5 %collective-permute-start.105 = (bf16[32,4096]{1,0:T(8,128)(2,1)S(1)}, bf16[32,4096]{1,0:T(8,128)(2,1)S(1)}, u32[]{:S(2)}, u32[]{:S(2)}) collective-permute-start(bf16[32,4096]{1,0:T(8,128)(2,1)S(1)} %add_convert_fusion.30), channel_id=1, source_target_pairs={{0,16},{1,17},{2,18},{3,19},{4,20},{5,21},{6,22},{7,23},{8,24},{9,... | collective-permute-start | bytes 786440 | tf_op jit(solution)/shard_map/ppermute | solution.py:66
  (296 other events, 2760.6 us)

commit v4 on v3

--- a/solution.py
+++ b/solution.py
@@ -118,10 +118,8 @@
 
 
 def sum_all(value, bits, devices):
-    for at in range(0, len(bits), 2):
-        masks = bits[at : at + 2]
-        if len(masks) == 2:
-            masks = masks + [masks[0] ^ masks[1]]
+    for at in range(0, len(bits), 3):
+        masks = place_masks(bits[at : at + 3])[1:]
         value = value + sum(swapped(value, mask, devices) for mask in masks)
     return value
 
@@ -169,16 +167,21 @@
 
 
 def columns_of(sets):
-    return [blocks[0].shape[1] if used is None else used for blocks, used in sets]
+    return [blocks[0].shape[1] if used is None else used[1] - used[0] for blocks, used in sets]
+
+
+def starts_of(sets):
+    return [0 if used is None else used[0] for _, used in sets]
 
 
 def two_sets(sets, first, span):
+    one, two = [start // span for start in starts_of(sets)]
     specs = [
-        pl.BlockSpec((block.shape[0], span), lambda j: (0, jnp.minimum(j, first - 1)))
+        pl.BlockSpec((block.shape[0], span), lambda j: (0, one + jnp.minimum(j, first - 1)))
         for block in sets[0][0]
     ]
     specs += [
-        pl.BlockSpec((block.shape[0], span), lambda j: (0, jnp.maximum(j - first, 0)))
+        pl.BlockSpec((block.shape[0], span), lambda j: (0, two + jnp.maximum(j - first, 0)))
         for block in sets[1][0]
     ]
     return specs
@@ -203,7 +206,7 @@
 def times_sets(left, sets, bias=None, hidden=None, bend=False):
     tokens = left[0].shape[0]
     columns = columns_of(sets)
-    span = span_of(*columns)
+    span = span_of(*columns, *starts_of(sets))
     first, steps = columns[0] // span, sum(columns) // span
     specs = two_sets(sets, first, span)
     count = len(sets[0][0])
@@ -260,7 +263,7 @@
 def back_sets(right, sets, perms, bias=None, exact=False, out=F32):
     tokens = right.shape[1]
     columns = columns_of(sets)
-    span = span_of(right.shape[2], *columns)
+    span = span_of(right.shape[2], *columns, *starts_of(sets))
     first, steps = columns[0] // span, sum(columns) // span
     specs = two_sets(sets, first, span)
     count = len(sets[0][0])
@@ -556,12 +559,13 @@
     return run(body, (tokens // TOKENS,), given, specs, outs, out_specs)
 
 
-def slim_back(d_resid, token_hot, arrays, plan, perm, n_embed):
-    width, wide = perm.shape[0], token_hot.shape[1]
+def slim_back(d_resid, token_hot, arrays, plan, perms, n_embed):
+    width, wide = perms[0].shape[0], token_hot.shape[1]
+    half = wide // 2
     rows = sum(arrays[which].shape[1] // width for which, _ in plan)
     room = rows + (-rows % 16)
 
-    def body(d_ref, hot_ref, perm_ref, *refs):
+    def body(d_ref, hot_ref, one_ref, two_ref, *refs):
         out_ref, gains = refs[-2], refs[-1]
         gains[...] = jnp.zeros_like(gains)
         at = 0
@@ -575,9 +579,11 @@
         total = matmul_tn(d_ref[...], hot_ref[...])
         chosen = jnp.where(place == own, 1.0, 0.0).astype(BF16)
         total = total + matmul_tn(gains[...].astype(BF16), chosen)
-        out_ref[...] = matmul(perm_ref[...], total.astype(BF16)).astype(BF16)
-
-    given = [d_resid, token_hot, perm] + list(arrays)
+        low = total.astype(BF16)
+        out_ref[:, :half] = matmul(one_ref[...], low[:, :half]).astype(BF16)
+        out_ref[:, half:] = matmul(two_ref[...], low[:, half:]).astype(BF16)
+
+    given = [d_resid, token_hot] + list(perms) + list(arrays)
     outs = jax.ShapeDtypeStruct((width, wide), BF16)
     specs = [whole(value) for value in given]
     scratch = [pltpu.VMEM((room, width), F32)]
@@ -716,13 +722,12 @@
     parts = spread(stack(parts), groups[1], devices)
     qkv_one = widen(stack(qkv_one), bits_z[1:], devices)
     qkv_two = widen(stack(qkv_two), bits_z[1:], devices)
-    perm_one, perm_one_t = hot_rows(source_rows(path_one + [1], me, rows))
-    perm_two, perm_two_t = hot_rows(source_rows(path_two + [1], me, rows))
-    parts, qkv_one, qkv_two, up = tie(parts, qkv_one, qkv_two, up)
+    parts, qkv_one, qkv_two, up, head16 = tie(parts, qkv_one, qkv_two, up, head16)
     for group in groups[2:]:
         parts = spread(stack(parts), group, devices)
     qkv_one, qkv_two = widen(stack(qkv_one), one_y, devices), widen(stack(qkv_two), two_x, devices)
-    parts, perm_one, perm_two, up = tie(parts, perm_one, perm_two, up)
+    head16 = widen(head16, bits_y, devices)
+    parts, up, me = tie(parts, up, me)
 
     facts = stack(parts)
     total_count = jnp.sum(facts[:, MAXIMG]).astype(F32)
@@ -739,7 +744,9 @@
     first = matmul(act_first, ada16[:, : cuts[0]]).astype(BF16)
     first = lend(first, [1], devices)
     row_info = widen(row_info, bits_x, devices)
-    first, row_info = tie(first, row_info)
+    first, row_info, me, head16 = tie(first, row_info, me, head16)
+    perm_one, perm_one_t = hot_rows(source_rows(path_one + [1], me, rows))
+    perm_two, perm_two_t = hot_rows(source_rows(path_two + [1], me, rows))
     for mask in reversed(bits_z):
         first = lend(added(*first), [mask], devices)
         (first,) = tie(first)
@@ -777,20 +784,20 @@
         ],
         axis=1,
     )
-    first, one_far, two_far, one_near_c, two_near_c, mods_rest, token_hot, mask_rows = tie(
-        first, one_far, two_far, one_near_c, two_near_c, mods_rest, token_hot, mask_rows
+    first, one_far, two_far, one_near_c, two_near_c, mods_rest, up, token_hot, mask_rows = tie(
+        first, one_far, two_far, one_near_c, two_near_c, mods_rest, up, token_hot, mask_rows
     )
     row_info = jnp.swapaxes(stack(row_info), 0, 1).reshape(2, -1)
 
     one_far_c, two_far_c = swap(one_far, 1), swap(two_far, 1)
     mods_rest = lend(mods_rest, [1], devices)
-    one_far_c, two_far_c, mods_rest, first, down, up = tie(
-        one_far_c, two_far_c, mods_rest, first, down, up
-    )
-
     half_up = half_ff + top
     up = stack(up)
     up_one, up_two = widen(up[:, :half_up], one_y, devices), widen(up[:, half_up:], two_x, devices)
+    one_far_c, two_far_c, mods_rest, first, down = tie(
+        one_far_c, two_far_c, mods_rest, first, down
+    )
+
     mods_rest = added(*mods_rest)
     cut = cuts[1] - cuts[0]
     mod_one = lend(mods_rest[:, :cut], bits_x, devices)
@@ -811,7 +818,7 @@
     first = first + ada_bias[:, : cuts[0]]
     mods = [first[:, :width], first[:, width:]]
     u_one, u_two = norm_ahead(resid_in, hot, mods[0], mods[1], [perm_one_t, perm_two_t])
-    w_qkv = ((blocks_one, half_qkv), (blocks_two, half_qkv))
+    w_qkv = ((blocks_one, (0, half_qkv)), (blocks_two, (0, half_qkv)))
     qkv_bias = jnp.concatenate(
         [gain_rows[1:2], jnp.zeros((1, width), F32), gain_rows[2:3]], axis=1
     )
@@ -826,61 +833,46 @@
         up_one = grow(up_one, mask, devices)
     for mask in bits_y[:-1]:
         up_two = grow(up_two, mask, devices)
-    proj_one, proj_two = up_one[:, half_ff:], up_two[:, half_ff:]
-    up_one, up_two = up_one[:, :half_ff], up_two[:, :half_ff]
-    proj_one_far, proj_two_far = swap(proj_one, bits_x[-1]), swap(proj_two, bits_y[-1])
     mod_one = lend(added(*mod_one), bits_y, devices)
     mod_two = lend(added(*mod_two), bits_x, devices)
-    head16 = widen(head16, bits_y, devices)
+    up_one_far, up_two_far = swap(up_one, bits_x[-1]), swap(up_two, bits_y[-1])
+    down = widen(stack(down), bits_z[1:], devices)
     mixture = attend(qkv, q_gain, k_gain, mask_rows)
-    mixture, proj_one_far, proj_two_far, up_one, up_two, mod_one, mod_two, head16, down = tie(
-        mixture, proj_one_far, proj_two_far, up_one, up_two, mod_one, mod_two, head16, down
-    )
-
-    up_one_far, up_two_far = swap(up_one, bits_x[-1]), swap(up_two, bits_y[-1])
+    mixture, mod_one, mod_two, down, up_one, up_two = tie(
+        mixture, mod_one, mod_two, down, up_one, up_two
+    )
+
     mods_rest = jnp.concatenate([added(*mod_one), added(*mod_two)], axis=1)
     mods_rest = lend(mods_rest, bits_z[-1:], devices)
-    proj_one_c, proj_two_c = swap(proj_one, 1), swap(proj_two, 1)
-    proj_one_fc, proj_two_fc = swap(proj_one_far, 1), swap(proj_two_far, 1)
+    up_one_c, up_two_c = swap(up_one, 1), swap(up_two, 1)
     mix_one = matmul(mixture, perm_one_t).astype(BF16)
     mix_two = matmul(mixture, perm_two_t).astype(BF16)
-    mix_one, mix_two, proj_one_c, proj_two_c, proj_one_fc, proj_two_fc, mods_rest = tie(
-        mix_one, mix_two, proj_one_c, proj_two_c, proj_one_fc, proj_two_fc, mods_rest
-    )
-    w_proj = (
-        ([proj_one, proj_one_far, proj_one_c, proj_one_fc], None),
-        ([proj_two, proj_two_far, proj_two_c, proj_two_fc], None),
+    mix_one, mix_two, mods_rest, up_one_c, up_two_c, down = tie(
+        mix_one, mix_two, mods_rest, up_one_c, up_two_c, down
     )
     mods_rest = lend(added(*mods_rest), bits_z[:-1], devices)
-    attn_out = times_sets([mix_one, mix_two], w_proj, gain_rows[3:4])
-    attn_out, mods_rest, down = tie(attn_out, mods_rest, down)
-    mods_rest = added(*mods_rest, F32) + ada_bias[:, cuts[0] :]
-    mods += [mods_rest[:, at : at + width] for at in range(0, 6 * width, width)]
-    up_one_c, up_two_c = swap(up_one, 1), swap(up_two, 1)
-    down = widen(stack(down), bits_z[1:], devices)
-    u_mid_one, u_mid_two, resid_mid = norm_ahead(
-        resid_in, hot, mods[3], mods[4], [perm_one_t, perm_two_t], mods[2], attn_out
-    )
-    u_mid_one, u_mid_two, up_one_far, up_two_far, up_one_c, up_two_c, down = tie(
-        u_mid_one, u_mid_two, up_one_far, up_two_far, up_one_c, up_two_c, down
-    )
-
-    up_one_fc, up_two_fc = swap(up_one_far, 1), swap(up_two_far, 1)
-    u_mid_one, u_mid_two, up_one_fc, up_two_fc, down = tie(
-        u_mid_one, u_mid_two, up_one_fc, up_two_fc, down
-    )
     down = stack(down)
     down_one = widen(down[:, :half_ff], one_y, devices)
     down_two = widen(down[:, half_ff:], two_x, devices)
+    mix_one, mix_two, mods_rest, up_one_far, up_two_far, head16 = tie(
+        mix_one, mix_two, mods_rest, up_one_far, up_two_far, head16
+    )
+    up_one_fc, up_two_fc = swap(up_one_far, 1), swap(up_two_far, 1)
     head16 = widen(stack(head16), bits_z[:1], devices)
-    w_up = (
-        ([up_one, up_one_far, up_one_c, up_one_fc], None),
-        ([up_two, up_two_far, up_two_c, up_two_fc], None),
-    )
-    up_bias = gain_rows[7:ada_at].reshape(1, -1)
-    hidden, active = times_sets([u_mid_one, u_mid_two], w_up, up_bias, bend=True)
-    active, down_one, down_two = tie(active, down_one, down_two)
-
+    mix_one, mix_two, up_one_fc, up_two_fc = tie(mix_one, mix_two, up_one_fc, up_two_fc)
+    blocks_one = [up_one, up_one_far, up_one_c, up_one_fc]
+    blocks_two = [up_two, up_two_far, up_two_c, up_two_fc]
+    w_up = ((blocks_one, (0, half_ff)), (blocks_two, (0, half_ff)))
+    w_proj = ((blocks_one, (half_ff, half_up)), (blocks_two, (half_ff, half_up)))
+    mods_rest = added(*mods_rest, F32) + ada_bias[:, cuts[0] :]
+    mods += [mods_rest[:, at : at + width] for at in range(0, 6 * width, width)]
+    attn_out = times_sets([mix_one, mix_two], w_proj, gain_rows[3:4])
+    u_mid_one, u_mid_two, resid_mid = norm_ahead(
+        resid_in, hot, mods[3], mods[4], [perm_one_t, perm_two_t], mods[2], attn_out
+    )
+    u_mid_one, u_mid_two, resid_mid, down_one, down_two = tie(
+        u_mid_one, u_mid_two, resid_mid, down_one, down_two
+    )
     down_one, down_two = stack(down_one), stack(down_two)
     for mask in bits_x[:-1]:
         down_one = grow(down_one, mask, devices)
@@ -888,6 +880,8 @@
         down_two = grow(down_two, mask, devices)
     down_one_far, down_two_far = swap(down_one, bits_x[-1]), swap(down_two, bits_y[-1])
     down_one_c, down_two_c = swap(down_one, 1), swap(down_two, 1)
+    up_bias = gain_rows[7:ada_at].reshape(1, -1)
+    hidden, active = times_sets([u_mid_one, u_mid_two], w_up, up_bias, bend=True)
     active, down_one_far, down_two_far, down_one_c, down_two_c, head16 = tie(
         active, down_one_far, down_two_far, down_one_c, down_two_c, head16
     )
@@ -1059,10 +1053,10 @@
         d_low, down_x1, down_x2, up_f1, up_f2, up_n1, up_n2, head_back, head_near
     )
     down_n1, down_f1, down_n2, down_f2 = turn(down_n1, down_n2, down_x1, down_x2)
+    d_low, down_f1, down_f2, up_f1, up_f2, head_back = tie(
+        d_low, down_f1, down_f2, up_f1, up_f2, head_back
+    )
     head_near, head_far = halves_of(head_near, head_back)
-    d_low, down_f1, down_f2, up_f1, up_f2, head_far = tie(
-        d_low, down_f1, down_f2, up_f1, up_f2, head_far
-    )
     down_x1, down_x2 = cross_back(down_f1, down_f2)
     up_x1, up_x2 = cross(up_f1, up_f2)
     head_back = swap(head_far, head_masks[-2])
@@ -1092,13 +1086,6 @@
     down_near, down_far = halves_of(down_near, down_back)
     d_u, down_far, qkv_b, up_x1, up_x2 = tie(d_u, down_far, qkv_b, up_x1, up_x2)
     down_back = swap(down_far, bits_z[-2])
-
-    def beside(one, two):
-        return jnp.concatenate([one, two], axis=1)
-
-    qkv_n1, qkv_f1, qkv_n2, qkv_f2 = grad_sets(ins, d_qkv, qkvs, qkv_b)
-    proj_n1, proj_f1, proj_n2, proj_f2 = grad_sets(mixes, d_low, projs, proj_b)
-    up_near, up_far = join(up_n1, up_n2, up_x1, up_x2)
     d_resid_in, d_shift_one, d_scale_one, word_bias, d_res16 = norm_back(
         resid_in, d_u, hot, hot_t, mods[1], beyond=d_resid_mid
     )
@@ -1115,21 +1102,58 @@
         ],
         axis=1,
     ).astype(BF16)
-    qkv_f1, qkv_f2 = beside(qkv_f1, proj_f1), beside(qkv_f2, proj_f2)
-    d_mod, d_res16, up_far, qkv_f1, qkv_f2, qkv_n1, qkv_n2, proj_n1, proj_n2 = tie(
-        d_mod, d_res16, up_far, qkv_f1, qkv_f2, qkv_n1, qkv_n2, proj_n1, proj_n2
-    )
+    ada_sums = jnp.sum(d_mod.astype(F32), axis=0, keepdims=True)
+    arrays = [word_bias, attn_sums, proj_bias, down_bias, up_bias_sum, ada_sums, bias_grad[None]]
+    plan = [(0, 0), (1, 2), (1, 3), (2, 0), (3, 0), (1, 0), (1, 1), (4, 0), (5, 0), (6, 0)]
+    d_slim = slim_back(d_res16, token_hot, arrays, plan, perms, n_embed)
+    d_slim, d_mod, qkv_b = tie(d_slim, d_mod, qkv_b)
+    slim_b = swap(d_slim[top:], 1)
+    qkv_n1, qkv_f1, qkv_n2, qkv_f2 = grad_sets(ins, d_qkv, qkvs, qkv_b)
+    proj_n1, proj_f1, proj_n2, proj_f2 = grad_sets(mixes, d_low, projs, proj_b)
+    (
+        qkv_n1,
+        qkv_f1,
+        qkv_n2,
+        qkv_f2,
+        proj_n1,
+        proj_f1,
+        proj_n2,
+        proj_f2,
+        slim_b,
+        down_back,
+        up_x1,
+        up_x2,
+    ) = tie(
+        qkv_n1,
+        qkv_f1,
+        qkv_n2,
+        qkv_f2,
+        proj_n1,
+        proj_f1,
+        proj_n2,
+        proj_f2,
+        slim_b,
+        down_back,
+        up_x1,
+        up_x2,
+    )
+
+    def beside(*parts):
+        return jnp.concatenate(parts, axis=1)
+
+    far_slim = added(d_slim[quarter:top], slim_b[quarter:])
+    qkv_f1 = beside(qkv_f1, proj_f1, far_slim[:, :half_slim])
+    qkv_f2 = beside(qkv_f2, proj_f2, far_slim[:, half_slim:])
+    up_near, up_far = join(up_n1, up_n2, up_x1, up_x2)
+    d_mod, up_far, qkv_f1, qkv_f2 = tie(d_mod, up_far, qkv_f1, qkv_f2)
     qkv_x1, qkv_x2 = cross(qkv_f1, qkv_f2)
     up_back = swap(up_far, bits_z[-1])
     all_mod = widen(d_mod, bits_z, devices)
-    ada_sums = jnp.sum(d_mod.astype(F32), axis=0, keepdims=True)
-    arrays = [word_bias, attn_sums, proj_bias, down_bias, up_bias_sum, ada_sums, bias_grad[None]]
-    plan = [(0, 0), (1, 2), (1, 3), (2, 0), (3, 0), (1, 0), (1, 1), (4, 0), (5, 0), (6, 0)]
-    d_slim = slim_back(d_res16, token_hot, arrays, plan, perm_one, n_embed)
-    d_slim = lend(d_slim, bits_x + [1], devices)
-    qkv_n1, qkv_n2 = beside(qkv_n1, proj_n1), beside(qkv_n2, proj_n2)
-    qkv_x1, qkv_x2, qkv_n1, qkv_n2, all_mod, d_slim, up_back, up_near, down_back = tie(
-        qkv_x1, qkv_x2, qkv_n1, qkv_n2, all_mod, d_slim, up_back, up_near, down_back
+    near_slim = added(d_slim[:quarter], slim_b[:quarter])
+    qkv_n1 = beside(qkv_n1, proj_n1, near_slim[:, :half_slim])
+    qkv_n2 = beside(qkv_n2, proj_n2, near_slim[:, half_slim:])
+    qkv_x1, qkv_x2, qkv_n1, qkv_n2, all_mod, up_back, up_near = tie(
+        qkv_x1, qkv_x2, qkv_n1, qkv_n2, all_mod, up_back, up_near
     )
     qkv_n1, qkv_f1, qkv_n2, qkv_f2 = turn(qkv_n1, qkv_n2, qkv_x1, qkv_x2)
     up_near, up_far = halves_of(up_near, up_back)
@@ -1138,15 +1162,14 @@
     all_mod = stack(all_mod)
     all_first = widen(all_mod[:, : cuts[1]], bits_y, devices)
     all_two = widen(all_mod[:, cuts[1] :], bits_x, devices)
-    qkv_x1, qkv_x2, qkv_n1, qkv_n2, up_back, all_first, all_two, d_slim = tie(
-        qkv_x1, qkv_x2, qkv_n1, qkv_n2, up_back, all_first, all_two, d_slim
+    qkv_x1, qkv_x2, qkv_n1, qkv_n2, up_back, all_first, all_two = tie(
+        qkv_x1, qkv_x2, qkv_n1, qkv_n2, up_back, all_first, all_two
     )
     near, far = join(qkv_n1, qkv_n2, qkv_x1, qkv_x2)
     attn_back = swap(far, bits_z[-1])
     all_two = widen(stack(all_two), bits_y, devices)
     all_first = widen(stack(all_first), bits_x, devices)
-    d_slim = lend(added(*d_slim), bits_z + bits_y, devices)
-    attn_back, near, all_two, all_first, d_slim = tie(attn_back, near, all_two, all_first, d_slim)
+    attn_back, near, all_two, all_first = tie(attn_back, near, all_two, all_first)
     near, far = halves_of(near, attn_back)
     attn_back = swap(far, bits_z[-2])
     all_two = grown([1], stack(all_two))
@@ -1157,22 +1180,7 @@
         near = added(near, back, BF16 if masks else F32)
         return keep_all(near, masks, devices)
 
-    attn_rows, up_rows, down_rows = (
-        close(near, attn_back),
-        close(up_near, up_back),
-        close(down_near, down_back),
-    )
-    slim_grad = added(*d_slim, F32).T
-    half_attn = half_qkv + top
-    attn_grad = jnp.concatenate(
-        [
-            attn_rows[:, :half_qkv],
-            attn_rows[:, half_attn : half_attn + half_qkv],
-            attn_rows[:, half_qkv:half_attn],
-            attn_rows[:, half_attn + half_qkv :],
-        ],
-        axis=1,
-    )
+    up_rows, down_rows = close(up_near, up_back), close(down_near, down_back)
     mlp_grad = jnp.stack([up_rows, down_rows])
     ada_grad = jnp.concatenate([matmul_tn(class_act, all_first), matmul_tn(act_two, all_two)], axis=1)
     d_class_act = matmul_nt(all_first, ada16[:, : cuts[1]]) + to_one(
@@ -1180,6 +1188,28 @@
     )
     _, silu_back = jax.vjp(jax.nn.silu, class_vec)
     d_class = precise_tn(class_hot.astype(F32), silu_back(d_class_act)[0])
+    squares_local = jnp.zeros((), F32)
+    for gradient in (mlp_grad, ada_grad, d_class, head_grad):
+        squares_local = squares_local + jnp.sum(gradient * gradient)
+    squares_local, mlp_grad, ada_grad, d_class, near, attn_back = tie(
+        squares_local, mlp_grad, ada_grad, d_class, near, attn_back
+    )
+    attn_rows = close(near, attn_back)
+    squares_local = squares_local + jnp.sum(attn_rows * attn_rows)
+    half_attn = half_qkv + top
+    half_all = half_attn + half_slim
+    attn_grad = jnp.concatenate(
+        [
+            attn_rows[:, :half_qkv],
+            attn_rows[:, half_all : half_all + half_qkv],
+            attn_rows[:, half_qkv:half_attn],
+            attn_rows[:, half_all + half_qkv : half_all + half_attn],
+        ],
+        axis=1,
+    )
+    slim_grad = jnp.concatenate(
+        [attn_rows[:, half_attn:half_all], attn_rows[:, half_all + half_attn :]], axis=1
+    ).T
     embed_grad = jnp.concatenate(
         [
             d_class,
@@ -1190,11 +1220,7 @@
         axis=0,
     )
     gains_grad = slim_grad[n_embed : n_embed + n_gains]
-
     gradients = (attn_grad, mlp_grad, ada_grad, embed_grad, gains_grad, head_grad)
-    squares_local = jnp.zeros((), F32)
-    for gradient in gradients:
-        squares_local = squares_local + jnp.sum(gradient * gradient)
     sums = sum_all(
         jnp.stack([squares_local, loss_part])[None], [1] + bits_x + bits_y + bits_z, devices
     )

time: 678 us -> 647 us (0.954)
  waiting for transfers between devices: 205 us -> 170 us
  local copies, waits for them, and re-layouts: 62.8 us -> 74.5 us
  starting transfers between devices: 103 us -> 94.1 us
    ppermute x115 -> x108, waiting for transfers between devices: 205 us -> 170 us  [swapped(): lax.ppermute(value, ('dp', 'vocab'), [(i, i ^ mask) for i in range(device...]
    ppermute x115 -> x108, starting transfers between devices: 103 us -> 94.1 us  [swapped(): lax.ppermute(value, ('dp', 'vocab'), [(i, i ^ mask) for i in range(device...]
    unnamed x529 -> x439, local copies, waits for them, and re-layouts: 42.1 us -> 47.2 us
    convert_element_type x32 -> x29, other arithmetic: 18.8 us -> 19.3 us  [added(): return (mine.astype(F32) + theirs.astype(F32)).astype(out)]
  transfers between devices with their start and end apart: 115 -> 108, of which waited for: 44 -> 42; matrix products, arithmetic and copies ran while one was open for 12% -> 14% of each run, Pallas kernels for 21% -> 23%
where the time goes in v4:
time: 647 us; the launch traced here: 636 us
  Pallas kernels  180 us (28%)
  waiting for transfers between devices  170 us (26%)
  starting transfers between devices  94.1 us (15%)
  local copies, waits for them, and re-layouts  74.5 us (12%)
  other arithmetic  72.7 us (11%)
  matrix products  32.7 us (5%)
  between operations  12 us (2%)
    pallas_call x25, Pallas kernels, run(): pl.pallas_call(body, grid=grid, in_specs=specs, out_shape=outs, out_specs...  180 us
    ppermute x108, waiting for transfers between devices, swapped(): lax.ppermute(value, ('dp', 'vocab'), [(i, i ^ mask) for i in range(device...  170 us
    ppermute x108, starting transfers between devices, swapped(): lax.ppermute(value, ('dp', 'vocab'), [(i, i ^ mask) for i in range(device...  94.1 us
    unnamed x439, local copies, waits for them, and re-layouts  47.2 us
    convert_element_type x29, other arithmetic, added(): return (mine.astype(F32) + theirs.astype(F32)).astype(out)  19.3 us
    dot_general x11, matrix products, matmul(): return jnp.dot(left, right, preferred_element_type=F32)  14.8 us
  transfers between devices with their start and end apart: 108, of which 42 were waited for; matrix products, arithmetic and copies ran while one was open for 14% of the time, Pallas kernels for 23%

profile of v4, /device:TPU:0, one launch (start us, length us, event | category | flops | bytes accessed | tf_op | source)
XLA Modules:
  0.0 635.5 jit_solution(8570360207641071193)
XLA Ops:
  3.5 4.0 collective-permute-start
  20.0 3.5 collective-permute-done.3
  54.3 7.9 %collective-permute-done.14 = bf16[64,2048]{1,0:T(8,128)(2,1)S(1)} collective-permute-done((bf16[64,2048]{1,0:T(8,128)(2,1)S(1)}, bf16[64,2048]{1,0:T(8,128)(2,1)S(1)}, u32[]{:S(2)}, u32[]{:S(2)}) %collective-permute-start.14) | collective-permute-done | bytes 262176 | tf_op jit(solution)/shard_map/ppermute | solution.py:66
  62.3 2.4 collective-permute-start.15
  64.7 2.6 fusion.6
  67.3 3.9 collective-permute-done.15
  82.8 9.8 %collective-permute-done.21 = bf16[32,5120]{1,0:T(8,128)(2,1)S(1)} collective-permute-done((bf16[32,5120]{1,0:T(8,128)(2,1)S(1)}, bf16[32,5120]{1,0:T(8,128)(2,1)S(1)}, u32[]{:S(2)}, u32[]{:S(2)}) %collective-permute-start.21) | collective-permute-done | bytes 327712 | tf_op jit(solution)/shard_map/ppermute | solution.py:66
  96.2 6.3 collective-permute-done.23.refs_6_.refs_5_
  102.6 7.4 %collective-permute-done.26 = bf16[64,5120]{1,0:T(8,128)(2,1)S(1)} collective-permute-done((bf16[64,5120]{1,0:T(8,128)(2,1)S(1)}, bf16[64,5120]{1,0:T(8,128)(2,1)S(1)}, u32[]{:S(2)}, u32[]{:S(2)}) %collective-permute-start.26) | collective-permute-done | bytes 655392 | tf_op jit(solution)/shard_map/ppermute | solution.py:66
  124.1 5.4 shard_map.457
  129.6 7.7 %shard_map.458.q_ref.k_ref.v_ref = f32[384,3072]{1,0:T(8,128)} custom-call(bf16[384,1024]{1,0:T(8,128)(2,1)S(1)} %get-tuple-element.378.one_ref, bf16[384,1024]{1,0:T(8,128)(2,1)S(1)} %get-tuple-element.379.two_ref, f32[1,3072]{1,0:T(1,128)S(1)} %pad_maximum_fusion.23.refs_0_, bf16[256,1792]{1,0:T(8,128)(2,1)S(1)} %constant_dynamic-update-slice_fusion.12.refs_1_.refs_0_, ...), custom_call_target="tpu_custom_call" | custom-call | flops 1000 | bytes 1000 | tf_op jit(solution)/shard_map/pallas_call | solution.py:149
  148.9 10.7 %shard_map.459 = bf16[384,1024]{1,0:T(8,128)(2,1)S(1)} custom-call(f32[384,3072]{1,0:T(8,128)S(1)} %copy-done, f32[384,3072]{1,0:T(8,128)S(1)} %copy-done, f32[384,3072]{1,0:T(8,128)S(1)} %copy-done, f32[1,1024]{1,0:T(1,128)S(1)} %get-tuple-element.758.qg_ref, f32[1,1024]{1,0:T(1,128)S(1)} %get-tuple-element.757.kg_ref, f32[384,384]{1,0:T(8,128)S(1)} %copy-done.36), custom_call_target="tpu_custom_call" | custom-call | flops 1000 | bytes 1000 | tf_op jit(solution)/shard_map/pallas_call | solution.py:149
  165.1 2.9 collective-permute-done.38
  171.6 8.0 %collective-permute-done.43.refs_6_.refs_5_ = bf16[256,2560]{1,0:T(8,128)(2,1)S(1)} collective-permute-done((bf16[256,2560]{1,0:T(8,128)(2,1)S(1)}, bf16[256,2560]{1,0:T(8,128)(2,1)S(1)}, u32[]{:S(2)}, u32[]{:S(2)}) %collective-permute-start.43) | collective-permute-done | bytes 1310752 | tf_op jit(solution)/shard_map/ppermute | solution.py:66
  180.4 2.5 collective-permute-done.44.refs_4_.refs_3_
  185.8 3.4 shard_map.460.refs_1_.refs_3_
  189.2 6.0 shard_map.461
  202.5 10.2 %shard_map.462 = (f32[384,4096]{1,0:T(8,128)}, bf16[384,4096]{1,0:T(8,128)(2,1)}) custom-call(bf16[384,1024]{1,0:T(8,128)(2,1)S(1)} %get-tuple-element.432.one_ref, bf16[384,1024]{1,0:T(8,128)(2,1)S(1)} %get-tuple-element.433.two_ref, f32[1,4096]{1,0:T(1,128)S(1)} %bitcast.110, bf16[256,2560]{1,0:T(8,128)(2,1)S(1)} %constant_dynamic-update-slice_fusion.22.refs_1_.refs_0_, ...), custom_call_target="tpu_custom_call" | custom-call | flops 1000 | bytes 1000 | tf_op jit(solution)/shard_map/pallas_call | solution.py:149
  212.6 13.1 %collective-permute-done.52 = bf16[256,1024]{1,0:T(8,128)(2,1)S(1)} collective-permute-done((bf16[256,1024]{1,0:T(8,128)(2,1)S(1)}, bf16[256,1024]{1,0:T(8,128)(2,1)S(1)}, u32[]{:S(2)}, u32[]{:S(2)}) %collective-permute-start.52) | collective-permute-done | bytes 524320 | tf_op jit(solution)/shard_map/ppermute | solution.py:66
  226.6 2.2 fusion.10.refs_2_
  231.0 12.8 %shard_map.463.refs_1_.refs_2_ = f32[384,1024]{1,0:T(8,128)} custom-call(bf16[1,384,4096]{2,1,0:T(8,128)(2,1)} %bitcast.100, bf16[1024,1024]{1,0:T(8,128)(2,1)} %get-tuple-element.846.one_ref, bf16[1024,1024]{1,0:T(8,128)(2,1)} %get-tuple-element.844.two_ref, f32[1,1024]{1,0:T(1,128)S(1)} %get-tuple-element.755.refs_0_, ...), custom_call_target="tpu_custom_call" | custom-call | flops 1000 | bytes 1000 | tf_op jit(solution)/shard_map/pallas_call | solution.py:149
  245.2 5.0 shard_map.464
  257.6 4.0 add_reduce_fusion.1
  262.7 11.1 %collective-permute-done.57 = bf16[384,1024]{1,0:T(8,128)(2,1)S(1)} collective-permute-done((bf16[384,1024]{1,0:T(8,128)(2,1)}, bf16[384,1024]{1,0:T(8,128)(2,1)S(1)}, u32[]{:S(2)}, u32[]{:S(2)}) %collective-permute-start.57) | collective-permute-done | bytes 786464 | tf_op jit(solution)/shard_map/ppermute | solution.py:66
  273.9 2.2 collective-permute-done.58
  286.8 2.2 collective-permute-done.61
  290.7 4.6 fusion.14
  304.2 2.8 fusion.41
  306.9 2.9 fusion.38
  309.8 13.1 %collective-permute-done.63 = bf16[384,1024]{1,0:T(8,128)(2,1)S(1)} collective-permute-done((bf16[384,1024]{1,0:T(8,128)(2,1)S(1)}, bf16[384,1024]{1,0:T(8,128)(2,1)S(1)}, u32[]{:S(2)}, u32[]{:S(2)}) %collective-permute-start.63) | collective-permute-done | bytes 786464 | tf_op jit(solution)/shard_map/ppermute | solution.py:66
  324.6 2.4 fusion.44.refs_1_
  327.0 7.5 %shard_map.465 = (f32[384,1024]{1,0:T(8,128)S(1)}, f32[8,1024]{1,0:T(8,128)S(1)}, f32[8,1024]{1,0:T(8,128)S(1)}, f32[1,1024]{1,0:T(1,128)S(1)}, f32[8,1024]{1,0:...) custom-call(bf16[384,8]{1,0:T(8,128)(2,1)S(1)} %fusion.80.hot_ref, ...), custom_call_target="tpu_custom_call" | custom-call | flops 1000 | bytes 1000 | tf_op jit(solution)/shard_map/pallas_call | solution.py:149
  335.7 4.6 shard_map.466
  340.4 11.1 %shard_map.467 = (bf16[384,4096]{1,0:T(8,128)(2,1)}, f32[1,4096]{1,0:T(1,128)S(1)}) custom-call(bf16[384,1024]{1,0:T(8,128)(2,1)S(1)} %get-tuple-element.464.one_ref, bf16[384,1024]{1,0:T(8,128)(2,1)S(1)} %get-tuple-element.465.two_ref, f32[384,4096]{1,0:T(8,128)} %get-tuple-element.466.refs_0_, bf16[256,2048]{1,0:T(8,128)(2,1)S(1)} %copy-done.29, ...), custom_call_target="tpu_custom_call" | custom-call | flops 1000 | bytes 1000 | tf_op jit(solution)/shard_map/pallas_call | solution.py:149
  355.5 4.5 shard_map.469
  360.0 6.7 %shard_map.468 = (bf16[256,2048]{1,0:T(8,128)(2,1)S(1)}, bf16[256,2048]{1,0:T(8,128)(2,1)}, bf16[256,2048]{1,0:T(8,128)(2,1)S(1)}, bf16[256,2048]{1,0:T(8,128)(2,1)}) custom-call(bf16[384,1024]{1,0:T(8,128)(2,1)S(1)} %get-tuple-element.464.one_ref, bf16[384,1024]{1,0:T(8,128)(2,1)S(1)} %get-tuple-element.465.two_ref, bf16[1,384,4096]{2,1,0:T(8,128)(2,1)} %bitcast.101, ...), custom_call_target="tpu_custom_call" | custom-call | flops 1000 | bytes 1000 | tf_op jit(solution)/shard_map/pallas_call | solution.py:149
  371.4 11.5 %shard_map.470.refs_1_ = f32[384,1024]{1,0:T(8,128)} custom-call(bf16[1,384,4096]{2,1,0:T(8,128)(2,1)} %bitcast.103, bf16[1024,1024]{1,0:T(8,128)(2,1)} %get-tuple-element.846.one_ref, bf16[1024,1024]{1,0:T(8,128)(2,1)} %get-tuple-element.844.two_ref, bf16[256,2560]{1,0:T(8,128)(2,1)S(1)} %constant_dynamic-update-slice_fusion.22.refs_1_.refs_0_, ...), custom_call_target="tpu_custom_call" | custom-call | flops 1000 | bytes 1000 | tf_op jit(solution)/shard_map/pallas_call | solution.py:149
  383.0 6.7 %shard_map.472 = (bf16[256,2048]{1,0:T(8,128)(2,1)S(1)}, bf16[256,2048]{1,0:T(8,128)(2,1)S(1)}, bf16[256,2048]{1,0:T(8,128)(2,1)S(1)}, bf16[256,2048]{1,0:T(8,128)(2,1)}) custom-call(bf16[384,1024]{1,0:T(8,128)(2,1)S(1)} %get-tuple-element.432.one_ref, bf16[384,1024]{1,0:T(8,128)(2,1)S(1)} %copy-done.14, bf16[1,384,4096]{2,1,0:T(8,128)(2,1)} %bitcast.104, ...), custom_call_target="tpu_custom_call" | custom-call | flops 1000 | bytes 1000 | tf_op jit(solution)/shard_map/pallas_call | solution.py:149
  391.7 5.2 shard_map.471
  397.0 3.0 add_convert_fusion.20
  400.0 2.5 add_convert_fusion.21
  404.3 2.4 add_convert_fusion.18
  410.8 6.1 shard_map.473.dm_ref
  418.2 21.5 %shard_map.474 = (bf16[3,384,1024]{2,1,0:T(8,128)(2,1)S(1)}, f32[8,1024]{1,0:T(8,128)S(1)}) custom-call(f32[384,3072]{1,0:T(8,128)} %shard_map.458.q_ref.k_ref.v_ref, f32[384,3072]{1,0:T(8,128)} %shard_map.458.q_ref.k_ref.v_ref, f32[384,3072]{1,0:T(8,128)} %shard_map.458.q_ref.k_ref.v_ref, f32[1,1024]{1,0:T(1,128)S(1)} %get-tuple-element.758.qg_ref, ...), custom_call_target="tpu_custom_call" | custom-call | flops 1000 | bytes 1000 | tf_op jit(solution)/shard_map/pallas_call | solution.py:149
  445.4 4.7 shard_map.476
  457.1 11.5 %shard_map.477.refs_1_ = f32[384,1024]{1,0:T(8,128)} custom-call(bf16[3,384,1024]{2,1,0:T(8,128)(2,1)} %copy-done.5, bf16[1024,1024]{1,0:T(8,128)(2,1)} %get-tuple-element.846.one_ref, bf16[1024,1024]{1,0:T(8,128)(2,1)} %get-tuple-element.844.two_ref, bf16[256,1792]{1,0:T(8,128)(2,1)S(1)} %copy-done.31, bf16[256,1792]{1,0:T(8,128)(2,1)S(1)} %copy-done.41, ...), custom_call_target="tpu_custom_call" | custom-call | flops 1000 | bytes 1000 | tf_op jit(solution)/shard_map/pallas_call | solution.py:149
  468.6 3.3 collective-permute-done.79
  474.5 4.5 shard_map.478
  479.3 3.8 shard_map.479
  492.3 6.3 shard_map.480
  508.3 4.8 collective-permute-done.84
  513.4 14.6 %collective-permute-done.85 = bf16[16,8192]{1,0:T(8,128)(2,1)S(1)} collective-permute-done((bf16[16,8192]{1,0:T(8,128)(2,1)S(1)}, bf16[16,8192]{1,0:T(8,128)(2,1)S(1)}, u32[]{:S(2)}, u32[]{:S(2)}) %collective-permute-start.85) | collective-permute-done | bytes 262176 | tf_op jit(solution)/shard_map/ppermute | solution.py:66
  528.0 5.0 collective-permute-done.82
  542.1 6.4 %collective-permute-done.89 = bf16[32,4096]{1,0:T(8,128)(2,1)S(1)} collective-permute-done((bf16[32,4096]{1,0:T(8,128)(2,1)S(1)}, bf16[32,4096]{1,0:T(8,128)(2,1)S(1)}, u32[]{:S(2)}, u32[]{:S(2)}) %collective-permute-start.89) | collective-permute-done | bytes 262176 | tf_op jit(solution)/shard_map/ppermute | solution.py:66
  548.5 3.8 collective-permute-done.88
  552.3 2.5 collective-permute-done.87
  559.8 5.0 collective-permute-done.93
  564.8 5.0 collective-permute-done.92
  574.2 3.4 collective-permute-done.96
  605.0 2.5 collective-permute-done.99
  613.9 2.9 collective-permute-done.107
  621.7 2.9 fusion.119
  625.7 2.4 fusion.125
  629.2 2.4 fusion.127
  (887 shorter events, 249.5 us)
Async XLA Ops:
  3.5 16.5 %collective-permute-start = (s32[1,128]{1,0:T(1,128)S(1)}, s32[1,128]{1,0:T(1,128)S(1)}, u32[]{:S(2)}, u32[]{:S(2)}) collective-permute-start(s32[1,128]{1,0:T(1,128)S(1)} %add_bitcast_fusion.4), channel_id=1, source_target_pairs={{0,16},{1,17},{2,18},{3,19},{4,20},{5,21},{6,22},{7,23},{8,24},{9,... | collective-permute-start | bytes 1544 | tf_op jit(solution)/shard_map/ppermute | solution.py:66
  7.5 12.5 %collective-permute-start.1 = (s32[1,128]{1,0:T(1,128)S(1)}, s32[1,128]{1,0:T(1,128)S(1)}, u32[]{:S(2)}, u32[]{:S(2)}) collective-permute-start(s32[1,128]{1,0:T(1,128)S(1)} %add_bitcast_fusion.4), channel_id=1, source_target_pairs={{0,8},{1,9},{2,10},{3,11},{4,12},{5,13},{6,14},{7,15},{8,0},{9,1},... | collective-permute-start | bytes 1544 | tf_op jit(solution)/shard_map/ppermute | solution.py:66
  12.2 11.3 %collective-permute-start.3 = (bf16[32,1792]{1,0:T(8,128)(2,1)S(1)}, bf16[32,1792]{1,0:T(8,128)(2,1)S(1)}, u32[]{:S(2)}, u32[]{:S(2)}) collective-permute-start(bf16[32,1792]{1,0:T(8,128)(2,1)S(1)} %pad_maximum_fusion.21), channel_id=1, source_target_pairs={{0,16},{1,17},{2,18},{3,19},{4,20},{5,21},{6,22},{7,23},{8,24},{9,... | collective-permute-start | bytes 344072 | tf_op jit(solution)/shard_map/ppermute | solution.py:66
  25.1 11.5 %collective-permute-start.8 = (bf16[64,1792]{1,0:T(8,128)(2,1)S(1)}, bf16[64,1792]{1,0:T(8,128)(2,1)}, u32[]{:S(2)}, u32[]{:S(2)}) collective-permute-start(bf16[64,1792]{1,0:T(8,128)(2,1)S(1)} %constant_dynamic-update-slice_fusion), channel_id=1, source_target_pairs={{0,8},{1,9},{2,10},{3,11},{4,12},{5,13},{6,14},{7,15},{8,0},{9,1},... | collective-permute-start | bytes 688136 | tf_op jit(solution)/shard_map/ppermute | solution.py:66
  31.6 20.6 %collective-permute-start.12 = (f32[1,2,384]{2,1,0:T(2,128)S(1)}, f32[1,2,384]{2,1,0:T(2,128)S(1)}, u32[]{:S(2)}, u32[]{:S(2)}) collective-permute-start(f32[1,2,384]{2,1,0:T(2,128)S(1)} %maximum_bitcast_fusion.1), channel_id=1, source_target_pairs={{0,2},{1,3},{2,0},{3,1},{4,6},{5,7},{6,4},{7,5},{8,10},{9,11},{10,... | collective-permute-start | bytes 9224 | tf_op jit(solution)/shard_map/ppermute | solution.py:66
  36.7 15.5 %collective-permute-start.13 = (bf16[128,1024]{1,0:T(8,128)(2,1)S(1)}, bf16[128,1024]{1,0:T(8,128)(2,1)}, u32[]{:S(2)}, u32[]{:S(2)}) collective-permute-start(bf16[128,1024]{1,0:T(8,128)(2,1)S(1)} %convert_element_type.580), channel_id=1, source_target_pairs={{0,4},{1,5},{2,6},{3,7},{4,0},{5,1},{6,2},{7,3},{8,12},{9,13},{10,... | collective-permute-start | bytes 786440 | tf_op jit(solution)/shard_map/ppermute | solution.py:66
  40.6 30.6 %collective-permute-start.16 = (bf16[128,1792]{1,0:T(8,128)(2,1)}, bf16[128,1792]{1,0:T(8,128)(2,1)}, u32[]{:S(2)}, u32[]{:S(2)}) collective-permute-start(bf16[128,1792]{1,0:T(8,128)(2,1)} %constant_dynamic-update-slice_fusion.6), channel_id=1, source_target_pairs={{0,4},{1,5},{2,6},{3,7},{4,0},{5,1},{6,2},{7,3},{8,12},{9,13},{10,... | collective-permute-start | bytes 1376264 | tf_op jit(solution)/shard_map/ppermute | solution.py:66
  43.4 27.8 %collective-permute-start.17 = (bf16[128,1792]{1,0:T(8,128)(2,1)}, bf16[128,1792]{1,0:T(8,128)(2,1)}, u32[]{:S(2)}, u32[]{:S(2)}) collective-permute-start(bf16[128,1792]{1,0:T(8,128)(2,1)} %constant_dynamic-update-slice_fusion.8), channel_id=1, source_target_pairs={{0,2},{1,3},{2,0},{3,1},{4,6},{5,7},{6,4},{7,5},{8,10},{9,11},{10,... | collective-permute-start | bytes 1376264 | tf_op jit(solution)/shard_map/ppermute | solution.py:66
  74.9 17.7 %collective-permute-start.21 = (bf16[32,5120]{1,0:T(8,128)(2,1)S(1)}, bf16[32,5120]{1,0:T(8,128)(2,1)S(1)}, u32[]{:S(2)}, u32[]{:S(2)}) collective-permute-start(bf16[32,5120]{1,0:T(8,128)(2,1)S(1)} %copy-done.114), channel_id=1, source_target_pairs={{0,16},{1,17},{2,18},{3,19},{4,20},{5,21},{6,22},{7,23},{8,24},{9,... | collective-permute-start | bytes 983048 | tf_op jit(solution)/shard_map/ppermute | solution.py:66
  80.6 22.0 %collective-permute-start.23 = (bf16[256,1792]{1,0:T(8,128)(2,1)}, bf16[256,1792]{1,0:T(8,128)(2,1)S(1)}, u32[]{:S(2)}, u32[]{:S(2)}) collective-permute-start(bf16[256,1792]{1,0:T(8,128)(2,1)} %constant_dynamic-update-slice_fusion.14.refs_5_.refs_4_), channel_id=1, source_target_pairs={{0,4},{1,5},{2,6},{3,7},{4,0},{5,1},{6,2},{7,3},{8,12},{9,13},{10,... | collective-permute-start | bytes 2752520 | tf_op jit(solution)/shard_map/ppermute | solution.py:66
  81.1 21.5 %collective-permute-start.22 = (bf16[256,1792]{1,0:T(8,128)(2,1)S(1)}, bf16[256,1792]{1,0:T(8,128)(2,1)S(1)}, u32[]{:S(2)}, u32[]{:S(2)}) collective-permute-start(bf16[256,1792]{1,0:T(8,128)(2,1)S(1)} %constant_dynamic-update-slice_fusion.12.refs_1_.refs_0_), channel_id=1, source_target_pairs={{0,2},{1,3},{2,0},{3,1},{4,6},{5,7},{6,4},{7,5},{8,10},{9,11},{10,... | collective-permute-start | bytes 2752520 | tf_op jit(solution)/shard_map/ppermute | solution.py:66
  92.6 17.4 %collective-permute-start.24 = (bf16[256,1792]{1,0:T(8,128)(2,1)S(1)}, bf16[256,1792]{1,0:T(8,128)(2,1)S(1)}, u32[]{:S(2)}, u32[]{:S(2)}) collective-permute-start(bf16[256,1792]{1,0:T(8,128)(2,1)S(1)} %constant_dynamic-update-slice_fusion.12.refs_1_.refs_0_), channel_id=1, source_target_pairs={{0,1},{1,0},{2,3},{3,2},{4,5},{5,4},{6,7},{7,6},{8,9},{9,8},{10,11... | collective-permute-start | bytes 2752520 | tf_op jit(solution)/shard_map/ppermute | solution.py:66
  92.7 17.3 %collective-permute-start.25 = (bf16[256,1792]{1,0:T(8,128)(2,1)}, bf16[256,1792]{1,0:T(8,128)(2,1)S(1)}, u32[]{:S(2)}, u32[]{:S(2)}) collective-permute-start(bf16[256,1792]{1,0:T(8,128)(2,1)} %constant_dynamic-update-slice_fusion.14.refs_5_.refs_4_), channel_id=1, source_target_pairs={{0,1},{1,0},{2,3},{3,2},{4,5},{5,4},{6,7},{7,6},{8,9},{9,8},{10,11... | collective-permute-start | bytes 2752520 | tf_op jit(solution)/shard_map/ppermute | solution.py:66
  93.2 16.8 %collective-permute-start.26 = (bf16[64,5120]{1,0:T(8,128)(2,1)S(1)}, bf16[64,5120]{1,0:T(8,128)(2,1)S(1)}, u32[]{:S(2)}, u32[]{:S(2)}) collective-permute-start(bf16[64,5120]{1,0:T(8,128)(2,1)S(1)} %constant_dynamic-update-slice_fusion.16), channel_id=1, source_target_pairs={{0,8},{1,9},{2,10},{3,11},{4,12},{5,13},{6,14},{7,15},{8,0},{9,1},... | collective-permute-start | bytes 1966088 | tf_op jit(solution)/shard_map/ppermute | solution.py:66
  112.0 25.3 %collective-permute-start.30 = (bf16[128,2560]{1,0:T(8,128)(2,1)S(1)}, bf16[128,2560]{1,0:T(8,128)(2,1)}, u32[]{:S(2)}, u32[]{:S(2)}) collective-permute-start(bf16[128,2560]{1,0:T(8,128)(2,1)S(1)} %get-tuple-element.395), channel_id=1, source_target_pairs={{0,4},{1,5},{2,6},{3,7},{4,0},{5,1},{6,2},{7,3},{8,12},{9,13},{10,... | collective-permute-start | bytes 1966088 | tf_op jit(solution)/shard_map/ppermute | solution.py:66
  113.5 23.8 %collective-permute-start.31 = (bf16[128,2560]{1,0:T(8,128)(2,1)}, bf16[128,2560]{1,0:T(8,128)(2,1)}, u32[]{:S(2)}, u32[]{:S(2)}) collective-permute-start(bf16[128,2560]{1,0:T(8,128)(2,1)} %get-tuple-element.397), channel_id=1, source_target_pairs={{0,2},{1,3},{2,0},{3,1},{4,6},{5,7},{6,4},{7,5},{8,10},{9,11},{10,... | collective-permute-start | bytes 1966088 | tf_op jit(solution)/shard_map/ppermute | solution.py:66
  118.8 20.2 %collective-permute-start.32 = (bf16[64,3072]{1,0:T(8,128)(2,1)S(1)}, bf16[64,3072]{1,0:T(8,128)(2,1)S(1)}, u32[]{:S(2)}, u32[]{:S(2)}) collective-permute-start(bf16[64,3072]{1,0:T(8,128)(2,1)S(1)} %get-tuple-element.743), channel_id=1, source_target_pairs={{0,2},{1,3},{2,0},{3,1},{4,6},{5,7},{6,4},{7,5},{8,10},{9,11},{10,... | collective-permute-start | bytes 1179656 | tf_op jit(solution)/shard_map/ppermute | solution.py:66
  120.4 18.6 %collective-permute-start.33 = (bf16[64,3072]{1,0:T(8,128)(2,1)S(1)}, bf16[64,3072]{1,0:T(8,128)(2,1)S(1)}, u32[]{:S(2)}, u32[]{:S(2)}) collective-permute-start(bf16[64,3072]{1,0:T(8,128)(2,1)S(1)} %get-tuple-element.741), channel_id=1, source_target_pairs={{0,4},{1,5},{2,6},{3,7},{4,0},{5,1},{6,2},{7,3},{8,12},{9,13},{10,... | collective-permute-start | bytes 1179656 | tf_op jit(solution)/shard_map/ppermute | solution.py:66
  122.0 15.3 %collective-permute-start.34 = (bf16[32,4096]{1,0:T(8,128)(2,1)S(1)}, bf16[32,4096]{1,0:T(8,128)(2,1)S(1)}, u32[]{:S(2)}, u32[]{:S(2)}) collective-permute-start(bf16[32,4096]{1,0:T(8,128)(2,1)S(1)} %copy-done.132), channel_id=1, source_target_pairs={{0,16},{1,17},{2,18},{3,19},{4,20},{5,21},{6,22},{7,23},{8,24},{9,... | collective-permute-start | bytes 786440 | tf_op jit(solution)/shard_map/ppermute | solution.py:66
  140.4 19.3 %collective-permute-start.37 = (bf16[64,4096]{1,0:T(8,128)(2,1)S(1)}, bf16[64,4096]{1,0:T(8,128)(2,1)S(1)}, u32[]{:S(2)}, u32[]{:S(2)}) collective-permute-start(bf16[64,4096]{1,0:T(8,128)(2,1)S(1)} %constant_dynamic-update-slice_fusion.20), channel_id=1, source_target_pairs={{0,8},{1,9},{2,10},{3,11},{4,12},{5,13},{6,14},{7,15},{8,0},{9,1},... | collective-permute-start | bytes 1572872 | tf_op jit(solution)/shard_map/ppermute | solution.py:66
  140.9 18.8 %collective-permute-start.36 = (bf16[32,3072]{1,0:T(8,128)(2,1)S(1)}, bf16[32,3072]{1,0:T(8,128)(2,1)S(1)}, u32[]{:S(2)}, u32[]{:S(2)}) collective-permute-start(bf16[32,3072]{1,0:T(8,128)(2,1)S(1)} %get-tuple-element.794), channel_id=1, source_target_pairs={{0,2},{1,3},{2,0},{3,1},{4,6},{5,7},{6,4},{7,5},{8,10},{9,11},{10,... | collective-permute-start | bytes 589832 | tf_op jit(solution)/shard_map/ppermute | solution.py:66
  143.6 16.1 %collective-permute-start.35 = (bf16[32,3072]{1,0:T(8,128)(2,1)S(1)}, bf16[32,3072]{1,0:T(8,128)(2,1)S(1)}, u32[]{:S(2)}, u32[]{:S(2)}) collective-permute-start(bf16[32,3072]{1,0:T(8,128)(2,1)S(1)} %get-tuple-element.796), channel_id=1, source_target_pairs={{0,4},{1,5},{2,6},{3,7},{4,0},{5,1},{6,2},{7,3},{8,12},{9,13},{10,... | collective-permute-start | bytes 589832 | tf_op jit(solution)/shard_map/ppermute | solution.py:66
  145.3 34.3 %collective-permute-start.43 = (bf16[256,2560]{1,0:T(8,128)(2,1)S(1)}, bf16[256,2560]{1,0:T(8,128)(2,1)S(1)}, u32[]{:S(2)}, u32[]{:S(2)}) collective-permute-start(bf16[256,2560]{1,0:T(8,128)(2,1)S(1)} %constant_dynamic-update-slice_fusion.24.refs_5_.refs_4_), channel_id=1, source_target_pairs={{0,4},{1,5},{2,6},{3,7},{4,0},{5,1},{6,2},{7,3},{8,12},{9,13},{10,... | collective-permute-start | bytes 3932168 | tf_op jit(solution)/shard_map/ppermute | solution.py:66
  148.0 31.8 %collective-permute-start.42 = (bf16[256,2560]{1,0:T(8,128)(2,1)S(1)}, bf16[256,2560]{1,0:T(8,128)(2,1)S(1)}, u32[]{:S(2)}, u32[]{:S(2)}) collective-permute-start(bf16[256,2560]{1,0:T(8,128)(2,1)S(1)} %constant_dynamic-update-slice_fusion.22.refs_1_.refs_0_), channel_id=1, source_target_pairs={{0,2},{1,3},{2,0},{3,1},{4,6},{5,7},{6,4},{7,5},{8,10},{9,11},{10,... | collective-permute-start | bytes 3932168 | tf_op jit(solution)/shard_map/ppermute | solution.py:66
  168.1 11.7 %collective-permute-start.41 = (bf16[8,6144]{1,0:T(8,128)(2,1)S(1)}, bf16[8,6144]{1,0:T(8,128)(2,1)S(1)}, u32[]{:S(2)}, u32[]{:S(2)}) collective-permute-start(bf16[8,6144]{1,0:T(8,128)(2,1)S(1)} %get-tuple-element.814), channel_id=1, source_target_pairs={{0,16},{1,17},{2,18},{3,19},{4,20},{5,21},{6,22},{7,23},{8,24},{9,... | collective-permute-start | bytes 294920 | tf_op jit(solution)/shard_map/ppermute | solution.py:66
  169.8 26.6 %collective-permute-start.46 = (bf16[128,2048]{1,0:T(8,128)(2,1)S(1)}, bf16[128,2048]{1,0:T(8,128)(2,1)S(1)}, u32[]{:S(2)}, u32[]{:S(2)}) collective-permute-start(bf16[128,2048]{1,0:T(8,128)(2,1)S(1)} %get-tuple-element.435), channel_id=1, source_target_pairs={{0,4},{1,5},{2,6},{3,7},{4,0},{5,1},{6,2},{7,3},{8,12},{9,13},{10,... | collective-permute-start | bytes 1572872 | tf_op jit(solution)/shard_map/ppermute | solution.py:66
  170.4 26.1 %collective-permute-start.47 = (bf16[128,2048]{1,0:T(8,128)(2,1)S(1)}, bf16[128,2048]{1,0:T(8,128)(2,1)S(1)}, u32[]{:S(2)}, u32[]{:S(2)}) collective-permute-start(bf16[128,2048]{1,0:T(8,128)(2,1)S(1)} %get-tuple-element.437), channel_id=1, source_target_pairs={{0,2},{1,3},{2,0},{3,1},{4,6},{5,7},{6,4},{7,5},{8,10},{9,11},{10,... | collective-permute-start | bytes 1572872 | tf_op jit(solution)/shard_map/ppermute | solution.py:66
  196.6 29.1 %collective-permute-start.49 = (bf16[256,2048]{1,0:T(8,128)(2,1)S(1)}, bf16[256,2048]{1,0:T(8,128)(2,1)S(1)}, u32[]{:S(2)}, u32[]{:S(2)}) collective-permute-start(bf16[256,2048]{1,0:T(8,128)(2,1)S(1)} %constant_dynamic-update-slice_fusion.30.refs_5_), channel_id=1, source_target_pairs={{0,4},{1,5},{2,6},{3,7},{4,0},{5,1},{6,2},{7,3},{8,12},{9,13},{10,... | collective-permute-start | bytes 3145736 | tf_op jit(solution)/shard_map/ppermute | solution.py:66
  197.2 28.5 %collective-permute-start.51 = (bf16[256,2048]{1,0:T(8,128)(2,1)S(1)}, bf16[256,2048]{1,0:T(8,128)(2,1)S(1)}, u32[]{:S(2)}, u32[]{:S(2)}) collective-permute-start(bf16[256,2048]{1,0:T(8,128)(2,1)S(1)} %constant_dynamic-update-slice_fusion.30.refs_5_), channel_id=1, source_target_pairs={{0,1},{1,0},{2,3},{3,2},{4,5},{5,4},{6,7},{7,6},{8,9},{9,8},{10,11... | collective-permute-start | bytes 3145736 | tf_op jit(solution)/shard_map/ppermute | solution.py:66
  197.3 28.4 %collective-permute-start.48 = (bf16[256,2048]{1,0:T(8,128)(2,1)S(1)}, bf16[256,2048]{1,0:T(8,128)(2,1)S(1)}, u32[]{:S(2)}, u32[]{:S(2)}) collective-permute-start(bf16[256,2048]{1,0:T(8,128)(2,1)S(1)} %constant_dynamic-update-slice_fusion.28.refs_1_), channel_id=1, source_target_pairs={{0,2},{1,3},{2,0},{3,1},{4,6},{5,7},{6,4},{7,5},{8,10},{9,11},{10,... | collective-permute-start | bytes 3145736 | tf_op jit(solution)/shard_map/ppermute | solution.py:66
  198.2 27.6 %collective-permute-start.50 = (bf16[256,2048]{1,0:T(8,128)(2,1)S(1)}, bf16[256,2048]{1,0:T(8,128)(2,1)S(1)}, u32[]{:S(2)}, u32[]{:S(2)}) collective-permute-start(bf16[256,2048]{1,0:T(8,128)(2,1)S(1)} %constant_dynamic-update-slice_fusion.28.refs_1_), channel_id=1, source_target_pairs={{0,1},{1,0},{2,3},{3,2},{4,5},{5,4},{6,7},{7,6},{8,9},{9,8},{10,11... | collective-permute-start | bytes 3145736 | tf_op jit(solution)/shard_map/ppermute | solution.py:66
  199.4 26.3 %collective-permute-start.52 = (bf16[256,1024]{1,0:T(8,128)(2,1)S(1)}, bf16[256,1024]{1,0:T(8,128)(2,1)S(1)}, u32[]{:S(2)}, u32[]{:S(2)}) collective-permute-start(bf16[256,1024]{1,0:T(8,128)(2,1)S(1)} %constant_dynamic-update-slice_fusion.32), channel_id=1, source_target_pairs={{0,16},{1,17},{2,18},{3,19},{4,20},{5,21},{6,22},{7,23},{8,24},{9,... | collective-permute-start | bytes 1572872 | tf_op jit(solution)/shard_map/ppermute | solution.py:66
  226.5 25.5 %collective-permute-start.55 = (bf16[512,1024]{1,0:T(8,128)(2,1)S(1)}, bf16[512,1024]{1,0:T(8,128)(2,1)}, u32[]{:S(2)}, u32[]{:S(2)}) collective-permute-start(bf16[512,1024]{1,0:T(8,128)(2,1)S(1)} %constant_dynamic-update-slice_fusion.34), channel_id=1, source_target_pairs={{0,8},{1,9},{2,10},{3,11},{4,12},{5,13},{6,14},{7,15},{8,0},{9,1},... | collective-permute-start | bytes 3145736 | tf_op jit(solution)/shard_map/ppermute | solution.py:66
  253.7 20.1 %collective-permute-start.57 = (bf16[384,1024]{1,0:T(8,128)(2,1)}, bf16[384,1024]{1,0:T(8,128)(2,1)S(1)}, u32[]{:S(2)}, u32[]{:S(2)}) collective-permute-start(bf16[384,1024]{1,0:T(8,128)(2,1)} %get-tuple-element.455), channel_id=1, source_target_pairs={{0,2},{1,3},{2,0},{3,1},{4,6},{5,7},{6,4},{7,5},{8,10},{9,11},{10,... | collective-permute-start | bytes 2359304 | tf_op jit(solution)/shard_map/ppermute | solution.py:66
  303.2 19.6 %collective-permute-start.63 = (bf16[384,1024]{1,0:T(8,128)(2,1)S(1)}, bf16[384,1024]{1,0:T(8,128)(2,1)S(1)}, u32[]{:S(2)}, u32[]{:S(2)}) collective-permute-start(bf16[384,1024]{1,0:T(8,128)(2,1)S(1)} %add_convert_fusion.1), channel_id=1, source_target_pairs={{0,2},{1,3},{2,0},{3,1},{4,6},{5,7},{6,4},{7,5},{8,10},{9,11},{10,... | collective-permute-start | bytes 2359304 | tf_op jit(solution)/shard_map/ppermute | solution.py:66
  340.4 11.1 %collective-permute-start.64 = (bf16[512,4096]{1,0:T(8,128)(2,1)}, bf16[512,4096]{1,0:T(8,128)(2,1)S(1)}, u32[]{:S(2)}, u32[]{:S(2)}) collective-permute-start(bf16[512,4096]{1,0:T(8,128)(2,1)} %shard_map.466), channel_id=1, source_target_pairs={{0,1},{1,0},{2,3},{3,2},{4,5},{5,4},{6,7},{7,6},{8,9},{9,8},{10,11... | collective-permute-start | bytes 12582920 | tf_op jit(solution)/shard_map/ppermute | solution.py:66
  367.7 15.3 %collective-permute-start.65 = (bf16[512,4096]{1,0:T(8,128)(2,1)}, bf16[512,4096]{1,0:T(8,128)(2,1)}, u32[]{:S(2)}, u32[]{:S(2)}) collective-permute-start(bf16[512,4096]{1,0:T(8,128)(2,1)} %shard_map.469), channel_id=1, source_target_pairs={{0,1},{1,0},{2,3},{3,2},{4,5},{5,4},{6,7},{7,6},{8,9},{9,8},{10,11... | collective-permute-start | bytes 12582920 | tf_op jit(solution)/shard_map/ppermute | solution.py:66
  368.2 28.7 %collective-permute-start.68 = (bf16[512,1024]{1,0:T(8,128)(2,1)}, bf16[512,1024]{1,0:T(8,128)(2,1)}, u32[]{:S(2)}, u32[]{:S(2)}) collective-permute-start(bf16[512,1024]{1,0:T(8,128)(2,1)} %fusion.38), channel_id=1, source_target_pairs={{0,8},{1,9},{2,10},{3,11},{4,12},{5,13},{6,14},{7,15},{8,0},{9,1},... | collective-permute-start | bytes 3145736 | tf_op jit(solution)/shard_map/ppermute | solution.py:66
  369.1 27.9 %collective-permute-start.66 = (bf16[256,2048]{1,0:T(8,128)(2,1)}, bf16[256,2048]{1,0:T(8,128)(2,1)}, u32[]{:S(2)}, u32[]{:S(2)}) collective-permute-start(bf16[256,2048]{1,0:T(8,128)(2,1)} %get-tuple-element.480), channel_id=1, source_target_pairs={{0,2},{1,3},{2,0},{3,1},{4,6},{5,7},{6,4},{7,5},{8,10},{9,11},{10,... | collective-permute-start | bytes 3145736 | tf_op jit(solution)/shard_map/ppermute | solution.py:66
  370.0 27.0 %collective-permute-start.67 = (bf16[256,2048]{1,0:T(8,128)(2,1)}, bf16[256,2048]{1,0:T(8,128)(2,1)}, u32[]{:S(2)}, u32[]{:S(2)}) collective-permute-start(bf16[256,2048]{1,0:T(8,128)(2,1)} %get-tuple-element.481), channel_id=1, source_target_pairs={{0,4},{1,5},{2,6},{3,7},{4,0},{5,1},{6,2},{7,3},{8,12},{9,13},{10,... | collective-permute-start | bytes 3145736 | tf_op jit(solution)/shard_map/ppermute | solution.py:66
  402.5 37.3 %collective-permute-start.71 = (bf16[256,2048]{1,0:T(8,128)(2,1)S(1)}, bf16[256,2048]{1,0:T(8,128)(2,1)S(1)}, u32[]{:S(2)}, u32[]{:S(2)}) collective-permute-start(bf16[256,2048]{1,0:T(8,128)(2,1)S(1)} %copy-done.81), channel_id=1, source_target_pairs={{0,2},{1,3},{2,0},{3,1},{4,6},{5,7},{6,4},{7,5},{8,10},{9,11},{10,... | collective-permute-start | bytes 3145736 | tf_op jit(solution)/shard_map/ppermute | solution.py:66
  403.7 36.1 %collective-permute-start.72 = (bf16[256,2048]{1,0:T(8,128)(2,1)}, bf16[256,2048]{1,0:T(8,128)(2,1)S(1)}, u32[]{:S(2)}, u32[]{:S(2)}) collective-permute-start(bf16[256,2048]{1,0:T(8,128)(2,1)} %get-tuple-element.502), channel_id=1, source_target_pairs={{0,4},{1,5},{2,6},{3,7},{4,0},{5,1},{6,2},{7,3},{8,12},{9,13},{10,... | collective-permute-start | bytes 3145736 | tf_op jit(solution)/shard_map/ppermute | solution.py:66
  406.6 33.1 %collective-permute-start.73 = (bf16[256,1024]{1,0:T(8,128)(2,1)}, bf16[256,1024]{1,0:T(8,128)(2,1)S(1)}, u32[]{:S(2)}, u32[]{:S(2)}) collective-permute-start(bf16[256,1024]{1,0:T(8,128)(2,1)} %get-tuple-element.734), channel_id=1, source_target_pairs={{0,16},{1,17},{2,18},{3,19},{4,20},{5,21},{6,22},{7,23},{8,24},{9,... | collective-permute-start | bytes 1572872 | tf_op jit(solution)/shard_map/ppermute | solution.py:66
  408.1 31.7 %collective-permute-start.69 = (bf16[128,2048]{1,0:T(8,128)(2,1)}, bf16[128,2048]{1,0:T(8,128)(2,1)}, u32[]{:S(2)}, u32[]{:S(2)}) collective-permute-start(bf16[128,2048]{1,0:T(8,128)(2,1)} %get-tuple-element.499), channel_id=1, source_target_pairs={{0,4},{1,5},{2,6},{3,7},{4,0},{5,1},{6,2},{7,3},{8,12},{9,13},{10,... | collective-permute-start | bytes 1572872 | tf_op jit(solution)/shard_map/ppermute | solution.py:66
  409.6 30.2 %collective-permute-start.70 = (bf16[128,2048]{1,0:T(8,128)(2,1)}, bf16[128,2048]{1,0:T(8,128)(2,1)S(1)}, u32[]{:S(2)}, u32[]{:S(2)}) collective-permute-start(bf16[128,2048]{1,0:T(8,128)(2,1)} %get-tuple-element.500), channel_id=1, source_target_pairs={{0,2},{1,3},{2,0},{3,1},{4,6},{5,7},{6,4},{7,5},{8,10},{9,11},{10,... | collective-permute-start | bytes 1572872 | tf_op jit(solution)/shard_map/ppermute | solution.py:66
  451.1 20.9 %collective-permute-start.75 = (bf16[512,3072]{1,0:T(8,128)(2,1)}, bf16[512,3072]{1,0:T(8,128)(2,1)}, u32[]{:S(2)}, u32[]{:S(2)}) collective-permute-start(bf16[512,3072]{1,0:T(8,128)(2,1)} %shard_map.476), channel_id=1, source_target_pairs={{0,1},{1,0},{2,3},{3,2},{4,5},{5,4},{6,7},{7,6},{8,9},{9,8},{10,11... | collective-permute-start | bytes 9437192 | tf_op jit(solution)/shard_map/ppermute | solution.py:66
  452.2 19.8 %collective-permute-start.76 = (bf16[128,2048]{1,0:T(8,128)(2,1)}, bf16[128,2048]{1,0:T(8,128)(2,1)S(1)}, u32[]{:S(2)}, u32[]{:S(2)}) collective-permute-start(bf16[128,2048]{1,0:T(8,128)(2,1)} %add_convert_fusion.17), channel_id=1, source_target_pairs={{0,4},{1,5},{2,6},{3,7},{4,0},{5,1},{6,2},{7,3},{8,12},{9,13},{10,... | collective-permute-start | bytes 1572872 | tf_op jit(solution)/shard_map/ppermute | solution.py:66
  452.8 19.2 %collective-permute-start.77 = (bf16[128,2048]{1,0:T(8,128)(2,1)S(1)}, bf16[128,2048]{1,0:T(8,128)(2,1)S(1)}, u32[]{:S(2)}, u32[]{:S(2)}) collective-permute-start(bf16[128,2048]{1,0:T(8,128)(2,1)S(1)} %copy-done.147), channel_id=1, source_target_pairs={{0,2},{1,3},{2,0},{3,1},{4,6},{5,7},{6,4},{7,5},{8,10},{9,11},{10,... | collective-permute-start | bytes 1572872 | tf_op jit(solution)/shard_map/ppermute | solution.py:66
  453.6 18.3 %collective-permute-start.78 = (bf16[64,4096]{1,0:T(8,128)(2,1)S(1)}, bf16[64,4096]{1,0:T(8,128)(2,1)S(1)}, u32[]{:S(2)}, u32[]{:S(2)}) collective-permute-start(bf16[64,4096]{1,0:T(8,128)(2,1)S(1)} %copy-done.152), channel_id=1, source_target_pairs={{0,8},{1,9},{2,10},{3,11},{4,12},{5,13},{6,14},{7,15},{8,0},{9,1},... | collective-permute-start | bytes 1572872 | tf_op jit(solution)/shard_map/ppermute | solution.py:66
  455.4 16.5 %collective-permute-start.79 = (bf16[128,1024]{1,0:T(8,128)(2,1)S(1)}, bf16[128,1024]{1,0:T(8,128)(2,1)S(1)}, u32[]{:S(2)}, u32[]{:S(2)}) collective-permute-start(bf16[128,1024]{1,0:T(8,128)(2,1)S(1)} %get-tuple-element.782), channel_id=1, source_target_pairs={{0,4},{1,5},{2,6},{3,7},{4,0},{5,1},{6,2},{7,3},{8,12},{9,13},{10,... | collective-permute-start | bytes 786440 | tf_op jit(solution)/shard_map/ppermute | solution.py:66
  484.9 15.6 %collective-permute-start.80 = (bf16[512,512]{1,0:T(8,128)(2,1)}, bf16[512,512]{1,0:T(8,128)(2,1)}, u32[]{:S(2)}, u32[]{:S(2)}) collective-permute-start(bf16[512,512]{1,0:T(8,128)(2,1)} %slice.721), channel_id=1, source_target_pairs={{0,1},{1,0},{2,3},{3,2},{4,5},{5,4},{6,7},{7,6},{8,9},{9,8},{10,11... | collective-permute-start | bytes 1572872 | tf_op jit(solution)/shard_map/ppermute | solution.py:66
  484.9 15.6 %collective-permute-start.81 = (bf16[32,4096]{1,0:T(8,128)(2,1)}, bf16[32,4096]{1,0:T(8,128)(2,1)}, u32[]{:S(2)}, u32[]{:S(2)}) collective-permute-start(bf16[32,4096]{1,0:T(8,128)(2,1)} %add_convert_fusion.34), channel_id=1, source_target_pairs={{0,16},{1,17},{2,18},{3,19},{4,20},{5,21},{6,22},{7,23},{8,24},{9,... | collective-permute-start | bytes 786440 | tf_op jit(solution)/shard_map/ppermute | solution.py:66
  505.1 27.9 %collective-permute-start.82 = (bf16[256,2304]{1,0:T(8,128)(2,1)S(1)}, bf16[256,2304]{1,0:T(8,128)(2,1)S(1)}, u32[]{:S(2)}, u32[]{:S(2)}) collective-permute-start(bf16[256,2304]{1,0:T(8,128)(2,1)S(1)} %pad_maximum_fusion.4), channel_id=1, source_target_pairs={{0,2},{1,3},{2,0},{3,1},{4,6},{5,7},{6,4},{7,5},{8,10},{9,11},{10,... | collective-permute-start | bytes 3538952 | tf_op jit(solution)/shard_map/ppermute | solution.py:66
  506.0 27.5 %collective-permute-start.83 = (bf16[256,2304]{1,0:T(8,128)(2,1)S(1)}, bf16[256,2304]{1,0:T(8,128)(2,1)S(1)}, u32[]{:S(2)}, u32[]{:S(2)}) collective-permute-start(bf16[256,2304]{1,0:T(8,128)(2,1)S(1)} %pad_maximum_fusion.5), channel_id=1, source_target_pairs={{0,4},{1,5},{2,6},{3,7},{4,0},{5,1},{6,2},{7,3},{8,12},{9,13},{10,... | collective-permute-start | bytes 3538952 | tf_op jit(solution)/shard_map/ppermute | solution.py:66
  506.6 21.4 %collective-permute-start.86 = (bf16[64,4096]{1,0:T(8,128)(2,1)S(1)}, bf16[64,4096]{1,0:T(8,128)(2,1)S(1)}, u32[]{:S(2)}, u32[]{:S(2)}) collective-permute-start(bf16[64,4096]{1,0:T(8,128)(2,1)S(1)} %pad_maximum_fusion.17), channel_id=1, source_target_pairs={{0,8},{1,9},{2,10},{3,11},{4,12},{5,13},{6,14},{7,15},{8,0},{9,1},... | collective-permute-start | bytes 1572872 | tf_op jit(solution)/shard_map/ppermute | solution.py:66
  513.2 14.8 %collective-permute-start.85 = (bf16[16,8192]{1,0:T(8,128)(2,1)S(1)}, bf16[16,8192]{1,0:T(8,128)(2,1)S(1)}, u32[]{:S(2)}, u32[]{:S(2)}) collective-permute-start(bf16[16,8192]{1,0:T(8,128)(2,1)S(1)} %constant_dynamic-update-slice_fusion.50), channel_id=1, source_target_pairs={{0,8},{1,9},{2,10},{3,11},{4,12},{5,13},{6,14},{7,15},{8,0},{9,1},... | collective-permute-start | bytes 786440 | tf_op jit(solution)/shard_map/ppermute | solution.py:66
  533.7 14.8 %collective-permute-start.90 = (bf16[32,5120]{1,0:T(8,128)(2,1)S(1)}, bf16[32,5120]{1,0:T(8,128)(2,1)S(1)}, u32[]{:S(2)}, u32[]{:S(2)}) collective-permute-start(bf16[32,5120]{1,0:T(8,128)(2,1)S(1)} %slice.875), channel_id=1, source_target_pairs={{0,4},{1,5},{2,6},{3,7},{4,0},{5,1},{6,2},{7,3},{8,12},{9,13},{10,... | collective-permute-start | bytes 983048 | tf_op jit(solution)/shard_map/ppermute | solution.py:66
  535.5 13.0 %collective-permute-start.89 = (bf16[32,4096]{1,0:T(8,128)(2,1)S(1)}, bf16[32,4096]{1,0:T(8,128)(2,1)S(1)}, u32[]{:S(2)}, u32[]{:S(2)}) collective-permute-start(bf16[32,4096]{1,0:T(8,128)(2,1)S(1)} %add_convert_fusion.30), channel_id=1, source_target_pairs={{0,16},{1,17},{2,18},{3,19},{4,20},{5,21},{6,22},{7,23},{8,24},{9,... | collective-permute-start | bytes 786440 | tf_op jit(solution)/shard_map/ppermute | solution.py:66
  537.4 14.9 %collective-permute-start.88 = (bf16[128,2304]{1,0:T(8,128)(2,1)S(1)}, bf16[128,2304]{1,0:T(8,128)(2,1)S(1)}, u32[]{:S(2)}, u32[]{:S(2)}) collective-permute-start(bf16[128,2304]{1,0:T(8,128)(2,1)S(1)} %get-tuple-element.730), channel_id=1, source_target_pairs={{0,2},{1,3},{2,0},{3,1},{4,6},{5,7},{6,4},{7,5},{8,10},{9,11},{10,... | collective-permute-start | bytes 1769480 | tf_op jit(solution)/shard_map/ppermute | solution.py:66
  538.7 16.1 %collective-permute-start.87 = (bf16[128,2304]{1,0:T(8,128)(2,1)S(1)}, bf16[128,2304]{1,0:T(8,128)(2,1)S(1)}, u32[]{:S(2)}, u32[]{:S(2)}) collective-permute-start(bf16[128,2304]{1,0:T(8,128)(2,1)S(1)} %get-tuple-element.732), channel_id=1, source_target_pairs={{0,4},{1,5},{2,6},{3,7},{4,0},{5,1},{6,2},{7,3},{8,12},{9,13},{10,... | collective-permute-start | bytes 1769480 | tf_op jit(solution)/shard_map/ppermute | solution.py:66
  554.8 14.9 %collective-permute-start.94 = (bf16[64,5120]{1,0:T(8,128)(2,1)S(1)}, bf16[64,5120]{1,0:T(8,128)(2,1)S(1)}, u32[]{:S(2)}, u32[]{:S(2)}) collective-permute-start(bf16[64,5120]{1,0:T(8,128)(2,1)S(1)} %constant_dynamic-update-slice_fusion.56), channel_id=1, source_target_pairs={{0,2},{1,3},{2,0},{3,1},{4,6},{5,7},{6,4},{7,5},{8,10},{9,11},{10,... | collective-permute-start | bytes 1966088 | tf_op jit(solution)/shard_map/ppermute | solution.py:66
  557.2 12.6 %collective-permute-start.92 = (bf16[64,4608]{1,0:T(8,128)(2,1)S(1)}, bf16[64,4608]{1,0:T(8,128)(2,1)S(1)}, u32[]{:S(2)}, u32[]{:S(2)}) collective-permute-start(bf16[64,4608]{1,0:T(8,128)(2,1)S(1)} %pad_maximum_fusion.13), channel_id=1, source_target_pairs={{0,8},{1,9},{2,10},{3,11},{4,12},{5,13},{6,14},{7,15},{8,0},{9,1},... | collective-permute-start | bytes 1769480 | tf_op jit(solution)/shard_map/ppermute | solution.py:66
  570.7 22.2 %collective-permute-start.97 = (bf16[32,4608]{1,0:T(8,128)(2,1)}, bf16[32,4608]{1,0:T(8,128)(2,1)}, u32[]{:S(2)}, u32[]{:S(2)}) collective-permute-start(bf16[32,4608]{1,0:T(8,128)(2,1)} %get-tuple-element.747), channel_id=1, source_target_pairs={{0,16},{1,17},{2,18},{3,19},{4,20},{5,21},{6,22},{7,23},{8,24},{9,... | collective-permute-start | bytes 884744 | tf_op jit(solution)/shard_map/ppermute | solution.py:66
  573.4 11.2 %collective-permute-start.95 = (bf16[128,5120]{1,0:T(8,128)(2,1)}, bf16[128,5120]{1,0:T(8,128)(2,1)}, u32[]{:S(2)}, u32[]{:S(2)}) collective-permute-start(bf16[128,5120]{1,0:T(8,128)(2,1)} %pad_maximum_fusion.3), channel_id=1, source_target_pairs={{0,1},{1,0},{2,3},{3,2},{4,5},{5,4},{6,7},{7,6},{8,9},{9,8},{10,11... | collective-permute-start | bytes 3932168 | tf_op jit(solution)/shard_map/ppermute | solution.py:66
  (243 other events, 1969.7 us)

commit v5 on v4

--- a/solution.py
+++ b/solution.py
@@ -118,8 +118,8 @@
 
 
 def sum_all(value, bits, devices):
-    for at in range(0, len(bits), 3):
-        masks = place_masks(bits[at : at + 3])[1:]
+    for at in range(0, len(bits), 2):
+        masks = place_masks(bits[at : at + 2])[1:]
         value = value + sum(swapped(value, mask, devices) for mask in masks)
     return value
 
@@ -153,7 +153,7 @@
         out_shape=outs,
         out_specs=out_specs,
         scratch_shapes=scratch,
-        compiler_params=pltpu.CompilerParams(vmem_limit_bytes=48 << 20),
+        compiler_params=pltpu.CompilerParams(vmem_limit_bytes=24 << 20),
         cost_estimate=pl.CostEstimate(flops=1000, bytes_accessed=1000, transcendentals=0),
     )(*given)
 

time: 647 us -> 606 us (0.937)
  Pallas kernels: 180 us -> 135 us
  waiting for transfers between devices: 170 us -> 196 us
  local copies, waits for them, and re-layouts: 74.5 us -> 62 us
  other arithmetic: 72.7 us -> 63.7 us
    pallas_call x25, Pallas kernels: 180 us -> 135 us  [run(): pl.pallas_call(body, grid=grid, in_specs=specs, out_shape=outs, out_specs...]
    ppermute x108 -> x105, waiting for transfers between devices: 170 us -> 196 us  [swapped(): lax.ppermute(value, ('dp', 'vocab'), [(i, i ^ mask) for i in range(device...]
    convert_element_type x29, other arithmetic: 19.3 us -> 12.4 us  [added(): return (mine.astype(F32) + theirs.astype(F32)).astype(out)]
    unnamed x439 -> x485, local copies, waits for them, and re-layouts: 47.2 us -> 41.1 us
    ppermute x108 -> x105, starting transfers between devices: 94.1 us -> 94 us  [swapped(): lax.ppermute(value, ('dp', 'vocab'), [(i, i ^ mask) for i in range(device...]
  transfers between devices with their start and end apart: 108 -> 105, of which waited for: 42 -> 48; matrix products, arithmetic and copies ran while one was open for 14% -> 14% of each run, Pallas kernels for 23% -> 19%
where the time goes in v5:
time: 606 us; the launch traced here: 596 us
  waiting for transfers between devices  196 us (32%)
  Pallas kernels  135 us (22%)
  starting transfers between devices  94 us (16%)
  other arithmetic  63.7 us (11%)
  local copies, waits for them, and re-layouts  62 us (10%)
  matrix products  32.5 us (5%)
  between operations  12.7 us (2%)
    ppermute x105, waiting for transfers between devices, swapped(): lax.ppermute(value, ('dp', 'vocab'), [(i, i ^ mask) for i in range(device...  196 us
    pallas_call x25, Pallas kernels, run(): pl.pallas_call(body, grid=grid, in_specs=specs, out_shape=outs, out_specs...  135 us
    ppermute x105, starting transfers between devices, swapped(): lax.ppermute(value, ('dp', 'vocab'), [(i, i ^ mask) for i in range(device...  94 us
    unnamed x485, local copies, waits for them, and re-layouts  41.1 us
    dot_general x11, matrix products, matmul(): return jnp.dot(left, right, preferred_element_type=F32)  14.7 us
    convert_element_type x29, other arithmetic, added(): return (mine.astype(F32) + theirs.astype(F32)).astype(out)  12.4 us
  transfers between devices with their start and end apart: 105, of which 48 were waited for; matrix products, arithmetic and copies ran while one was open for 14% of the time, Pallas kernels for 19%

profile of v5, /device:TPU:0, one launch (start us, length us, event | category | flops | bytes accessed | tf_op | source)
XLA Modules:
  0.0 595.6 jit_solution(16692901848240264403)
XLA Ops:
  3.5 4.0 collective-permute-start
  20.7 2.8 collective-permute-done.3
  52.8 7.9 %collective-permute-done.14 = bf16[64,2048]{1,0:T(8,128)(2,1)S(1)} collective-permute-done((bf16[64,2048]{1,0:T(8,128)(2,1)S(1)}, bf16[64,2048]{1,0:T(8,128)(2,1)S(1)}, u32[]{:S(2)}, u32[]{:S(2)}) %collective-permute-start.14) | collective-permute-done | bytes 262176 | tf_op jit(solution)/shard_map/ppermute | solution.py:66
  60.7 2.4 collective-permute-start.15
  63.1 2.6 fusion.6
  65.7 3.9 collective-permute-done.15
  81.4 8.9 %collective-permute-done.21 = bf16[32,5120]{1,0:T(8,128)(2,1)} collective-permute-done((bf16[32,5120]{1,0:T(8,128)(2,1)S(1)}, bf16[32,5120]{1,0:T(8,128)(2,1)}, u32[]{:S(2)}, u32[]{:S(2)}) %collective-permute-start.21) | collective-permute-done | bytes 327712 | tf_op jit(solution)/shard_map/ppermute | solution.py:66
  93.4 7.5 %collective-permute-done.23.refs_6_.refs_5_ = bf16[256,1792]{1,0:T(8,128)(2,1)S(1)} collective-permute-done((bf16[256,1792]{1,0:T(8,128)(2,1)}, bf16[256,1792]{1,0:T(8,128)(2,1)S(1)}, u32[]{:S(2)}, u32[]{:S(2)}) %collective-permute-start.23) | collective-permute-done | bytes 917536 | tf_op jit(solution)/shard_map/ppermute | solution.py:66
  100.9 7.9 %collective-permute-done.26 = bf16[64,5120]{1,0:T(8,128)(2,1)S(1)} collective-permute-done((bf16[64,5120]{1,0:T(8,128)(2,1)S(1)}, bf16[64,5120]{1,0:T(8,128)(2,1)S(1)}, u32[]{:S(2)}, u32[]{:S(2)}) %collective-permute-start.26) | collective-permute-done | bytes 655392 | tf_op jit(solution)/shard_map/ppermute | solution.py:66
  123.0 3.2 shard_map.457
  126.3 5.2 shard_map.458.q_ref.k_ref.v_ref
  131.6 2.4 collective-permute-done.34
  133.9 2.8 collective-permute-done.32
  142.0 10.7 %shard_map.459 = bf16[384,1024]{1,0:T(8,128)(2,1)S(1)} custom-call(f32[384,3072]{1,0:T(8,128)S(1)} %shard_map.458.q_ref.k_ref.v_ref, f32[384,3072]{1,0:T(8,128)S(1)} %shard_map.458.q_ref.k_ref.v_ref, f32[384,3072]{1,0:T(8,128)S(1)} %shard_map.458.q_ref.k_ref.v_ref, f32[1,1024]{1,0:T(1,128)S(1)} %get-tuple-element.758.qg_ref, ...), custom_call_target="tpu_custom_call" | custom-call | flops 1000 | bytes 1000 | tf_op jit(solution)/shard_map/pallas_call | solution.py:149
  157.4 3.0 collective-permute-done.38
  164.3 10.9 %collective-permute-done.43.refs_6_.refs_5_ = bf16[256,2560]{1,0:T(8,128)(2,1)S(1)} collective-permute-done((bf16[256,2560]{1,0:T(8,128)(2,1)S(1)}, bf16[256,2560]{1,0:T(8,128)(2,1)S(1)}, u32[]{:S(2)}, u32[]{:S(2)}) %collective-permute-start.43) | collective-permute-done | bytes 1310752 | tf_op jit(solution)/shard_map/ppermute | solution.py:66
  175.8 2.4 collective-permute-done.44.refs_4_.refs_3_
  181.7 3.6 shard_map.461
  190.4 7.4 %shard_map.462 = (f32[384,4096]{1,0:T(8,128)S(1)}, bf16[384,4096]{1,0:T(8,128)(2,1)S(1)}) custom-call(bf16[384,1024]{1,0:T(8,128)(2,1)S(1)} %get-tuple-element.432.one_ref, bf16[384,1024]{1,0:T(8,128)(2,1)S(1)} %get-tuple-element.433.two_ref, f32[1,4096]{1,0:T(1,128)S(1)} %bitcast.114, ...), custom_call_target="tpu_custom_call" | custom-call | flops 1000 | bytes 1000 | tf_op jit(solution)/shard_map/pallas_call | solution.py:149
  197.8 2.7 copy-done.58
  200.5 13.9 %collective-permute-done.52 = bf16[256,1024]{1,0:T(8,128)(2,1)S(1)} collective-permute-done((bf16[256,1024]{1,0:T(8,128)(2,1)S(1)}, bf16[256,1024]{1,0:T(8,128)(2,1)S(1)}, u32[]{:S(2)}, u32[]{:S(2)}) %collective-permute-start.52) | collective-permute-done | bytes 524320 | tf_op jit(solution)/shard_map/ppermute | solution.py:66
  218.7 9.1 %shard_map.463.refs_1_.refs_2_ = f32[384,1024]{1,0:T(8,128)S(1)} custom-call(bf16[1,384,4096]{2,1,0:T(8,128)(2,1)S(1)} %bitcast.102, bf16[1024,1024]{1,0:T(8,128)(2,1)S(1)} %get-tuple-element.846.one_ref, bf16[1024,1024]{1,0:T(8,128)(2,1)S(1)} %get-tuple-element.844.two_ref, f32[1,1024]{1,0:T(1,128)S(1)} %get-tuple-element.755.refs_0_, ...), custom_call_target="tpu_custom_call" | custom-call | flops 1000 | bytes 1000 | tf_op jit(solution)/shard_map/pallas_call | solution.py:149
  230.7 3.5 shard_map.464
  235.3 4.9 collective-permute-done.55
  245.8 4.0 add_reduce_fusion.1
  251.0 12.1 %collective-permute-done.57 = bf16[384,1024]{1,0:T(8,128)(2,1)S(1)} collective-permute-done((bf16[384,1024]{1,0:T(8,128)(2,1)}, bf16[384,1024]{1,0:T(8,128)(2,1)S(1)}, u32[]{:S(2)}, u32[]{:S(2)}) %collective-permute-start.57) | collective-permute-done | bytes 786464 | tf_op jit(solution)/shard_map/ppermute | solution.py:66
  263.2 2.2 collective-permute-done.58
  276.1 2.5 collective-permute-done.61
  280.3 4.6 fusion.14
  293.7 2.8 fusion.41
  296.5 2.8 fusion.38
  299.3 13.2 %collective-permute-done.63 = bf16[384,1024]{1,0:T(8,128)(2,1)S(1)} collective-permute-done((bf16[384,1024]{1,0:T(8,128)(2,1)S(1)}, bf16[384,1024]{1,0:T(8,128)(2,1)S(1)}, u32[]{:S(2)}, u32[]{:S(2)}) %collective-permute-start.63) | collective-permute-done | bytes 786464 | tf_op jit(solution)/shard_map/ppermute | solution.py:66
  317.0 4.8 shard_map.465
  323.0 3.9 shard_map.466
  327.1 8.8 %shard_map.467 = (bf16[384,4096]{1,0:T(8,128)(2,1)S(1)}, f32[1,4096]{1,0:T(1,128)S(1)}) custom-call(bf16[384,1024]{1,0:T(8,128)(2,1)S(1)} %get-tuple-element.464.one_ref, bf16[384,1024]{1,0:T(8,128)(2,1)S(1)} %get-tuple-element.465.two_ref, f32[384,4096]{1,0:T(8,128)S(1)} %bitcast.112, bf16[256,2048]{1,0:T(8,128)(2,1)S(1)} %copy-done.52, ...), custom_call_target="tpu_custom_call" | custom-call | flops 1000 | bytes 1000 | tf_op jit(solution)/shard_map/pallas_call | solution.py:149
  336.0 4.8 shard_map.469
  340.8 4.7 shard_map.468
  348.7 7.9 %shard_map.470.refs_1_ = f32[384,1024]{1,0:T(8,128)S(1)} custom-call(bf16[1,384,4096]{2,1,0:T(8,128)(2,1)S(1)} %bitcast.106, bf16[1024,1024]{1,0:T(8,128)(2,1)S(1)} %copy-done.2, bf16[1024,1024]{1,0:T(8,128)(2,1)S(1)} %get-tuple-element.844.two_ref, bf16[256,2560]{1,0:T(8,128)(2,1)S(1)} %constant_dynamic-update-slice_fusion.22.refs_1_.refs_0_, ...), custom_call_target="tpu_custom_call" | custom-call | flops 1000 | bytes 1000 | tf_op jit(solution)/shard_map/pallas_call | solution.py:149
  356.6 5.0 shard_map.472
  362.6 2.9 shard_map.471
  365.5 5.9 collective-permute-done.68
  382.7 3.5 shard_map.473.dm_ref
  387.5 20.9 %shard_map.474 = (bf16[3,384,1024]{2,1,0:T(8,128)(2,1)S(1)}, f32[8,1024]{1,0:T(8,128)S(1)}) custom-call(f32[384,3072]{1,0:T(8,128)S(1)} %bitcast.101, f32[384,3072]{1,0:T(8,128)S(1)} %bitcast.101, f32[384,3072]{1,0:T(8,128)S(1)} %bitcast.101, f32[1,1024]{1,0:T(1,128)S(1)} %get-tuple-element.758.qg_ref, f32[1,1024]{1,0:T(1,128)S(1)} %get-tuple-element.757.kg_ref, ...), custom_call_target="tpu_custom_call" | custom-call | flops 1000 | bytes 1000 | tf_op jit(solution)/shard_map/pallas_call | solution.py:149
  408.5 2.7 collective-permute-done.69
  413.7 3.9 shard_map.476
  423.5 7.9 %shard_map.477.refs_1_ = f32[384,1024]{1,0:T(8,128)S(1)} custom-call(bf16[3,384,1024]{2,1,0:T(8,128)(2,1)S(1)} %get-tuple-element.517.right_ref, bf16[1024,1024]{1,0:T(8,128)(2,1)S(1)} %copy-done.2, bf16[1024,1024]{1,0:T(8,128)(2,1)S(1)} %get-tuple-element.844.two_ref, bf16[256,1792]{1,0:T(8,128)(2,1)S(1)} %copy-done.54, bf16[256,1792]{1,0:T(8,128)(2,1)S(1)} %copy-done.66, ...), custom_call_target="tpu_custom_call" | custom-call | flops 1000 | bytes 1000 | tf_op jit(solution)/shard_map/pallas_call | solution.py:149
  431.4 6.9 %collective-permute-done.79 = bf16[128,1024]{1,0:T(8,128)(2,1)S(1)} collective-permute-done((bf16[128,1024]{1,0:T(8,128)(2,1)S(1)}, bf16[128,1024]{1,0:T(8,128)(2,1)S(1)}, u32[]{:S(2)}, u32[]{:S(2)}) %collective-permute-start.79) | collective-permute-done | bytes 262176 | tf_op jit(solution)/shard_map/ppermute | solution.py:66
  439.4 2.9 shard_map.478
  442.6 2.1 shard_map.479
  457.4 4.1 shard_map.480
  471.6 3.8 collective-permute-done.84
  475.7 16.0 %collective-permute-done.85 = bf16[16,8192]{1,0:T(8,128)(2,1)S(1)} collective-permute-done((bf16[16,8192]{1,0:T(8,128)(2,1)S(1)}, bf16[16,8192]{1,0:T(8,128)(2,1)S(1)}, u32[]{:S(2)}, u32[]{:S(2)}) %collective-permute-start.85) | collective-permute-done | bytes 262176 | tf_op jit(solution)/shard_map/ppermute | solution.py:66
  491.7 3.8 collective-permute-done.82
  505.5 6.4 %collective-permute-done.89 = bf16[32,4096]{1,0:T(8,128)(2,1)S(1)} collective-permute-done((bf16[32,4096]{1,0:T(8,128)(2,1)S(1)}, bf16[32,4096]{1,0:T(8,128)(2,1)S(1)}, u32[]{:S(2)}, u32[]{:S(2)}) %collective-permute-start.89) | collective-permute-done | bytes 262176 | tf_op jit(solution)/shard_map/ppermute | solution.py:66
  511.9 4.2 collective-permute-done.88
  524.1 3.2 collective-permute-done.93
  527.3 5.8 collective-permute-done.92
  537.6 3.4 collective-permute-done.96
  568.0 2.4 collective-permute-start.103
  571.0 2.3 collective-permute-done.103
  574.8 2.1 collective-permute-done.104
  581.8 2.9 fusion.119
  585.8 2.4 fusion.125
  589.2 2.4 fusion.127
  (930 shorter events, 240.5 us)
Async XLA Ops:
  3.5 17.2 %collective-permute-start = (s32[1,128]{1,0:T(1,128)S(1)}, s32[1,128]{1,0:T(1,128)S(1)}, u32[]{:S(2)}, u32[]{:S(2)}) collective-permute-start(s32[1,128]{1,0:T(1,128)S(1)} %add_bitcast_fusion.4), channel_id=1, source_target_pairs={{0,16},{1,17},{2,18},{3,19},{4,20},{5,21},{6,22},{7,23},{8,24},{9,... | collective-permute-start | bytes 1544 | tf_op jit(solution)/shard_map/ppermute | solution.py:66
  7.5 13.1 %collective-permute-start.1 = (s32[1,128]{1,0:T(1,128)S(1)}, s32[1,128]{1,0:T(1,128)S(1)}, u32[]{:S(2)}, u32[]{:S(2)}) collective-permute-start(s32[1,128]{1,0:T(1,128)S(1)} %add_bitcast_fusion.4), channel_id=1, source_target_pairs={{0,8},{1,9},{2,10},{3,11},{4,12},{5,13},{6,14},{7,15},{8,0},{9,1},... | collective-permute-start | bytes 1544 | tf_op jit(solution)/shard_map/ppermute | solution.py:66
  9.1 11.6 %collective-permute-start.2 = (s32[1,128]{1,0:T(1,128)S(1)}, s32[1,128]{1,0:T(1,128)S(1)}, u32[]{:S(2)}, u32[]{:S(2)}) collective-permute-start(s32[1,128]{1,0:T(1,128)S(1)} %add_bitcast_fusion.4), channel_id=1, source_target_pairs={{0,24},{1,25},{2,26},{3,27},{4,28},{5,29},{6,30},{7,31},{8,16},{9,... | collective-permute-start | bytes 1544 | tf_op jit(solution)/shard_map/ppermute | solution.py:66
  12.2 11.3 %collective-permute-start.3 = (bf16[32,1792]{1,0:T(8,128)(2,1)S(1)}, bf16[32,1792]{1,0:T(8,128)(2,1)S(1)}, u32[]{:S(2)}, u32[]{:S(2)}) collective-permute-start(bf16[32,1792]{1,0:T(8,128)(2,1)S(1)} %pad_maximum_fusion.21), channel_id=1, source_target_pairs={{0,16},{1,17},{2,18},{3,19},{4,20},{5,21},{6,22},{7,23},{8,24},{9,... | collective-permute-start | bytes 344072 | tf_op jit(solution)/shard_map/ppermute | solution.py:66
  25.0 11.4 %collective-permute-start.8 = (bf16[64,1792]{1,0:T(8,128)(2,1)S(1)}, bf16[64,1792]{1,0:T(8,128)(2,1)S(1)}, u32[]{:S(2)}, u32[]{:S(2)}) collective-permute-start(bf16[64,1792]{1,0:T(8,128)(2,1)S(1)} %constant_dynamic-update-slice_fusion), channel_id=1, source_target_pairs={{0,8},{1,9},{2,10},{3,11},{4,12},{5,13},{6,14},{7,15},{8,0},{9,1},... | collective-permute-start | bytes 688136 | tf_op jit(solution)/shard_map/ppermute | solution.py:66
  31.6 19.0 %collective-permute-start.12 = (f32[1,2,384]{2,1,0:T(2,128)S(1)}, f32[1,2,384]{2,1,0:T(2,128)S(1)}, u32[]{:S(2)}, u32[]{:S(2)}) collective-permute-start(f32[1,2,384]{2,1,0:T(2,128)S(1)} %maximum_bitcast_fusion.1), channel_id=1, source_target_pairs={{0,2},{1,3},{2,0},{3,1},{4,6},{5,7},{6,4},{7,5},{8,10},{9,11},{10,... | collective-permute-start | bytes 9224 | tf_op jit(solution)/shard_map/ppermute | solution.py:66
  36.5 14.1 %collective-permute-start.13 = (bf16[128,1024]{1,0:T(8,128)(2,1)S(1)}, bf16[128,1024]{1,0:T(8,128)(2,1)}, u32[]{:S(2)}, u32[]{:S(2)}) collective-permute-start(bf16[128,1024]{1,0:T(8,128)(2,1)S(1)} %convert_element_type.580), channel_id=1, source_target_pairs={{0,4},{1,5},{2,6},{3,7},{4,0},{5,1},{6,2},{7,3},{8,12},{9,13},{10,... | collective-permute-start | bytes 786440 | tf_op jit(solution)/shard_map/ppermute | solution.py:66
  39.5 30.1 %collective-permute-start.16 = (bf16[128,1792]{1,0:T(8,128)(2,1)}, bf16[128,1792]{1,0:T(8,128)(2,1)}, u32[]{:S(2)}, u32[]{:S(2)}) collective-permute-start(bf16[128,1792]{1,0:T(8,128)(2,1)} %constant_dynamic-update-slice_fusion.6), channel_id=1, source_target_pairs={{0,4},{1,5},{2,6},{3,7},{4,0},{5,1},{6,2},{7,3},{8,12},{9,13},{10,... | collective-permute-start | bytes 1376264 | tf_op jit(solution)/shard_map/ppermute | solution.py:66
  41.5 28.2 %collective-permute-start.17 = (bf16[128,1792]{1,0:T(8,128)(2,1)}, bf16[128,1792]{1,0:T(8,128)(2,1)}, u32[]{:S(2)}, u32[]{:S(2)}) collective-permute-start(bf16[128,1792]{1,0:T(8,128)(2,1)} %constant_dynamic-update-slice_fusion.8), channel_id=1, source_target_pairs={{0,2},{1,3},{2,0},{3,1},{4,6},{5,7},{6,4},{7,5},{8,10},{9,11},{10,... | collective-permute-start | bytes 1376264 | tf_op jit(solution)/shard_map/ppermute | solution.py:66
  72.5 17.9 %collective-permute-start.21 = (bf16[32,5120]{1,0:T(8,128)(2,1)S(1)}, bf16[32,5120]{1,0:T(8,128)(2,1)}, u32[]{:S(2)}, u32[]{:S(2)}) collective-permute-start(bf16[32,5120]{1,0:T(8,128)(2,1)S(1)} %copy-done.143), channel_id=1, source_target_pairs={{0,16},{1,17},{2,18},{3,19},{4,20},{5,21},{6,22},{7,23},{8,24},{9,... | collective-permute-start | bytes 983048 | tf_op jit(solution)/shard_map/ppermute | solution.py:66
  78.8 22.1 %collective-permute-start.23 = (bf16[256,1792]{1,0:T(8,128)(2,1)}, bf16[256,1792]{1,0:T(8,128)(2,1)S(1)}, u32[]{:S(2)}, u32[]{:S(2)}) collective-permute-start(bf16[256,1792]{1,0:T(8,128)(2,1)} %copy-done.55), channel_id=1, source_target_pairs={{0,4},{1,5},{2,6},{3,7},{4,0},{5,1},{6,2},{7,3},{8,12},{9,13},{10,... | collective-permute-start | bytes 2752520 | tf_op jit(solution)/shard_map/ppermute | solution.py:66
  79.3 21.6 %collective-permute-start.22 = (bf16[256,1792]{1,0:T(8,128)(2,1)S(1)}, bf16[256,1792]{1,0:T(8,128)(2,1)S(1)}, u32[]{:S(2)}, u32[]{:S(2)}) collective-permute-start(bf16[256,1792]{1,0:T(8,128)(2,1)S(1)} %constant_dynamic-update-slice_fusion.12.refs_1_.refs_0_), channel_id=1, source_target_pairs={{0,2},{1,3},{2,0},{3,1},{4,6},{5,7},{6,4},{7,5},{8,10},{9,11},{10,... | collective-permute-start | bytes 2752520 | tf_op jit(solution)/shard_map/ppermute | solution.py:66
  90.4 18.4 %collective-permute-start.24 = (bf16[256,1792]{1,0:T(8,128)(2,1)S(1)}, bf16[256,1792]{1,0:T(8,128)(2,1)S(1)}, u32[]{:S(2)}, u32[]{:S(2)}) collective-permute-start(bf16[256,1792]{1,0:T(8,128)(2,1)S(1)} %constant_dynamic-update-slice_fusion.12.refs_1_.refs_0_), channel_id=1, source_target_pairs={{0,1},{1,0},{2,3},{3,2},{4,5},{5,4},{6,7},{7,6},{8,9},{9,8},{10,11... | collective-permute-start | bytes 2752520 | tf_op jit(solution)/shard_map/ppermute | solution.py:66
  90.5 18.3 %collective-permute-start.25 = (bf16[256,1792]{1,0:T(8,128)(2,1)}, bf16[256,1792]{1,0:T(8,128)(2,1)S(1)}, u32[]{:S(2)}, u32[]{:S(2)}) collective-permute-start(bf16[256,1792]{1,0:T(8,128)(2,1)} %copy-done.55), channel_id=1, source_target_pairs={{0,1},{1,0},{2,3},{3,2},{4,5},{5,4},{6,7},{7,6},{8,9},{9,8},{10,11... | collective-permute-start | bytes 2752520 | tf_op jit(solution)/shard_map/ppermute | solution.py:66
  92.0 16.8 %collective-permute-start.26 = (bf16[64,5120]{1,0:T(8,128)(2,1)S(1)}, bf16[64,5120]{1,0:T(8,128)(2,1)S(1)}, u32[]{:S(2)}, u32[]{:S(2)}) collective-permute-start(bf16[64,5120]{1,0:T(8,128)(2,1)S(1)} %constant_dynamic-update-slice_fusion.16), channel_id=1, source_target_pairs={{0,8},{1,9},{2,10},{3,11},{4,12},{5,13},{6,14},{7,15},{8,0},{9,1},... | collective-permute-start | bytes 1966088 | tf_op jit(solution)/shard_map/ppermute | solution.py:66
  109.9 21.6 %collective-permute-start.30 = (bf16[128,2560]{1,0:T(8,128)(2,1)S(1)}, bf16[128,2560]{1,0:T(8,128)(2,1)S(1)}, u32[]{:S(2)}, u32[]{:S(2)}) collective-permute-start(bf16[128,2560]{1,0:T(8,128)(2,1)S(1)} %get-tuple-element.395), channel_id=1, source_target_pairs={{0,4},{1,5},{2,6},{3,7},{4,0},{5,1},{6,2},{7,3},{8,12},{9,13},{10,... | collective-permute-start | bytes 1966088 | tf_op jit(solution)/shard_map/ppermute | solution.py:66
  111.5 20.0 %collective-permute-start.31 = (bf16[128,2560]{1,0:T(8,128)(2,1)S(1)}, bf16[128,2560]{1,0:T(8,128)(2,1)S(1)}, u32[]{:S(2)}, u32[]{:S(2)}) collective-permute-start(bf16[128,2560]{1,0:T(8,128)(2,1)S(1)} %get-tuple-element.397), channel_id=1, source_target_pairs={{0,2},{1,3},{2,0},{3,1},{4,6},{5,7},{6,4},{7,5},{8,10},{9,11},{10,... | collective-permute-start | bytes 1966088 | tf_op jit(solution)/shard_map/ppermute | solution.py:66
  116.7 20.1 %collective-permute-start.32 = (bf16[64,3072]{1,0:T(8,128)(2,1)S(1)}, bf16[64,3072]{1,0:T(8,128)(2,1)S(1)}, u32[]{:S(2)}, u32[]{:S(2)}) collective-permute-start(bf16[64,3072]{1,0:T(8,128)(2,1)S(1)} %get-tuple-element.743), channel_id=1, source_target_pairs={{0,2},{1,3},{2,0},{3,1},{4,6},{5,7},{6,4},{7,5},{8,10},{9,11},{10,... | collective-permute-start | bytes 1179656 | tf_op jit(solution)/shard_map/ppermute | solution.py:66
  118.2 18.6 %collective-permute-start.33 = (bf16[64,3072]{1,0:T(8,128)(2,1)S(1)}, bf16[64,3072]{1,0:T(8,128)(2,1)S(1)}, u32[]{:S(2)}, u32[]{:S(2)}) collective-permute-start(bf16[64,3072]{1,0:T(8,128)(2,1)S(1)} %get-tuple-element.741), channel_id=1, source_target_pairs={{0,4},{1,5},{2,6},{3,7},{4,0},{5,1},{6,2},{7,3},{8,12},{9,13},{10,... | collective-permute-start | bytes 1179656 | tf_op jit(solution)/shard_map/ppermute | solution.py:66
  119.8 14.1 %collective-permute-start.34 = (bf16[32,4096]{1,0:T(8,128)(2,1)S(1)}, bf16[32,4096]{1,0:T(8,128)(2,1)S(1)}, u32[]{:S(2)}, u32[]{:S(2)}) collective-permute-start(bf16[32,4096]{1,0:T(8,128)(2,1)S(1)} %copy-done.161), channel_id=1, source_target_pairs={{0,16},{1,17},{2,18},{3,19},{4,20},{5,21},{6,22},{7,23},{8,24},{9,... | collective-permute-start | bytes 786440 | tf_op jit(solution)/shard_map/ppermute | solution.py:66
  136.9 15.8 %collective-permute-start.37 = (bf16[64,4096]{1,0:T(8,128)(2,1)S(1)}, bf16[64,4096]{1,0:T(8,128)(2,1)S(1)}, u32[]{:S(2)}, u32[]{:S(2)}) collective-permute-start(bf16[64,4096]{1,0:T(8,128)(2,1)S(1)} %constant_dynamic-update-slice_fusion.20), channel_id=1, source_target_pairs={{0,8},{1,9},{2,10},{3,11},{4,12},{5,13},{6,14},{7,15},{8,0},{9,1},... | collective-permute-start | bytes 1572872 | tf_op jit(solution)/shard_map/ppermute | solution.py:66
  137.4 15.3 %collective-permute-start.36 = (bf16[32,3072]{1,0:T(8,128)(2,1)S(1)}, bf16[32,3072]{1,0:T(8,128)(2,1)S(1)}, u32[]{:S(2)}, u32[]{:S(2)}) collective-permute-start(bf16[32,3072]{1,0:T(8,128)(2,1)S(1)} %get-tuple-element.794), channel_id=1, source_target_pairs={{0,2},{1,3},{2,0},{3,1},{4,6},{5,7},{6,4},{7,5},{8,10},{9,11},{10,... | collective-permute-start | bytes 589832 | tf_op jit(solution)/shard_map/ppermute | solution.py:66
  139.1 13.6 %collective-permute-start.35 = (bf16[32,3072]{1,0:T(8,128)(2,1)S(1)}, bf16[32,3072]{1,0:T(8,128)(2,1)S(1)}, u32[]{:S(2)}, u32[]{:S(2)}) collective-permute-start(bf16[32,3072]{1,0:T(8,128)(2,1)S(1)} %get-tuple-element.796), channel_id=1, source_target_pairs={{0,4},{1,5},{2,6},{3,7},{4,0},{5,1},{6,2},{7,3},{8,12},{9,13},{10,... | collective-permute-start | bytes 589832 | tf_op jit(solution)/shard_map/ppermute | solution.py:66
  139.7 35.4 %collective-permute-start.43 = (bf16[256,2560]{1,0:T(8,128)(2,1)S(1)}, bf16[256,2560]{1,0:T(8,128)(2,1)S(1)}, u32[]{:S(2)}, u32[]{:S(2)}) collective-permute-start(bf16[256,2560]{1,0:T(8,128)(2,1)S(1)} %constant_dynamic-update-slice_fusion.24.refs_5_.refs_4_), channel_id=1, source_target_pairs={{0,4},{1,5},{2,6},{3,7},{4,0},{5,1},{6,2},{7,3},{8,12},{9,13},{10,... | collective-permute-start | bytes 3932168 | tf_op jit(solution)/shard_map/ppermute | solution.py:66
  141.4 33.7 %collective-permute-start.42 = (bf16[256,2560]{1,0:T(8,128)(2,1)S(1)}, bf16[256,2560]{1,0:T(8,128)(2,1)S(1)}, u32[]{:S(2)}, u32[]{:S(2)}) collective-permute-start(bf16[256,2560]{1,0:T(8,128)(2,1)S(1)} %constant_dynamic-update-slice_fusion.22.refs_1_.refs_0_), channel_id=1, source_target_pairs={{0,2},{1,3},{2,0},{3,1},{4,6},{5,7},{6,4},{7,5},{8,10},{9,11},{10,... | collective-permute-start | bytes 3932168 | tf_op jit(solution)/shard_map/ppermute | solution.py:66
  160.5 14.6 %collective-permute-start.41 = (bf16[8,6144]{1,0:T(8,128)(2,1)S(1)}, bf16[8,6144]{1,0:T(8,128)(2,1)S(1)}, u32[]{:S(2)}, u32[]{:S(2)}) collective-permute-start(bf16[8,6144]{1,0:T(8,128)(2,1)S(1)} %get-tuple-element.814), channel_id=1, source_target_pairs={{0,16},{1,17},{2,18},{3,19},{4,20},{5,21},{6,22},{7,23},{8,24},{9,... | collective-permute-start | bytes 294920 | tf_op jit(solution)/shard_map/ppermute | solution.py:66
  162.2 23.2 %collective-permute-start.46 = (bf16[128,2048]{1,0:T(8,128)(2,1)S(1)}, bf16[128,2048]{1,0:T(8,128)(2,1)S(1)}, u32[]{:S(2)}, u32[]{:S(2)}) collective-permute-start(bf16[128,2048]{1,0:T(8,128)(2,1)S(1)} %get-tuple-element.435), channel_id=1, source_target_pairs={{0,4},{1,5},{2,6},{3,7},{4,0},{5,1},{6,2},{7,3},{8,12},{9,13},{10,... | collective-permute-start | bytes 1572872 | tf_op jit(solution)/shard_map/ppermute | solution.py:66
  162.7 22.7 %collective-permute-start.47 = (bf16[128,2048]{1,0:T(8,128)(2,1)S(1)}, bf16[128,2048]{1,0:T(8,128)(2,1)S(1)}, u32[]{:S(2)}, u32[]{:S(2)}) collective-permute-start(bf16[128,2048]{1,0:T(8,128)(2,1)S(1)} %get-tuple-element.437), channel_id=1, source_target_pairs={{0,2},{1,3},{2,0},{3,1},{4,6},{5,7},{6,4},{7,5},{8,10},{9,11},{10,... | collective-permute-start | bytes 1572872 | tf_op jit(solution)/shard_map/ppermute | solution.py:66
  185.6 28.8 %collective-permute-start.49 = (bf16[256,2048]{1,0:T(8,128)(2,1)S(1)}, bf16[256,2048]{1,0:T(8,128)(2,1)S(1)}, u32[]{:S(2)}, u32[]{:S(2)}) collective-permute-start(bf16[256,2048]{1,0:T(8,128)(2,1)S(1)} %constant_dynamic-update-slice_fusion.30.refs_5_), channel_id=1, source_target_pairs={{0,4},{1,5},{2,6},{3,7},{4,0},{5,1},{6,2},{7,3},{8,12},{9,13},{10,... | collective-permute-start | bytes 3145736 | tf_op jit(solution)/shard_map/ppermute | solution.py:66
  186.1 28.3 %collective-permute-start.51 = (bf16[256,2048]{1,0:T(8,128)(2,1)S(1)}, bf16[256,2048]{1,0:T(8,128)(2,1)S(1)}, u32[]{:S(2)}, u32[]{:S(2)}) collective-permute-start(bf16[256,2048]{1,0:T(8,128)(2,1)S(1)} %constant_dynamic-update-slice_fusion.30.refs_5_), channel_id=1, source_target_pairs={{0,1},{1,0},{2,3},{3,2},{4,5},{5,4},{6,7},{7,6},{8,9},{9,8},{10,11... | collective-permute-start | bytes 3145736 | tf_op jit(solution)/shard_map/ppermute | solution.py:66
  186.2 28.1 %collective-permute-start.48 = (bf16[256,2048]{1,0:T(8,128)(2,1)S(1)}, bf16[256,2048]{1,0:T(8,128)(2,1)S(1)}, u32[]{:S(2)}, u32[]{:S(2)}) collective-permute-start(bf16[256,2048]{1,0:T(8,128)(2,1)S(1)} %constant_dynamic-update-slice_fusion.28.refs_1_), channel_id=1, source_target_pairs={{0,2},{1,3},{2,0},{3,1},{4,6},{5,7},{6,4},{7,5},{8,10},{9,11},{10,... | collective-permute-start | bytes 3145736 | tf_op jit(solution)/shard_map/ppermute | solution.py:66
  186.8 27.6 %collective-permute-start.50 = (bf16[256,2048]{1,0:T(8,128)(2,1)S(1)}, bf16[256,2048]{1,0:T(8,128)(2,1)S(1)}, u32[]{:S(2)}, u32[]{:S(2)}) collective-permute-start(bf16[256,2048]{1,0:T(8,128)(2,1)S(1)} %constant_dynamic-update-slice_fusion.28.refs_1_), channel_id=1, source_target_pairs={{0,1},{1,0},{2,3},{3,2},{4,5},{5,4},{6,7},{7,6},{8,9},{9,8},{10,11... | collective-permute-start | bytes 3145736 | tf_op jit(solution)/shard_map/ppermute | solution.py:66
  188.2 26.2 %collective-permute-start.52 = (bf16[256,1024]{1,0:T(8,128)(2,1)S(1)}, bf16[256,1024]{1,0:T(8,128)(2,1)S(1)}, u32[]{:S(2)}, u32[]{:S(2)}) collective-permute-start(bf16[256,1024]{1,0:T(8,128)(2,1)S(1)} %constant_dynamic-update-slice_fusion.32), channel_id=1, source_target_pairs={{0,16},{1,17},{2,18},{3,19},{4,20},{5,21},{6,22},{7,23},{8,24},{9,... | collective-permute-start | bytes 1572872 | tf_op jit(solution)/shard_map/ppermute | solution.py:66
  215.1 25.2 %collective-permute-start.55 = (bf16[512,1024]{1,0:T(8,128)(2,1)S(1)}, bf16[512,1024]{1,0:T(8,128)(2,1)S(1)}, u32[]{:S(2)}, u32[]{:S(2)}) collective-permute-start(bf16[512,1024]{1,0:T(8,128)(2,1)S(1)} %constant_dynamic-update-slice_fusion.34), channel_id=1, source_target_pairs={{0,8},{1,9},{2,10},{3,11},{4,12},{5,13},{6,14},{7,15},{8,0},{9,1},... | collective-permute-start | bytes 3145736 | tf_op jit(solution)/shard_map/ppermute | solution.py:66
  242.9 20.2 %collective-permute-start.57 = (bf16[384,1024]{1,0:T(8,128)(2,1)}, bf16[384,1024]{1,0:T(8,128)(2,1)S(1)}, u32[]{:S(2)}, u32[]{:S(2)}) collective-permute-start(bf16[384,1024]{1,0:T(8,128)(2,1)} %get-tuple-element.455), channel_id=1, source_target_pairs={{0,2},{1,3},{2,0},{3,1},{4,6},{5,7},{6,4},{7,5},{8,10},{9,11},{10,... | collective-permute-start | bytes 2359304 | tf_op jit(solution)/shard_map/ppermute | solution.py:66
  292.8 19.6 %collective-permute-start.63 = (bf16[384,1024]{1,0:T(8,128)(2,1)S(1)}, bf16[384,1024]{1,0:T(8,128)(2,1)S(1)}, u32[]{:S(2)}, u32[]{:S(2)}) collective-permute-start(bf16[384,1024]{1,0:T(8,128)(2,1)S(1)} %add_convert_fusion.1), channel_id=1, source_target_pairs={{0,2},{1,3},{2,0},{3,1},{4,6},{5,7},{6,4},{7,5},{8,10},{9,11},{10,... | collective-permute-start | bytes 2359304 | tf_op jit(solution)/shard_map/ppermute | solution.py:66
  345.6 11.0 %collective-permute-start.65 = (bf16[512,4096]{1,0:T(8,128)(2,1)}, bf16[512,4096]{1,0:T(8,128)(2,1)S(1)}, u32[]{:S(2)}, u32[]{:S(2)}) collective-permute-start(bf16[512,4096]{1,0:T(8,128)(2,1)} %shard_map.469), channel_id=1, source_target_pairs={{0,1},{1,0},{2,3},{3,2},{4,5},{5,4},{6,7},{7,6},{8,9},{9,8},{10,11... | collective-permute-start | bytes 12582920 | tf_op jit(solution)/shard_map/ppermute | solution.py:66
  346.0 25.4 %collective-permute-start.68 = (bf16[512,1024]{1,0:T(8,128)(2,1)}, bf16[512,1024]{1,0:T(8,128)(2,1)}, u32[]{:S(2)}, u32[]{:S(2)}) collective-permute-start(bf16[512,1024]{1,0:T(8,128)(2,1)} %fusion.38), channel_id=1, source_target_pairs={{0,8},{1,9},{2,10},{3,11},{4,12},{5,13},{6,14},{7,15},{8,0},{9,1},... | collective-permute-start | bytes 3145736 | tf_op jit(solution)/shard_map/ppermute | solution.py:66
  346.3 25.2 %collective-permute-start.66 = (bf16[256,2048]{1,0:T(8,128)(2,1)}, bf16[256,2048]{1,0:T(8,128)(2,1)}, u32[]{:S(2)}, u32[]{:S(2)}) collective-permute-start(bf16[256,2048]{1,0:T(8,128)(2,1)} %get-tuple-element.480), channel_id=1, source_target_pairs={{0,2},{1,3},{2,0},{3,1},{4,6},{5,7},{6,4},{7,5},{8,10},{9,11},{10,... | collective-permute-start | bytes 3145736 | tf_op jit(solution)/shard_map/ppermute | solution.py:66
  347.1 24.7 %collective-permute-start.67 = (bf16[256,2048]{1,0:T(8,128)(2,1)S(1)}, bf16[256,2048]{1,0:T(8,128)(2,1)}, u32[]{:S(2)}, u32[]{:S(2)}) collective-permute-start(bf16[256,2048]{1,0:T(8,128)(2,1)S(1)} %get-tuple-element.481), channel_id=1, source_target_pairs={{0,4},{1,5},{2,6},{3,7},{4,0},{5,1},{6,2},{7,3},{8,12},{9,13},{10,... | collective-permute-start | bytes 3145736 | tf_op jit(solution)/shard_map/ppermute | solution.py:66
  375.2 36.0 %collective-permute-start.71 = (bf16[256,2048]{1,0:T(8,128)(2,1)}, bf16[256,2048]{1,0:T(8,128)(2,1)S(1)}, u32[]{:S(2)}, u32[]{:S(2)}) collective-permute-start(bf16[256,2048]{1,0:T(8,128)(2,1)} %get-tuple-element.501), channel_id=1, source_target_pairs={{0,2},{1,3},{2,0},{3,1},{4,6},{5,7},{6,4},{7,5},{8,10},{9,11},{10,... | collective-permute-start | bytes 3145736 | tf_op jit(solution)/shard_map/ppermute | solution.py:66
  376.5 34.7 %collective-permute-start.72 = (bf16[256,2048]{1,0:T(8,128)(2,1)S(1)}, bf16[256,2048]{1,0:T(8,128)(2,1)S(1)}, u32[]{:S(2)}, u32[]{:S(2)}) collective-permute-start(bf16[256,2048]{1,0:T(8,128)(2,1)S(1)} %get-tuple-element.502), channel_id=1, source_target_pairs={{0,4},{1,5},{2,6},{3,7},{4,0},{5,1},{6,2},{7,3},{8,12},{9,13},{10,... | collective-permute-start | bytes 3145736 | tf_op jit(solution)/shard_map/ppermute | solution.py:66
  379.7 28.8 %collective-permute-start.73 = (bf16[256,1024]{1,0:T(8,128)(2,1)S(1)}, bf16[256,1024]{1,0:T(8,128)(2,1)S(1)}, u32[]{:S(2)}, u32[]{:S(2)}) collective-permute-start(bf16[256,1024]{1,0:T(8,128)(2,1)S(1)} %get-tuple-element.734), channel_id=1, source_target_pairs={{0,16},{1,17},{2,18},{3,19},{4,20},{5,21},{6,22},{7,23},{8,24},{9,... | collective-permute-start | bytes 1572872 | tf_op jit(solution)/shard_map/ppermute | solution.py:66
  381.4 29.8 %collective-permute-start.69 = (bf16[128,2048]{1,0:T(8,128)(2,1)S(1)}, bf16[128,2048]{1,0:T(8,128)(2,1)S(1)}, u32[]{:S(2)}, u32[]{:S(2)}) collective-permute-start(bf16[128,2048]{1,0:T(8,128)(2,1)S(1)} %get-tuple-element.499), channel_id=1, source_target_pairs={{0,4},{1,5},{2,6},{3,7},{4,0},{5,1},{6,2},{7,3},{8,12},{9,13},{10,... | collective-permute-start | bytes 1572872 | tf_op jit(solution)/shard_map/ppermute | solution.py:66
  381.9 29.3 %collective-permute-start.70 = (bf16[128,2048]{1,0:T(8,128)(2,1)S(1)}, bf16[128,2048]{1,0:T(8,128)(2,1)S(1)}, u32[]{:S(2)}, u32[]{:S(2)}) collective-permute-start(bf16[128,2048]{1,0:T(8,128)(2,1)S(1)} %get-tuple-element.500), channel_id=1, source_target_pairs={{0,2},{1,3},{2,0},{3,1},{4,6},{5,7},{6,4},{7,5},{8,10},{9,11},{10,... | collective-permute-start | bytes 1572872 | tf_op jit(solution)/shard_map/ppermute | solution.py:66
  417.6 20.8 %collective-permute-start.75 = (bf16[512,3072]{1,0:T(8,128)(2,1)S(1)}, bf16[512,3072]{1,0:T(8,128)(2,1)S(1)}, u32[]{:S(2)}, u32[]{:S(2)}) collective-permute-start(bf16[512,3072]{1,0:T(8,128)(2,1)S(1)} %shard_map.476), channel_id=1, source_target_pairs={{0,1},{1,0},{2,3},{3,2},{4,5},{5,4},{6,7},{7,6},{8,9},{9,8},{10,11... | collective-permute-start | bytes 9437192 | tf_op jit(solution)/shard_map/ppermute | solution.py:66
  418.5 19.8 %collective-permute-start.76 = (bf16[128,2048]{1,0:T(8,128)(2,1)S(1)}, bf16[128,2048]{1,0:T(8,128)(2,1)S(1)}, u32[]{:S(2)}, u32[]{:S(2)}) collective-permute-start(bf16[128,2048]{1,0:T(8,128)(2,1)S(1)} %add_convert_fusion.17), channel_id=1, source_target_pairs={{0,4},{1,5},{2,6},{3,7},{4,0},{5,1},{6,2},{7,3},{8,12},{9,13},{10,... | collective-permute-start | bytes 1572872 | tf_op jit(solution)/shard_map/ppermute | solution.py:66
  420.1 18.2 %collective-permute-start.77 = (bf16[128,2048]{1,0:T(8,128)(2,1)S(1)}, bf16[128,2048]{1,0:T(8,128)(2,1)S(1)}, u32[]{:S(2)}, u32[]{:S(2)}) collective-permute-start(bf16[128,2048]{1,0:T(8,128)(2,1)S(1)} %add_convert_fusion.16), channel_id=1, source_target_pairs={{0,2},{1,3},{2,0},{3,1},{4,6},{5,7},{6,4},{7,5},{8,10},{9,11},{10,... | collective-permute-start | bytes 1572872 | tf_op jit(solution)/shard_map/ppermute | solution.py:66
  421.1 17.2 %collective-permute-start.78 = (bf16[64,4096]{1,0:T(8,128)(2,1)S(1)}, bf16[64,4096]{1,0:T(8,128)(2,1)S(1)}, u32[]{:S(2)}, u32[]{:S(2)}) collective-permute-start(bf16[64,4096]{1,0:T(8,128)(2,1)S(1)} %pad_maximum_fusion.15), channel_id=1, source_target_pairs={{0,8},{1,9},{2,10},{3,11},{4,12},{5,13},{6,14},{7,15},{8,0},{9,1},... | collective-permute-start | bytes 1572872 | tf_op jit(solution)/shard_map/ppermute | solution.py:66
  422.8 15.5 %collective-permute-start.79 = (bf16[128,1024]{1,0:T(8,128)(2,1)S(1)}, bf16[128,1024]{1,0:T(8,128)(2,1)S(1)}, u32[]{:S(2)}, u32[]{:S(2)}) collective-permute-start(bf16[128,1024]{1,0:T(8,128)(2,1)S(1)} %get-tuple-element.782), channel_id=1, source_target_pairs={{0,4},{1,5},{2,6},{3,7},{4,0},{5,1},{6,2},{7,3},{8,12},{9,13},{10,... | collective-permute-start | bytes 786440 | tf_op jit(solution)/shard_map/ppermute | solution.py:66
  446.5 15.8 %collective-permute-start.80 = (bf16[512,512]{1,0:T(8,128)(2,1)}, bf16[512,512]{1,0:T(8,128)(2,1)}, u32[]{:S(2)}, u32[]{:S(2)}) collective-permute-start(bf16[512,512]{1,0:T(8,128)(2,1)} %slice.721), channel_id=1, source_target_pairs={{0,1},{1,0},{2,3},{3,2},{4,5},{5,4},{6,7},{7,6},{8,9},{9,8},{10,11... | collective-permute-start | bytes 1572872 | tf_op jit(solution)/shard_map/ppermute | solution.py:66
  446.5 15.8 %collective-permute-start.81 = (bf16[32,4096]{1,0:T(8,128)(2,1)}, bf16[32,4096]{1,0:T(8,128)(2,1)}, u32[]{:S(2)}, u32[]{:S(2)}) collective-permute-start(bf16[32,4096]{1,0:T(8,128)(2,1)} %add_convert_fusion.34), channel_id=1, source_target_pairs={{0,16},{1,17},{2,18},{3,19},{4,20},{5,21},{6,22},{7,23},{8,24},{9,... | collective-permute-start | bytes 786440 | tf_op jit(solution)/shard_map/ppermute | solution.py:66
  467.5 27.9 %collective-permute-start.82 = (bf16[256,2304]{1,0:T(8,128)(2,1)S(1)}, bf16[256,2304]{1,0:T(8,128)(2,1)S(1)}, u32[]{:S(2)}, u32[]{:S(2)}) collective-permute-start(bf16[256,2304]{1,0:T(8,128)(2,1)S(1)} %pad_maximum_fusion.4), channel_id=1, source_target_pairs={{0,2},{1,3},{2,0},{3,1},{4,6},{5,7},{6,4},{7,5},{8,10},{9,11},{10,... | collective-permute-start | bytes 3538952 | tf_op jit(solution)/shard_map/ppermute | solution.py:66
  468.6 27.5 %collective-permute-start.83 = (bf16[256,2304]{1,0:T(8,128)(2,1)S(1)}, bf16[256,2304]{1,0:T(8,128)(2,1)S(1)}, u32[]{:S(2)}, u32[]{:S(2)}) collective-permute-start(bf16[256,2304]{1,0:T(8,128)(2,1)S(1)} %pad_maximum_fusion.5), channel_id=1, source_target_pairs={{0,4},{1,5},{2,6},{3,7},{4,0},{5,1},{6,2},{7,3},{8,12},{9,13},{10,... | collective-permute-start | bytes 3538952 | tf_op jit(solution)/shard_map/ppermute | solution.py:66
  470.1 21.5 %collective-permute-start.86 = (bf16[64,4096]{1,0:T(8,128)(2,1)S(1)}, bf16[64,4096]{1,0:T(8,128)(2,1)S(1)}, u32[]{:S(2)}, u32[]{:S(2)}) collective-permute-start(bf16[64,4096]{1,0:T(8,128)(2,1)S(1)} %pad_maximum_fusion.17), channel_id=1, source_target_pairs={{0,8},{1,9},{2,10},{3,11},{4,12},{5,13},{6,14},{7,15},{8,0},{9,1},... | collective-permute-start | bytes 1572872 | tf_op jit(solution)/shard_map/ppermute | solution.py:66
  475.5 16.1 %collective-permute-start.85 = (bf16[16,8192]{1,0:T(8,128)(2,1)S(1)}, bf16[16,8192]{1,0:T(8,128)(2,1)S(1)}, u32[]{:S(2)}, u32[]{:S(2)}) collective-permute-start(bf16[16,8192]{1,0:T(8,128)(2,1)S(1)} %constant_dynamic-update-slice_fusion.50), channel_id=1, source_target_pairs={{0,8},{1,9},{2,10},{3,11},{4,12},{5,13},{6,14},{7,15},{8,0},{9,1},... | collective-permute-start | bytes 786440 | tf_op jit(solution)/shard_map/ppermute | solution.py:66
  496.2 15.7 %collective-permute-start.90 = (bf16[32,5120]{1,0:T(8,128)(2,1)S(1)}, bf16[32,5120]{1,0:T(8,128)(2,1)S(1)}, u32[]{:S(2)}, u32[]{:S(2)}) collective-permute-start(bf16[32,5120]{1,0:T(8,128)(2,1)S(1)} %slice.875), channel_id=1, source_target_pairs={{0,4},{1,5},{2,6},{3,7},{4,0},{5,1},{6,2},{7,3},{8,12},{9,13},{10,... | collective-permute-start | bytes 983048 | tf_op jit(solution)/shard_map/ppermute | solution.py:66
  498.9 13.0 %collective-permute-start.89 = (bf16[32,4096]{1,0:T(8,128)(2,1)S(1)}, bf16[32,4096]{1,0:T(8,128)(2,1)S(1)}, u32[]{:S(2)}, u32[]{:S(2)}) collective-permute-start(bf16[32,4096]{1,0:T(8,128)(2,1)S(1)} %add_convert_fusion.30), channel_id=1, source_target_pairs={{0,16},{1,17},{2,18},{3,19},{4,20},{5,21},{6,22},{7,23},{8,24},{9,... | collective-permute-start | bytes 786440 | tf_op jit(solution)/shard_map/ppermute | solution.py:66
  500.9 15.3 %collective-permute-start.88 = (bf16[128,2304]{1,0:T(8,128)(2,1)S(1)}, bf16[128,2304]{1,0:T(8,128)(2,1)S(1)}, u32[]{:S(2)}, u32[]{:S(2)}) collective-permute-start(bf16[128,2304]{1,0:T(8,128)(2,1)S(1)} %get-tuple-element.730), channel_id=1, source_target_pairs={{0,2},{1,3},{2,0},{3,1},{4,6},{5,7},{6,4},{7,5},{8,10},{9,11},{10,... | collective-permute-start | bytes 1769480 | tf_op jit(solution)/shard_map/ppermute | solution.py:66
  502.0 15.3 %collective-permute-start.87 = (bf16[128,2304]{1,0:T(8,128)(2,1)S(1)}, bf16[128,2304]{1,0:T(8,128)(2,1)S(1)}, u32[]{:S(2)}, u32[]{:S(2)}) collective-permute-start(bf16[128,2304]{1,0:T(8,128)(2,1)S(1)} %get-tuple-element.732), channel_id=1, source_target_pairs={{0,4},{1,5},{2,6},{3,7},{4,0},{5,1},{6,2},{7,3},{8,12},{9,13},{10,... | collective-permute-start | bytes 1769480 | tf_op jit(solution)/shard_map/ppermute | solution.py:66
  517.4 15.8 %collective-permute-start.94 = (bf16[64,5120]{1,0:T(8,128)(2,1)S(1)}, bf16[64,5120]{1,0:T(8,128)(2,1)S(1)}, u32[]{:S(2)}, u32[]{:S(2)}) collective-permute-start(bf16[64,5120]{1,0:T(8,128)(2,1)S(1)} %constant_dynamic-update-slice_fusion.56), channel_id=1, source_target_pairs={{0,2},{1,3},{2,0},{3,1},{4,6},{5,7},{6,4},{7,5},{8,10},{9,11},{10,... | collective-permute-start | bytes 1966088 | tf_op jit(solution)/shard_map/ppermute | solution.py:66
  520.5 12.6 %collective-permute-start.92 = (bf16[64,4608]{1,0:T(8,128)(2,1)S(1)}, bf16[64,4608]{1,0:T(8,128)(2,1)S(1)}, u32[]{:S(2)}, u32[]{:S(2)}) collective-permute-start(bf16[64,4608]{1,0:T(8,128)(2,1)S(1)} %pad_maximum_fusion.13), channel_id=1, source_target_pairs={{0,8},{1,9},{2,10},{3,11},{4,12},{5,13},{6,14},{7,15},{8,0},{9,1},... | collective-permute-start | bytes 1769480 | tf_op jit(solution)/shard_map/ppermute | solution.py:66
  534.1 22.2 %collective-permute-start.97 = (bf16[32,4608]{1,0:T(8,128)(2,1)}, bf16[32,4608]{1,0:T(8,128)(2,1)}, u32[]{:S(2)}, u32[]{:S(2)}) collective-permute-start(bf16[32,4608]{1,0:T(8,128)(2,1)} %get-tuple-element.747), channel_id=1, source_target_pairs={{0,16},{1,17},{2,18},{3,19},{4,20},{5,21},{6,22},{7,23},{8,24},{9,... | collective-permute-start | bytes 884744 | tf_op jit(solution)/shard_map/ppermute | solution.py:66
  536.8 11.1 %collective-permute-start.95 = (bf16[128,5120]{1,0:T(8,128)(2,1)}, bf16[128,5120]{1,0:T(8,128)(2,1)}, u32[]{:S(2)}, u32[]{:S(2)}) collective-permute-start(bf16[128,5120]{1,0:T(8,128)(2,1)} %pad_maximum_fusion.3), channel_id=1, source_target_pairs={{0,1},{1,0},{2,3},{3,2},{4,5},{5,4},{6,7},{7,6},{8,9},{9,8},{10,11... | collective-permute-start | bytes 3932168 | tf_op jit(solution)/shard_map/ppermute | solution.py:66
  (263 other events, 2329.7 us)

commit v6 on v5

--- a/solution.py
+++ b/solution.py
@@ -1079,10 +1079,9 @@
     head_near = added(head_near, head_back)
     head_grad = lend(head_near, head_masks[:-2], devices)
     d_u = back_sets(d_qkv, w_qkv, perms)
-    d_u, qkv_b, up_x1, up_x2, down_back, down_near, head_grad = tie(
-        d_u, qkv_b, up_x1, up_x2, down_back, down_near, head_grad
-    )
-    head_grad = added(*head_grad, F32)
+    d_u, qkv_b, up_x1, up_x2, down_back, down_near = tie(
+        d_u, qkv_b, up_x1, up_x2, down_back, down_near
+    )
     down_near, down_far = halves_of(down_near, down_back)
     d_u, down_far, qkv_b, up_x1, up_x2 = tie(d_u, down_far, qkv_b, up_x1, up_x2)
     down_back = swap(down_far, bits_z[-2])
@@ -1123,6 +1122,7 @@
         down_back,
         up_x1,
         up_x2,
+        head_grad,
     ) = tie(
         qkv_n1,
         qkv_f1,
@@ -1136,7 +1136,9 @@
         down_back,
         up_x1,
         up_x2,
-    )
+        head_grad,
+    )
+    head_grad = added(*head_grad, F32)
 
     def beside(*parts):
         return jnp.concatenate(parts, axis=1)

time: 606 us -> 601 us (level)
    unnamed x485 -> x481, local copies, waits for them, and re-layouts: 41.1 us -> 39.3 us
  transfers between devices with their start and end apart: 105 -> 105, of which waited for: 48 -> 50; matrix products, arithmetic and copies ran while one was open for 14% -> 14% of each run, Pallas kernels for 19% -> 19%
where the time goes in v6:
time: 601 us; the launch traced here: 591 us
  waiting for transfers between devices  192 us (32%)
  Pallas kernels  134 us (22%)
  starting transfers between devices  92.8 us (15%)
  other arithmetic  64.7 us (11%)
  local copies, waits for them, and re-layouts  61.5 us (10%)
  matrix products  32.5 us (5%)
  between operations  12.7 us (2%)
    ppermute x105, waiting for transfers between devices, swapped(): lax.ppermute(value, ('dp', 'vocab'), [(i, i ^ mask) for i in range(device...  192 us
    pallas_call x25, Pallas kernels, run(): pl.pallas_call(body, grid=grid, in_specs=specs, out_shape=outs, out_specs...  134 us
    ppermute x105, starting transfers between devices, swapped(): lax.ppermute(value, ('dp', 'vocab'), [(i, i ^ mask) for i in range(device...  92.8 us
    unnamed x481, local copies, waits for them, and re-layouts  39.3 us
    dot_general x11, matrix products, matmul(): return jnp.dot(left, right, preferred_element_type=F32)  14.6 us
    convert_element_type x29, other arithmetic, added(): return (mine.astype(F32) + theirs.astype(F32)).astype(out)  12.4 us
  transfers between devices with their start and end apart: 105, of which 50 were waited for; matrix products, arithmetic and copies ran while one was open for 14% of the time, Pallas kernels for 19%

profile of v6, /device:TPU:0, one launch (start us, length us, event | category | flops | bytes accessed | tf_op | source)
XLA Modules:
  0.0 590.7 jit_solution(5563119791826077403)
XLA Ops:
  3.5 4.0 collective-permute-start
  20.7 2.8 collective-permute-done.3
  25.0 2.1 collective-permute-start.8
  52.8 7.9 %collective-permute-done.14 = bf16[64,2048]{1,0:T(8,128)(2,1)S(1)} collective-permute-done((bf16[64,2048]{1,0:T(8,128)(2,1)S(1)}, bf16[64,2048]{1,0:T(8,128)(2,1)S(1)}, u32[]{:S(2)}, u32[]{:S(2)}) %collective-permute-start.14) | collective-permute-done | bytes 262176 | tf_op jit(solution)/shard_map/ppermute | solution.py:66
  60.7 2.4 collective-permute-start.15
  63.1 2.6 fusion.6
  65.7 3.9 collective-permute-done.15
  81.4 8.9 %collective-permute-done.21 = bf16[32,5120]{1,0:T(8,128)(2,1)} collective-permute-done((bf16[32,5120]{1,0:T(8,128)(2,1)S(1)}, bf16[32,5120]{1,0:T(8,128)(2,1)}, u32[]{:S(2)}, u32[]{:S(2)}) %collective-permute-start.21) | collective-permute-done | bytes 327712 | tf_op jit(solution)/shard_map/ppermute | solution.py:66
  93.4 7.5 %collective-permute-done.23.refs_6_.refs_5_ = bf16[256,1792]{1,0:T(8,128)(2,1)S(1)} collective-permute-done((bf16[256,1792]{1,0:T(8,128)(2,1)}, bf16[256,1792]{1,0:T(8,128)(2,1)S(1)}, u32[]{:S(2)}, u32[]{:S(2)}) %collective-permute-start.23) | collective-permute-done | bytes 917536 | tf_op jit(solution)/shard_map/ppermute | solution.py:66
  100.9 7.9 %collective-permute-done.26 = bf16[64,5120]{1,0:T(8,128)(2,1)S(1)} collective-permute-done((bf16[64,5120]{1,0:T(8,128)(2,1)S(1)}, bf16[64,5120]{1,0:T(8,128)(2,1)S(1)}, u32[]{:S(2)}, u32[]{:S(2)}) %collective-permute-start.26) | collective-permute-done | bytes 655392 | tf_op jit(solution)/shard_map/ppermute | solution.py:66
  123.0 3.2 shard_map.457
  126.3 5.2 shard_map.458.q_ref.k_ref.v_ref
  131.6 2.4 collective-permute-done.34
  133.9 2.8 collective-permute-done.32
  142.0 10.7 %shard_map.459 = bf16[384,1024]{1,0:T(8,128)(2,1)S(1)} custom-call(f32[384,3072]{1,0:T(8,128)S(1)} %shard_map.458.q_ref.k_ref.v_ref, f32[384,3072]{1,0:T(8,128)S(1)} %shard_map.458.q_ref.k_ref.v_ref, f32[384,3072]{1,0:T(8,128)S(1)} %shard_map.458.q_ref.k_ref.v_ref, f32[1,1024]{1,0:T(1,128)S(1)} %get-tuple-element.758.qg_ref, ...), custom_call_target="tpu_custom_call" | custom-call | flops 1000 | bytes 1000 | tf_op jit(solution)/shard_map/pallas_call | solution.py:149
  157.4 3.0 collective-permute-done.38
  164.3 10.9 %collective-permute-done.43.refs_6_.refs_5_ = bf16[256,2560]{1,0:T(8,128)(2,1)S(1)} collective-permute-done((bf16[256,2560]{1,0:T(8,128)(2,1)S(1)}, bf16[256,2560]{1,0:T(8,128)(2,1)S(1)}, u32[]{:S(2)}, u32[]{:S(2)}) %collective-permute-start.43) | collective-permute-done | bytes 1310752 | tf_op jit(solution)/shard_map/ppermute | solution.py:66
  175.8 2.4 collective-permute-done.44.refs_4_.refs_3_
  181.7 3.7 shard_map.461
  190.4 7.4 %shard_map.462 = (f32[384,4096]{1,0:T(8,128)S(1)}, bf16[384,4096]{1,0:T(8,128)(2,1)S(1)}) custom-call(bf16[384,1024]{1,0:T(8,128)(2,1)S(1)} %get-tuple-element.432.one_ref, bf16[384,1024]{1,0:T(8,128)(2,1)S(1)} %get-tuple-element.433.two_ref, f32[1,4096]{1,0:T(1,128)S(1)} %bitcast.114, ...), custom_call_target="tpu_custom_call" | custom-call | flops 1000 | bytes 1000 | tf_op jit(solution)/shard_map/pallas_call | solution.py:149
  197.8 2.7 copy-done.58
  200.5 13.8 %collective-permute-done.52 = bf16[256,1024]{1,0:T(8,128)(2,1)S(1)} collective-permute-done((bf16[256,1024]{1,0:T(8,128)(2,1)S(1)}, bf16[256,1024]{1,0:T(8,128)(2,1)S(1)}, u32[]{:S(2)}, u32[]{:S(2)}) %collective-permute-start.52) | collective-permute-done | bytes 524320 | tf_op jit(solution)/shard_map/ppermute | solution.py:66
  218.7 9.1 %shard_map.463.refs_1_.refs_2_ = f32[384,1024]{1,0:T(8,128)S(1)} custom-call(bf16[1,384,4096]{2,1,0:T(8,128)(2,1)S(1)} %bitcast.102, bf16[1024,1024]{1,0:T(8,128)(2,1)S(1)} %get-tuple-element.846.one_ref, bf16[1024,1024]{1,0:T(8,128)(2,1)S(1)} %get-tuple-element.844.two_ref, f32[1,1024]{1,0:T(1,128)S(1)} %get-tuple-element.755.refs_0_, ...), custom_call_target="tpu_custom_call" | custom-call | flops 1000 | bytes 1000 | tf_op jit(solution)/shard_map/pallas_call | solution.py:149
  230.7 3.4 shard_map.464
  235.3 4.9 collective-permute-done.55
  245.9 4.0 add_reduce_fusion.1
  251.0 12.1 %collective-permute-done.57 = bf16[384,1024]{1,0:T(8,128)(2,1)S(1)} collective-permute-done((bf16[384,1024]{1,0:T(8,128)(2,1)}, bf16[384,1024]{1,0:T(8,128)(2,1)S(1)}, u32[]{:S(2)}, u32[]{:S(2)}) %collective-permute-start.57) | collective-permute-done | bytes 786464 | tf_op jit(solution)/shard_map/ppermute | solution.py:66
  263.2 2.2 collective-permute-done.58
  276.1 2.5 collective-permute-done.61
  280.3 4.6 fusion.14
  293.7 2.8 fusion.41
  296.5 2.8 fusion.38
  299.3 13.3 %collective-permute-done.63 = bf16[384,1024]{1,0:T(8,128)(2,1)S(1)} collective-permute-done((bf16[384,1024]{1,0:T(8,128)(2,1)S(1)}, bf16[384,1024]{1,0:T(8,128)(2,1)S(1)}, u32[]{:S(2)}, u32[]{:S(2)}) %collective-permute-start.63) | collective-permute-done | bytes 786464 | tf_op jit(solution)/shard_map/ppermute | solution.py:66
  317.0 4.8 shard_map.465
  323.1 3.9 shard_map.466
  327.2 8.8 %shard_map.467 = (bf16[384,4096]{1,0:T(8,128)(2,1)S(1)}, f32[1,4096]{1,0:T(1,128)S(1)}) custom-call(bf16[384,1024]{1,0:T(8,128)(2,1)S(1)} %get-tuple-element.464.one_ref, bf16[384,1024]{1,0:T(8,128)(2,1)S(1)} %get-tuple-element.465.two_ref, f32[384,4096]{1,0:T(8,128)S(1)} %bitcast.112, bf16[256,2048]{1,0:T(8,128)(2,1)S(1)} %copy-done.52, ...), custom_call_target="tpu_custom_call" | custom-call | flops 1000 | bytes 1000 | tf_op jit(solution)/shard_map/pallas_call | solution.py:149
  336.1 4.7 shard_map.469
  340.8 4.1 shard_map.468
  348.1 7.8 %shard_map.470.refs_1_ = f32[384,1024]{1,0:T(8,128)S(1)} custom-call(bf16[1,384,4096]{2,1,0:T(8,128)(2,1)S(1)} %bitcast.106, bf16[1024,1024]{1,0:T(8,128)(2,1)S(1)} %copy-done.2, bf16[1024,1024]{1,0:T(8,128)(2,1)S(1)} %get-tuple-element.844.two_ref, bf16[256,2560]{1,0:T(8,128)(2,1)S(1)} %constant_dynamic-update-slice_fusion.22.refs_1_.refs_0_, ...), custom_call_target="tpu_custom_call" | custom-call | flops 1000 | bytes 1000 | tf_op jit(solution)/shard_map/pallas_call | solution.py:149
  356.1 5.1 shard_map.472
  361.2 2.9 shard_map.471
  364.2 6.7 %collective-permute-done.68 = bf16[512,1024]{1,0:T(8,128)(2,1)} collective-permute-done((bf16[512,1024]{1,0:T(8,128)(2,1)}, bf16[512,1024]{1,0:T(8,128)(2,1)}, u32[]{:S(2)}, u32[]{:S(2)}) %collective-permute-start.68) | collective-permute-done | bytes 1048608 | tf_op jit(solution)/shard_map/ppermute | solution.py:66
  382.2 3.5 shard_map.473.dm_ref
  387.1 20.9 %shard_map.474 = (bf16[3,384,1024]{2,1,0:T(8,128)(2,1)S(1)}, f32[8,1024]{1,0:T(8,128)S(1)}) custom-call(f32[384,3072]{1,0:T(8,128)S(1)} %bitcast.101, f32[384,3072]{1,0:T(8,128)S(1)} %bitcast.101, f32[384,3072]{1,0:T(8,128)S(1)} %bitcast.101, f32[1,1024]{1,0:T(1,128)S(1)} %get-tuple-element.758.qg_ref, f32[1,1024]{1,0:T(1,128)S(1)} %get-tuple-element.757.kg_ref, ...), custom_call_target="tpu_custom_call" | custom-call | flops 1000 | bytes 1000 | tf_op jit(solution)/shard_map/pallas_call | solution.py:149
  408.0 3.0 collective-permute-done.69
  413.1 3.9 shard_map.476
  421.9 7.9 %shard_map.477.refs_1_ = f32[384,1024]{1,0:T(8,128)S(1)} custom-call(bf16[3,384,1024]{2,1,0:T(8,128)(2,1)S(1)} %get-tuple-element.517.right_ref, bf16[1024,1024]{1,0:T(8,128)(2,1)S(1)} %copy-done.2, bf16[1024,1024]{1,0:T(8,128)(2,1)S(1)} %get-tuple-element.844.two_ref, bf16[256,1792]{1,0:T(8,128)(2,1)S(1)} %copy-done.54, bf16[256,1792]{1,0:T(8,128)(2,1)S(1)} %copy-done.66, ...), custom_call_target="tpu_custom_call" | custom-call | flops 1000 | bytes 1000 | tf_op jit(solution)/shard_map/pallas_call | solution.py:149
  429.8 2.3 collective-permute-done.76
  435.0 2.9 shard_map.478
  438.1 2.1 shard_map.479
  453.6 4.0 shard_map.480
  467.9 3.0 collective-permute-done.84
  471.0 16.1 %collective-permute-done.85 = bf16[16,8192]{1,0:T(8,128)(2,1)S(1)} collective-permute-done((bf16[16,8192]{1,0:T(8,128)(2,1)S(1)}, bf16[16,8192]{1,0:T(8,128)(2,1)S(1)}, u32[]{:S(2)}, u32[]{:S(2)}) %collective-permute-start.85) | collective-permute-done | bytes 262176 | tf_op jit(solution)/shard_map/ppermute | solution.py:66
  487.1 3.8 collective-permute-done.82
  501.1 5.8 collective-permute-done.89
  506.8 4.0 collective-permute-done.88
  518.8 3.2 collective-permute-done.93
  522.0 5.5 collective-permute-done.92
  531.7 3.4 collective-permute-done.96
  566.0 2.5 collective-permute-done.103
  569.4 2.7 collective-permute-done.104
  577.0 2.8 fusion.119
  580.9 2.4 fusion.125
  584.3 2.4 fusion.127
  (926 shorter events, 241.1 us)
Async XLA Ops:
  3.5 17.2 %collective-permute-start = (s32[1,128]{1,0:T(1,128)S(1)}, s32[1,128]{1,0:T(1,128)S(1)}, u32[]{:S(2)}, u32[]{:S(2)}) collective-permute-start(s32[1,128]{1,0:T(1,128)S(1)} %add_bitcast_fusion.4), channel_id=1, source_target_pairs={{0,16},{1,17},{2,18},{3,19},{4,20},{5,21},{6,22},{7,23},{8,24},{9,... | collective-permute-start | bytes 1544 | tf_op jit(solution)/shard_map/ppermute | solution.py:66
  7.5 13.1 %collective-permute-start.1 = (s32[1,128]{1,0:T(1,128)S(1)}, s32[1,128]{1,0:T(1,128)S(1)}, u32[]{:S(2)}, u32[]{:S(2)}) collective-permute-start(s32[1,128]{1,0:T(1,128)S(1)} %add_bitcast_fusion.4), channel_id=1, source_target_pairs={{0,8},{1,9},{2,10},{3,11},{4,12},{5,13},{6,14},{7,15},{8,0},{9,1},... | collective-permute-start | bytes 1544 | tf_op jit(solution)/shard_map/ppermute | solution.py:66
  9.1 11.6 %collective-permute-start.2 = (s32[1,128]{1,0:T(1,128)S(1)}, s32[1,128]{1,0:T(1,128)S(1)}, u32[]{:S(2)}, u32[]{:S(2)}) collective-permute-start(s32[1,128]{1,0:T(1,128)S(1)} %add_bitcast_fusion.4), channel_id=1, source_target_pairs={{0,24},{1,25},{2,26},{3,27},{4,28},{5,29},{6,30},{7,31},{8,16},{9,... | collective-permute-start | bytes 1544 | tf_op jit(solution)/shard_map/ppermute | solution.py:66
  12.2 11.3 %collective-permute-start.3 = (bf16[32,1792]{1,0:T(8,128)(2,1)S(1)}, bf16[32,1792]{1,0:T(8,128)(2,1)S(1)}, u32[]{:S(2)}, u32[]{:S(2)}) collective-permute-start(bf16[32,1792]{1,0:T(8,128)(2,1)S(1)} %pad_maximum_fusion.21), channel_id=1, source_target_pairs={{0,16},{1,17},{2,18},{3,19},{4,20},{5,21},{6,22},{7,23},{8,24},{9,... | collective-permute-start | bytes 344072 | tf_op jit(solution)/shard_map/ppermute | solution.py:66
  25.0 11.4 %collective-permute-start.8 = (bf16[64,1792]{1,0:T(8,128)(2,1)S(1)}, bf16[64,1792]{1,0:T(8,128)(2,1)S(1)}, u32[]{:S(2)}, u32[]{:S(2)}) collective-permute-start(bf16[64,1792]{1,0:T(8,128)(2,1)S(1)} %constant_dynamic-update-slice_fusion), channel_id=1, source_target_pairs={{0,8},{1,9},{2,10},{3,11},{4,12},{5,13},{6,14},{7,15},{8,0},{9,1},... | collective-permute-start | bytes 688136 | tf_op jit(solution)/shard_map/ppermute | solution.py:66
  31.6 19.0 %collective-permute-start.12 = (f32[1,2,384]{2,1,0:T(2,128)S(1)}, f32[1,2,384]{2,1,0:T(2,128)S(1)}, u32[]{:S(2)}, u32[]{:S(2)}) collective-permute-start(f32[1,2,384]{2,1,0:T(2,128)S(1)} %maximum_bitcast_fusion.1), channel_id=1, source_target_pairs={{0,2},{1,3},{2,0},{3,1},{4,6},{5,7},{6,4},{7,5},{8,10},{9,11},{10,... | collective-permute-start | bytes 9224 | tf_op jit(solution)/shard_map/ppermute | solution.py:66
  36.5 14.1 %collective-permute-start.13 = (bf16[128,1024]{1,0:T(8,128)(2,1)S(1)}, bf16[128,1024]{1,0:T(8,128)(2,1)}, u32[]{:S(2)}, u32[]{:S(2)}) collective-permute-start(bf16[128,1024]{1,0:T(8,128)(2,1)S(1)} %convert_element_type.580), channel_id=1, source_target_pairs={{0,4},{1,5},{2,6},{3,7},{4,0},{5,1},{6,2},{7,3},{8,12},{9,13},{10,... | collective-permute-start | bytes 786440 | tf_op jit(solution)/shard_map/ppermute | solution.py:66
  39.5 30.1 %collective-permute-start.16 = (bf16[128,1792]{1,0:T(8,128)(2,1)}, bf16[128,1792]{1,0:T(8,128)(2,1)}, u32[]{:S(2)}, u32[]{:S(2)}) collective-permute-start(bf16[128,1792]{1,0:T(8,128)(2,1)} %constant_dynamic-update-slice_fusion.6), channel_id=1, source_target_pairs={{0,4},{1,5},{2,6},{3,7},{4,0},{5,1},{6,2},{7,3},{8,12},{9,13},{10,... | collective-permute-start | bytes 1376264 | tf_op jit(solution)/shard_map/ppermute | solution.py:66
  41.5 28.2 %collective-permute-start.17 = (bf16[128,1792]{1,0:T(8,128)(2,1)}, bf16[128,1792]{1,0:T(8,128)(2,1)}, u32[]{:S(2)}, u32[]{:S(2)}) collective-permute-start(bf16[128,1792]{1,0:T(8,128)(2,1)} %constant_dynamic-update-slice_fusion.8), channel_id=1, source_target_pairs={{0,2},{1,3},{2,0},{3,1},{4,6},{5,7},{6,4},{7,5},{8,10},{9,11},{10,... | collective-permute-start | bytes 1376264 | tf_op jit(solution)/shard_map/ppermute | solution.py:66
  72.5 17.9 %collective-permute-start.21 = (bf16[32,5120]{1,0:T(8,128)(2,1)S(1)}, bf16[32,5120]{1,0:T(8,128)(2,1)}, u32[]{:S(2)}, u32[]{:S(2)}) collective-permute-start(bf16[32,5120]{1,0:T(8,128)(2,1)S(1)} %copy-done.142), channel_id=1, source_target_pairs={{0,16},{1,17},{2,18},{3,19},{4,20},{5,21},{6,22},{7,23},{8,24},{9,... | collective-permute-start | bytes 983048 | tf_op jit(solution)/shard_map/ppermute | solution.py:66
  78.8 22.1 %collective-permute-start.23 = (bf16[256,1792]{1,0:T(8,128)(2,1)}, bf16[256,1792]{1,0:T(8,128)(2,1)S(1)}, u32[]{:S(2)}, u32[]{:S(2)}) collective-permute-start(bf16[256,1792]{1,0:T(8,128)(2,1)} %copy-done.55), channel_id=1, source_target_pairs={{0,4},{1,5},{2,6},{3,7},{4,0},{5,1},{6,2},{7,3},{8,12},{9,13},{10,... | collective-permute-start | bytes 2752520 | tf_op jit(solution)/shard_map/ppermute | solution.py:66
  79.3 21.6 %collective-permute-start.22 = (bf16[256,1792]{1,0:T(8,128)(2,1)S(1)}, bf16[256,1792]{1,0:T(8,128)(2,1)S(1)}, u32[]{:S(2)}, u32[]{:S(2)}) collective-permute-start(bf16[256,1792]{1,0:T(8,128)(2,1)S(1)} %constant_dynamic-update-slice_fusion.12.refs_1_.refs_0_), channel_id=1, source_target_pairs={{0,2},{1,3},{2,0},{3,1},{4,6},{5,7},{6,4},{7,5},{8,10},{9,11},{10,... | collective-permute-start | bytes 2752520 | tf_op jit(solution)/shard_map/ppermute | solution.py:66
  90.4 18.4 %collective-permute-start.24 = (bf16[256,1792]{1,0:T(8,128)(2,1)S(1)}, bf16[256,1792]{1,0:T(8,128)(2,1)S(1)}, u32[]{:S(2)}, u32[]{:S(2)}) collective-permute-start(bf16[256,1792]{1,0:T(8,128)(2,1)S(1)} %constant_dynamic-update-slice_fusion.12.refs_1_.refs_0_), channel_id=1, source_target_pairs={{0,1},{1,0},{2,3},{3,2},{4,5},{5,4},{6,7},{7,6},{8,9},{9,8},{10,11... | collective-permute-start | bytes 2752520 | tf_op jit(solution)/shard_map/ppermute | solution.py:66
  90.5 18.3 %collective-permute-start.25 = (bf16[256,1792]{1,0:T(8,128)(2,1)}, bf16[256,1792]{1,0:T(8,128)(2,1)S(1)}, u32[]{:S(2)}, u32[]{:S(2)}) collective-permute-start(bf16[256,1792]{1,0:T(8,128)(2,1)} %copy-done.55), channel_id=1, source_target_pairs={{0,1},{1,0},{2,3},{3,2},{4,5},{5,4},{6,7},{7,6},{8,9},{9,8},{10,11... | collective-permute-start | bytes 2752520 | tf_op jit(solution)/shard_map/ppermute | solution.py:66
  92.0 16.8 %collective-permute-start.26 = (bf16[64,5120]{1,0:T(8,128)(2,1)S(1)}, bf16[64,5120]{1,0:T(8,128)(2,1)S(1)}, u32[]{:S(2)}, u32[]{:S(2)}) collective-permute-start(bf16[64,5120]{1,0:T(8,128)(2,1)S(1)} %constant_dynamic-update-slice_fusion.16), channel_id=1, source_target_pairs={{0,8},{1,9},{2,10},{3,11},{4,12},{5,13},{6,14},{7,15},{8,0},{9,1},... | collective-permute-start | bytes 1966088 | tf_op jit(solution)/shard_map/ppermute | solution.py:66
  109.9 21.6 %collective-permute-start.30 = (bf16[128,2560]{1,0:T(8,128)(2,1)S(1)}, bf16[128,2560]{1,0:T(8,128)(2,1)S(1)}, u32[]{:S(2)}, u32[]{:S(2)}) collective-permute-start(bf16[128,2560]{1,0:T(8,128)(2,1)S(1)} %get-tuple-element.395), channel_id=1, source_target_pairs={{0,4},{1,5},{2,6},{3,7},{4,0},{5,1},{6,2},{7,3},{8,12},{9,13},{10,... | collective-permute-start | bytes 1966088 | tf_op jit(solution)/shard_map/ppermute | solution.py:66
  111.5 20.0 %collective-permute-start.31 = (bf16[128,2560]{1,0:T(8,128)(2,1)S(1)}, bf16[128,2560]{1,0:T(8,128)(2,1)S(1)}, u32[]{:S(2)}, u32[]{:S(2)}) collective-permute-start(bf16[128,2560]{1,0:T(8,128)(2,1)S(1)} %get-tuple-element.397), channel_id=1, source_target_pairs={{0,2},{1,3},{2,0},{3,1},{4,6},{5,7},{6,4},{7,5},{8,10},{9,11},{10,... | collective-permute-start | bytes 1966088 | tf_op jit(solution)/shard_map/ppermute | solution.py:66
  116.7 20.1 %collective-permute-start.32 = (bf16[64,3072]{1,0:T(8,128)(2,1)S(1)}, bf16[64,3072]{1,0:T(8,128)(2,1)S(1)}, u32[]{:S(2)}, u32[]{:S(2)}) collective-permute-start(bf16[64,3072]{1,0:T(8,128)(2,1)S(1)} %get-tuple-element.743), channel_id=1, source_target_pairs={{0,2},{1,3},{2,0},{3,1},{4,6},{5,7},{6,4},{7,5},{8,10},{9,11},{10,... | collective-permute-start | bytes 1179656 | tf_op jit(solution)/shard_map/ppermute | solution.py:66
  118.2 18.6 %collective-permute-start.33 = (bf16[64,3072]{1,0:T(8,128)(2,1)S(1)}, bf16[64,3072]{1,0:T(8,128)(2,1)S(1)}, u32[]{:S(2)}, u32[]{:S(2)}) collective-permute-start(bf16[64,3072]{1,0:T(8,128)(2,1)S(1)} %get-tuple-element.741), channel_id=1, source_target_pairs={{0,4},{1,5},{2,6},{3,7},{4,0},{5,1},{6,2},{7,3},{8,12},{9,13},{10,... | collective-permute-start | bytes 1179656 | tf_op jit(solution)/shard_map/ppermute | solution.py:66
  119.8 14.1 %collective-permute-start.34 = (bf16[32,4096]{1,0:T(8,128)(2,1)S(1)}, bf16[32,4096]{1,0:T(8,128)(2,1)S(1)}, u32[]{:S(2)}, u32[]{:S(2)}) collective-permute-start(bf16[32,4096]{1,0:T(8,128)(2,1)S(1)} %copy-done.157), channel_id=1, source_target_pairs={{0,16},{1,17},{2,18},{3,19},{4,20},{5,21},{6,22},{7,23},{8,24},{9,... | collective-permute-start | bytes 786440 | tf_op jit(solution)/shard_map/ppermute | solution.py:66
  136.9 15.8 %collective-permute-start.37 = (bf16[64,4096]{1,0:T(8,128)(2,1)S(1)}, bf16[64,4096]{1,0:T(8,128)(2,1)S(1)}, u32[]{:S(2)}, u32[]{:S(2)}) collective-permute-start(bf16[64,4096]{1,0:T(8,128)(2,1)S(1)} %constant_dynamic-update-slice_fusion.20), channel_id=1, source_target_pairs={{0,8},{1,9},{2,10},{3,11},{4,12},{5,13},{6,14},{7,15},{8,0},{9,1},... | collective-permute-start | bytes 1572872 | tf_op jit(solution)/shard_map/ppermute | solution.py:66
  137.4 15.3 %collective-permute-start.36 = (bf16[32,3072]{1,0:T(8,128)(2,1)S(1)}, bf16[32,3072]{1,0:T(8,128)(2,1)S(1)}, u32[]{:S(2)}, u32[]{:S(2)}) collective-permute-start(bf16[32,3072]{1,0:T(8,128)(2,1)S(1)} %get-tuple-element.794), channel_id=1, source_target_pairs={{0,2},{1,3},{2,0},{3,1},{4,6},{5,7},{6,4},{7,5},{8,10},{9,11},{10,... | collective-permute-start | bytes 589832 | tf_op jit(solution)/shard_map/ppermute | solution.py:66
  139.1 13.6 %collective-permute-start.35 = (bf16[32,3072]{1,0:T(8,128)(2,1)S(1)}, bf16[32,3072]{1,0:T(8,128)(2,1)S(1)}, u32[]{:S(2)}, u32[]{:S(2)}) collective-permute-start(bf16[32,3072]{1,0:T(8,128)(2,1)S(1)} %get-tuple-element.796), channel_id=1, source_target_pairs={{0,4},{1,5},{2,6},{3,7},{4,0},{5,1},{6,2},{7,3},{8,12},{9,13},{10,... | collective-permute-start | bytes 589832 | tf_op jit(solution)/shard_map/ppermute | solution.py:66
  139.7 35.4 %collective-permute-start.43 = (bf16[256,2560]{1,0:T(8,128)(2,1)S(1)}, bf16[256,2560]{1,0:T(8,128)(2,1)S(1)}, u32[]{:S(2)}, u32[]{:S(2)}) collective-permute-start(bf16[256,2560]{1,0:T(8,128)(2,1)S(1)} %constant_dynamic-update-slice_fusion.24.refs_5_.refs_4_), channel_id=1, source_target_pairs={{0,4},{1,5},{2,6},{3,7},{4,0},{5,1},{6,2},{7,3},{8,12},{9,13},{10,... | collective-permute-start | bytes 3932168 | tf_op jit(solution)/shard_map/ppermute | solution.py:66
  141.4 33.7 %collective-permute-start.42 = (bf16[256,2560]{1,0:T(8,128)(2,1)S(1)}, bf16[256,2560]{1,0:T(8,128)(2,1)S(1)}, u32[]{:S(2)}, u32[]{:S(2)}) collective-permute-start(bf16[256,2560]{1,0:T(8,128)(2,1)S(1)} %constant_dynamic-update-slice_fusion.22.refs_1_.refs_0_), channel_id=1, source_target_pairs={{0,2},{1,3},{2,0},{3,1},{4,6},{5,7},{6,4},{7,5},{8,10},{9,11},{10,... | collective-permute-start | bytes 3932168 | tf_op jit(solution)/shard_map/ppermute | solution.py:66
  160.5 14.6 %collective-permute-start.41 = (bf16[8,6144]{1,0:T(8,128)(2,1)S(1)}, bf16[8,6144]{1,0:T(8,128)(2,1)S(1)}, u32[]{:S(2)}, u32[]{:S(2)}) collective-permute-start(bf16[8,6144]{1,0:T(8,128)(2,1)S(1)} %get-tuple-element.814), channel_id=1, source_target_pairs={{0,16},{1,17},{2,18},{3,19},{4,20},{5,21},{6,22},{7,23},{8,24},{9,... | collective-permute-start | bytes 294920 | tf_op jit(solution)/shard_map/ppermute | solution.py:66
  162.2 23.2 %collective-permute-start.46 = (bf16[128,2048]{1,0:T(8,128)(2,1)S(1)}, bf16[128,2048]{1,0:T(8,128)(2,1)S(1)}, u32[]{:S(2)}, u32[]{:S(2)}) collective-permute-start(bf16[128,2048]{1,0:T(8,128)(2,1)S(1)} %get-tuple-element.435), channel_id=1, source_target_pairs={{0,4},{1,5},{2,6},{3,7},{4,0},{5,1},{6,2},{7,3},{8,12},{9,13},{10,... | collective-permute-start | bytes 1572872 | tf_op jit(solution)/shard_map/ppermute | solution.py:66
  162.8 22.7 %collective-permute-start.47 = (bf16[128,2048]{1,0:T(8,128)(2,1)S(1)}, bf16[128,2048]{1,0:T(8,128)(2,1)S(1)}, u32[]{:S(2)}, u32[]{:S(2)}) collective-permute-start(bf16[128,2048]{1,0:T(8,128)(2,1)S(1)} %get-tuple-element.437), channel_id=1, source_target_pairs={{0,2},{1,3},{2,0},{3,1},{4,6},{5,7},{6,4},{7,5},{8,10},{9,11},{10,... | collective-permute-start | bytes 1572872 | tf_op jit(solution)/shard_map/ppermute | solution.py:66
  185.6 28.8 %collective-permute-start.49 = (bf16[256,2048]{1,0:T(8,128)(2,1)S(1)}, bf16[256,2048]{1,0:T(8,128)(2,1)S(1)}, u32[]{:S(2)}, u32[]{:S(2)}) collective-permute-start(bf16[256,2048]{1,0:T(8,128)(2,1)S(1)} %constant_dynamic-update-slice_fusion.30.refs_5_), channel_id=1, source_target_pairs={{0,4},{1,5},{2,6},{3,7},{4,0},{5,1},{6,2},{7,3},{8,12},{9,13},{10,... | collective-permute-start | bytes 3145736 | tf_op jit(solution)/shard_map/ppermute | solution.py:66
  186.1 28.2 %collective-permute-start.51 = (bf16[256,2048]{1,0:T(8,128)(2,1)S(1)}, bf16[256,2048]{1,0:T(8,128)(2,1)S(1)}, u32[]{:S(2)}, u32[]{:S(2)}) collective-permute-start(bf16[256,2048]{1,0:T(8,128)(2,1)S(1)} %constant_dynamic-update-slice_fusion.30.refs_5_), channel_id=1, source_target_pairs={{0,1},{1,0},{2,3},{3,2},{4,5},{5,4},{6,7},{7,6},{8,9},{9,8},{10,11... | collective-permute-start | bytes 3145736 | tf_op jit(solution)/shard_map/ppermute | solution.py:66
  186.2 28.1 %collective-permute-start.48 = (bf16[256,2048]{1,0:T(8,128)(2,1)S(1)}, bf16[256,2048]{1,0:T(8,128)(2,1)S(1)}, u32[]{:S(2)}, u32[]{:S(2)}) collective-permute-start(bf16[256,2048]{1,0:T(8,128)(2,1)S(1)} %constant_dynamic-update-slice_fusion.28.refs_1_), channel_id=1, source_target_pairs={{0,2},{1,3},{2,0},{3,1},{4,6},{5,7},{6,4},{7,5},{8,10},{9,11},{10,... | collective-permute-start | bytes 3145736 | tf_op jit(solution)/shard_map/ppermute | solution.py:66
  186.8 27.6 %collective-permute-start.50 = (bf16[256,2048]{1,0:T(8,128)(2,1)S(1)}, bf16[256,2048]{1,0:T(8,128)(2,1)S(1)}, u32[]{:S(2)}, u32[]{:S(2)}) collective-permute-start(bf16[256,2048]{1,0:T(8,128)(2,1)S(1)} %constant_dynamic-update-slice_fusion.28.refs_1_), channel_id=1, source_target_pairs={{0,1},{1,0},{2,3},{3,2},{4,5},{5,4},{6,7},{7,6},{8,9},{9,8},{10,11... | collective-permute-start | bytes 3145736 | tf_op jit(solution)/shard_map/ppermute | solution.py:66
  188.2 26.2 %collective-permute-start.52 = (bf16[256,1024]{1,0:T(8,128)(2,1)S(1)}, bf16[256,1024]{1,0:T(8,128)(2,1)S(1)}, u32[]{:S(2)}, u32[]{:S(2)}) collective-permute-start(bf16[256,1024]{1,0:T(8,128)(2,1)S(1)} %constant_dynamic-update-slice_fusion.32), channel_id=1, source_target_pairs={{0,16},{1,17},{2,18},{3,19},{4,20},{5,21},{6,22},{7,23},{8,24},{9,... | collective-permute-start | bytes 1572872 | tf_op jit(solution)/shard_map/ppermute | solution.py:66
  215.1 25.2 %collective-permute-start.55 = (bf16[512,1024]{1,0:T(8,128)(2,1)S(1)}, bf16[512,1024]{1,0:T(8,128)(2,1)S(1)}, u32[]{:S(2)}, u32[]{:S(2)}) collective-permute-start(bf16[512,1024]{1,0:T(8,128)(2,1)S(1)} %constant_dynamic-update-slice_fusion.34), channel_id=1, source_target_pairs={{0,8},{1,9},{2,10},{3,11},{4,12},{5,13},{6,14},{7,15},{8,0},{9,1},... | collective-permute-start | bytes 3145736 | tf_op jit(solution)/shard_map/ppermute | solution.py:66
  242.9 20.2 %collective-permute-start.57 = (bf16[384,1024]{1,0:T(8,128)(2,1)}, bf16[384,1024]{1,0:T(8,128)(2,1)S(1)}, u32[]{:S(2)}, u32[]{:S(2)}) collective-permute-start(bf16[384,1024]{1,0:T(8,128)(2,1)} %get-tuple-element.455), channel_id=1, source_target_pairs={{0,2},{1,3},{2,0},{3,1},{4,6},{5,7},{6,4},{7,5},{8,10},{9,11},{10,... | collective-permute-start | bytes 2359304 | tf_op jit(solution)/shard_map/ppermute | solution.py:66
  292.9 19.6 %collective-permute-start.63 = (bf16[384,1024]{1,0:T(8,128)(2,1)S(1)}, bf16[384,1024]{1,0:T(8,128)(2,1)S(1)}, u32[]{:S(2)}, u32[]{:S(2)}) collective-permute-start(bf16[384,1024]{1,0:T(8,128)(2,1)S(1)} %add_convert_fusion.1), channel_id=1, source_target_pairs={{0,2},{1,3},{2,0},{3,1},{4,6},{5,7},{6,4},{7,5},{8,10},{9,11},{10,... | collective-permute-start | bytes 2359304 | tf_op jit(solution)/shard_map/ppermute | solution.py:66
  345.0 11.1 %collective-permute-start.65 = (bf16[512,4096]{1,0:T(8,128)(2,1)}, bf16[512,4096]{1,0:T(8,128)(2,1)S(1)}, u32[]{:S(2)}, u32[]{:S(2)}) collective-permute-start(bf16[512,4096]{1,0:T(8,128)(2,1)} %shard_map.469), channel_id=1, source_target_pairs={{0,1},{1,0},{2,3},{3,2},{4,5},{5,4},{6,7},{7,6},{8,9},{9,8},{10,11... | collective-permute-start | bytes 12582920 | tf_op jit(solution)/shard_map/ppermute | solution.py:66
  345.5 25.5 %collective-permute-start.68 = (bf16[512,1024]{1,0:T(8,128)(2,1)}, bf16[512,1024]{1,0:T(8,128)(2,1)}, u32[]{:S(2)}, u32[]{:S(2)}) collective-permute-start(bf16[512,1024]{1,0:T(8,128)(2,1)} %fusion.38), channel_id=1, source_target_pairs={{0,8},{1,9},{2,10},{3,11},{4,12},{5,13},{6,14},{7,15},{8,0},{9,1},... | collective-permute-start | bytes 3145736 | tf_op jit(solution)/shard_map/ppermute | solution.py:66
  345.8 25.2 %collective-permute-start.66 = (bf16[256,2048]{1,0:T(8,128)(2,1)S(1)}, bf16[256,2048]{1,0:T(8,128)(2,1)}, u32[]{:S(2)}, u32[]{:S(2)}) collective-permute-start(bf16[256,2048]{1,0:T(8,128)(2,1)S(1)} %get-tuple-element.480), channel_id=1, source_target_pairs={{0,2},{1,3},{2,0},{3,1},{4,6},{5,7},{6,4},{7,5},{8,10},{9,11},{10,... | collective-permute-start | bytes 3145736 | tf_op jit(solution)/shard_map/ppermute | solution.py:66
  346.5 24.8 %collective-permute-start.67 = (bf16[256,2048]{1,0:T(8,128)(2,1)S(1)}, bf16[256,2048]{1,0:T(8,128)(2,1)}, u32[]{:S(2)}, u32[]{:S(2)}) collective-permute-start(bf16[256,2048]{1,0:T(8,128)(2,1)S(1)} %get-tuple-element.481), channel_id=1, source_target_pairs={{0,4},{1,5},{2,6},{3,7},{4,0},{5,1},{6,2},{7,3},{8,12},{9,13},{10,... | collective-permute-start | bytes 3145736 | tf_op jit(solution)/shard_map/ppermute | solution.py:66
  374.7 36.3 %collective-permute-start.71 = (bf16[256,2048]{1,0:T(8,128)(2,1)}, bf16[256,2048]{1,0:T(8,128)(2,1)S(1)}, u32[]{:S(2)}, u32[]{:S(2)}) collective-permute-start(bf16[256,2048]{1,0:T(8,128)(2,1)} %get-tuple-element.501), channel_id=1, source_target_pairs={{0,2},{1,3},{2,0},{3,1},{4,6},{5,7},{6,4},{7,5},{8,10},{9,11},{10,... | collective-permute-start | bytes 3145736 | tf_op jit(solution)/shard_map/ppermute | solution.py:66
  376.1 34.9 %collective-permute-start.72 = (bf16[256,2048]{1,0:T(8,128)(2,1)}, bf16[256,2048]{1,0:T(8,128)(2,1)S(1)}, u32[]{:S(2)}, u32[]{:S(2)}) collective-permute-start(bf16[256,2048]{1,0:T(8,128)(2,1)} %get-tuple-element.502), channel_id=1, source_target_pairs={{0,4},{1,5},{2,6},{3,7},{4,0},{5,1},{6,2},{7,3},{8,12},{9,13},{10,... | collective-permute-start | bytes 3145736 | tf_op jit(solution)/shard_map/ppermute | solution.py:66
  379.2 28.8 %collective-permute-start.73 = (bf16[256,1024]{1,0:T(8,128)(2,1)S(1)}, bf16[256,1024]{1,0:T(8,128)(2,1)S(1)}, u32[]{:S(2)}, u32[]{:S(2)}) collective-permute-start(bf16[256,1024]{1,0:T(8,128)(2,1)S(1)} %get-tuple-element.734), channel_id=1, source_target_pairs={{0,16},{1,17},{2,18},{3,19},{4,20},{5,21},{6,22},{7,23},{8,24},{9,... | collective-permute-start | bytes 1572872 | tf_op jit(solution)/shard_map/ppermute | solution.py:66
  380.9 30.1 %collective-permute-start.69 = (bf16[128,2048]{1,0:T(8,128)(2,1)S(1)}, bf16[128,2048]{1,0:T(8,128)(2,1)S(1)}, u32[]{:S(2)}, u32[]{:S(2)}) collective-permute-start(bf16[128,2048]{1,0:T(8,128)(2,1)S(1)} %get-tuple-element.499), channel_id=1, source_target_pairs={{0,4},{1,5},{2,6},{3,7},{4,0},{5,1},{6,2},{7,3},{8,12},{9,13},{10,... | collective-permute-start | bytes 1572872 | tf_op jit(solution)/shard_map/ppermute | solution.py:66
  381.4 29.6 %collective-permute-start.70 = (bf16[128,2048]{1,0:T(8,128)(2,1)S(1)}, bf16[128,2048]{1,0:T(8,128)(2,1)S(1)}, u32[]{:S(2)}, u32[]{:S(2)}) collective-permute-start(bf16[128,2048]{1,0:T(8,128)(2,1)S(1)} %get-tuple-element.500), channel_id=1, source_target_pairs={{0,2},{1,3},{2,0},{3,1},{4,6},{5,7},{6,4},{7,5},{8,10},{9,11},{10,... | collective-permute-start | bytes 1572872 | tf_op jit(solution)/shard_map/ppermute | solution.py:66
  417.1 16.9 %collective-permute-start.75 = (bf16[512,3072]{1,0:T(8,128)(2,1)S(1)}, bf16[512,3072]{1,0:T(8,128)(2,1)S(1)}, u32[]{:S(2)}, u32[]{:S(2)}) collective-permute-start(bf16[512,3072]{1,0:T(8,128)(2,1)S(1)} %shard_map.476), channel_id=1, source_target_pairs={{0,1},{1,0},{2,3},{3,2},{4,5},{5,4},{6,7},{7,6},{8,9},{9,8},{10,11... | collective-permute-start | bytes 9437192 | tf_op jit(solution)/shard_map/ppermute | solution.py:66
  417.7 14.4 %collective-permute-start.76 = (bf16[128,2048]{1,0:T(8,128)(2,1)S(1)}, bf16[128,2048]{1,0:T(8,128)(2,1)S(1)}, u32[]{:S(2)}, u32[]{:S(2)}) collective-permute-start(bf16[128,2048]{1,0:T(8,128)(2,1)S(1)} %add_convert_fusion.17), channel_id=1, source_target_pairs={{0,4},{1,5},{2,6},{3,7},{4,0},{5,1},{6,2},{7,3},{8,12},{9,13},{10,... | collective-permute-start | bytes 1572872 | tf_op jit(solution)/shard_map/ppermute | solution.py:66
  419.3 14.0 %collective-permute-start.77 = (bf16[128,2048]{1,0:T(8,128)(2,1)S(1)}, bf16[128,2048]{1,0:T(8,128)(2,1)S(1)}, u32[]{:S(2)}, u32[]{:S(2)}) collective-permute-start(bf16[128,2048]{1,0:T(8,128)(2,1)S(1)} %add_convert_fusion.16), channel_id=1, source_target_pairs={{0,2},{1,3},{2,0},{3,1},{4,6},{5,7},{6,4},{7,5},{8,10},{9,11},{10,... | collective-permute-start | bytes 1572872 | tf_op jit(solution)/shard_map/ppermute | solution.py:66
  420.3 13.8 %collective-permute-start.78 = (bf16[64,4096]{1,0:T(8,128)(2,1)S(1)}, bf16[64,4096]{1,0:T(8,128)(2,1)S(1)}, u32[]{:S(2)}, u32[]{:S(2)}) collective-permute-start(bf16[64,4096]{1,0:T(8,128)(2,1)S(1)} %pad_maximum_fusion.15), channel_id=1, source_target_pairs={{0,8},{1,9},{2,10},{3,11},{4,12},{5,13},{6,14},{7,15},{8,0},{9,1},... | collective-permute-start | bytes 1572872 | tf_op jit(solution)/shard_map/ppermute | solution.py:66
  441.2 16.7 %collective-permute-start.79 = (bf16[512,512]{1,0:T(8,128)(2,1)}, bf16[512,512]{1,0:T(8,128)(2,1)}, u32[]{:S(2)}, u32[]{:S(2)}) collective-permute-start(bf16[512,512]{1,0:T(8,128)(2,1)} %slice.719), channel_id=1, source_target_pairs={{0,1},{1,0},{2,3},{3,2},{4,5},{5,4},{6,7},{7,6},{8,9},{9,8},{10,11... | collective-permute-start | bytes 1572872 | tf_op jit(solution)/shard_map/ppermute | solution.py:66
  442.4 15.3 %collective-permute-start.81 = (bf16[128,1024]{1,0:T(8,128)(2,1)}, bf16[128,1024]{1,0:T(8,128)(2,1)}, u32[]{:S(2)}, u32[]{:S(2)}) collective-permute-start(bf16[128,1024]{1,0:T(8,128)(2,1)} %get-tuple-element.782), channel_id=1, source_target_pairs={{0,4},{1,5},{2,6},{3,7},{4,0},{5,1},{6,2},{7,3},{8,12},{9,13},{10,... | collective-permute-start | bytes 786440 | tf_op jit(solution)/shard_map/ppermute | solution.py:66
  442.9 15.0 %collective-permute-start.80 = (bf16[32,4096]{1,0:T(8,128)(2,1)}, bf16[32,4096]{1,0:T(8,128)(2,1)}, u32[]{:S(2)}, u32[]{:S(2)}) collective-permute-start(bf16[32,4096]{1,0:T(8,128)(2,1)} %add_convert_fusion.34), channel_id=1, source_target_pairs={{0,16},{1,17},{2,18},{3,19},{4,20},{5,21},{6,22},{7,23},{8,24},{9,... | collective-permute-start | bytes 786440 | tf_op jit(solution)/shard_map/ppermute | solution.py:66
  463.5 27.4 %collective-permute-start.82 = (bf16[256,2304]{1,0:T(8,128)(2,1)S(1)}, bf16[256,2304]{1,0:T(8,128)(2,1)S(1)}, u32[]{:S(2)}, u32[]{:S(2)}) collective-permute-start(bf16[256,2304]{1,0:T(8,128)(2,1)S(1)} %pad_maximum_fusion.4), channel_id=1, source_target_pairs={{0,2},{1,3},{2,0},{3,1},{4,6},{5,7},{6,4},{7,5},{8,10},{9,11},{10,... | collective-permute-start | bytes 3538952 | tf_op jit(solution)/shard_map/ppermute | solution.py:66
  464.6 27.0 %collective-permute-start.83 = (bf16[256,2304]{1,0:T(8,128)(2,1)S(1)}, bf16[256,2304]{1,0:T(8,128)(2,1)S(1)}, u32[]{:S(2)}, u32[]{:S(2)}) collective-permute-start(bf16[256,2304]{1,0:T(8,128)(2,1)S(1)} %pad_maximum_fusion.5), channel_id=1, source_target_pairs={{0,4},{1,5},{2,6},{3,7},{4,0},{5,1},{6,2},{7,3},{8,12},{9,13},{10,... | collective-permute-start | bytes 3538952 | tf_op jit(solution)/shard_map/ppermute | solution.py:66
  466.1 20.9 %collective-permute-start.86 = (bf16[64,4096]{1,0:T(8,128)(2,1)S(1)}, bf16[64,4096]{1,0:T(8,128)(2,1)S(1)}, u32[]{:S(2)}, u32[]{:S(2)}) collective-permute-start(bf16[64,4096]{1,0:T(8,128)(2,1)S(1)} %pad_maximum_fusion.17), channel_id=1, source_target_pairs={{0,8},{1,9},{2,10},{3,11},{4,12},{5,13},{6,14},{7,15},{8,0},{9,1},... | collective-permute-start | bytes 1572872 | tf_op jit(solution)/shard_map/ppermute | solution.py:66
  470.9 16.2 %collective-permute-start.85 = (bf16[16,8192]{1,0:T(8,128)(2,1)S(1)}, bf16[16,8192]{1,0:T(8,128)(2,1)S(1)}, u32[]{:S(2)}, u32[]{:S(2)}) collective-permute-start(bf16[16,8192]{1,0:T(8,128)(2,1)S(1)} %constant_dynamic-update-slice_fusion.50), channel_id=1, source_target_pairs={{0,8},{1,9},{2,10},{3,11},{4,12},{5,13},{6,14},{7,15},{8,0},{9,1},... | collective-permute-start | bytes 786440 | tf_op jit(solution)/shard_map/ppermute | solution.py:66
  491.7 15.1 %collective-permute-start.90 = (bf16[32,5120]{1,0:T(8,128)(2,1)S(1)}, bf16[32,5120]{1,0:T(8,128)(2,1)S(1)}, u32[]{:S(2)}, u32[]{:S(2)}) collective-permute-start(bf16[32,5120]{1,0:T(8,128)(2,1)S(1)} %slice.875), channel_id=1, source_target_pairs={{0,4},{1,5},{2,6},{3,7},{4,0},{5,1},{6,2},{7,3},{8,12},{9,13},{10,... | collective-permute-start | bytes 983048 | tf_op jit(solution)/shard_map/ppermute | solution.py:66
  494.4 12.5 %collective-permute-start.89 = (bf16[32,4096]{1,0:T(8,128)(2,1)S(1)}, bf16[32,4096]{1,0:T(8,128)(2,1)S(1)}, u32[]{:S(2)}, u32[]{:S(2)}) collective-permute-start(bf16[32,4096]{1,0:T(8,128)(2,1)S(1)} %add_convert_fusion.30), channel_id=1, source_target_pairs={{0,16},{1,17},{2,18},{3,19},{4,20},{5,21},{6,22},{7,23},{8,24},{9,... | collective-permute-start | bytes 786440 | tf_op jit(solution)/shard_map/ppermute | solution.py:66
  496.1 14.7 %collective-permute-start.88 = (bf16[128,2304]{1,0:T(8,128)(2,1)S(1)}, bf16[128,2304]{1,0:T(8,128)(2,1)S(1)}, u32[]{:S(2)}, u32[]{:S(2)}) collective-permute-start(bf16[128,2304]{1,0:T(8,128)(2,1)S(1)} %get-tuple-element.730), channel_id=1, source_target_pairs={{0,2},{1,3},{2,0},{3,1},{4,6},{5,7},{6,4},{7,5},{8,10},{9,11},{10,... | collective-permute-start | bytes 1769480 | tf_op jit(solution)/shard_map/ppermute | solution.py:66
  497.7 14.6 %collective-permute-start.87 = (bf16[128,2304]{1,0:T(8,128)(2,1)S(1)}, bf16[128,2304]{1,0:T(8,128)(2,1)S(1)}, u32[]{:S(2)}, u32[]{:S(2)}) collective-permute-start(bf16[128,2304]{1,0:T(8,128)(2,1)S(1)} %get-tuple-element.732), channel_id=1, source_target_pairs={{0,4},{1,5},{2,6},{3,7},{4,0},{5,1},{6,2},{7,3},{8,12},{9,13},{10,... | collective-permute-start | bytes 1769480 | tf_op jit(solution)/shard_map/ppermute | solution.py:66
  512.3 15.1 %collective-permute-start.94 = (bf16[64,5120]{1,0:T(8,128)(2,1)S(1)}, bf16[64,5120]{1,0:T(8,128)(2,1)S(1)}, u32[]{:S(2)}, u32[]{:S(2)}) collective-permute-start(bf16[64,5120]{1,0:T(8,128)(2,1)S(1)} %constant_dynamic-update-slice_fusion.56), channel_id=1, source_target_pairs={{0,2},{1,3},{2,0},{3,1},{4,6},{5,7},{6,4},{7,5},{8,10},{9,11},{10,... | collective-permute-start | bytes 1966088 | tf_op jit(solution)/shard_map/ppermute | solution.py:66
  515.4 12.0 %collective-permute-start.92 = (bf16[64,4608]{1,0:T(8,128)(2,1)S(1)}, bf16[64,4608]{1,0:T(8,128)(2,1)S(1)}, u32[]{:S(2)}, u32[]{:S(2)}) collective-permute-start(bf16[64,4608]{1,0:T(8,128)(2,1)S(1)} %pad_maximum_fusion.13), channel_id=1, source_target_pairs={{0,8},{1,9},{2,10},{3,11},{4,12},{5,13},{6,14},{7,15},{8,0},{9,1},... | collective-permute-start | bytes 1769480 | tf_op jit(solution)/shard_map/ppermute | solution.py:66
  528.4 21.9 %collective-permute-start.97 = (bf16[32,4608]{1,0:T(8,128)(2,1)}, bf16[32,4608]{1,0:T(8,128)(2,1)}, u32[]{:S(2)}, u32[]{:S(2)}) collective-permute-start(bf16[32,4608]{1,0:T(8,128)(2,1)} %get-tuple-element.747), channel_id=1, source_target_pairs={{0,16},{1,17},{2,18},{3,19},{4,20},{5,21},{6,22},{7,23},{8,24},{9,... | collective-permute-start | bytes 884744 | tf_op jit(solution)/shard_map/ppermute | solution.py:66
  530.9 11.1 %collective-permute-start.95 = (bf16[128,5120]{1,0:T(8,128)(2,1)}, bf16[128,5120]{1,0:T(8,128)(2,1)}, u32[]{:S(2)}, u32[]{:S(2)}) collective-permute-start(bf16[128,5120]{1,0:T(8,128)(2,1)} %pad_maximum_fusion.3), channel_id=1, source_target_pairs={{0,1},{1,0},{2,3},{3,2},{4,5},{5,4},{6,7},{7,6},{8,9},{9,8},{10,11... | collective-permute-start | bytes 3932168 | tf_op jit(solution)/shard_map/ppermute | solution.py:66
  (261 other events, 2327.6 us)
